TPU v7x, 32 devices: a whole 2x2x4 slice. The times are simulated.
32 devices in a mesh: fields: 2 (over x), vel: 8 (over z, y), rows: 2 (over core).
Axes of the slice: x: 2, y: 2, z: 4, core: 2. Of those that a mesh axis runs over, the one named last changes fastest.
Arguments:
- images: float32 [16, 64, 4096], P(('fields', 'vel'), 'rows'), parts along dimension 0, may hold values from -6 to 6
- variance: float32 [16, 64, 4096], P(('fields', 'vel'), 'rows'), parts along dimension 0, may hold values from 0.5 to 2
- spread_kernel: float32 [21, 21], replicated, may hold values from 0.05 to 1
- shifts: int32 [576, 3, 2], P(('fields', 'vel')), parts along dimension 0, may hold values from -16 to 16, as said below
- epoch_owner: int32 [6], P('fields'), parts along dimension 0, may hold values from 0 to 7, as said below
- valid_rows: int32 [6, 2], P('fields'), parts along dimension 0, may hold values from 0 to 64, as said below
Outputs:
- likelihood: float32 [576, 64, 4096], P(('fields', 'vel'), 'rows'), parts along dimension 0
There are 2 independent parts, one for each index of `fields`. A program takes and returns all parts, laid end to end along the dimension named above; an argument that names none is the same for every part. Nothing has to cross between parts.
Inputs may be any that keep to these rules, and one draw needn't show every extreme that they name: `shifts`: each entry lies in -16 to 16; both ends are taken in every draw. `epoch_owner`: the epochs are held by distinct slots. `valid_rows`: in each row the first entry is below the second; the first epoch starts at row 0 and the last ends at row 64.
All inputs are finite; a program needn't handle non-finite values.
Results may differ from a plain program's by a relative error of at most 0.0003.
Values sent between devices are 32-bit elements; how exact they have to be, the bound alone decides.
No kernel may reach another device: no remote copies, remote signals or barrier semaphores. Data moves between devices by JAX's collectives and lax.ppermute only.
A program may use at most 128 MiB of HBM per device.

v0:
```python
import jax
import jax.numpy as jnp
from jax import lax
from jax.sharding import PartitionSpec as P

MAXS = 16
EPOCHS = 3


def with_halo(value, sides, width):
    for axis, dim in sides:
        count, length = (lax.axis_size(axis), value.shape[dim])
        up = [(i, (i + 1) % count) for i in range(count - 1)]
        down = [(j, i) for i, j in up]
        last = lax.slice_in_dim(value, length - width, length, axis=dim)
        initial = lax.slice_in_dim(value, 0, width, axis=dim)
        before = lax.ppermute(last, axis, up)
        after = lax.ppermute(initial, axis, down)
        value = jnp.concatenate([before, value, after], axis=dim)
    return value


def spread(value, axis, root):
    mine = lax.axis_index(axis) == root
    return lax.psum(jnp.where(mine, value, jnp.zeros_like(value)), axis)


def band_matrix(kernels, ksize):
    inner = jnp.arange(128 + ksize - 1, dtype=jnp.int32)[:, None, None]
    outer = jnp.arange(128, dtype=jnp.int32)[None, :, None]
    offsets = jnp.arange(ksize, dtype=jnp.int32)[None, None, :]
    onehot = (inner - outer == offsets).astype(jnp.float32)
    return jnp.einsum("fkj,cdj->fkcd", kernels, onehot, precision=lax.Precision.HIGHEST)


def correlate_pair(extended, banded, ksize):
    half = ksize // 2
    height = extended.shape[1] - (ksize - 1)
    columns = extended.shape[2]
    blocks = columns // 128
    padded = jnp.pad(extended, ((0, 0), (0, 0), (half, 128 - half)))

    def add_row(offset, summed):
        row_band = lax.dynamic_slice_in_dim(padded, offset, height, 1)
        leading = row_band[:, :, :columns].reshape(2, height, blocks, 128)
        trailing = row_band[:, :, 128:].reshape(2, height, blocks, 128)[..., : ksize - 1]
        window = jnp.concatenate([leading, trailing], axis=3)
        weights = lax.dynamic_index_in_dim(banded, offset, 1, keepdims=False)
        return summed + jnp.einsum(
            "fhbc,fcd->fhbd", window, weights, precision=lax.Precision.HIGHEST
        )

    summed = lax.fori_loop(0, ksize, add_row, jnp.zeros((2, height, blocks, 128), jnp.float32))
    return summed.reshape(2, height, columns)


def local(images, variance, spread_kernel, shifts, epoch_owner, valid_rows):
    exposure = images[0]
    noise_var = variance[0]
    band_rows = exposure.shape[0]
    columns = exposure.shape[1]
    ksize = spread_kernel.shape[0]
    half = ksize // 2
    kernel_norm = spread_kernel / jnp.sum(spread_kernel)
    kernel_sq = kernel_norm * kernel_norm
    floor = 0.5 * jnp.sum(kernel_sq)
    vel_index = lax.axis_index("vel")
    row_index = lax.axis_index("rows")
    owned = epoch_owner == vel_index
    lower_row = jnp.sum(jnp.where(owned, valid_rows[:, 0], 0))
    upper_row = jnp.sum(jnp.where(owned, valid_rows[:, 1], 0))
    row_ids = row_index * band_rows + jnp.arange(band_rows, dtype=jnp.int32)[:, None]
    usable = (row_ids >= lower_row) & (row_ids < upper_row)
    weighted = jnp.where(usable, exposure / noise_var, jnp.float32(0.0))
    inverse = jnp.where(usable, 1.0 / noise_var, jnp.float32(0.0))
    fields_pair = jnp.stack([weighted, inverse])
    extended = with_halo(fields_pair, (("rows", 1),), half)
    banded = band_matrix(jnp.stack([kernel_norm, kernel_sq]), ksize)
    correlated = correlate_pair(extended, banded, ksize)
    narrow = jnp.stack([spread(correlated, "vel", epoch_owner[epoch]) for epoch in range(EPOCHS)])
    stacked = with_halo(narrow, (("rows", 2),), MAXS)
    padded_all = jnp.pad(stacked, ((0, 0), (0, 0), (0, 0), (128, 128)))

    def one_velocity(shift):
        summed = jnp.zeros((2, band_rows, columns), jnp.float32)
        for epoch in range(EPOCHS):
            start_row = MAXS + shift[epoch, 0]
            start_col = 128 + shift[epoch, 1]
            summed = summed + lax.dynamic_slice(
                padded_all[epoch], (jnp.int32(0), start_row, start_col), (2, band_rows, columns)
            )
        return summed[0] / jnp.sqrt(jnp.maximum(summed[1], floor))

    return lax.map(one_velocity, shifts)


def solution(mesh):
    in_specs = (
        P(("fields", "vel"), "rows", None),
        P(("fields", "vel"), "rows", None),
        P(),
        P(("fields", "vel"), None, None),
        P("fields"),
        P("fields", None),
    )
    out_specs = P(("fields", "vel"), "rows", None)
    return jax.shard_map(local, mesh=mesh, in_specs=in_specs, out_specs=out_specs, check_vma=False)
```

profile of v0, /device:TPU:0, one launch (start us, length us, event | category | flops | bytes accessed | tf_op | source)
XLA Modules:
  0.0 799.3 jit_solution(17309083965974283387)
XLA Ops:
  25.3 131.3 %while.28 = (s32[]{:T(128)}, f32[2,32,32,128]{3,2,1,0:T(8,128)S(1)}, f32[2,52,4224]{2,1,0:T(8,128)}, f32[2,21,148,128]{3,1,2,0:T(8,128)}, s32[]{:T(128)}, /*index=5*/s32[]{:T(128)}, s32[]{}) while((s32[]{:T(128)}, f32[2,32,32,128]{3,2,1,0:T(8,128)S(1)}, f32[2,52,4224]{2,1,0:T(8,128)}, f32[2,21,148,128]{3,1,2,0:T(8,128)}, ...), condition=%wide.region_4.5_spmd.clone, body=%wide.region_3.4_spmd.clone.sunk | while | flops 466395136 | bytes 12152943 | solution.py:53
  162.7 133.0 %all-reduce.5.cloned.1.call-done = (f32[1,2,32,4096]{3,2,1,0:T(8,128)}, f32[1,2,32,4096]{3,2,1,0:T(8,128)}, f32[1,2,32,4096]{3,2,1,0:T(8,128)}) async-done(((f32[1,2,32,4096]{3,2,1,0:T(8,128)}, f32[1,2,32,4096]{3,2,1,0:T(8,128)}, f32[1,2,32,4096]{3,2,1,0:T(8,128)}), (f32[1,2,32,4096]{3,2,1,0:T(8,128)}, f32[1,2,32,4096]{3,2,1,0:T(8,128)}, f32[1,2,32,4096]{3,2,1,0:T(8,128)})) %all-reduce.5.cloned.1.call-update) | async-done | bytes 3145744 | tf_op jit(solution)/shard_map/psum | solution.py:25
  304.6 3.5 collective-permute-done.3
  308.1 4.4 select_maximum_fusion
  312.5 480.0 %while.27 = (s32[]{:T(128)}, f32[36,32,4096]{2,1,0:T(8,128)}, f32[3,2,64,4352]{3,2,1,0:T(8,128)}, s32[36,3,2]{1,2,0:T(2,128)S(1)}, f32[]{:T(128)}, /*index=5*/s3...) while((s32[]{:T(128)}, f32[36,32,4096]{2,1,0:T(8,128)}, ...), condition=%wide.region_10.11_spmd, body=%wide.region_9.10_spmd.sunk | while | flops 786458 | bytes 19138044 | solution.py:94
  320.6 3.4 fusion.36
  334.0 3.4 fusion.36
  347.3 3.4 fusion.36
  360.6 3.4 fusion.36
  373.9 3.4 fusion.36
  387.3 3.4 fusion.36
  400.6 3.4 fusion.36
  413.9 3.4 fusion.36
  427.3 3.4 fusion.36
  440.6 3.4 fusion.36
  454.0 3.4 fusion.36
  467.3 3.4 fusion.36
  480.6 3.4 fusion.36
  494.0 3.4 fusion.36
  507.3 3.4 fusion.36
  520.6 3.4 fusion.36
  534.0 3.4 fusion.36
  547.3 3.4 fusion.36
  560.6 3.4 fusion.36
  (306 shorter events, 307.7 us)
Async XLA Ops:
  6.5 10.8 %copy-start.3 = (s32[3]{0:T(128)S(1)}, s32[3]{0:T(128)}, u32[]{:S(2)}) copy-start(s32[3]{0:T(128)} %param.14) | copy-start | bytes 40
  6.5 8.9 %copy-start.2 = (f32[21,21]{1,0:T(8,128)S(1)}, f32[21,21]{1,0:T(8,128)}, u32[]{:S(2)}) copy-start(f32[21,21]{1,0:T(8,128)} %param.12) | copy-start | bytes 5296
  6.5 289.2 %all-reduce.5.cloned.1.call-start = ((), (), s32[]{:S(2)}) async-start(), calls=%async_computation | async-start | bytes 6291456 | tf_op jit(solution)/shard_map/psum | solution.py:25
  11.7 11.6 %collective-permute-start = (f32[2,10,4096]{2,1,0:T(8,128)}, f32[2,10,4096]{2,1,0:T(8,128)S(1)}, u32[]{:S(2)}, u32[]{:S(2)}) collective-permute-start(f32[2,10,4096]{2,1,0:T(8,128)} %get-tuple-element.238), channel_id=1, source_target_pairs={{0,1},{2,3},{4,5},{6,7},{8,9},{10,11},{12,13},{14,15},{16,17},{18,... | collective-permute-start | bytes 983048 | tf_op jit(solution)/shard_map/ppermute | solution.py:17
  14.1 9.2 %collective-permute-start.1 = (f32[2,10,4096]{2,1,0:T(8,128)}, f32[2,10,4096]{2,1,0:T(8,128)S(1)}, u32[]{:S(2)}, u32[]{:S(2)}) collective-permute-start(f32[2,10,4096]{2,1,0:T(8,128)} %get-tuple-element.239), channel_id=1, source_target_pairs={{1,0},{3,2},{5,4},{7,6},{9,8},{11,10},{13,12},{15,14},{17,16},{19,... | collective-permute-start | bytes 983048 | tf_op jit(solution)/shard_map/ppermute | solution.py:18
  295.8 1.5 copy-start.1
  295.8 1.9 copy-start
  297.7 6.1 copy-start.4
  299.5 5.1 collective-permute-start.2
  302.5 5.6 collective-permute-start.3
Sparse Core Ops, SparseCore 0:
  162.9 132.8 all-reduce.4
where the time goes:
time: 805 us; the launch traced here: 799 us
  loops' own time  270 us (34%)
  local copies, waits for them, and re-layouts  238 us (30%)
  waiting for transfers between devices  137 us (17%)
  other arithmetic  79.5 us (10%)
  matrix products  51.7 us (6%)
  between operations  16.1 us (2%)
    another operation x1, loops' own time, local(): return lax.map(one_velocity, shifts)  269 us
    psum x1, waiting for transfers between devices, spread(): return lax.psum(jnp.where(mine, value, jnp.zeros_like(value)), axis)  133 us
    slice x36, local copies, waits for them, and re-layouts, one_velocity(): padded_all[epoch]  123 us
    dot_general x21, matrix products, add_row(): jnp.einsum('fhbc,fcd->fhbd', window, weights, precision=lax.Precision.HIG...  48.3 us
    slice x21, local copies, waits for them, and re-layouts, add_row(): leading = row_band[:, :, :columns].reshape(2, height, blocks, 128)  44.7 us
    add x36, other arithmetic, one_velocity(): summed + lax.dynamic_slice(padded_all[epoch], (jnp.int32(0), start_row, s...  33.2 us
    dynamic_update_slice x36, other arithmetic, local(): return lax.map(one_velocity, shifts)  31.5 us
    dynamic_slice x21, local copies, waits for them, and re-layouts, add_row(): weights = lax.dynamic_index_in_dim(banded, offset, 1, keepdims=False)  29.3 us
  transfers between devices with their start and end apart: 5, of which 3 were waited for; matrix products, arithmetic and copies ran while one was open for 1% of the time, Pallas kernels for 0%

commit v1 on v0

v1 whole, which is shorter than its diff:
```python
import functools
import jax
import jax.numpy as jnp
from jax import lax
from jax.experimental import pallas as pl
from jax.experimental.pallas import tpu as pltpu
from jax.sharding import PartitionSpec as P

LANES = 128
MAXS = 16
VMEM = 48 << 20


def band_kernel(taps, high_ref, both_ref):
    kinds, ksize = both_ref.shape[0], both_ref.shape[1]
    skip = LANES - MAXS - ksize // 2
    inner = lax.broadcasted_iota(jnp.int32, (2 * LANES, LANES), 0)
    outer = lax.broadcasted_iota(jnp.int32, (2 * LANES, LANES), 1)
    offset = inner - outer - skip

    def one(index, _):
        kind, row = index // ksize, index % ksize
        band = jnp.zeros((2 * LANES, LANES), jnp.float32)
        for col in range(ksize):
            band = jnp.where(offset == col, taps[index * ksize + col], band)
        high = band.astype(jnp.bfloat16)
        low = (band - high.astype(jnp.float32)).astype(jnp.bfloat16)
        high_ref[kind, row] = high
        both_ref[kind, row, :, :LANES] = high
        both_ref[kind, row, :, LANES:] = low
        return 0

    lax.fori_loop(0, kinds * ksize, one, 0)


def bands(taps, ksize):
    shape = (2, ksize, 2 * LANES)
    return pl.pallas_call(
        band_kernel,
        in_specs=[pl.BlockSpec(memory_space=pltpu.SMEM)],
        out_specs=[pl.BlockSpec(memory_space=pltpu.VMEM)] * 2,
        out_shape=[
            jax.ShapeDtypeStruct(shape + (LANES,), jnp.bfloat16),
            jax.ShapeDtypeStruct(shape + (2 * LANES,), jnp.bfloat16),
        ],
        compiler_params=pltpu.CompilerParams(vmem_limit_bytes=VMEM),
        cost_estimate=pl.CostEstimate(flops=0, bytes_accessed=24 << 20, transcendentals=0),
    )(taps)


def correlate_kernel(place, wide, border, high_ref, both_ref, edge_ref, inner_ref, ext, summed):
    epochs, kinds, height, width = wide.shape
    ksize = high_ref.shape[1]
    tiles = width // LANES - 1
    first, lower = place[0] == 0, place[1]
    at_border = pl.multiple_of((1 - lower) * (MAXS + height), MAXS)
    ext[...] = jnp.zeros_like(ext)
    for tile in range(tiles + 1):
        columns = slice(tile * LANES, (tile + 1) * LANES)
        ext[:, :, tile, MAXS : MAXS + height] = wide[:, :, :, columns]
        ext[:, :, tile, pl.ds(at_border, MAXS)] = border[:, :, :, columns]

    blank = tiles + 1
    ahead = jnp.where(first, blank, 0)
    windows = [(ahead, 1)] + [(tile, tile + 1) for tile in range(1, tiles)] + [(0, blank)]
    lane = lax.broadcasted_iota(jnp.int32, (height, LANES), 1)
    wrapped = jnp.logical_and(first, lane < MAXS)
    for kind in range(kinds):
        summed[...] = jnp.zeros_like(summed)

        def add_row(row, _):
            rows = pl.ds(row + MAXS - ksize // 2, height)
            window = jnp.concatenate(
                [
                    jnp.concatenate([ext[epoch, kind, left, rows], ext[epoch, kind, right, rows]], axis=1)
                    for epoch in range(epochs)
                    for left, right in windows
                ],
                axis=0,
            )
            high = window.astype(jnp.bfloat16)
            low = (window - high.astype(jnp.float32)).astype(jnp.bfloat16)
            pair = jnp.dot(high, both_ref[kind, row], preferred_element_type=jnp.float32)
            rest = jnp.dot(low, high_ref[kind, row], preferred_element_type=jnp.float32)
            summed[...] += pair[:, :LANES] + (pair[:, LANES:] + rest)
            return 0

        lax.fori_loop(0, ksize, add_row, 0)
        for epoch in range(epochs):
            base = epoch * (tiles + 1) * height
            over = base + tiles * height
            summed[base : base + height] = jnp.where(
                wrapped, summed[over : over + height], summed[base : base + height]
            )
            for tile in range(tiles):
                start = base + tile * height
                at_edge = pl.multiple_of(start + (1 - lower) * (height - MAXS), MAXS)
                at_inner = pl.multiple_of(start + lower * MAXS, MAXS)
                edge_ref[epoch, kind, tile] = summed[pl.ds(at_edge, MAXS)]
                inner_ref[epoch, kind, tile] = summed[pl.ds(at_inner, MAXS)]


def correlate(place, wide, border, high, both):
    epochs, kinds, height, width = wide.shape
    tiles = width // LANES - 1
    half = jax.ShapeDtypeStruct((epochs, kinds, tiles, MAXS, LANES), jnp.float32)
    flops = 3 * 2 * epochs * kinds * (tiles + 1) * height * high.shape[1] * 2 * LANES * LANES
    return pl.pallas_call(
        correlate_kernel,
        in_specs=[pl.BlockSpec(memory_space=pltpu.SMEM)] + [pl.BlockSpec(memory_space=pltpu.VMEM)] * 4,
        out_specs=[pl.BlockSpec(memory_space=pltpu.VMEM)] * 2,
        out_shape=[half, half],
        scratch_shapes=[
            pltpu.VMEM((epochs, kinds, tiles + 2, height + 2 * MAXS, LANES), jnp.float32),
            pltpu.VMEM((epochs * (tiles + 1) * height, LANES), jnp.float32),
        ],
        compiler_params=pltpu.CompilerParams(vmem_limit_bytes=VMEM),
        cost_estimate=pl.CostEstimate(flops=flops, bytes_accessed=12 << 20, transcendentals=0),
    )(place, wide, border, high, both)


def stack_kernel(place, shifts, floor, *refs, group, parts, blocks):
    sources, out_ref, held = refs[: 6 * parts], refs[-2], refs[-1]
    part, base = pl.program_id(0), pl.program_id(1) * group
    epochs, kinds, count = held.shape[0], held.shape[1], held.shape[2]
    tiles = count - 1
    lower = place[parts]
    lane = lax.broadcasted_iota(jnp.int32, (1, LANES), 1)
    at = [pl.multiple_of(row, MAXS) for row in (32 - 16 * lower, 16 + 16 * lower, 48 - 48 * lower)]

    for index in range(parts):

        @pl.when(jnp.logical_and(part == index, pl.program_id(1) == 0))
        def _():
            block = place[index]
            keep_first = jnp.where(jnp.logical_and(block == 0, lane < MAXS), 0.0, 1.0) > 0.5
            keep_last = jnp.where(jnp.logical_and(block == blocks - 1, lane >= MAXS), 0.0, 1.0) > 0.5
            blank = pl.multiple_of(48 * lower, MAXS)
            held[:, :, :, pl.ds(blank, MAXS)] = jnp.zeros((epochs, kinds, count, MAXS, LANES), jnp.float32)
            for piece in range(3):
                own, nearby = sources[6 * index + piece], sources[6 * index + 3 + piece]
                rows = pl.ds(at[piece], MAXS)
                for epoch in range(epochs):
                    for kind in range(kinds):
                        held[epoch, kind, 0, rows] = jnp.where(keep_first, own[epoch, kind, 0], 0.0)
                        for tile in range(1, tiles):
                            held[epoch, kind, tile, rows] = own[epoch, kind, tile]
                        held[epoch, kind, tiles, rows] = jnp.where(keep_last, nearby[epoch, kind, 0], 0.0)

    low = floor[0]
    height = out_ref.shape[1]
    across = lax.broadcasted_iota(jnp.int32, (8, LANES), 1)

    def one_velocity(local_index, _):
        start = (base + local_index) * epochs * 2
        rows = [shifts[start + 2 * epoch] + MAXS for epoch in range(epochs)]
        cols = [shifts[start + 2 * epoch + 1] + MAXS for epoch in range(epochs)]
        beyond = [across < col for col in cols]
        turn = [jnp.where(col == 0, 0, LANES - col) for col in cols]
        for top in range(0, height, 8):
            totals = [[None] * tiles for _ in range(kinds)]
            for epoch in range(epochs):
                for kind in range(kinds):
                    loaded = [held[epoch, kind, tile, pl.ds(rows[epoch] + top, 8)] for tile in range(count)]
                    for tile in range(tiles):
                        merged = jnp.where(beyond[epoch], loaded[tile + 1], loaded[tile])
                        moved = pltpu.roll(merged, turn[epoch], 1)
                        totals[kind][tile] = moved if epoch == 0 else totals[kind][tile] + moved
            for tile in range(tiles):
                out_ref[local_index, top : top + 8, tile * LANES : (tile + 1) * LANES] = totals[0][tile] * lax.rsqrt(
                    jnp.maximum(totals[1][tile], low)
                )
        return 0

    lax.fori_loop(0, group, one_velocity, 0)


def stack_blocks(place, shifts, floor, sources, out, out_shape, parts, blocks):
    epochs, kinds, tiles = sources[0].shape[:3]
    velocities, height, columns = out_shape.shape
    group = next(size for size in (12, 9, 8, 6, 4, 3, 2, 1) if velocities % size == 0)
    width = tiles * LANES
    whole = pl.BlockSpec((epochs, kinds, tiles, MAXS, LANES), lambda *_: (0, 0, 0, 0, 0))
    front = pl.BlockSpec((epochs, kinds, 1, MAXS, LANES), lambda *_: (0, 0, 0, 0, 0))
    in_specs = [whole] * 3 + [front] * 3
    in_specs = in_specs * parts
    operands = list(sources)
    aliases = {}
    if out is not None:
        in_specs.append(pl.BlockSpec(memory_space=pl.ANY))
        operands.append(out)
        aliases = {3 + len(sources): 0}
    work = parts * velocities * height * width
    return pl.pallas_call(
        functools.partial(stack_kernel, group=group, parts=parts, blocks=blocks),
        grid_spec=pltpu.PrefetchScalarGridSpec(
            num_scalar_prefetch=3,
            grid=(parts, velocities // group),
            in_specs=in_specs,
            out_specs=pl.BlockSpec((group, height, width), lambda part, chunk, place, *_: (chunk, 0, place[part])),
            scratch_shapes=[pltpu.VMEM((epochs, kinds, tiles + 1, height + 2 * MAXS, LANES), jnp.float32)],
        ),
        out_shape=out_shape,
        input_output_aliases=aliases,
        compiler_params=pltpu.CompilerParams(vmem_limit_bytes=VMEM),
        cost_estimate=pl.CostEstimate(flops=16 * work, bytes_accessed=16 * work, transcendentals=work),
    )(place, shifts, floor, *operands)


def local(images, variance, spread_kernel, shifts, epoch_owner, valid_rows):
    exposure, noise_var = images[0], variance[0]
    height, columns = exposure.shape
    ksize = spread_kernel.shape[0]
    epochs = epoch_owner.shape[0]
    blocks = lax.axis_size("vel")
    width = columns // blocks
    me, lower = lax.axis_index("vel"), lax.axis_index("rows")
    swap = [(0, 1), (1, 0)]

    order = list(range(0, blocks, 2)) + list(range(1, blocks, 2))[::-1]
    right = [(order[i], order[(i + 1) % blocks]) for i in range(blocks)]
    left = [(b, a) for a, b in right]

    def position(index):
        return jnp.where(index % 2 == 0, index // 2, blocks - 1 - index // 2)

    mine = position(me)
    kernel_norm = spread_kernel / jnp.sum(spread_kernel)
    kernel_sq = kernel_norm * kernel_norm
    floor = (0.5 * jnp.sum(kernel_sq)).reshape(1)
    high, both = bands(jnp.stack([kernel_norm, kernel_sq]).reshape(-1), ksize)

    chunks = []
    for step in range(blocks):
        start = position(me ^ step) * width
        chunk = jnp.stack(
            [
                lax.dynamic_slice_in_dim(exposure, start, width, 1),
                lax.dynamic_slice_in_dim(noise_var, start, width, 1),
            ]
        )
        if step:
            chunk = lax.ppermute(chunk, "vel", [(i, i ^ step) for i in range(blocks)])
        chunks.append(chunk)
    row_ids = lower * height + jnp.arange(height, dtype=jnp.int32)[:, None]
    fields = []
    for epoch in range(epochs):
        key = epoch_owner[epoch] ^ me
        chosen = chunks[0]
        for step in range(1, blocks):
            chosen = jnp.where(key == step, chunks[step], chosen)
        usable = (row_ids >= valid_rows[epoch, 0]) & (row_ids < valid_rows[epoch, 1])
        fields.append(
            jnp.stack([jnp.where(usable, chosen[0] / chosen[1], 0.0), jnp.where(usable, 1.0 / chosen[1], 0.0)])
        )
    field = jnp.stack(fields)
    before = lax.ppermute(field[..., width - LANES :], "vel", right)
    wide = jnp.concatenate([before, field], axis=3)
    border = lax.ppermute(jnp.where(lower == 0, wide[:, :, height - MAXS :], wide[:, :, :MAXS]), "rows", swap)
    place = jnp.stack([mine, lower]).astype(jnp.int32)
    edge, inner = correlate(place, wide, border, high, both)

    def with_border(edge, inner):
        return edge, inner, lax.ppermute(edge, "rows", swap)

    flat_shifts = shifts.reshape(-1)
    out_shape = jax.ShapeDtypeStruct((shifts.shape[0], height, columns), jnp.float32)
    have = {0: with_border(edge, inner)}
    out = None
    half = blocks // 2
    for step in range(1, half + 1):
        if step < half:
            for sign, ring in ((-1, right), (1, left)):
                edge, inner, _ = have[sign * (step - 1)]
                have[sign * step] = with_border(
                    lax.ppermute(edge, "vel", ring), lax.ppermute(inner, "vel", ring)
                )
        else:
            edge = lax.ppermute(have[1 - step][0], "vel", right)
            inner = lax.ppermute(have[step - 1][1], "vel", left)
            have[step] = have[-step] = with_border(edge, inner)
        now = [step - 1, -step]
        sources = []
        for offset in now:
            sources += list(have[offset]) + list(have[offset + 1])
        place = jnp.stack([(mine + offset) % blocks for offset in now] + [lower]).astype(jnp.int32)
        out = stack_blocks(place, flat_shifts, floor, sources, out, out_shape, len(now), blocks)
    return out


def solution(mesh):
    in_specs = (
        P(("fields", "vel"), "rows", None),
        P(("fields", "vel"), "rows", None),
        P(),
        P(("fields", "vel"), None, None),
        P("fields"),
        P("fields", None),
    )
    out_specs = P(("fields", "vel"), "rows", None)
    return jax.shard_map(local, mesh=mesh, in_specs=in_specs, out_specs=out_specs, check_vma=False)
```

time: 805 us -> 161 us (0.20)
  loops' own time: 270 us -> 0 us
  local copies, waits for them, and re-layouts: 238 us -> 4.66 us
  waiting for transfers between devices: 137 us -> 25.3 us
  Pallas kernels: 0 us -> 86.8 us
  other arithmetic: 79.5 us -> 8.02 us
  matrix products: 51.7 us -> 0 us
  starting transfers between devices: 7.93 us -> 32.7 us
  between operations: 16.1 us -> 2.87 us
    another operation x2 -> x0, loops' own time: 270 us -> none  [the longest x1 269 us: local(): return lax.map(one_velocity, shifts)]
    slice x95 -> x2, local copies, waits for them, and re-layouts: 194 us -> 2.93 us  [the longest x1 1.55 us: local(): valid_rows[epoch, 0]]
    psum x1 -> x0, waiting for transfers between devices: 133 us -> none  [spread(): return lax.psum(jnp.where(mine, value, jnp.zeros_like(value)), axis)]
    pallas_call x0 -> x6, Pallas kernels: none -> 86.8 us  [the longest x4 61.8 us: stack_blocks(): pl.pallas_call(functools.partial(stack_kernel, group=group, parts=parts,...]
    dot_general x22 -> x0, matrix products: 51.7 us -> none  [the longest x21 48.3 us: add_row(): jnp.einsum('fhbc,fcd->fhbd', window, weights, precision=lax.Precision.HIG...]
    add x36 -> x0, other arithmetic: 33.2 us -> none  [one_velocity(): summed + lax.dynamic_slice(padded_all[epoch], (jnp.int32(0), start_row, s...]
    dynamic_update_slice x36 -> x0, other arithmetic: 31.5 us -> none  [local(): return lax.map(one_velocity, shifts)]
    dynamic_slice x21 -> x1, local copies, waits for them, and re-layouts: 29.3 us -> 1.35 us  [local(): lax.dynamic_slice_in_dim(noise_var, start, width, 1)]
  transfers between devices with their start and end apart: 5 -> 31, of which waited for: 3 -> 12; matrix products, arithmetic and copies ran while one was open for 1% -> 7% of each run, Pallas kernels for 0% -> 35%
where the time goes in v1:
time: 161 us; the launch traced here: 160 us
  Pallas kernels  86.8 us (54%)
  starting transfers between devices  32.7 us (20%)
  waiting for transfers between devices  25.3 us (16%)
  other arithmetic  8.02 us (5%)
  local copies, waits for them, and re-layouts  4.66 us (3%)
  between operations  2.87 us (2%)
    pallas_call x4, Pallas kernels, stack_blocks(): pl.pallas_call(functools.partial(stack_kernel, group=group, parts=parts,...  61.8 us
    pallas_call x1, Pallas kernels, correlate(): pl.pallas_call(correlate_kernel, in_specs=[pl.BlockSpec(memory_space=pltp...  15.4 us
    ppermute x7, starting transfers between devices, local(): chunk = lax.ppermute(chunk, 'vel', [(i, i ^ step) for i in range(blocks)])  12.8 us
    ppermute x6, waiting for transfers between devices, local(): lax.ppermute(edge, 'vel', ring)  10.3 us
    pallas_call x1, Pallas kernels, bands(): pl.pallas_call(band_kernel, in_specs=[pl.BlockSpec(memory_space=pltpu.SME...  9.72 us
    ppermute x6, waiting for transfers between devices, local(): lax.ppermute(inner, 'vel', ring)  8.33 us
    ppermute x6, starting transfers between devices, local(): lax.ppermute(inner, 'vel', ring)  8.05 us
    ppermute x7, waiting for transfers between devices, local(): chunk = lax.ppermute(chunk, 'vel', [(i, i ^ step) for i in range(blocks)])  5.72 us
  transfers between devices with their start and end apart: 31, of which 12 were waited for; matrix products, arithmetic and copies ran while one was open for 7% of the time, Pallas kernels for 35%

profile of v1, /device:TPU:0, one launch (start us, length us, event | category | flops | bytes accessed | tf_op | source)
XLA Modules:
  0.0 160.4 jit_solution(13603642829136202562)
XLA Ops:
  1.4 3.1 %collective-permute-start.5 = (f32[2,32,512]{2,1,0:T(8,128)S(1)}, f32[2,32,512]{2,1,0:T(8,128)S(1)}, u32[]{:S(2)}, u32[]{:S(2)}) collective-permute-start(f32[2,32,512]{2,1,0:T(8,128)S(1)} %pad_maximum_fusion.5), channel_id=1, source_target_pairs={{0,4},{2,6},{4,0},{6,2},{8,12},{10,14},{12,8},{14,10},{1,5},{3,7},... | collective-permute-start | bytes 393224 | tf_op jit(solution)/shard_map/ppermute | solution.py:243
  6.2 3.0 %collective-permute-start.3 = (f32[2,32,512]{2,1,0:T(8,128)S(1)}, f32[2,32,512]{2,1,0:T(8,128)S(1)}, u32[]{:S(2)}, u32[]{:S(2)}) collective-permute-start(f32[2,32,512]{2,1,0:T(8,128)S(1)} %pad_maximum_fusion.3), channel_id=1, source_target_pairs={{0,8},{2,10},{4,12},{6,14},{8,0},{10,2},{12,4},{14,6},{1,9},{3,11}... | collective-permute-start | bytes 393224 | tf_op jit(solution)/shard_map/ppermute | solution.py:243
  13.5 3.7 %collective-permute-start.1 = (f32[2,32,512]{2,1,0:T(8,128)S(1)}, f32[2,32,512]{2,1,0:T(8,128)S(1)}, u32[]{:S(2)}, u32[]{:S(2)}) collective-permute-start(f32[2,32,512]{2,1,0:T(8,128)S(1)} %pad_maximum_fusion.1), channel_id=1, source_target_pairs={{0,12},{2,14},{4,8},{6,10},{8,4},{10,6},{12,0},{14,2},{1,13},{3,15... | collective-permute-start | bytes 393224 | tf_op jit(solution)/shard_map/ppermute | solution.py:243
  20.4 2.5 %compare_and_fusion = (pred[32]{0:T(512)(128)(4,1)S(1)}, pred[32]{0:T(512)(128)(4,1)S(1)}) fusion(s32[]{:T(128)} %bitcast.14, s32[]{:T(128)} %bitcast.13, s32[]{:T(128)S(6)} %mul.31, s32[]{:T(128)} %bitcast.10, s32[]{:T(128)} %bitcast.9), kind=kLoop, calls=%fused_computation.47 | loop fusion | flops 224 | bytes 84 | tf_op jit(solution)/shard_map/and | solution.py:252
  22.9 5.7 %collective-permute-done.2 = f32[2,32,512]{2,1,0:T(8,128)S(1)} collective-permute-done((f32[2,32,512]{2,1,0:T(8,128)S(1)}, f32[2,32,512]{2,1,0:T(8,128)S(1)}, u32[]{:S(2)}, u32[]{:S(2)}) %collective-permute-start.2) | collective-permute-done | bytes 131104 | tf_op jit(solution)/shard_map/ppermute | solution.py:243
  29.3 5.1 %collective-permute-start.7 = (f32[3,2,32,128]{3,2,1,0:T(8,128)S(1)}, f32[3,2,32,128]{3,2,1,0:T(8,128)S(1)}, u32[]{:S(2)}, u32[]{:S(2)}) collective-permute-start(f32[3,2,32,128]{3,2,1,0:T(8,128)S(1)} %pad_maximum_fusion.8), channel_id=1, source_target_pairs={{0,4},{4,8},{8,12},{12,14},{14,10},{10,6},{6,2},{2,0},{1,5},{5,9},... | collective-permute-start | bytes 294920 | tf_op jit(solution)/shard_map/ppermute | solution.py:257
  36.7 2.0 %fusion.3 = (f32[1,21,21]{2,1,0:T(8,128)S(1)}, f32[1,21,21]{2,1,0:T(8,128)S(1)}, f32[]{:T(128)}) fusion(f32[21,21]{1,0:T(8,128)} %param.8, f32[]{:T(128)} %reduce_sum.18), kind=kLoop, calls=%fused_computation.56 | loop fusion | flops 1322 | bytes 5300 | tf_op jit(solution)/shard_map/stack | solution.py:231
  38.8 9.7 %shard_map.64 = (bf16[2,21,256,128]{3,2,1,0:T(8,128)(2,1)S(1)}, bf16[2,21,256,256]{3,2,1,0:T(8,128)(2,1)}) custom-call(f32[882]{0:T(1024)S(1)} %reshape.110.taps), custom_call_target="tpu_custom_call" | custom-call | bytes 25165824 | tf_op jit(solution)/shard_map/pallas_call | solution.py:38
  48.6 15.4 %shard_map.65 = (f32[3,2,4,16,128]{4,3,2,1,0:T(8,128)S(1)}, f32[3,2,4,16,128]{4,3,2,1,0:T(8,128)S(1)}) custom-call(s32[2]{0:T(128)S(1)} %pad_add_fusion.place, f32[3,2,32,640]{3,2,1,0:T(8,128)S(1)} %maximum_maximum_fusion.wide, f32[3,2,16,640]{3,2,1,0:T(8,128)S(1)} %collective-permute-done.8.border, bf16[2,21,256,128]{3,2,1,0:T(8,128)(2,1)S(1)} %get-tuple-element.9.high_ref, ...), custom_call_target="tpu_custom_call" | custom-call | flops 3963617280 | bytes 12582912 | tf_op jit(solution)/shard_map/pallas_call | solution.py:108
  64.6 1.9 %collective-permute-start.16 = (f32[3,2,4,16,128]{4,3,2,1,0:T(8,128)S(1)}, f32[3,2,4,16,128]{4,3,2,1,0:T(8,128)S(1)}, u32[]{:S(2)}, u32[]{:S(2)}) collective-permute-start(f32[3,2,4,16,128]{4,3,2,1,0:T(8,128)S(1)} %get-tuple-element.11.refs_0_.refs_9_), channel_id=1, source_target_pairs={{0,4},{4,8},{8,12},{12,14},{14,10},{10,6},{6,2},{2,0},{1,5},{5,9},... | collective-permute-start | bytes 589832 | tf_op jit(solution)/shard_map/ppermute | solution.py:276
  68.6 3.5 %collective-permute-done.9.refs_3_.refs_0_ = f32[3,2,4,16,128]{4,3,2,1,0:T(8,128)S(1)} collective-permute-done((f32[3,2,4,16,128]{4,3,2,1,0:T(8,128)S(1)}, f32[3,2,4,16,128]{4,3,2,1,0:T(8,128)S(1)}, u32[]{:S(2)}, u32[]{:S(2)}) %collective-permute-start.9) | collective-permute-done | bytes 196640 | tf_op jit(solution)/shard_map/ppermute | solution.py:276
  72.7 1.6 %collective-permute-start.17 = (f32[3,2,4,16,128]{4,3,2,1,0:T(8,128)S(1)}, f32[3,2,4,16,128]{4,3,2,1,0:T(8,128)S(1)}, u32[]{:S(2)}, u32[]{:S(2)}) collective-permute-start(f32[3,2,4,16,128]{4,3,2,1,0:T(8,128)S(1)} %collective-permute-done.16.refs_6_.refs_9_), channel_id=1, source_target_pairs={{0,4},{4,8},{8,12},{12,14},{14,10},{10,6},{6,2},{2,0},{1,5},{5,9},... | collective-permute-start | bytes 589832 | tf_op jit(solution)/shard_map/ppermute | solution.py:276
  74.3 1.9 %collective-permute-done.12.refs_4_.refs_1_ = f32[3,2,4,16,128]{4,3,2,1,0:T(8,128)S(1)} collective-permute-done((f32[3,2,4,16,128]{4,3,2,1,0:T(8,128)S(1)}, f32[3,2,4,16,128]{4,3,2,1,0:T(8,128)S(1)}, u32[]{:S(2)}, u32[]{:S(2)}) %collective-permute-start.12) | collective-permute-done | bytes 196640 | tf_op jit(solution)/shard_map/ppermute | solution.py:276
  76.9 2.0 %collective-permute-start.13 = (f32[3,2,4,16,128]{4,3,2,1,0:T(8,128)S(1)}, f32[3,2,4,16,128]{4,3,2,1,0:T(8,128)S(1)}, u32[]{:S(2)}, u32[]{:S(2)}) collective-permute-start(f32[3,2,4,16,128]{4,3,2,1,0:T(8,128)S(1)} %collective-permute-done.12.refs_4_.refs_1_), channel_id=1, source_target_pairs={{4,0},{8,4},{12,8},{14,12},{10,14},{6,10},{2,6},{0,2},{5,1},{9,5},... | collective-permute-start | bytes 589832 | tf_op jit(solution)/shard_map/ppermute | solution.py:276
  78.9 1.8 %collective-permute-done.17.refs_6_.refs_9_ = f32[3,2,4,16,128]{4,3,2,1,0:T(8,128)S(1)} collective-permute-done((f32[3,2,4,16,128]{4,3,2,1,0:T(8,128)S(1)}, f32[3,2,4,16,128]{4,3,2,1,0:T(8,128)S(1)}, u32[]{:S(2)}, u32[]{:S(2)}) %collective-permute-start.17) | collective-permute-done | bytes 196640 | tf_op jit(solution)/shard_map/ppermute | solution.py:276
  82.3 1.7 %collective-permute-done.10.refs_3_.refs_0_ = f32[3,2,4,16,128]{4,3,2,1,0:T(8,128)S(1)} collective-permute-done((f32[3,2,4,16,128]{4,3,2,1,0:T(8,128)S(1)}, f32[3,2,4,16,128]{4,3,2,1,0:T(8,128)S(1)}, u32[]{:S(2)}, u32[]{:S(2)}) %collective-permute-start.10) | collective-permute-done | bytes 196640 | tf_op jit(solution)/shard_map/ppermute | solution.py:276
  84.6 3.0 %collective-permute-done.13.refs_4_.refs_1_ = f32[3,2,4,16,128]{4,3,2,1,0:T(8,128)S(1)} collective-permute-done((f32[3,2,4,16,128]{4,3,2,1,0:T(8,128)S(1)}, f32[3,2,4,16,128]{4,3,2,1,0:T(8,128)S(1)}, u32[]{:S(2)}, u32[]{:S(2)}) %collective-permute-start.13) | collective-permute-done | bytes 196640 | tf_op jit(solution)/shard_map/ppermute | solution.py:276
  87.6 1.7 %collective-permute-start.14 = (f32[3,2,4,16,128]{4,3,2,1,0:T(8,128)S(1)}, f32[3,2,4,16,128]{4,3,2,1,0:T(8,128)}, u32[]{:S(2)}, u32[]{:S(2)}) collective-permute-start(f32[3,2,4,16,128]{4,3,2,1,0:T(8,128)S(1)} %collective-permute-done.13.refs_4_.refs_1_), channel_id=1, source_target_pairs={{4,0},{8,4},{12,8},{14,12},{10,14},{6,10},{2,6},{0,2},{5,1},{9,5},... | collective-permute-start | bytes 589832 | tf_op jit(solution)/shard_map/ppermute | solution.py:276
  91.7 2.2 %collective-permute-start.24 = (f32[3,2,4,16,128]{4,3,2,1,0:T(8,128)S(1)}, f32[3,2,4,16,128]{4,3,2,1,0:T(8,128)S(1)}, u32[]{:S(2)}, u32[]{:S(2)}) collective-permute-start(f32[3,2,4,16,128]{4,3,2,1,0:T(8,128)S(1)} %collective-permute-done.23.refs_7_.refs_10_), channel_id=1, source_target_pairs={{0,4},{4,8},{8,12},{12,14},{14,10},{10,6},{6,2},{2,0},{1,5},{5,9},... | collective-permute-start | bytes 589832 | tf_op jit(solution)/shard_map/ppermute | solution.py:276
  95.4 2.7 %collective-permute-done.14.refs_4_.refs_1_ = f32[3,2,4,16,128]{4,3,2,1,0:T(8,128)} collective-permute-done((f32[3,2,4,16,128]{4,3,2,1,0:T(8,128)S(1)}, f32[3,2,4,16,128]{4,3,2,1,0:T(8,128)}, u32[]{:S(2)}, u32[]{:S(2)}) %collective-permute-start.14) | collective-permute-done | bytes 196640 | tf_op jit(solution)/shard_map/ppermute | solution.py:276
  98.6 15.0 %shard_map.66.refs_12_ = f32[36,32,4096]{2,1,0:T(8,128)} custom-call(s32[3]{0:T(128)S(1)} %add_add_fusion.3.place, s32[216]{0:T(256)S(1)} %reshape.108.shifts, f32[1]{0:T(128)} %bitcast.3.floor, f32[3,2,4,16,128]{4,3,2,1,0:T(8,128)S(1)} %get-tuple-element.11.refs_0_.refs_9_, f32[3,2,4,16,128]{4,3,2,1,0:T(8,128)S(1)} %get-tuple-element.12.refs_1_.refs_10_, ...), custom_call_target="tpu_custom_call" | custom-call | flops 18874368 | bytes 18874368 | tf_op jit(solution)/shard_map/pallas_call | solution.py:194
  113.6 15.0 %shard_map.67.refs_12_ = f32[36,32,4096]{2,1,0:T(8,128)} custom-call(s32[3]{0:T(128)S(1)} %add_add_fusion.2.place, s32[216]{0:T(256)S(1)} %reshape.108.shifts, f32[1]{0:T(128)} %bitcast.3.floor, f32[3,2,4,16,128]{4,3,2,1,0:T(8,128)S(1)} %collective-permute-done.9.refs_3_.refs_0_, ...), custom_call_target="tpu_custom_call", output_to_operand_aliasing={{}: (15, {})} | custom-call | flops 18874368 | bytes 18874368 | tf_op jit(solution)/shard_map/pallas_call | solution.py:194
  128.5 15.8 %shard_map.68.refs_12_ = f32[36,32,4096]{2,1,0:T(8,128)} custom-call(s32[3]{0:T(128)S(1)} %get-tuple-element.48.place, s32[216]{0:T(256)S(1)} %reshape.108.shifts, f32[1]{0:T(128)} %bitcast.3.floor, f32[3,2,4,16,128]{4,3,2,1,0:T(8,128)S(1)} %collective-permute-done.10.refs_3_.refs_0_, ...), custom_call_target="tpu_custom_call", output_to_operand_aliasing={{}: (15, {})} | custom-call | flops 18874368 | bytes 18874368 | tf_op jit(solution)/shard_map/pallas_call | solution.py:194
  144.3 16.0 %shard_map.69 = f32[36,32,4096]{2,1,0:T(8,128)} custom-call(s32[3]{0:T(128)S(1)} %get-tuple-element.47.place, s32[216]{0:T(256)S(1)} %reshape.108.shifts, f32[1]{0:T(128)} %bitcast.3.floor, f32[3,2,4,16,128]{4,3,2,1,0:T(8,128)S(1)} %collective-permute-done.11.refs_3_.refs_0_, ...), custom_call_target="tpu_custom_call", output_to_operand_aliasing={{}: (15, {})} | custom-call | flops 18874368 | bytes 18874368 | tf_op jit(solution)/shard_map/pallas_call | solution.py:194
  (80 shorter events, 21.5 us)
Async XLA Ops:
  1.4 12.2 %collective-permute-start.5 = (f32[2,32,512]{2,1,0:T(8,128)S(1)}, f32[2,32,512]{2,1,0:T(8,128)S(1)}, u32[]{:S(2)}, u32[]{:S(2)}) collective-permute-start(f32[2,32,512]{2,1,0:T(8,128)S(1)} %pad_maximum_fusion.5), channel_id=1, source_target_pairs={{0,4},{2,6},{4,0},{6,2},{8,12},{10,14},{12,8},{14,10},{1,5},{3,7},... | collective-permute-start | bytes 393224 | tf_op jit(solution)/shard_map/ppermute | solution.py:243
  4.5 12.7 %collective-permute-start.6 = (f32[2,32,512]{2,1,0:T(8,128)S(1)}, f32[2,32,512]{2,1,0:T(8,128)S(1)}, u32[]{:S(2)}, u32[]{:S(2)}) collective-permute-start(f32[2,32,512]{2,1,0:T(8,128)S(1)} %pad_maximum_fusion.6), channel_id=1, source_target_pairs={{0,2},{2,0},{4,6},{6,4},{8,10},{10,8},{12,14},{14,12},{1,3},{3,1},... | collective-permute-start | bytes 393224 | tf_op jit(solution)/shard_map/ppermute | solution.py:243
  6.1 16.8 %collective-permute-start.4 = (f32[2,32,512]{2,1,0:T(8,128)S(1)}, f32[2,32,512]{2,1,0:T(8,128)S(1)}, u32[]{:S(2)}, u32[]{:S(2)}) collective-permute-start(f32[2,32,512]{2,1,0:T(8,128)S(1)} %pad_maximum_fusion.4), channel_id=1, source_target_pairs={{0,6},{2,4},{4,2},{6,0},{8,14},{10,12},{12,10},{14,8},{1,7},{3,5},... | collective-permute-start | bytes 393224 | tf_op jit(solution)/shard_map/ppermute | solution.py:243
  6.2 16.7 %collective-permute-start.3 = (f32[2,32,512]{2,1,0:T(8,128)S(1)}, f32[2,32,512]{2,1,0:T(8,128)S(1)}, u32[]{:S(2)}, u32[]{:S(2)}) collective-permute-start(f32[2,32,512]{2,1,0:T(8,128)S(1)} %pad_maximum_fusion.3), channel_id=1, source_target_pairs={{0,8},{2,10},{4,12},{6,14},{8,0},{10,2},{12,4},{14,6},{1,9},{3,11}... | collective-permute-start | bytes 393224 | tf_op jit(solution)/shard_map/ppermute | solution.py:243
  9.2 19.4 %collective-permute-start.2 = (f32[2,32,512]{2,1,0:T(8,128)S(1)}, f32[2,32,512]{2,1,0:T(8,128)S(1)}, u32[]{:S(2)}, u32[]{:S(2)}) collective-permute-start(f32[2,32,512]{2,1,0:T(8,128)S(1)} %pad_maximum_fusion.2), channel_id=1, source_target_pairs={{0,10},{2,8},{4,14},{6,12},{8,2},{10,0},{12,6},{14,4},{1,11},{3,9}... | collective-permute-start | bytes 393224 | tf_op jit(solution)/shard_map/ppermute | solution.py:243
  13.5 15.1 %collective-permute-start.1 = (f32[2,32,512]{2,1,0:T(8,128)S(1)}, f32[2,32,512]{2,1,0:T(8,128)S(1)}, u32[]{:S(2)}, u32[]{:S(2)}) collective-permute-start(f32[2,32,512]{2,1,0:T(8,128)S(1)} %pad_maximum_fusion.1), channel_id=1, source_target_pairs={{0,12},{2,14},{4,8},{6,10},{8,4},{10,6},{12,0},{14,2},{1,13},{3,15... | collective-permute-start | bytes 393224 | tf_op jit(solution)/shard_map/ppermute | solution.py:243
  17.2 11.4 %collective-permute-start = (f32[2,32,512]{2,1,0:T(8,128)S(1)}, f32[2,32,512]{2,1,0:T(8,128)S(1)}, u32[]{:S(2)}, u32[]{:S(2)}) collective-permute-start(f32[2,32,512]{2,1,0:T(8,128)S(1)} %pad_maximum_fusion), channel_id=1, source_target_pairs={{0,14},{2,12},{4,10},{6,8},{8,6},{10,4},{12,2},{14,0},{1,15},{3,13... | collective-permute-start | bytes 393224 | tf_op jit(solution)/shard_map/ppermute | solution.py:243
  36.6 12.0 %collective-permute-start.8 = (f32[3,2,16,640]{3,2,1,0:T(8,128)S(1)}, f32[3,2,16,640]{3,2,1,0:T(8,128)S(1)}, u32[]{:S(2)}, u32[]{:S(2)}) collective-permute-start(f32[3,2,16,640]{3,2,1,0:T(8,128)S(1)} %slice_select_fusion), channel_id=1, source_target_pairs={{0,1},{1,0},{2,3},{3,2},{4,5},{5,4},{6,7},{7,6},{8,9},{9,8},{10,11... | collective-permute-start | bytes 737288 | tf_op jit(solution)/shard_map/ppermute | solution.py:259
  64.0 8.2 %collective-permute-start.9 = (f32[3,2,4,16,128]{4,3,2,1,0:T(8,128)S(1)}, f32[3,2,4,16,128]{4,3,2,1,0:T(8,128)S(1)}, u32[]{:S(2)}, u32[]{:S(2)}) collective-permute-start(f32[3,2,4,16,128]{4,3,2,1,0:T(8,128)S(1)} %get-tuple-element.11.refs_0_.refs_9_), channel_id=1, source_target_pairs={{4,0},{8,4},{12,8},{14,12},{10,14},{6,10},{2,6},{0,2},{5,1},{9,5},... | collective-permute-start | bytes 589832 | tf_op jit(solution)/shard_map/ppermute | solution.py:276
  64.6 8.1 %collective-permute-start.16 = (f32[3,2,4,16,128]{4,3,2,1,0:T(8,128)S(1)}, f32[3,2,4,16,128]{4,3,2,1,0:T(8,128)S(1)}, u32[]{:S(2)}, u32[]{:S(2)}) collective-permute-start(f32[3,2,4,16,128]{4,3,2,1,0:T(8,128)S(1)} %get-tuple-element.11.refs_0_.refs_9_), channel_id=1, source_target_pairs={{0,4},{4,8},{8,12},{12,14},{14,10},{10,6},{6,2},{2,0},{1,5},{5,9},... | collective-permute-start | bytes 589832 | tf_op jit(solution)/shard_map/ppermute | solution.py:276
  66.5 9.7 %collective-permute-start.12 = (f32[3,2,4,16,128]{4,3,2,1,0:T(8,128)S(1)}, f32[3,2,4,16,128]{4,3,2,1,0:T(8,128)S(1)}, u32[]{:S(2)}, u32[]{:S(2)}) collective-permute-start(f32[3,2,4,16,128]{4,3,2,1,0:T(8,128)S(1)} %get-tuple-element.12.refs_1_.refs_10_), channel_id=1, source_target_pairs={{4,0},{8,4},{12,8},{14,12},{10,14},{6,10},{2,6},{0,2},{5,1},{9,5},... | collective-permute-start | bytes 589832 | tf_op jit(solution)/shard_map/ppermute | solution.py:276
  67.0 9.9 %collective-permute-start.22 = (f32[3,2,4,16,128]{4,3,2,1,0:T(8,128)S(1)}, f32[3,2,4,16,128]{4,3,2,1,0:T(8,128)S(1)}, u32[]{:S(2)}, u32[]{:S(2)}) collective-permute-start(f32[3,2,4,16,128]{4,3,2,1,0:T(8,128)S(1)} %get-tuple-element.12.refs_1_.refs_10_), channel_id=1, source_target_pairs={{0,4},{4,8},{8,12},{12,14},{14,10},{10,6},{6,2},{2,0},{1,5},{5,9},... | collective-permute-start | bytes 589832 | tf_op jit(solution)/shard_map/ppermute | solution.py:276
  68.6 8.3 %collective-permute-start.30 = (f32[3,2,4,16,128]{4,3,2,1,0:T(8,128)S(1)}, f32[3,2,4,16,128]{4,3,2,1,0:T(8,128)S(1)}, u32[]{:S(2)}, u32[]{:S(2)}) collective-permute-start(f32[3,2,4,16,128]{4,3,2,1,0:T(8,128)S(1)} %get-tuple-element.11.refs_0_.refs_9_), channel_id=1, source_target_pairs={{0,1},{1,0},{2,3},{3,2},{4,5},{5,4},{6,7},{7,6},{8,9},{9,8},{10,11... | collective-permute-start | bytes 589832 | tf_op jit(solution)/shard_map/ppermute | solution.py:264
  72.7 8.1 %collective-permute-start.17 = (f32[3,2,4,16,128]{4,3,2,1,0:T(8,128)S(1)}, f32[3,2,4,16,128]{4,3,2,1,0:T(8,128)S(1)}, u32[]{:S(2)}, u32[]{:S(2)}) collective-permute-start(f32[3,2,4,16,128]{4,3,2,1,0:T(8,128)S(1)} %collective-permute-done.16.refs_6_.refs_9_), channel_id=1, source_target_pairs={{0,4},{4,8},{8,12},{12,14},{14,10},{10,6},{6,2},{2,0},{1,5},{5,9},... | collective-permute-start | bytes 589832 | tf_op jit(solution)/shard_map/ppermute | solution.py:276
  76.9 10.7 %collective-permute-start.13 = (f32[3,2,4,16,128]{4,3,2,1,0:T(8,128)S(1)}, f32[3,2,4,16,128]{4,3,2,1,0:T(8,128)S(1)}, u32[]{:S(2)}, u32[]{:S(2)}) collective-permute-start(f32[3,2,4,16,128]{4,3,2,1,0:T(8,128)S(1)} %collective-permute-done.12.refs_4_.refs_1_), channel_id=1, source_target_pairs={{4,0},{8,4},{12,8},{14,12},{10,14},{6,10},{2,6},{0,2},{5,1},{9,5},... | collective-permute-start | bytes 589832 | tf_op jit(solution)/shard_map/ppermute | solution.py:276
  78.9 8.7 %collective-permute-start.23 = (f32[3,2,4,16,128]{4,3,2,1,0:T(8,128)S(1)}, f32[3,2,4,16,128]{4,3,2,1,0:T(8,128)S(1)}, u32[]{:S(2)}, u32[]{:S(2)}) collective-permute-start(f32[3,2,4,16,128]{4,3,2,1,0:T(8,128)S(1)} %collective-permute-done.22.refs_7_.refs_10_), channel_id=1, source_target_pairs={{0,4},{4,8},{8,12},{12,14},{14,10},{10,6},{6,2},{2,0},{1,5},{5,9},... | collective-permute-start | bytes 589832 | tf_op jit(solution)/shard_map/ppermute | solution.py:276
  80.7 9.7 %collective-permute-start.18 = (f32[3,2,4,16,128]{4,3,2,1,0:T(8,128)S(1)}, f32[3,2,4,16,128]{4,3,2,1,0:T(8,128)S(1)}, u32[]{:S(2)}, u32[]{:S(2)}) collective-permute-start(f32[3,2,4,16,128]{4,3,2,1,0:T(8,128)S(1)} %collective-permute-done.17.refs_6_.refs_9_), channel_id=1, source_target_pairs={{0,4},{4,8},{8,12},{12,14},{14,10},{10,6},{6,2},{2,0},{1,5},{5,9},... | collective-permute-start | bytes 589832 | tf_op jit(solution)/shard_map/ppermute | solution.py:276
  84.1 9.8 %collective-permute-start.27 = (f32[3,2,4,16,128]{4,3,2,1,0:T(8,128)S(1)}, f32[3,2,4,16,128]{4,3,2,1,0:T(8,128)S(1)}, u32[]{:S(2)}, u32[]{:S(2)}) collective-permute-start(f32[3,2,4,16,128]{4,3,2,1,0:T(8,128)S(1)} %collective-permute-done.17.refs_6_.refs_9_), channel_id=1, source_target_pairs={{0,1},{1,0},{2,3},{3,2},{4,5},{5,4},{6,7},{7,6},{8,9},{9,8},{10,11... | collective-permute-start | bytes 589832 | tf_op jit(solution)/shard_map/ppermute | solution.py:264
  87.6 10.5 %collective-permute-start.14 = (f32[3,2,4,16,128]{4,3,2,1,0:T(8,128)S(1)}, f32[3,2,4,16,128]{4,3,2,1,0:T(8,128)}, u32[]{:S(2)}, u32[]{:S(2)}) collective-permute-start(f32[3,2,4,16,128]{4,3,2,1,0:T(8,128)S(1)} %collective-permute-done.13.refs_4_.refs_1_), channel_id=1, source_target_pairs={{4,0},{8,4},{12,8},{14,12},{10,14},{6,10},{2,6},{0,2},{5,1},{9,5},... | collective-permute-start | bytes 589832 | tf_op jit(solution)/shard_map/ppermute | solution.py:276
  91.7 36.8 %collective-permute-start.24 = (f32[3,2,4,16,128]{4,3,2,1,0:T(8,128)S(1)}, f32[3,2,4,16,128]{4,3,2,1,0:T(8,128)S(1)}, u32[]{:S(2)}, u32[]{:S(2)}) collective-permute-start(f32[3,2,4,16,128]{4,3,2,1,0:T(8,128)S(1)} %collective-permute-done.23.refs_7_.refs_10_), channel_id=1, source_target_pairs={{0,4},{4,8},{8,12},{12,14},{14,10},{10,6},{6,2},{2,0},{1,5},{5,9},... | collective-permute-start | bytes 589832 | tf_op jit(solution)/shard_map/ppermute | solution.py:276
  93.9 34.7 %collective-permute-start.25 = (f32[3,2,4,16,128]{4,3,2,1,0:T(8,128)S(1)}, f32[3,2,4,16,128]{4,3,2,1,0:T(8,128)S(1)}, u32[]{:S(2)}, u32[]{:S(2)}) collective-permute-start(f32[3,2,4,16,128]{4,3,2,1,0:T(8,128)S(1)} %collective-permute-done.18.refs_6_.refs_9_), channel_id=1, source_target_pairs={{0,1},{1,0},{2,3},{3,2},{4,5},{5,4},{6,7},{7,6},{8,9},{9,8},{10,11... | collective-permute-start | bytes 589832 | tf_op jit(solution)/shard_map/ppermute | solution.py:264
  95.4 33.1 %collective-permute-start.15 = (f32[3,2,4,16,128]{4,3,2,1,0:T(8,128)S(1)}, f32[3,2,4,16,128]{4,3,2,1,0:T(8,128)S(1)}, u32[]{:S(2)}, u32[]{:S(2)}) collective-permute-start(f32[3,2,4,16,128]{4,3,2,1,0:T(8,128)S(1)} %collective-permute-done.11.refs_3_.refs_0_), channel_id=1, source_target_pairs={{0,1},{1,0},{2,3},{3,2},{4,5},{5,4},{6,7},{7,6},{8,9},{9,8},{10,11... | collective-permute-start | bytes 589832 | tf_op jit(solution)/shard_map/ppermute | solution.py:264
  98.2 46.2 %collective-permute-start.20 = (f32[3,2,4,16,128]{4,3,2,1,0:T(8,128)}, f32[3,2,4,16,128]{4,3,2,1,0:T(8,128)S(1)}, u32[]{:S(2)}, u32[]{:S(2)}) collective-permute-start(f32[3,2,4,16,128]{4,3,2,1,0:T(8,128)} %collective-permute-done.14.refs_4_.refs_1_), channel_id=1, source_target_pairs={{4,0},{8,4},{12,8},{14,12},{10,14},{6,10},{2,6},{0,2},{5,1},{9,5},... | collective-permute-start | bytes 589832 | tf_op jit(solution)/shard_map/ppermute | solution.py:280
  98.4 45.9 %collective-permute-start.21 = (f32[3,2,4,16,128]{4,3,2,1,0:T(8,128)}, f32[3,2,4,16,128]{4,3,2,1,0:T(8,128)S(1)}, u32[]{:S(2)}, u32[]{:S(2)}) collective-permute-start(f32[3,2,4,16,128]{4,3,2,1,0:T(8,128)} %collective-permute-done.19.refs_3_.refs_6_), channel_id=1, source_target_pairs={{0,1},{1,0},{2,3},{3,2},{4,5},{5,4},{6,7},{7,6},{8,9},{9,8},{10,11... | collective-permute-start | bytes 589832 | tf_op jit(solution)/shard_map/ppermute | solution.py:264
  (8 other events, 143.2 us)

commit v2 on v1

--- a/solution.py
+++ b/solution.py
@@ -48,7 +48,7 @@
     )(taps)
 
 
-def correlate_kernel(place, wide, border, high_ref, both_ref, edge_ref, inner_ref, ext, summed):
+def correlate_kernel(place, wide, border, high_ref, both_ref, rows_ref, ext, summed):
     epochs, kinds, height, width = wide.shape
     ksize = high_ref.shape[1]
     tiles = width // LANES - 1
@@ -96,20 +96,19 @@
                 start = base + tile * height
                 at_edge = pl.multiple_of(start + (1 - lower) * (height - MAXS), MAXS)
                 at_inner = pl.multiple_of(start + lower * MAXS, MAXS)
-                edge_ref[epoch, kind, tile] = summed[pl.ds(at_edge, MAXS)]
-                inner_ref[epoch, kind, tile] = summed[pl.ds(at_inner, MAXS)]
+                rows_ref[0, epoch, kind, tile] = summed[pl.ds(at_edge, MAXS)]
+                rows_ref[1, epoch, kind, tile] = summed[pl.ds(at_inner, MAXS)]
 
 
 def correlate(place, wide, border, high, both):
     epochs, kinds, height, width = wide.shape
     tiles = width // LANES - 1
-    half = jax.ShapeDtypeStruct((epochs, kinds, tiles, MAXS, LANES), jnp.float32)
     flops = 3 * 2 * epochs * kinds * (tiles + 1) * height * high.shape[1] * 2 * LANES * LANES
     return pl.pallas_call(
         correlate_kernel,
         in_specs=[pl.BlockSpec(memory_space=pltpu.SMEM)] + [pl.BlockSpec(memory_space=pltpu.VMEM)] * 4,
-        out_specs=[pl.BlockSpec(memory_space=pltpu.VMEM)] * 2,
-        out_shape=[half, half],
+        out_specs=pl.BlockSpec(memory_space=pltpu.VMEM),
+        out_shape=jax.ShapeDtypeStruct((2, epochs, kinds, tiles, MAXS, LANES), jnp.float32),
         scratch_shapes=[
             pltpu.VMEM((epochs, kinds, tiles + 2, height + 2 * MAXS, LANES), jnp.float32),
             pltpu.VMEM((epochs * (tiles + 1) * height, LANES), jnp.float32),
@@ -142,10 +141,10 @@
                 rows = pl.ds(at[piece], MAXS)
                 for epoch in range(epochs):
                     for kind in range(kinds):
-                        held[epoch, kind, 0, rows] = jnp.where(keep_first, own[epoch, kind, 0], 0.0)
+                        held[epoch, kind, 0, rows] = jnp.where(keep_first, own[0, epoch, kind, 0], 0.0)
                         for tile in range(1, tiles):
-                            held[epoch, kind, tile, rows] = own[epoch, kind, tile]
-                        held[epoch, kind, tiles, rows] = jnp.where(keep_last, nearby[epoch, kind, 0], 0.0)
+                            held[epoch, kind, tile, rows] = own[0, epoch, kind, tile]
+                        held[epoch, kind, tiles, rows] = jnp.where(keep_last, nearby[0, epoch, kind, 0], 0.0)
 
     low = floor[0]
     height = out_ref.shape[1]
@@ -176,15 +175,17 @@
 
 
 def stack_blocks(place, shifts, floor, sources, out, out_shape, parts, blocks):
-    epochs, kinds, tiles = sources[0].shape[:3]
+    epochs, kinds, tiles = sources[0][0].shape[1:4]
     velocities, height, columns = out_shape.shape
     group = next(size for size in (12, 9, 8, 6, 4, 3, 2, 1) if velocities % size == 0)
     width = tiles * LANES
-    whole = pl.BlockSpec((epochs, kinds, tiles, MAXS, LANES), lambda *_: (0, 0, 0, 0, 0))
-    front = pl.BlockSpec((epochs, kinds, 1, MAXS, LANES), lambda *_: (0, 0, 0, 0, 0))
-    in_specs = [whole] * 3 + [front] * 3
-    in_specs = in_specs * parts
-    operands = list(sources)
+    in_specs, operands = [], []
+    for index, (array, slot) in enumerate(sources):
+        depth = tiles if index % 6 < 3 else 1
+        in_specs.append(
+            pl.BlockSpec((1, epochs, kinds, depth, MAXS, LANES), functools.partial(lambda at, *_: (at, 0, 0, 0, 0, 0), slot))
+        )
+        operands.append(array)
     aliases = {}
     if out is not None:
         in_specs.append(pl.BlockSpec(memory_space=pl.ANY))
@@ -203,7 +204,7 @@
         out_shape=out_shape,
         input_output_aliases=aliases,
         compiler_params=pltpu.CompilerParams(vmem_limit_bytes=VMEM),
-        cost_estimate=pl.CostEstimate(flops=16 * work, bytes_accessed=16 * work, transcendentals=work),
+        cost_estimate=pl.CostEstimate(flops=16 * work, bytes_accessed=24 * work, transcendentals=work),
     )(place, shifts, floor, *operands)
 
 
@@ -228,7 +229,7 @@
     kernel_norm = spread_kernel / jnp.sum(spread_kernel)
     kernel_sq = kernel_norm * kernel_norm
     floor = (0.5 * jnp.sum(kernel_sq)).reshape(1)
-    high, both = bands(jnp.stack([kernel_norm, kernel_sq]).reshape(-1), ksize)
+    taps = jnp.stack([kernel_norm, kernel_sq]).reshape(-1)
 
     chunks = []
     for step in range(blocks):
@@ -241,7 +242,11 @@
         )
         if step:
             chunk = lax.ppermute(chunk, "vel", [(i, i ^ step) for i in range(blocks)])
+        if step == 1:
+            chunk, taps = lax.optimization_barrier((chunk, taps))
         chunks.append(chunk)
+    high, both = bands(taps, ksize)
+    chunks[-1], high, both = lax.optimization_barrier((chunks[-1], high, both))
     row_ids = lower * height + jnp.arange(height, dtype=jnp.int32)[:, None]
     fields = []
     for epoch in range(epochs):
@@ -258,27 +263,29 @@
     wide = jnp.concatenate([before, field], axis=3)
     border = lax.ppermute(jnp.where(lower == 0, wide[:, :, height - MAXS :], wide[:, :, :MAXS]), "rows", swap)
     place = jnp.stack([mine, lower]).astype(jnp.int32)
-    edge, inner = correlate(place, wide, border, high, both)
-
-    def with_border(edge, inner):
-        return edge, inner, lax.ppermute(edge, "rows", swap)
+    payload = correlate(place, wide, border, high, both)
 
     flat_shifts = shifts.reshape(-1)
     out_shape = jax.ShapeDtypeStruct((shifts.shape[0], height, columns), jnp.float32)
-    have = {0: with_border(edge, inner)}
+    border = lax.ppermute(payload[:1], "rows", swap)
+    have = {0: ((payload, 0), (payload, 1), (border, 0))}
+    behind = ahead = payload
+    half = blocks // 2
     out = None
-    half = blocks // 2
     for step in range(1, half + 1):
         if step < half:
-            for sign, ring in ((-1, right), (1, left)):
-                edge, inner, _ = have[sign * (step - 1)]
-                have[sign * step] = with_border(
-                    lax.ppermute(edge, "vel", ring), lax.ppermute(inner, "vel", ring)
-                )
+            behind, ahead = lax.ppermute(behind, "vel", right), lax.ppermute(ahead, "vel", left)
+            if out is not None:
+                behind, ahead, out = lax.optimization_barrier((behind, ahead, out))
+            border = lax.ppermute(jnp.concatenate([behind[:1], ahead[:1]]), "rows", swap)
+            have[-step] = ((behind, 0), (behind, 1), (border, 0))
+            have[step] = ((ahead, 0), (ahead, 1), (border, 1))
         else:
-            edge = lax.ppermute(have[1 - step][0], "vel", right)
-            inner = lax.ppermute(have[step - 1][1], "vel", left)
-            have[step] = have[-step] = with_border(edge, inner)
+            edge, inner = lax.ppermute(behind[:1], "vel", right), lax.ppermute(ahead[1:], "vel", left)
+            if out is not None:
+                edge, inner, out = lax.optimization_barrier((edge, inner, out))
+            border = lax.ppermute(edge, "rows", swap)
+            have[step] = have[-step] = ((edge, 0), (inner, 0), (border, 0))
         now = [step - 1, -step]
         sources = []
         for offset in now:

time: 161 us -> 149 us (0.925)
  waiting for transfers between devices: 25.3 us -> 15.4 us
  starting transfers between devices: 32.7 us -> 24.2 us
  other arithmetic: 8.02 us -> 14.9 us
  Pallas kernels: 86.8 us -> 84.8 us
    ppermute x22 -> x13, waiting for transfers between devices: 18.7 us -> 11.7 us  [the longest x3 9.41 us: local(): lax.ppermute(ahead, 'vel', left)]
    ppermute x7, waiting for transfers between devices: 5.72 us -> 0.02 us  [local(): chunk = lax.ppermute(chunk, 'vel', [(i, i ^ step) for i in range(blocks)])]
    ppermute x22 -> x13, starting transfers between devices: 14.7 us -> 9.13 us  [the longest x3 4.17 us: local(): lax.ppermute(ahead, 'vel', left)]
    another operation x7, other arithmetic: 0.07 us -> 3.32 us  [local(): jnp.stack([lax.dynamic_slice_in_dim(exposure, start, width, 1), lax.dynam...]
    select_n x3, other arithmetic: 0.28 us -> 2.92 us  [local(): chosen = jnp.where(key == step, chunks[step], chosen)]
    ppermute x1, starting transfers between devices: 5.08 us -> 2.57 us  [local(): before = lax.ppermute(field[..., width - LANES:], 'vel', right)]
    pallas_call x4, Pallas kernels: 61.8 us -> 59.8 us  [stack_blocks(): pl.pallas_call(functools.partial(stack_kernel, group=group, parts=parts,...]
  transfers between devices with their start and end apart: 31 -> 22, of which waited for: 12 -> 6; matrix products, arithmetic and copies ran while one was open for 7% -> 9% of each run, Pallas kernels for 35% -> 37%
where the time goes in v2:
time: 149 us; the launch traced here: 148 us
  Pallas kernels  84.8 us (57%)
  starting transfers between devices  24.2 us (16%)
  waiting for transfers between devices  15.4 us (10%)
  other arithmetic  14.9 us (10%)
  local copies, waits for them, and re-layouts  6.12 us (4%)
  between operations  2.92 us (2%)
    pallas_call x4, Pallas kernels, stack_blocks(): pl.pallas_call(functools.partial(stack_kernel, group=group, parts=parts,...  59.8 us
    pallas_call x1, Pallas kernels, correlate(): pl.pallas_call(correlate_kernel, in_specs=[pl.BlockSpec(memory_space=pltp...  15.3 us
    ppermute x7, starting transfers between devices, local(): chunk = lax.ppermute(chunk, 'vel', [(i, i ^ step) for i in range(blocks)])  12.4 us
    pallas_call x1, Pallas kernels, bands(): pl.pallas_call(band_kernel, in_specs=[pl.BlockSpec(memory_space=pltpu.SME...  9.72 us
    ppermute x3, waiting for transfers between devices, local(): lax.ppermute(ahead, 'vel', left)  9.41 us
    ppermute x3, starting transfers between devices, local(): lax.ppermute(ahead, 'vel', left)  4.17 us
    and x2, other arithmetic, local(): (row_ids >= valid_rows[epoch, 0]) & (row_ids < valid_rows[epoch, 1])  3.62 us
    another operation x7, other arithmetic, local(): jnp.stack([lax.dynamic_slice_in_dim(exposure, start, width, 1), lax.dynam...  3.32 us
  transfers between devices with their start and end apart: 22, of which 6 were waited for; matrix products, arithmetic and copies ran while one was open for 9% of the time, Pallas kernels for 37%

profile of v2, /device:TPU:0, one launch (start us, length us, event | category | flops | bytes accessed | tf_op | source)
XLA Modules:
  0.0 148.4 jit_solution(1494468689057491425)
XLA Ops:
  0.0 2.0 %constant_dynamic-slice_fusion = (f32[1,32,512]{2,1,0:T(8,128)S(1)}, f32[1,32,512]{2,1,0:T(8,128)S(1)}, f32[1,32,512]{2,1,0:T(8,128)S(1)}, f32[1,32,512]{2,1,0:T...) fusion(f32[1,32,4096]{2,1,0:T(8,128)} %param.7, ...), kind=kLoop, calls=%fused_computation.34 | loop fusion | bytes 2097184 | tf_op jit(solution)/shard_map/dynamic_slice | solution.py:240
  2.6 3.0 %collective-permute-start.6 = (f32[2,32,512]{2,1,0:T(8,128)}, f32[2,32,512]{2,1,0:T(8,128)S(1)}, u32[]{:S(2)}, u32[]{:S(2)}) collective-permute-start(f32[2,32,512]{2,1,0:T(8,128)} %pad_maximum_fusion.9), channel_id=1, source_target_pairs={{0,4},{2,6},{4,0},{6,2},{8,12},{10,14},{12,8},{14,10},{1,5},{3,7},... | collective-permute-start | bytes 393224 | tf_op jit(solution)/shard_map/ppermute | solution.py:244
  5.7 3.5 %collective-permute-start = (f32[2,32,512]{2,1,0:T(8,128)S(1)}, f32[2,32,512]{2,1,0:T(8,128)S(1)}, u32[]{:S(2)}, u32[]{:S(2)}) collective-permute-start(f32[2,32,512]{2,1,0:T(8,128)S(1)} %pad_maximum_fusion.3), channel_id=1, source_target_pairs={{0,14},{2,12},{4,10},{6,8},{8,6},{10,4},{12,2},{14,0},{1,15},{3,13... | collective-permute-start | bytes 393224 | tf_op jit(solution)/shard_map/ppermute | solution.py:244
  10.4 1.3 collective-permute-start.2
  12.4 1.7 %collective-permute-start.3 = (f32[2,32,512]{2,1,0:T(8,128)}, f32[2,32,512]{2,1,0:T(8,128)S(1)}, u32[]{:S(2)}, u32[]{:S(2)}) collective-permute-start(f32[2,32,512]{2,1,0:T(8,128)} %pad_maximum_fusion.6), channel_id=1, source_target_pairs={{0,10},{2,8},{4,14},{6,12},{8,2},{10,0},{12,6},{14,4},{1,11},{3,9}... | collective-permute-start | bytes 393224 | tf_op jit(solution)/shard_map/ppermute | solution.py:244
  14.2 1.5 %fusion.5 = (s32[1,1]{0,1:T(1,128)}, s32[1,1]{0,1:T(1,128)}, s32[1,1]{0,1:T(1,128)}, s32[1,1]{0,1:T(1,128)}, s32[1,1]{0,1:T(1,128)}, /*index=5*/s32[1,1]{0,1:T(1,128)}) fusion(s32[3,2]{0,1:T(2,128)} %param.11), kind=kLoop, calls=%fused_computation.61 | loop fusion | bytes 48 | tf_op jit(solution)/shard_map/slice | solution.py:257
  15.7 1.3 reduce_sum.18
  17.0 2.0 %fusion.3 = (f32[1,21,21]{2,1,0:T(8,128)S(1)}, f32[1,21,21]{2,1,0:T(8,128)S(1)}, f32[]{:T(128)}) fusion(f32[21,21]{1,0:T(8,128)} %param.8, f32[]{:T(128)} %reduce_sum.18), kind=kLoop, calls=%fused_computation.59 | loop fusion | flops 1322 | bytes 5300 | tf_op jit(solution)/shard_map/stack | solution.py:232
  19.7 1.4 fusion.6
  21.8 2.1 %collective-permute-start.4 = (f32[2,32,512]{2,1,0:T(8,128)}, f32[2,32,512]{2,1,0:T(8,128)}, u32[]{:S(2)}, u32[]{:S(2)}) collective-permute-start(f32[2,32,512]{2,1,0:T(8,128)} %pad_maximum_fusion.7), channel_id=1, source_target_pairs={{0,8},{2,10},{4,12},{6,14},{8,0},{10,2},{12,4},{14,6},{1,9},{3,11}... | collective-permute-start | bytes 393224 | tf_op jit(solution)/shard_map/ppermute | solution.py:244
  27.4 2.4 %compare_and_fusion = (pred[32]{0:T(512)(128)(4,1)S(1)}, pred[32]{0:T(512)(128)(4,1)S(1)}) fusion(s32[]{:T(128)} %bitcast.16, s32[]{:T(128)} %bitcast.15, s32[]{:T(128)S(6)} %mul.31, s32[]{:T(128)} %bitcast.12, s32[]{:T(128)} %bitcast.11), kind=kLoop, calls=%fused_computation.50 | loop fusion | flops 224 | bytes 84 | tf_op jit(solution)/shard_map/and | solution.py:257
  29.8 9.7 %shard_map.64 = (bf16[2,21,256,128]{3,2,1,0:T(8,128)(2,1)S(1)}, bf16[2,21,256,256]{3,2,1,0:T(8,128)(2,1)}) custom-call(f32[882]{0:T(1024)S(1)} %reshape.110.taps), custom_call_target="tpu_custom_call" | custom-call | bytes 25165824 | tf_op jit(solution)/shard_map/pallas_call | solution.py:38
  42.8 2.6 %collective-permute-start.7 = (f32[3,2,32,128]{3,2,1,0:T(8,128)S(1)}, f32[3,2,32,128]{3,2,1,0:T(8,128)S(1)}, u32[]{:S(2)}, u32[]{:S(2)}) collective-permute-start(f32[3,2,32,128]{3,2,1,0:T(8,128)S(1)} %pad_maximum_fusion.11), channel_id=1, source_target_pairs={{0,4},{4,8},{8,12},{12,14},{14,10},{10,6},{6,2},{2,0},{1,5},{5,9},... | collective-permute-start | bytes 294920 | tf_op jit(solution)/shard_map/ppermute | solution.py:262
  45.4 2.2 %collective-permute-done.7 = f32[3,2,32,128]{3,2,1,0:T(8,128)S(1)} collective-permute-done((f32[3,2,32,128]{3,2,1,0:T(8,128)S(1)}, f32[3,2,32,128]{3,2,1,0:T(8,128)S(1)}, u32[]{:S(2)}, u32[]{:S(2)}) %collective-permute-start.7) | collective-permute-done | bytes 98336 | tf_op jit(solution)/shard_map/ppermute | solution.py:262
  48.7 1.4 collective-permute-done.8.border
  50.2 15.3 %shard_map.65.refs_0_.refs_1_.refs_9_.refs_10_ = f32[2,3,2,4,16,128]{5,4,3,2,1,0:T(8,128)S(1)} custom-call(s32[2]{0:T(128)S(1)} %pad_add_fusion.place, f32[3,2,32,640]{3,2,1,0:T(8,128)S(1)} %maximum_maximum_fusion.wide, f32[3,2,16,640]{3,2,1,0:T(8,128)S(1)} %collective-permute-done.8.border, bf16[2,21,256,128]{3,2,1,0:T(8,128)(2,1)S(1)} %get-tuple-element.26.high_ref, ...), custom_call_target="tpu_custom_call" | custom-call | flops 3963617280 | bytes 12582912 | tf_op jit(solution)/shard_map/pallas_call | solution.py:107
  65.5 1.5 %collective-permute-start.11 = (f32[2,3,2,4,16,128]{5,4,3,2,1,0:T(8,128)S(1)}, f32[2,3,2,4,16,128]{5,4,3,2,1,0:T(8,128)S(1)}, u32[]{:S(2)}, u32[]{:S(2)}) collective-permute-start(f32[2,3,2,4,16,128]{5,4,3,2,1,0:T(8,128)S(1)} %shard_map.65.refs_0_.refs_1_.refs_9_.refs_10_), channel_id=1, source_target_pairs={{4,0},{8,4},{12,8},{14,12},{10,14},{6,10},{2,6},{0,2},{5,1},{9,5},... | collective-permute-start | bytes 1179656 | tf_op jit(solution)/shard_map/ppermute | solution.py:277
  68.0 9.4 %collective-permute-done.11.refs_3_.refs_4_.refs_0_.refs_1_ = f32[2,3,2,4,16,128]{5,4,3,2,1,0:T(8,128)S(1)} collective-permute-done((f32[2,3,2,4,16,128]{5,4,3,2,1,0:T(8,128)S(1)}, f32[2,3,2,4,16,128]{5,4,3,2,1,0:T(8,128)S(1)}, u32[]{:S(2)}, u32[]{:S(2)}) %collective-permute-start.11) | collective-permute-done | bytes 393248 | tf_op jit(solution)/shard_map/ppermute | solution.py:277
  78.1 1.8 %collective-permute-start.12 = (f32[2,3,2,4,16,128]{5,4,3,2,1,0:T(8,128)S(1)}, f32[2,3,2,4,16,128]{5,4,3,2,1,0:T(8,128)S(1)}, u32[]{:S(2)}, u32[]{:S(2)}) collective-permute-start(f32[2,3,2,4,16,128]{5,4,3,2,1,0:T(8,128)S(1)} %collective-permute-done.11.refs_3_.refs_4_.refs_0_.refs_1_), channel_id=1, source_target_pairs={{4,0},{8,4},{12,8},{14,12},{10,14},{6,10},{2,6},{0,2},{5,1},{9,5},... | collective-permute-start | bytes 1179656 | tf_op jit(solution)/shard_map/ppermute | solution.py:277
  81.7 15.0 %shard_map.66.refs_12_ = f32[36,32,4096]{2,1,0:T(8,128)} custom-call(s32[3]{0:T(128)S(1)} %add_add_fusion.1.place, s32[216]{0:T(256)S(1)} %reshape.108.shifts, f32[1]{0:T(128)} %bitcast.3.floor, f32[2,3,2,4,16,128]{5,4,3,2,1,0:T(8,128)S(1)} %shard_map.65.refs_0_.refs_1_.refs_9_.refs_10_, ...), custom_call_target="tpu_custom_call" | custom-call | flops 18874368 | bytes 28311552 | tf_op jit(solution)/shard_map/pallas_call | solution.py:195
  99.1 15.0 %shard_map.67.refs_12_ = f32[36,32,4096]{2,1,0:T(8,128)} custom-call(s32[3]{0:T(128)S(1)} %add_add_fusion.2.place, s32[216]{0:T(256)S(1)} %reshape.108.shifts, f32[1]{0:T(128)} %bitcast.3.floor, f32[2,3,2,4,16,128]{5,4,3,2,1,0:T(8,128)S(1)} %collective-permute-done.11.refs_3_.refs_4_.refs_0_.refs_1_, ...), custom_call_target="tpu_custom_call", output_to_operand_aliasing={{}: (15, {})} | custom-call | flops 18874368 | bytes 28311552 | tf_op jit(solution)/shard_map/pallas_call | solution.py:195
  117.1 15.0 %shard_map.68.refs_12_ = f32[36,32,4096]{2,1,0:T(8,128)} custom-call(s32[3]{0:T(128)S(1)} %add_add_fusion.3.place, s32[216]{0:T(256)S(1)} %reshape.108.shifts, f32[1]{0:T(128)} %bitcast.3.floor, f32[2,3,2,4,16,128]{5,4,3,2,1,0:T(8,128)S(1)} %collective-permute-done.12.refs_3_.refs_4_.refs_0_.refs_1_, ...), custom_call_target="tpu_custom_call", output_to_operand_aliasing={{}: (15, {})} | custom-call | flops 18874368 | bytes 28311552 | tf_op jit(solution)/shard_map/pallas_call | solution.py:195
  132.2 1.3 collective-permute-done.21.refs_5_.refs_8_
  133.5 15.0 %shard_map.69 = f32[36,32,4096]{2,1,0:T(8,128)} custom-call(s32[3]{0:T(128)S(1)} %add_add_fusion.place, s32[216]{0:T(256)S(1)} %reshape.108.shifts, f32[1]{0:T(128)} %bitcast.3.floor, f32[2,3,2,4,16,128]{5,4,3,2,1,0:T(8,128)S(1)} %collective-permute-done.16.refs_3_.refs_4_.refs_0_.refs_1_, ...), custom_call_target="tpu_custom_call", output_to_operand_aliasing={{}: (15, {})} | custom-call | flops 18874368 | bytes 28311552 | tf_op jit(solution)/shard_map/pallas_call | solution.py:195
  (75 shorter events, 18.0 us)
Async XLA Ops:
  0.0 80.3 %copy-start.1 = (s32[36,3,2]{0,2,1:T(2,128)S(1)}, s32[36,3,2]{0,2,1:T(2,128)}, u32[]{:S(2)}) copy-start(s32[36,3,2]{0,2,1:T(2,128)} %param.9) | copy-start | bytes 2596
  2.6 36.9 %collective-permute-start.6 = (f32[2,32,512]{2,1,0:T(8,128)}, f32[2,32,512]{2,1,0:T(8,128)S(1)}, u32[]{:S(2)}, u32[]{:S(2)}) collective-permute-start(f32[2,32,512]{2,1,0:T(8,128)} %pad_maximum_fusion.9), channel_id=1, source_target_pairs={{0,4},{2,6},{4,0},{6,2},{8,12},{10,14},{12,8},{14,10},{1,5},{3,7},... | collective-permute-start | bytes 393224 | tf_op jit(solution)/shard_map/ppermute | solution.py:244
  5.7 16.1 %collective-permute-start = (f32[2,32,512]{2,1,0:T(8,128)S(1)}, f32[2,32,512]{2,1,0:T(8,128)S(1)}, u32[]{:S(2)}, u32[]{:S(2)}) collective-permute-start(f32[2,32,512]{2,1,0:T(8,128)S(1)} %pad_maximum_fusion.3), channel_id=1, source_target_pairs={{0,14},{2,12},{4,10},{6,8},{8,6},{10,4},{12,2},{14,0},{1,15},{3,13... | collective-permute-start | bytes 393224 | tf_op jit(solution)/shard_map/ppermute | solution.py:244
  9.2 14.8 %collective-permute-start.1 = (f32[2,32,512]{2,1,0:T(8,128)S(1)}, f32[2,32,512]{2,1,0:T(8,128)S(1)}, u32[]{:S(2)}, u32[]{:S(2)}) collective-permute-start(f32[2,32,512]{2,1,0:T(8,128)S(1)} %pad_maximum_fusion.4), channel_id=1, source_target_pairs={{0,2},{2,0},{4,6},{6,4},{8,10},{10,8},{12,14},{14,12},{1,3},{3,1},... | collective-permute-start | bytes 393224 | tf_op jit(solution)/shard_map/ppermute | solution.py:244
  10.4 29.1 %collective-permute-start.2 = (f32[2,32,512]{2,1,0:T(8,128)}, f32[2,32,512]{2,1,0:T(8,128)S(1)}, u32[]{:S(2)}, u32[]{:S(2)}) collective-permute-start(f32[2,32,512]{2,1,0:T(8,128)} %pad_maximum_fusion.5), channel_id=1, source_target_pairs={{0,12},{2,14},{4,8},{6,10},{8,4},{10,6},{12,0},{14,2},{1,13},{3,15... | collective-permute-start | bytes 393224 | tf_op jit(solution)/shard_map/ppermute | solution.py:244
  12.4 27.1 %collective-permute-start.3 = (f32[2,32,512]{2,1,0:T(8,128)}, f32[2,32,512]{2,1,0:T(8,128)S(1)}, u32[]{:S(2)}, u32[]{:S(2)}) collective-permute-start(f32[2,32,512]{2,1,0:T(8,128)} %pad_maximum_fusion.6), channel_id=1, source_target_pairs={{0,10},{2,8},{4,14},{6,12},{8,2},{10,0},{12,6},{14,4},{1,11},{3,9}... | collective-permute-start | bytes 393224 | tf_op jit(solution)/shard_map/ppermute | solution.py:244
  21.8 17.7 %collective-permute-start.4 = (f32[2,32,512]{2,1,0:T(8,128)}, f32[2,32,512]{2,1,0:T(8,128)}, u32[]{:S(2)}, u32[]{:S(2)}) collective-permute-start(f32[2,32,512]{2,1,0:T(8,128)} %pad_maximum_fusion.7), channel_id=1, source_target_pairs={{0,8},{2,10},{4,12},{6,14},{8,0},{10,2},{12,4},{14,6},{1,9},{3,11}... | collective-permute-start | bytes 393224 | tf_op jit(solution)/shard_map/ppermute | solution.py:244
  23.9 15.6 %collective-permute-start.5 = (f32[2,32,512]{2,1,0:T(8,128)}, f32[2,32,512]{2,1,0:T(8,128)}, u32[]{:S(2)}, u32[]{:S(2)}) collective-permute-start(f32[2,32,512]{2,1,0:T(8,128)} %pad_maximum_fusion.8), channel_id=1, source_target_pairs={{0,6},{2,4},{4,2},{6,0},{8,14},{10,12},{12,10},{14,8},{1,7},{3,5},... | collective-permute-start | bytes 393224 | tf_op jit(solution)/shard_map/ppermute | solution.py:244
  40.6 2.2 %copy-start = (f32[1,2,32,512]{3,2,1,0:T(8,128)}, f32[1,2,32,512]{3,2,1,0:T(8,128)S(1)}, u32[]{:S(2)}) copy-start(f32[1,2,32,512]{3,2,1,0:T(8,128)S(1)} %maximum_bitcast_fusion.2) | copy-start | bytes 393220
  42.8 4.8 %collective-permute-start.7 = (f32[3,2,32,128]{3,2,1,0:T(8,128)S(1)}, f32[3,2,32,128]{3,2,1,0:T(8,128)S(1)}, u32[]{:S(2)}, u32[]{:S(2)}) collective-permute-start(f32[3,2,32,128]{3,2,1,0:T(8,128)S(1)} %pad_maximum_fusion.11), channel_id=1, source_target_pairs={{0,4},{4,8},{8,12},{12,14},{14,10},{10,6},{6,2},{2,0},{1,5},{5,9},... | collective-permute-start | bytes 294920 | tf_op jit(solution)/shard_map/ppermute | solution.py:262
  48.6 1.6 %collective-permute-start.8 = (f32[3,2,16,640]{3,2,1,0:T(8,128)S(1)}, f32[3,2,16,640]{3,2,1,0:T(8,128)S(1)}, u32[]{:S(2)}, u32[]{:S(2)}) collective-permute-start(f32[3,2,16,640]{3,2,1,0:T(8,128)S(1)} %slice_select_fusion), channel_id=1, source_target_pairs={{0,1},{1,0},{2,3},{3,2},{4,5},{5,4},{6,7},{7,6},{8,9},{9,8},{10,11... | collective-permute-start | bytes 737288 | tf_op jit(solution)/shard_map/ppermute | solution.py:264
  65.5 11.9 %collective-permute-start.11 = (f32[2,3,2,4,16,128]{5,4,3,2,1,0:T(8,128)S(1)}, f32[2,3,2,4,16,128]{5,4,3,2,1,0:T(8,128)S(1)}, u32[]{:S(2)}, u32[]{:S(2)}) collective-permute-start(f32[2,3,2,4,16,128]{5,4,3,2,1,0:T(8,128)S(1)} %shard_map.65.refs_0_.refs_1_.refs_9_.refs_10_), channel_id=1, source_target_pairs={{4,0},{8,4},{12,8},{14,12},{10,14},{6,10},{2,6},{0,2},{5,1},{9,5},... | collective-permute-start | bytes 1179656 | tf_op jit(solution)/shard_map/ppermute | solution.py:277
  67.0 11.0 %collective-permute-start.9 = (f32[2,3,2,4,16,128]{5,4,3,2,1,0:T(8,128)S(1)}, f32[2,3,2,4,16,128]{5,4,3,2,1,0:T(8,128)S(1)}, u32[]{:S(2)}, u32[]{:S(2)}) collective-permute-start(f32[2,3,2,4,16,128]{5,4,3,2,1,0:T(8,128)S(1)} %shard_map.65.refs_0_.refs_1_.refs_9_.refs_10_), channel_id=1, source_target_pairs={{0,4},{4,8},{8,12},{12,14},{14,10},{10,6},{6,2},{2,0},{1,5},{5,9},... | collective-permute-start | bytes 1179656 | tf_op jit(solution)/shard_map/ppermute | solution.py:277
  78.1 3.7 %collective-permute-start.14 = (f32[2,3,2,4,16,128]{5,4,3,2,1,0:T(8,128)S(1)}, f32[2,3,2,4,16,128]{5,4,3,2,1,0:T(8,128)S(1)}, u32[]{:S(2)}, u32[]{:S(2)}) collective-permute-start(f32[2,3,2,4,16,128]{5,4,3,2,1,0:T(8,128)S(1)} %pad_maximum_fusion), channel_id=1, source_target_pairs={{0,1},{1,0},{2,3},{3,2},{4,5},{5,4},{6,7},{7,6},{8,9},{9,8},{10,11... | collective-permute-start | bytes 1179656 | tf_op jit(solution)/shard_map/ppermute | solution.py:280
  78.1 18.6 %collective-permute-start.12 = (f32[2,3,2,4,16,128]{5,4,3,2,1,0:T(8,128)S(1)}, f32[2,3,2,4,16,128]{5,4,3,2,1,0:T(8,128)S(1)}, u32[]{:S(2)}, u32[]{:S(2)}) collective-permute-start(f32[2,3,2,4,16,128]{5,4,3,2,1,0:T(8,128)S(1)} %collective-permute-done.11.refs_3_.refs_4_.refs_0_.refs_1_), channel_id=1, source_target_pairs={{4,0},{8,4},{12,8},{14,12},{10,14},{6,10},{2,6},{0,2},{5,1},{9,5},... | collective-permute-start | bytes 1179656 | tf_op jit(solution)/shard_map/ppermute | solution.py:277
  79.9 16.8 %collective-permute-start.10 = (f32[2,3,2,4,16,128]{5,4,3,2,1,0:T(8,128)S(1)}, f32[2,3,2,4,16,128]{5,4,3,2,1,0:T(8,128)S(1)}, u32[]{:S(2)}, u32[]{:S(2)}) collective-permute-start(f32[2,3,2,4,16,128]{5,4,3,2,1,0:T(8,128)S(1)} %collective-permute-done.9.refs_6_.refs_7_.refs_9_.refs_10_), channel_id=1, source_target_pairs={{0,4},{4,8},{8,12},{12,14},{14,10},{10,6},{6,2},{2,0},{1,5},{5,9},... | collective-permute-start | bytes 1179656 | tf_op jit(solution)/shard_map/ppermute | solution.py:277
  80.2 1.5 %collective-permute-start.13 = (f32[1,3,2,4,16,128]{5,4,3,2,1,0:T(8,128)S(1)}, f32[1,3,2,4,16,128]{5,4,3,2,1,0:T(8,128)S(1)}, u32[]{:S(2)}, u32[]{:S(2)}) collective-permute-start(f32[1,3,2,4,16,128]{5,4,3,2,1,0:T(8,128)S(1)} %slice.116), channel_id=1, source_target_pairs={{0,1},{1,0},{2,3},{3,2},{4,5},{5,4},{6,7},{7,6},{8,9},{9,8},{10,11... | collective-permute-start | bytes 589832 | tf_op jit(solution)/shard_map/ppermute | solution.py:270
  96.8 2.3 %collective-permute-start.17 = (f32[2,3,2,4,16,128]{5,4,3,2,1,0:T(8,128)S(1)}, f32[2,3,2,4,16,128]{5,4,3,2,1,0:T(8,128)S(1)}, u32[]{:S(2)}, u32[]{:S(2)}) collective-permute-start(f32[2,3,2,4,16,128]{5,4,3,2,1,0:T(8,128)S(1)} %pad_maximum_fusion.1), channel_id=1, source_target_pairs={{0,1},{1,0},{2,3},{3,2},{4,5},{5,4},{6,7},{7,6},{8,9},{9,8},{10,11... | collective-permute-start | bytes 1179656 | tf_op jit(solution)/shard_map/ppermute | solution.py:280
  97.0 17.1 %collective-permute-start.15 = (f32[2,3,2,4,16,128]{5,4,3,2,1,0:T(8,128)S(1)}, f32[2,3,2,4,16,128]{5,4,3,2,1,0:T(8,128)S(1)}, u32[]{:S(2)}, u32[]{:S(2)}) collective-permute-start(f32[2,3,2,4,16,128]{5,4,3,2,1,0:T(8,128)S(1)} %collective-permute-done.10.refs_6_.refs_7_.refs_9_.refs_10_), channel_id=1, source_target_pairs={{0,4},{4,8},{8,12},{12,14},{14,10},{10,6},{6,2},{2,0},{1,5},{5,9},... | collective-permute-start | bytes 1179656 | tf_op jit(solution)/shard_map/ppermute | solution.py:277
  98.2 15.9 %collective-permute-start.16 = (f32[2,3,2,4,16,128]{5,4,3,2,1,0:T(8,128)S(1)}, f32[2,3,2,4,16,128]{5,4,3,2,1,0:T(8,128)S(1)}, u32[]{:S(2)}, u32[]{:S(2)}) collective-permute-start(f32[2,3,2,4,16,128]{5,4,3,2,1,0:T(8,128)S(1)} %collective-permute-done.12.refs_3_.refs_4_.refs_0_.refs_1_), channel_id=1, source_target_pairs={{4,0},{8,4},{12,8},{14,12},{10,14},{6,10},{2,6},{0,2},{5,1},{9,5},... | collective-permute-start | bytes 1179656 | tf_op jit(solution)/shard_map/ppermute | solution.py:277
  114.8 2.2 %collective-permute-start.18 = (f32[2,3,2,4,16,128]{5,4,3,2,1,0:T(8,128)S(1)}, f32[2,3,2,4,16,128]{5,4,3,2,1,0:T(8,128)S(1)}, u32[]{:S(2)}, u32[]{:S(2)}) collective-permute-start(f32[2,3,2,4,16,128]{5,4,3,2,1,0:T(8,128)S(1)} %pad_maximum_fusion.2), channel_id=1, source_target_pairs={{0,1},{1,0},{2,3},{3,2},{4,5},{5,4},{6,7},{7,6},{8,9},{9,8},{10,11... | collective-permute-start | bytes 1179656 | tf_op jit(solution)/shard_map/ppermute | solution.py:280
  114.9 17.1 %collective-permute-start.19 = (f32[1,3,2,4,16,128]{5,4,3,2,1,0:T(8,128)S(1)}, f32[1,3,2,4,16,128]{5,4,3,2,1,0:T(8,128)S(1)}, u32[]{:S(2)}, u32[]{:S(2)}) collective-permute-start(f32[1,3,2,4,16,128]{5,4,3,2,1,0:T(8,128)S(1)} %slice.105), channel_id=1, source_target_pairs={{0,4},{4,8},{8,12},{12,14},{14,10},{10,6},{6,2},{2,0},{1,5},{5,9},... | collective-permute-start | bytes 589832 | tf_op jit(solution)/shard_map/ppermute | solution.py:284
  116.1 15.9 %collective-permute-start.20 = (f32[1,3,2,4,16,128]{5,4,3,2,1,0:T(8,128)}, f32[1,3,2,4,16,128]{5,4,3,2,1,0:T(8,128)S(1)}, u32[]{:S(2)}, u32[]{:S(2)}) collective-permute-start(f32[1,3,2,4,16,128]{5,4,3,2,1,0:T(8,128)} %get-tuple-element.53), channel_id=1, source_target_pairs={{4,0},{8,4},{12,8},{14,12},{10,14},{6,10},{2,6},{0,2},{5,1},{9,5},... | collective-permute-start | bytes 589832 | tf_op jit(solution)/shard_map/ppermute | solution.py:284
  132.0 1.4 collective-permute-start.21

commit v3 on v2

--- a/solution.py
+++ b/solution.py
@@ -119,13 +119,18 @@
 
 
 def stack_kernel(place, shifts, floor, *refs, group, parts, blocks):
-    sources, out_ref, held = refs[: 6 * parts], refs[-2], refs[-1]
+    sources, out_ref = refs[: 6 * parts], refs[-6]
+    raw, whole, packed, near_packed, scale = refs[-5:]
     part, base = pl.program_id(0), pl.program_id(1) * group
-    epochs, kinds, count = held.shape[0], held.shape[1], held.shape[2]
+    epochs, count, reach = whole.shape[:3]
     tiles = count - 1
     lower = place[parts]
     lane = lax.broadcasted_iota(jnp.int32, (1, LANES), 1)
     at = [pl.multiple_of(row, MAXS) for row in (32 - 16 * lower, 16 + 16 * lower, 48 - 48 * lower)]
+    blank = pl.multiple_of(48 * lower, MAXS)
+    most_psi = ((1 << 23) - 1) // epochs
+    most_high = 255 // epochs
+    most_phi = most_high * 64 + 63
 
     for index in range(parts):
 
@@ -134,21 +139,54 @@
             block = place[index]
             keep_first = jnp.where(jnp.logical_and(block == 0, lane < MAXS), 0.0, 1.0) > 0.5
             keep_last = jnp.where(jnp.logical_and(block == blocks - 1, lane >= MAXS), 0.0, 1.0) > 0.5
-            blank = pl.multiple_of(48 * lower, MAXS)
-            held[:, :, :, pl.ds(blank, MAXS)] = jnp.zeros((epochs, kinds, count, MAXS, LANES), jnp.float32)
+            for epoch in range(epochs):
+                for kind in range(2):
+                    for tile in range(count):
+                        raw[epoch, kind, tile, pl.ds(blank, MAXS)] = jnp.zeros((MAXS, LANES), jnp.float32)
+            tops = [jnp.zeros((MAXS, LANES), jnp.float32) for _ in range(2)]
             for piece in range(3):
                 own, nearby = sources[6 * index + piece], sources[6 * index + 3 + piece]
                 rows = pl.ds(at[piece], MAXS)
                 for epoch in range(epochs):
-                    for kind in range(kinds):
-                        held[epoch, kind, 0, rows] = jnp.where(keep_first, own[0, epoch, kind, 0], 0.0)
-                        for tile in range(1, tiles):
-                            held[epoch, kind, tile, rows] = own[0, epoch, kind, tile]
-                        held[epoch, kind, tiles, rows] = jnp.where(keep_last, nearby[0, epoch, kind, 0], 0.0)
-
-    low = floor[0]
+                    for kind in range(2):
+                        for tile in range(count):
+                            if tile == tiles:
+                                value = jnp.where(keep_last, nearby[0, epoch, kind, 0], 0.0)
+                            elif tile == 0:
+                                value = jnp.where(keep_first, own[0, epoch, kind, 0], 0.0)
+                            else:
+                                value = own[0, epoch, kind, tile]
+                            tops[kind] = jnp.maximum(tops[kind], jnp.abs(value))
+                            raw[epoch, kind, tile, rows] = value
+            tops = [jnp.full((8, LANES), jnp.maximum(jnp.max(top), 1e-30), jnp.float32) for top in tops]
+            per_psi, per_phi = most_psi / tops[0], most_phi / tops[1]
+            scale[0] = floor[0] * per_phi
+            scale[1] = jnp.sqrt(per_phi) / per_psi
+
+            def quantize(index, _):
+                rows = pl.ds(pl.multiple_of(index * 8, 8), 8)
+                for epoch in range(epochs):
+                    lows = []
+                    for tile in range(count):
+                        psi = jnp.floor(raw[epoch, 0, tile, rows] * per_psi + 0.5).astype(jnp.int32)
+                        phi = jnp.floor(jnp.maximum(raw[epoch, 1, tile, rows], 0.0) * per_phi + 0.5).astype(jnp.int32)
+                        psi = jnp.clip(psi, -most_psi, most_psi)
+                        phi = jnp.minimum(phi, most_phi)
+                        whole[epoch, tile, rows] = psi * 256 + (phi >> 6)
+                        lows.append(phi & 63)
+                    here, nearby = lows[0], lows[1]
+                    for tile in range(1, tiles):
+                        here = here + (lows[tile] << (8 * tile))
+                        nearby = nearby + (lows[tile + 1] << (8 * tile))
+                    packed[epoch, rows] = here
+                    near_packed[epoch, rows] = nearby
+                return 0
+
+            lax.fori_loop(0, reach // 8, quantize, 0)
+
     height = out_ref.shape[1]
     across = lax.broadcasted_iota(jnp.int32, (8, LANES), 1)
+    least, unit = scale[0], scale[1]
 
     def one_velocity(local_index, _):
         start = (base + local_index) * epochs * 2
@@ -157,28 +195,31 @@
         beyond = [across < col for col in cols]
         turn = [jnp.where(col == 0, 0, LANES - col) for col in cols]
         for top in range(0, height, 8):
-            totals = [[None] * tiles for _ in range(kinds)]
+            totals, low_total = [None] * tiles, None
             for epoch in range(epochs):
-                for kind in range(kinds):
-                    loaded = [held[epoch, kind, tile, pl.ds(rows[epoch] + top, 8)] for tile in range(count)]
-                    for tile in range(tiles):
-                        merged = jnp.where(beyond[epoch], loaded[tile + 1], loaded[tile])
-                        moved = pltpu.roll(merged, turn[epoch], 1)
-                        totals[kind][tile] = moved if epoch == 0 else totals[kind][tile] + moved
+                here = pl.ds(rows[epoch] + top, 8)
+                loaded = [whole[epoch, tile, here] for tile in range(count)]
+                for tile in range(tiles):
+                    moved = pltpu.roll(jnp.where(beyond[epoch], loaded[tile + 1], loaded[tile]), turn[epoch], 1)
+                    totals[tile] = moved if epoch == 0 else totals[tile] + moved
+                moved = pltpu.roll(jnp.where(beyond[epoch], near_packed[epoch, here], packed[epoch, here]), turn[epoch], 1)
+                low_total = moved if epoch == 0 else low_total + moved
             for tile in range(tiles):
-                out_ref[local_index, top : top + 8, tile * LANES : (tile + 1) * LANES] = totals[0][tile] * lax.rsqrt(
-                    jnp.maximum(totals[1][tile], low)
+                psi = (totals[tile] >> 8).astype(jnp.float32)
+                phi = (((totals[tile] & 255) << 6) + ((low_total >> (8 * tile)) & 255)).astype(jnp.float32)
+                out_ref[local_index, top : top + 8, tile * LANES : (tile + 1) * LANES] = (
+                    psi * unit * lax.rsqrt(jnp.maximum(phi, least))
                 )
         return 0
 
-    lax.fori_loop(0, group, one_velocity, 0)
+    lax.fori_loop(0, group, one_velocity, 0, unroll=True)
 
 
 def stack_blocks(place, shifts, floor, sources, out, out_shape, parts, blocks):
     epochs, kinds, tiles = sources[0][0].shape[1:4]
     velocities, height, columns = out_shape.shape
     group = next(size for size in (12, 9, 8, 6, 4, 3, 2, 1) if velocities % size == 0)
-    width = tiles * LANES
+    width, reach = tiles * LANES, height + 2 * MAXS
     in_specs, operands = [], []
     for index, (array, slot) in enumerate(sources):
         depth = tiles if index % 6 < 3 else 1
@@ -199,7 +240,13 @@
             grid=(parts, velocities // group),
             in_specs=in_specs,
             out_specs=pl.BlockSpec((group, height, width), lambda part, chunk, place, *_: (chunk, 0, place[part])),
-            scratch_shapes=[pltpu.VMEM((epochs, kinds, tiles + 1, height + 2 * MAXS, LANES), jnp.float32)],
+            scratch_shapes=[
+                pltpu.VMEM((epochs, kinds, tiles + 1, reach, LANES), jnp.float32),
+                pltpu.VMEM((epochs, tiles + 1, reach, LANES), jnp.int32),
+                pltpu.VMEM((epochs, reach, LANES), jnp.int32),
+                pltpu.VMEM((epochs, reach, LANES), jnp.int32),
+                pltpu.VMEM((2, 8, LANES), jnp.float32),
+            ],
         ),
         out_shape=out_shape,
         input_output_aliases=aliases,

time: 149 us -> 125 us (0.84)
  Pallas kernels: 84.8 us -> 58.4 us
  waiting for transfers between devices: 15.4 us -> 17.3 us
    pallas_call x4, Pallas kernels: 59.8 us -> 33.4 us  [stack_blocks(): pl.pallas_call(functools.partial(stack_kernel, group=group, parts=parts,...]
    ppermute x3, waiting for transfers between devices: 0.59 us -> 2.53 us  [local(): lax.ppermute(behind, 'vel', right)]
  transfers between devices with their start and end apart: 22 -> 22, of which waited for: 6 -> 8; matrix products, arithmetic and copies ran while one was open for 9% -> 11% of each run, Pallas kernels for 37% -> 28%
where the time goes in v3:
time: 125 us; the launch traced here: 124 us
  Pallas kernels  58.4 us (47%)
  starting transfers between devices  24.2 us (19%)
  waiting for transfers between devices  17.3 us (14%)
  other arithmetic  14.9 us (12%)
  local copies, waits for them, and re-layouts  6.12 us (5%)
  between operations  2.93 us (2%)
    pallas_call x4, Pallas kernels, stack_blocks(): pl.pallas_call(functools.partial(stack_kernel, group=group, parts=parts,...  33.4 us
    pallas_call x1, Pallas kernels, correlate(): pl.pallas_call(correlate_kernel, in_specs=[pl.BlockSpec(memory_space=pltp...  15.3 us
    ppermute x7, starting transfers between devices, local(): chunk = lax.ppermute(chunk, 'vel', [(i, i ^ step) for i in range(blocks)])  12.4 us
    pallas_call x1, Pallas kernels, bands(): pl.pallas_call(band_kernel, in_specs=[pl.BlockSpec(memory_space=pltpu.SME...  9.72 us
    ppermute x3, waiting for transfers between devices, local(): lax.ppermute(ahead, 'vel', left)  9.34 us
    ppermute x3, starting transfers between devices, local(): lax.ppermute(ahead, 'vel', left)  4.91 us
    and x2, other arithmetic, local(): (row_ids >= valid_rows[epoch, 0]) & (row_ids < valid_rows[epoch, 1])  3.62 us
    another operation x7, other arithmetic, local(): jnp.stack([lax.dynamic_slice_in_dim(exposure, start, width, 1), lax.dynam...  3.32 us
  transfers between devices with their start and end apart: 22, of which 8 were waited for; matrix products, arithmetic and copies ran while one was open for 11% of the time, Pallas kernels for 28%

profile of v3, /device:TPU:0, one launch (start us, length us, event | category | flops | bytes accessed | tf_op | source)
XLA Modules:
  0.0 123.9 jit_solution(10681287155064047607)
XLA Ops:
  0.0 2.0 %constant_dynamic-slice_fusion = (f32[1,32,512]{2,1,0:T(8,128)S(1)}, f32[1,32,512]{2,1,0:T(8,128)S(1)}, f32[1,32,512]{2,1,0:T(8,128)S(1)}, f32[1,32,512]{2,1,0:T...) fusion(f32[1,32,4096]{2,1,0:T(8,128)} %param.7, ...), kind=kLoop, calls=%fused_computation.34 | loop fusion | bytes 2097184 | tf_op jit(solution)/shard_map/dynamic_slice | solution.py:287
  2.6 3.0 %collective-permute-start.6 = (f32[2,32,512]{2,1,0:T(8,128)}, f32[2,32,512]{2,1,0:T(8,128)S(1)}, u32[]{:S(2)}, u32[]{:S(2)}) collective-permute-start(f32[2,32,512]{2,1,0:T(8,128)} %pad_maximum_fusion.9), channel_id=1, source_target_pairs={{0,4},{2,6},{4,0},{6,2},{8,12},{10,14},{12,8},{14,10},{1,5},{3,7},... | collective-permute-start | bytes 393224 | tf_op jit(solution)/shard_map/ppermute | solution.py:291
  5.7 3.5 %collective-permute-start = (f32[2,32,512]{2,1,0:T(8,128)S(1)}, f32[2,32,512]{2,1,0:T(8,128)S(1)}, u32[]{:S(2)}, u32[]{:S(2)}) collective-permute-start(f32[2,32,512]{2,1,0:T(8,128)S(1)} %pad_maximum_fusion.3), channel_id=1, source_target_pairs={{0,14},{2,12},{4,10},{6,8},{8,6},{10,4},{12,2},{14,0},{1,15},{3,13... | collective-permute-start | bytes 393224 | tf_op jit(solution)/shard_map/ppermute | solution.py:291
  10.4 1.3 %collective-permute-start.2 = (f32[2,32,512]{2,1,0:T(8,128)}, f32[2,32,512]{2,1,0:T(8,128)S(1)}, u32[]{:S(2)}, u32[]{:S(2)}) collective-permute-start(f32[2,32,512]{2,1,0:T(8,128)} %pad_maximum_fusion.5), channel_id=1, source_target_pairs={{0,12},{2,14},{4,8},{6,10},{8,4},{10,6},{12,0},{14,2},{1,13},{3,15... | collective-permute-start | bytes 393224 | tf_op jit(solution)/shard_map/ppermute | solution.py:291
  12.4 1.7 %collective-permute-start.3 = (f32[2,32,512]{2,1,0:T(8,128)}, f32[2,32,512]{2,1,0:T(8,128)S(1)}, u32[]{:S(2)}, u32[]{:S(2)}) collective-permute-start(f32[2,32,512]{2,1,0:T(8,128)} %pad_maximum_fusion.6), channel_id=1, source_target_pairs={{0,10},{2,8},{4,14},{6,12},{8,2},{10,0},{12,6},{14,4},{1,11},{3,9}... | collective-permute-start | bytes 393224 | tf_op jit(solution)/shard_map/ppermute | solution.py:291
  14.2 1.5 %fusion.5 = (s32[1,1]{0,1:T(1,128)}, s32[1,1]{0,1:T(1,128)}, s32[1,1]{0,1:T(1,128)}, s32[1,1]{0,1:T(1,128)}, s32[1,1]{0,1:T(1,128)}, /*index=5*/s32[1,1]{0,1:T(1,128)}) fusion(s32[3,2]{0,1:T(2,128)} %param.11), kind=kLoop, calls=%fused_computation.61 | loop fusion | bytes 48 | tf_op jit(solution)/shard_map/slice | solution.py:304
  17.0 2.0 %fusion.3 = (f32[1,21,21]{2,1,0:T(8,128)S(1)}, f32[1,21,21]{2,1,0:T(8,128)S(1)}, f32[]{:T(128)}) fusion(f32[21,21]{1,0:T(8,128)} %param.8, f32[]{:T(128)} %reduce_sum.18), kind=kLoop, calls=%fused_computation.59 | loop fusion | flops 1322 | bytes 5300 | tf_op jit(solution)/shard_map/stack | solution.py:279
  19.7 1.4 %fusion.6 = (s32[1]{0:T(128)}, s32[1]{0:T(128)}, s32[1]{0:T(128)}) fusion(s32[3]{0:T(128)} %param.10), kind=kLoop, calls=%fused_computation.62 | loop fusion | bytes 24 | tf_op jit(solution)/shard_map/slice | solution.py:300
  21.8 2.1 %collective-permute-start.4 = (f32[2,32,512]{2,1,0:T(8,128)}, f32[2,32,512]{2,1,0:T(8,128)}, u32[]{:S(2)}, u32[]{:S(2)}) collective-permute-start(f32[2,32,512]{2,1,0:T(8,128)} %pad_maximum_fusion.7), channel_id=1, source_target_pairs={{0,8},{2,10},{4,12},{6,14},{8,0},{10,2},{12,4},{14,6},{1,9},{3,11}... | collective-permute-start | bytes 393224 | tf_op jit(solution)/shard_map/ppermute | solution.py:291
  27.4 2.4 %compare_and_fusion = (pred[32]{0:T(512)(128)(4,1)S(1)}, pred[32]{0:T(512)(128)(4,1)S(1)}) fusion(s32[]{:T(128)} %bitcast.16, s32[]{:T(128)} %bitcast.15, s32[]{:T(128)S(6)} %mul.31, s32[]{:T(128)} %bitcast.12, s32[]{:T(128)} %bitcast.11), kind=kLoop, calls=%fused_computation.50 | loop fusion | flops 224 | bytes 84 | tf_op jit(solution)/shard_map/and | solution.py:304
  29.8 9.7 %shard_map.64 = (bf16[2,21,256,128]{3,2,1,0:T(8,128)(2,1)S(1)}, bf16[2,21,256,256]{3,2,1,0:T(8,128)(2,1)}) custom-call(f32[882]{0:T(1024)S(1)} %reshape.110.taps), custom_call_target="tpu_custom_call" | custom-call | bytes 25165824 | tf_op jit(solution)/shard_map/pallas_call | solution.py:38
  42.8 2.6 %collective-permute-start.7 = (f32[3,2,32,128]{3,2,1,0:T(8,128)S(1)}, f32[3,2,32,128]{3,2,1,0:T(8,128)S(1)}, u32[]{:S(2)}, u32[]{:S(2)}) collective-permute-start(f32[3,2,32,128]{3,2,1,0:T(8,128)S(1)} %pad_maximum_fusion.11), channel_id=1, source_target_pairs={{0,4},{4,8},{8,12},{12,14},{14,10},{10,6},{6,2},{2,0},{1,5},{5,9},... | collective-permute-start | bytes 294920 | tf_op jit(solution)/shard_map/ppermute | solution.py:309
  45.5 2.2 %collective-permute-done.7 = f32[3,2,32,128]{3,2,1,0:T(8,128)S(1)} collective-permute-done((f32[3,2,32,128]{3,2,1,0:T(8,128)S(1)}, f32[3,2,32,128]{3,2,1,0:T(8,128)S(1)}, u32[]{:S(2)}, u32[]{:S(2)}) %collective-permute-start.7) | collective-permute-done | bytes 98336 | tf_op jit(solution)/shard_map/ppermute | solution.py:309
  48.8 1.4 %collective-permute-done.8.border = f32[3,2,16,640]{3,2,1,0:T(8,128)S(1)} collective-permute-done((f32[3,2,16,640]{3,2,1,0:T(8,128)S(1)}, f32[3,2,16,640]{3,2,1,0:T(8,128)S(1)}, u32[]{:S(2)}, u32[]{:S(2)}) %collective-permute-start.8) | collective-permute-done | bytes 245792 | tf_op jit(solution)/shard_map/ppermute | solution.py:311
  50.2 15.3 %shard_map.65.refs_0_.refs_1_.refs_9_.refs_10_ = f32[2,3,2,4,16,128]{5,4,3,2,1,0:T(8,128)S(1)} custom-call(s32[2]{0:T(128)S(1)} %pad_add_fusion.place, f32[3,2,32,640]{3,2,1,0:T(8,128)S(1)} %maximum_maximum_fusion.wide, f32[3,2,16,640]{3,2,1,0:T(8,128)S(1)} %collective-permute-done.8.border, bf16[2,21,256,128]{3,2,1,0:T(8,128)(2,1)S(1)} %get-tuple-element.26.high_ref, ...), custom_call_target="tpu_custom_call" | custom-call | flops 3963617280 | bytes 12582912 | tf_op jit(solution)/shard_map/pallas_call | solution.py:107
  65.5 1.5 %collective-permute-start.11 = (f32[2,3,2,4,16,128]{5,4,3,2,1,0:T(8,128)S(1)}, f32[2,3,2,4,16,128]{5,4,3,2,1,0:T(8,128)S(1)}, u32[]{:S(2)}, u32[]{:S(2)}) collective-permute-start(f32[2,3,2,4,16,128]{5,4,3,2,1,0:T(8,128)S(1)} %shard_map.65.refs_0_.refs_1_.refs_9_.refs_10_), channel_id=1, source_target_pairs={{4,0},{8,4},{12,8},{14,12},{10,14},{6,10},{2,6},{0,2},{5,1},{9,5},... | collective-permute-start | bytes 1179656 | tf_op jit(solution)/shard_map/ppermute | solution.py:324
  68.1 9.3 %collective-permute-done.11.refs_3_.refs_4_.refs_0_.refs_1_ = f32[2,3,2,4,16,128]{5,4,3,2,1,0:T(8,128)S(1)} collective-permute-done((f32[2,3,2,4,16,128]{5,4,3,2,1,0:T(8,128)S(1)}, f32[2,3,2,4,16,128]{5,4,3,2,1,0:T(8,128)S(1)}, u32[]{:S(2)}, u32[]{:S(2)}) %collective-permute-start.11) | collective-permute-done | bytes 393248 | tf_op jit(solution)/shard_map/ppermute | solution.py:324
  78.1 1.8 %collective-permute-start.12 = (f32[2,3,2,4,16,128]{5,4,3,2,1,0:T(8,128)S(1)}, f32[2,3,2,4,16,128]{5,4,3,2,1,0:T(8,128)S(1)}, u32[]{:S(2)}, u32[]{:S(2)}) collective-permute-start(f32[2,3,2,4,16,128]{5,4,3,2,1,0:T(8,128)S(1)} %collective-permute-done.11.refs_3_.refs_4_.refs_0_.refs_1_), channel_id=1, source_target_pairs={{4,0},{8,4},{12,8},{14,12},{10,14},{6,10},{2,6},{0,2},{5,1},{9,5},... | collective-permute-start | bytes 1179656 | tf_op jit(solution)/shard_map/ppermute | solution.py:324
  81.7 8.3 %shard_map.66.refs_12_ = f32[36,32,4096]{2,1,0:T(8,128)} custom-call(s32[3]{0:T(128)S(1)} %add_add_fusion.1.place, s32[216]{0:T(256)S(1)} %reshape.108.shifts, f32[1]{0:T(128)} %bitcast.3.floor, f32[2,3,2,4,16,128]{5,4,3,2,1,0:T(8,128)S(1)} %shard_map.65.refs_0_.refs_1_.refs_9_.refs_10_, ...), custom_call_target="tpu_custom_call" | custom-call | flops 18874368 | bytes 28311552 | tf_op jit(solution)/shard_map/pallas_call | solution.py:236
  91.6 1.7 %collective-permute-start.16 = (f32[2,3,2,4,16,128]{5,4,3,2,1,0:T(8,128)S(1)}, f32[2,3,2,4,16,128]{5,4,3,2,1,0:T(8,128)S(1)}, u32[]{:S(2)}, u32[]{:S(2)}) collective-permute-start(f32[2,3,2,4,16,128]{5,4,3,2,1,0:T(8,128)S(1)} %collective-permute-done.12.refs_3_.refs_4_.refs_0_.refs_1_), channel_id=1, source_target_pairs={{4,0},{8,4},{12,8},{14,12},{10,14},{6,10},{2,6},{0,2},{5,1},{9,5},... | collective-permute-start | bytes 1179656 | tf_op jit(solution)/shard_map/ppermute | solution.py:324
  93.4 8.3 %shard_map.67.refs_12_ = f32[36,32,4096]{2,1,0:T(8,128)} custom-call(s32[3]{0:T(128)S(1)} %add_add_fusion.2.place, s32[216]{0:T(256)S(1)} %reshape.108.shifts, f32[1]{0:T(128)} %bitcast.3.floor, f32[2,3,2,4,16,128]{5,4,3,2,1,0:T(8,128)S(1)} %collective-permute-done.11.refs_3_.refs_4_.refs_0_.refs_1_, ...), custom_call_target="tpu_custom_call", output_to_operand_aliasing={{}: (15, {})} | custom-call | flops 18874368 | bytes 28311552 | tf_op jit(solution)/shard_map/pallas_call | solution.py:236
  103.6 1.7 %collective-permute-start.19 = (f32[1,3,2,4,16,128]{5,4,3,2,1,0:T(8,128)S(1)}, f32[1,3,2,4,16,128]{5,4,3,2,1,0:T(8,128)S(1)}, u32[]{:S(2)}, u32[]{:S(2)}) collective-permute-start(f32[1,3,2,4,16,128]{5,4,3,2,1,0:T(8,128)S(1)} %slice.105), channel_id=1, source_target_pairs={{0,4},{4,8},{8,12},{12,14},{14,10},{10,6},{6,2},{2,0},{1,5},{5,9},... | collective-permute-start | bytes 589832 | tf_op jit(solution)/shard_map/ppermute | solution.py:331
  105.7 8.3 %shard_map.68.refs_12_ = f32[36,32,4096]{2,1,0:T(8,128)} custom-call(s32[3]{0:T(128)S(1)} %add_add_fusion.3.place, s32[216]{0:T(256)S(1)} %reshape.108.shifts, f32[1]{0:T(128)} %bitcast.3.floor, f32[2,3,2,4,16,128]{5,4,3,2,1,0:T(8,128)S(1)} %collective-permute-done.12.refs_3_.refs_4_.refs_0_.refs_1_, ...), custom_call_target="tpu_custom_call", output_to_operand_aliasing={{}: (15, {})} | custom-call | flops 18874368 | bytes 28311552 | tf_op jit(solution)/shard_map/pallas_call | solution.py:236
  115.5 8.3 %shard_map.69 = f32[36,32,4096]{2,1,0:T(8,128)} custom-call(s32[3]{0:T(128)S(1)} %add_add_fusion.place, s32[216]{0:T(256)S(1)} %reshape.108.shifts, f32[1]{0:T(128)} %bitcast.3.floor, f32[2,3,2,4,16,128]{5,4,3,2,1,0:T(8,128)S(1)} %collective-permute-done.16.refs_3_.refs_4_.refs_0_.refs_1_, ...), custom_call_target="tpu_custom_call", output_to_operand_aliasing={{}: (15, {})} | custom-call | flops 18874368 | bytes 28311552 | tf_op jit(solution)/shard_map/pallas_call | solution.py:236
  (75 shorter events, 19.2 us)
Async XLA Ops:
  0.0 80.3 %copy-start.1 = (s32[36,3,2]{0,2,1:T(2,128)S(1)}, s32[36,3,2]{0,2,1:T(2,128)}, u32[]{:S(2)}) copy-start(s32[36,3,2]{0,2,1:T(2,128)} %param.9) | copy-start | bytes 2596
  2.6 36.9 %collective-permute-start.6 = (f32[2,32,512]{2,1,0:T(8,128)}, f32[2,32,512]{2,1,0:T(8,128)S(1)}, u32[]{:S(2)}, u32[]{:S(2)}) collective-permute-start(f32[2,32,512]{2,1,0:T(8,128)} %pad_maximum_fusion.9), channel_id=1, source_target_pairs={{0,4},{2,6},{4,0},{6,2},{8,12},{10,14},{12,8},{14,10},{1,5},{3,7},... | collective-permute-start | bytes 393224 | tf_op jit(solution)/shard_map/ppermute | solution.py:291
  5.7 16.1 %collective-permute-start = (f32[2,32,512]{2,1,0:T(8,128)S(1)}, f32[2,32,512]{2,1,0:T(8,128)S(1)}, u32[]{:S(2)}, u32[]{:S(2)}) collective-permute-start(f32[2,32,512]{2,1,0:T(8,128)S(1)} %pad_maximum_fusion.3), channel_id=1, source_target_pairs={{0,14},{2,12},{4,10},{6,8},{8,6},{10,4},{12,2},{14,0},{1,15},{3,13... | collective-permute-start | bytes 393224 | tf_op jit(solution)/shard_map/ppermute | solution.py:291
  9.2 14.8 %collective-permute-start.1 = (f32[2,32,512]{2,1,0:T(8,128)S(1)}, f32[2,32,512]{2,1,0:T(8,128)S(1)}, u32[]{:S(2)}, u32[]{:S(2)}) collective-permute-start(f32[2,32,512]{2,1,0:T(8,128)S(1)} %pad_maximum_fusion.4), channel_id=1, source_target_pairs={{0,2},{2,0},{4,6},{6,4},{8,10},{10,8},{12,14},{14,12},{1,3},{3,1},... | collective-permute-start | bytes 393224 | tf_op jit(solution)/shard_map/ppermute | solution.py:291
  10.4 29.1 %collective-permute-start.2 = (f32[2,32,512]{2,1,0:T(8,128)}, f32[2,32,512]{2,1,0:T(8,128)S(1)}, u32[]{:S(2)}, u32[]{:S(2)}) collective-permute-start(f32[2,32,512]{2,1,0:T(8,128)} %pad_maximum_fusion.5), channel_id=1, source_target_pairs={{0,12},{2,14},{4,8},{6,10},{8,4},{10,6},{12,0},{14,2},{1,13},{3,15... | collective-permute-start | bytes 393224 | tf_op jit(solution)/shard_map/ppermute | solution.py:291
  12.4 27.1 %collective-permute-start.3 = (f32[2,32,512]{2,1,0:T(8,128)}, f32[2,32,512]{2,1,0:T(8,128)S(1)}, u32[]{:S(2)}, u32[]{:S(2)}) collective-permute-start(f32[2,32,512]{2,1,0:T(8,128)} %pad_maximum_fusion.6), channel_id=1, source_target_pairs={{0,10},{2,8},{4,14},{6,12},{8,2},{10,0},{12,6},{14,4},{1,11},{3,9}... | collective-permute-start | bytes 393224 | tf_op jit(solution)/shard_map/ppermute | solution.py:291
  21.8 17.7 %collective-permute-start.4 = (f32[2,32,512]{2,1,0:T(8,128)}, f32[2,32,512]{2,1,0:T(8,128)}, u32[]{:S(2)}, u32[]{:S(2)}) collective-permute-start(f32[2,32,512]{2,1,0:T(8,128)} %pad_maximum_fusion.7), channel_id=1, source_target_pairs={{0,8},{2,10},{4,12},{6,14},{8,0},{10,2},{12,4},{14,6},{1,9},{3,11}... | collective-permute-start | bytes 393224 | tf_op jit(solution)/shard_map/ppermute | solution.py:291
  23.9 15.6 %collective-permute-start.5 = (f32[2,32,512]{2,1,0:T(8,128)}, f32[2,32,512]{2,1,0:T(8,128)}, u32[]{:S(2)}, u32[]{:S(2)}) collective-permute-start(f32[2,32,512]{2,1,0:T(8,128)} %pad_maximum_fusion.8), channel_id=1, source_target_pairs={{0,6},{2,4},{4,2},{6,0},{8,14},{10,12},{12,10},{14,8},{1,7},{3,5},... | collective-permute-start | bytes 393224 | tf_op jit(solution)/shard_map/ppermute | solution.py:291
  40.6 2.2 %copy-start = (f32[1,2,32,512]{3,2,1,0:T(8,128)}, f32[1,2,32,512]{3,2,1,0:T(8,128)S(1)}, u32[]{:S(2)}) copy-start(f32[1,2,32,512]{3,2,1,0:T(8,128)S(1)} %maximum_bitcast_fusion.2) | copy-start | bytes 393220
  42.8 4.8 %collective-permute-start.7 = (f32[3,2,32,128]{3,2,1,0:T(8,128)S(1)}, f32[3,2,32,128]{3,2,1,0:T(8,128)S(1)}, u32[]{:S(2)}, u32[]{:S(2)}) collective-permute-start(f32[3,2,32,128]{3,2,1,0:T(8,128)S(1)} %pad_maximum_fusion.11), channel_id=1, source_target_pairs={{0,4},{4,8},{8,12},{12,14},{14,10},{10,6},{6,2},{2,0},{1,5},{5,9},... | collective-permute-start | bytes 294920 | tf_op jit(solution)/shard_map/ppermute | solution.py:309
  48.6 1.6 %collective-permute-start.8 = (f32[3,2,16,640]{3,2,1,0:T(8,128)S(1)}, f32[3,2,16,640]{3,2,1,0:T(8,128)S(1)}, u32[]{:S(2)}, u32[]{:S(2)}) collective-permute-start(f32[3,2,16,640]{3,2,1,0:T(8,128)S(1)} %slice_select_fusion), channel_id=1, source_target_pairs={{0,1},{1,0},{2,3},{3,2},{4,5},{5,4},{6,7},{7,6},{8,9},{9,8},{10,11... | collective-permute-start | bytes 737288 | tf_op jit(solution)/shard_map/ppermute | solution.py:311
  65.5 11.9 %collective-permute-start.11 = (f32[2,3,2,4,16,128]{5,4,3,2,1,0:T(8,128)S(1)}, f32[2,3,2,4,16,128]{5,4,3,2,1,0:T(8,128)S(1)}, u32[]{:S(2)}, u32[]{:S(2)}) collective-permute-start(f32[2,3,2,4,16,128]{5,4,3,2,1,0:T(8,128)S(1)} %shard_map.65.refs_0_.refs_1_.refs_9_.refs_10_), channel_id=1, source_target_pairs={{4,0},{8,4},{12,8},{14,12},{10,14},{6,10},{2,6},{0,2},{5,1},{9,5},... | collective-permute-start | bytes 1179656 | tf_op jit(solution)/shard_map/ppermute | solution.py:324
  67.0 10.9 %collective-permute-start.9 = (f32[2,3,2,4,16,128]{5,4,3,2,1,0:T(8,128)S(1)}, f32[2,3,2,4,16,128]{5,4,3,2,1,0:T(8,128)S(1)}, u32[]{:S(2)}, u32[]{:S(2)}) collective-permute-start(f32[2,3,2,4,16,128]{5,4,3,2,1,0:T(8,128)S(1)} %shard_map.65.refs_0_.refs_1_.refs_9_.refs_10_), channel_id=1, source_target_pairs={{0,4},{4,8},{8,12},{12,14},{14,10},{10,6},{6,2},{2,0},{1,5},{5,9},... | collective-permute-start | bytes 1179656 | tf_op jit(solution)/shard_map/ppermute | solution.py:324
  78.0 3.7 %collective-permute-start.14 = (f32[2,3,2,4,16,128]{5,4,3,2,1,0:T(8,128)S(1)}, f32[2,3,2,4,16,128]{5,4,3,2,1,0:T(8,128)S(1)}, u32[]{:S(2)}, u32[]{:S(2)}) collective-permute-start(f32[2,3,2,4,16,128]{5,4,3,2,1,0:T(8,128)S(1)} %pad_maximum_fusion), channel_id=1, source_target_pairs={{0,1},{1,0},{2,3},{3,2},{4,5},{5,4},{6,7},{7,6},{8,9},{9,8},{10,11... | collective-permute-start | bytes 1179656 | tf_op jit(solution)/shard_map/ppermute | solution.py:327
  78.1 11.9 %collective-permute-start.12 = (f32[2,3,2,4,16,128]{5,4,3,2,1,0:T(8,128)S(1)}, f32[2,3,2,4,16,128]{5,4,3,2,1,0:T(8,128)S(1)}, u32[]{:S(2)}, u32[]{:S(2)}) collective-permute-start(f32[2,3,2,4,16,128]{5,4,3,2,1,0:T(8,128)S(1)} %collective-permute-done.11.refs_3_.refs_4_.refs_0_.refs_1_), channel_id=1, source_target_pairs={{4,0},{8,4},{12,8},{14,12},{10,14},{6,10},{2,6},{0,2},{5,1},{9,5},... | collective-permute-start | bytes 1179656 | tf_op jit(solution)/shard_map/ppermute | solution.py:324
  79.9 11.2 %collective-permute-start.10 = (f32[2,3,2,4,16,128]{5,4,3,2,1,0:T(8,128)S(1)}, f32[2,3,2,4,16,128]{5,4,3,2,1,0:T(8,128)S(1)}, u32[]{:S(2)}, u32[]{:S(2)}) collective-permute-start(f32[2,3,2,4,16,128]{5,4,3,2,1,0:T(8,128)S(1)} %collective-permute-done.9.refs_6_.refs_7_.refs_9_.refs_10_), channel_id=1, source_target_pairs={{0,4},{4,8},{8,12},{12,14},{14,10},{10,6},{6,2},{2,0},{1,5},{5,9},... | collective-permute-start | bytes 1179656 | tf_op jit(solution)/shard_map/ppermute | solution.py:324
  80.2 1.5 %collective-permute-start.13 = (f32[1,3,2,4,16,128]{5,4,3,2,1,0:T(8,128)S(1)}, f32[1,3,2,4,16,128]{5,4,3,2,1,0:T(8,128)S(1)}, u32[]{:S(2)}, u32[]{:S(2)}) collective-permute-start(f32[1,3,2,4,16,128]{5,4,3,2,1,0:T(8,128)S(1)} %slice.116), channel_id=1, source_target_pairs={{0,1},{1,0},{2,3},{3,2},{4,5},{5,4},{6,7},{7,6},{8,9},{9,8},{10,11... | collective-permute-start | bytes 589832 | tf_op jit(solution)/shard_map/ppermute | solution.py:317
  91.1 2.2 %collective-permute-start.17 = (f32[2,3,2,4,16,128]{5,4,3,2,1,0:T(8,128)S(1)}, f32[2,3,2,4,16,128]{5,4,3,2,1,0:T(8,128)S(1)}, u32[]{:S(2)}, u32[]{:S(2)}) collective-permute-start(f32[2,3,2,4,16,128]{5,4,3,2,1,0:T(8,128)S(1)} %pad_maximum_fusion.1), channel_id=1, source_target_pairs={{0,1},{1,0},{2,3},{3,2},{4,5},{5,4},{6,7},{7,6},{8,9},{9,8},{10,11... | collective-permute-start | bytes 1179656 | tf_op jit(solution)/shard_map/ppermute | solution.py:327
  91.2 11.5 %collective-permute-start.15 = (f32[2,3,2,4,16,128]{5,4,3,2,1,0:T(8,128)S(1)}, f32[2,3,2,4,16,128]{5,4,3,2,1,0:T(8,128)S(1)}, u32[]{:S(2)}, u32[]{:S(2)}) collective-permute-start(f32[2,3,2,4,16,128]{5,4,3,2,1,0:T(8,128)S(1)} %collective-permute-done.10.refs_6_.refs_7_.refs_9_.refs_10_), channel_id=1, source_target_pairs={{0,4},{4,8},{8,12},{12,14},{14,10},{10,6},{6,2},{2,0},{1,5},{5,9},... | collective-permute-start | bytes 1179656 | tf_op jit(solution)/shard_map/ppermute | solution.py:324
  91.6 11.1 %collective-permute-start.16 = (f32[2,3,2,4,16,128]{5,4,3,2,1,0:T(8,128)S(1)}, f32[2,3,2,4,16,128]{5,4,3,2,1,0:T(8,128)S(1)}, u32[]{:S(2)}, u32[]{:S(2)}) collective-permute-start(f32[2,3,2,4,16,128]{5,4,3,2,1,0:T(8,128)S(1)} %collective-permute-done.12.refs_3_.refs_4_.refs_0_.refs_1_), channel_id=1, source_target_pairs={{4,0},{8,4},{12,8},{14,12},{10,14},{6,10},{2,6},{0,2},{5,1},{9,5},... | collective-permute-start | bytes 1179656 | tf_op jit(solution)/shard_map/ppermute | solution.py:324
  103.5 2.2 %collective-permute-start.18 = (f32[2,3,2,4,16,128]{5,4,3,2,1,0:T(8,128)S(1)}, f32[2,3,2,4,16,128]{5,4,3,2,1,0:T(8,128)S(1)}, u32[]{:S(2)}, u32[]{:S(2)}) collective-permute-start(f32[2,3,2,4,16,128]{5,4,3,2,1,0:T(8,128)S(1)} %pad_maximum_fusion.2), channel_id=1, source_target_pairs={{0,1},{1,0},{2,3},{3,2},{4,5},{5,4},{6,7},{7,6},{8,9},{9,8},{10,11... | collective-permute-start | bytes 1179656 | tf_op jit(solution)/shard_map/ppermute | solution.py:327
  103.6 10.5 %collective-permute-start.19 = (f32[1,3,2,4,16,128]{5,4,3,2,1,0:T(8,128)S(1)}, f32[1,3,2,4,16,128]{5,4,3,2,1,0:T(8,128)S(1)}, u32[]{:S(2)}, u32[]{:S(2)}) collective-permute-start(f32[1,3,2,4,16,128]{5,4,3,2,1,0:T(8,128)S(1)} %slice.105), channel_id=1, source_target_pairs={{0,4},{4,8},{8,12},{12,14},{14,10},{10,6},{6,2},{2,0},{1,5},{5,9},... | collective-permute-start | bytes 589832 | tf_op jit(solution)/shard_map/ppermute | solution.py:331
  105.3 8.8 %collective-permute-start.20 = (f32[1,3,2,4,16,128]{5,4,3,2,1,0:T(8,128)}, f32[1,3,2,4,16,128]{5,4,3,2,1,0:T(8,128)S(1)}, u32[]{:S(2)}, u32[]{:S(2)}) collective-permute-start(f32[1,3,2,4,16,128]{5,4,3,2,1,0:T(8,128)} %get-tuple-element.53), channel_id=1, source_target_pairs={{4,0},{8,4},{12,8},{14,12},{10,14},{6,10},{2,6},{0,2},{5,1},{9,5},... | collective-permute-start | bytes 589832 | tf_op jit(solution)/shard_map/ppermute | solution.py:331
  114.1 1.4 %collective-permute-start.21 = (f32[1,3,2,4,16,128]{5,4,3,2,1,0:T(8,128)S(1)}, f32[1,3,2,4,16,128]{5,4,3,2,1,0:T(8,128)S(1)}, u32[]{:S(2)}, u32[]{:S(2)}) collective-permute-start(f32[1,3,2,4,16,128]{5,4,3,2,1,0:T(8,128)S(1)} %collective-permute-done.19.refs_3_.refs_6_), channel_id=1, source_target_pairs={{0,1},{1,0},{2,3},{3,2},{4,5},{5,4},{6,7},{7,6},{8,9},{9,8},{10,11... | collective-permute-start | bytes 589832 | tf_op jit(solution)/shard_map/ppermute | solution.py:334

commit v4 on v3

--- a/solution.py
+++ b/solution.py
@@ -8,114 +8,190 @@
 
 LANES = 128
 MAXS = 16
-VMEM = 48 << 20
-
-
-def band_kernel(taps, high_ref, both_ref):
-    kinds, ksize = both_ref.shape[0], both_ref.shape[1]
+VMEM = 24 << 20
+
+
+def band_kernel(taps, kernel, bands_ref, floor_ref):
+    ksize = kernel.shape[0]
     skip = LANES - MAXS - ksize // 2
-    inner = lax.broadcasted_iota(jnp.int32, (2 * LANES, LANES), 0)
-    outer = lax.broadcasted_iota(jnp.int32, (2 * LANES, LANES), 1)
-    offset = inner - outer - skip
-
-    def one(index, _):
-        kind, row = index // ksize, index % ksize
-        band = jnp.zeros((2 * LANES, LANES), jnp.float32)
+    top = skip // 8 * 8
+    shape = (2 * LANES - top, LANES)
+    offset = lax.broadcasted_iota(jnp.int32, shape, 0) - lax.broadcasted_iota(jnp.int32, shape, 1) + (top - skip)
+    total = jnp.full((8, LANES), jnp.sum(kernel[...]), jnp.float32)
+    norm = kernel[...] / total[:1, :1]
+    floor_ref[...] = jnp.full(floor_ref.shape, 0.5 * jnp.sum(norm * norm), jnp.float32)
+    bands_ref[:, :, :top] = jnp.zeros(bands_ref.shape[:2] + (top, 2 * LANES), jnp.bfloat16)
+
+    def one(row, _):
+        band = jnp.zeros(shape, jnp.float32)
         for col in range(ksize):
-            band = jnp.where(offset == col, taps[index * ksize + col], band)
-        high = band.astype(jnp.bfloat16)
-        low = (band - high.astype(jnp.float32)).astype(jnp.bfloat16)
-        high_ref[kind, row] = high
-        both_ref[kind, row, :, :LANES] = high
-        both_ref[kind, row, :, LANES:] = low
+            band = jnp.where(offset == col, taps[row * ksize + col], band)
+        band = band / total[:1]
+        for kind, value in enumerate((band, band * band)):
+            high = value.astype(jnp.bfloat16)
+            bands_ref[kind, row, top:, :LANES] = high
+            bands_ref[kind, row, top:, LANES:] = (value - high.astype(jnp.float32)).astype(jnp.bfloat16)
         return 0
 
-    lax.fori_loop(0, kinds * ksize, one, 0)
-
-
-def bands(taps, ksize):
-    shape = (2, ksize, 2 * LANES)
+    lax.fori_loop(0, ksize, one, 0)
+
+
+def make_bands(spread_kernel):
+    ksize = spread_kernel.shape[0]
     return pl.pallas_call(
         band_kernel,
-        in_specs=[pl.BlockSpec(memory_space=pltpu.SMEM)],
+        in_specs=[pl.BlockSpec(memory_space=pltpu.SMEM), pl.BlockSpec(memory_space=pltpu.VMEM)],
         out_specs=[pl.BlockSpec(memory_space=pltpu.VMEM)] * 2,
         out_shape=[
-            jax.ShapeDtypeStruct(shape + (LANES,), jnp.bfloat16),
-            jax.ShapeDtypeStruct(shape + (2 * LANES,), jnp.bfloat16),
+            jax.ShapeDtypeStruct((2, ksize, 2 * LANES, 2 * LANES), jnp.bfloat16),
+            jax.ShapeDtypeStruct((8, LANES), jnp.float32),
         ],
         compiler_params=pltpu.CompilerParams(vmem_limit_bytes=VMEM),
-        cost_estimate=pl.CostEstimate(flops=0, bytes_accessed=24 << 20, transcendentals=0),
-    )(taps)
-
-
-def correlate_kernel(place, wide, border, high_ref, both_ref, rows_ref, ext, summed):
-    epochs, kinds, height, width = wide.shape
-    ksize = high_ref.shape[1]
-    tiles = width // LANES - 1
+        cost_estimate=pl.CostEstimate(flops=0, bytes_accessed=20 << 20, transcendentals=0),
+    )(spread_kernel.reshape(-1), spread_kernel)
+
+
+def cut_kernel(starts, exposure, noise_var, *chunk_refs):
+    for index, ref in enumerate(chunk_refs):
+        columns = pl.ds(pl.multiple_of(starts[index], LANES), ref.shape[2])
+        ref[0] = exposure[:, columns]
+        ref[1] = noise_var[:, columns]
+
+
+def cut(starts, exposure, noise_var, blocks):
+    height, columns = exposure.shape
+    return pl.pallas_call(
+        cut_kernel,
+        in_specs=[pl.BlockSpec(memory_space=pltpu.SMEM)] + [pl.BlockSpec(memory_space=pltpu.VMEM)] * 2,
+        out_specs=[pl.BlockSpec(memory_space=pltpu.VMEM)] * blocks,
+        out_shape=[jax.ShapeDtypeStruct((2, height, columns // blocks), jnp.float32)] * blocks,
+        compiler_params=pltpu.CompilerParams(vmem_limit_bytes=VMEM),
+        cost_estimate=pl.CostEstimate(flops=0, bytes_accessed=16 * height * columns, transcendentals=0),
+    )(starts, exposure, noise_var)
+
+
+def pick_kernel(place, owner, valid, *refs):
+    chunks, (own, last, edges, corner, chosen) = refs[:-5], refs[-5:]
+    epochs, _, tiles, height, _ = own.shape
+    me, lower = place[0], place[1]
+    for epoch in range(epochs):
+        for step, chunk in enumerate(chunks):
+
+            @pl.when(owner[epoch] ^ me == step)
+            def _():
+                chosen[epoch] = chunk[...]
+
+    row_ids = lower * height + lax.broadcasted_iota(jnp.int32, (height, LANES), 0)
+    for epoch in range(epochs):
+        usable = jnp.logical_and(row_ids >= valid[2 * epoch], row_ids < valid[2 * epoch + 1])
+        for tile in range(tiles):
+            columns = slice(tile * LANES, (tile + 1) * LANES)
+            inverse = jnp.where(usable, 1.0 / chosen[epoch, 1, :, columns], 0.0)
+            weighted = jnp.where(usable, chosen[epoch, 0, :, columns] / chosen[epoch, 1, :, columns], 0.0)
+            own[epoch, 0, tile] = weighted
+            own[epoch, 1, tile] = inverse
+    rows = pl.ds(pl.multiple_of((1 - lower) * (height - MAXS), MAXS), MAXS)
+    edges[...] = own[:, :, :, rows]
+    last[...] = own[:, :, tiles - 1]
+    corner[...] = own[:, :, tiles - 1, rows]
+
+
+def pick(place, owner, valid, chunks):
+    _, height, width = chunks[0].shape
+    epochs, tiles = owner.shape[0], width // LANES
+    shapes = [(tiles, height), (height,), (tiles, MAXS), (MAXS,)]
+    return pl.pallas_call(
+        pick_kernel,
+        in_specs=[pl.BlockSpec(memory_space=pltpu.SMEM)] * 3 + [pl.BlockSpec(memory_space=pltpu.VMEM)] * len(chunks),
+        out_specs=[pl.BlockSpec(memory_space=pltpu.VMEM)] * 4,
+        out_shape=[jax.ShapeDtypeStruct((epochs, 2) + shape + (LANES,), jnp.float32) for shape in shapes],
+        scratch_shapes=[pltpu.VMEM((epochs, 2, height, width), jnp.float32)],
+        compiler_params=pltpu.CompilerParams(vmem_limit_bytes=VMEM),
+        cost_estimate=pl.CostEstimate(flops=0, bytes_accessed=4 << 20, transcendentals=0),
+    )(place, owner, valid.reshape(-1), *chunks)
+
+
+def correlate_kernel(place, own, before, border, corner, bands_ref, rows_ref, ext, high, low, summed):
+    epochs, kinds, tiles, height, _ = own.shape
+    ksize = bands_ref.shape[1]
+    members = high.shape[2] // (height + 2 * MAXS)
     first, lower = place[0] == 0, place[1]
-    at_border = pl.multiple_of((1 - lower) * (MAXS + height), MAXS)
-    ext[...] = jnp.zeros_like(ext)
-    for tile in range(tiles + 1):
-        columns = slice(tile * LANES, (tile + 1) * LANES)
-        ext[:, :, tile, MAXS : MAXS + height] = wide[:, :, :, columns]
-        ext[:, :, tile, pl.ds(at_border, MAXS)] = border[:, :, :, columns]
-
-    blank = tiles + 1
-    ahead = jnp.where(first, blank, 0)
-    windows = [(ahead, 1)] + [(tile, tile + 1) for tile in range(1, tiles)] + [(0, blank)]
-    lane = lax.broadcasted_iota(jnp.int32, (height, LANES), 1)
+    at_border = (1 - lower) * (MAXS + height)
+    summed_rows = height * members
+    blank = pl.ds(pl.multiple_of(lower * (MAXS + height) * members, 8), MAXS * members)
+    ext[:, :, blank] = jnp.zeros((kinds, 2, MAXS * members, LANES), jnp.float32)
+    nothing = jnp.zeros((height, LANES), jnp.float32)
+    keep = jnp.where(first, 0.0, 1.0)
+
+    def put(kind, half, member, value, beyond):
+        ext[kind, half, pl.ds(MAXS * members + member, height, stride=members)] = value
+        ext[kind, half, pl.ds(at_border * members + member, MAXS, stride=members)] = beyond
+
+    for epoch in range(epochs):
+        base = epoch * (tiles + 1)
+        for kind in range(kinds):
+            for tile in range(tiles):
+                put(kind, 1, base + tile, own[epoch, kind, tile], border[epoch, kind, tile])
+                if tile + 1 < tiles:
+                    put(kind, 0, base + tile + 1, own[epoch, kind, tile], border[epoch, kind, tile])
+            put(kind, 0, base, before[epoch, kind] * keep, corner[epoch, kind] * keep)
+            put(kind, 0, base + tiles, before[epoch, kind], corner[epoch, kind])
+            put(kind, 1, base + tiles, nothing, nothing[:MAXS])
+
+    def split(index, _):
+        rows = pl.ds(pl.multiple_of(index * 128, 128), 128)
+        for kind in range(kinds):
+            for half in range(2):
+                value = ext[kind, half, rows]
+                part = value.astype(jnp.bfloat16)
+                high[kind, half, rows] = part
+                low[kind, half, rows] = (value - part.astype(jnp.float32)).astype(jnp.bfloat16)
+        return 0
+
+    lax.fori_loop(0, ext.shape[2] // 128, split, 0)
+
+    lane = lax.broadcasted_iota(jnp.int32, (MAXS, LANES), 1)
     wrapped = jnp.logical_and(first, lane < MAXS)
     for kind in range(kinds):
-        summed[...] = jnp.zeros_like(summed)
-
-        def add_row(row, _):
-            rows = pl.ds(row + MAXS - ksize // 2, height)
-            window = jnp.concatenate(
-                [
-                    jnp.concatenate([ext[epoch, kind, left, rows], ext[epoch, kind, right, rows]], axis=1)
-                    for epoch in range(epochs)
-                    for left, right in windows
-                ],
-                axis=0,
-            )
-            high = window.astype(jnp.bfloat16)
-            low = (window - high.astype(jnp.float32)).astype(jnp.bfloat16)
-            pair = jnp.dot(high, both_ref[kind, row], preferred_element_type=jnp.float32)
-            rest = jnp.dot(low, high_ref[kind, row], preferred_element_type=jnp.float32)
-            summed[...] += pair[:, :LANES] + (pair[:, LANES:] + rest)
-            return 0
-
-        lax.fori_loop(0, ksize, add_row, 0)
-        for epoch in range(epochs):
-            base = epoch * (tiles + 1) * height
-            over = base + tiles * height
-            summed[base : base + height] = jnp.where(
-                wrapped, summed[over : over + height], summed[base : base + height]
-            )
-            for tile in range(tiles):
-                start = base + tile * height
-                at_edge = pl.multiple_of(start + (1 - lower) * (height - MAXS), MAXS)
-                at_inner = pl.multiple_of(start + lower * MAXS, MAXS)
-                rows_ref[0, epoch, kind, tile] = summed[pl.ds(at_edge, MAXS)]
-                rows_ref[1, epoch, kind, tile] = summed[pl.ds(at_inner, MAXS)]
-
-
-def correlate(place, wide, border, high, both):
-    epochs, kinds, height, width = wide.shape
-    tiles = width // LANES - 1
-    flops = 3 * 2 * epochs * kinds * (tiles + 1) * height * high.shape[1] * 2 * LANES * LANES
+        offsets = [pl.ds((row + MAXS - ksize // 2) * members, summed_rows) for row in range(ksize)]
+        upper = jnp.concatenate([high[kind, half, rows] for rows in offsets for half in range(2)], axis=1)
+        rest = jnp.concatenate([low[kind, half, rows] for rows in offsets for half in range(2)], axis=1)
+        weights = bands_ref[kind].reshape(ksize * 2 * LANES, 2 * LANES)
+        pair = jnp.dot(upper, weights, preferred_element_type=jnp.float32)
+        more = jnp.dot(rest, weights[:, :LANES], preferred_element_type=jnp.float32)
+        summed[...] = pair[:, :LANES] + (pair[:, LANES:] + more)
+        for half in range(2):
+            start = (1 - lower if half == 0 else lower) * (height - MAXS)
+            for epoch in range(epochs):
+                base = epoch * (tiles + 1)
+
+                def rows_of(tile):
+                    return summed[pl.ds(start * members + base + tile, MAXS, stride=members)]
+
+                rows_ref[half, epoch, kind, 0] = jnp.where(wrapped, rows_of(tiles), rows_of(0))
+                for tile in range(1, tiles):
+                    rows_ref[half, epoch, kind, tile] = rows_of(tile)
+
+
+def correlate(place, own, before, border, corner, bands):
+    epochs, kinds, tiles, height, _ = own.shape
+    members = -(-epochs * (tiles + 1) // 16) * 16
+    depth = (height + 2 * MAXS) * members
+    flops = 2 * 2 * kinds * members * height * bands.shape[1] * 4 * LANES * LANES
     return pl.pallas_call(
         correlate_kernel,
-        in_specs=[pl.BlockSpec(memory_space=pltpu.SMEM)] + [pl.BlockSpec(memory_space=pltpu.VMEM)] * 4,
+        in_specs=[pl.BlockSpec(memory_space=pltpu.SMEM)] + [pl.BlockSpec(memory_space=pltpu.VMEM)] * 5,
         out_specs=pl.BlockSpec(memory_space=pltpu.VMEM),
         out_shape=jax.ShapeDtypeStruct((2, epochs, kinds, tiles, MAXS, LANES), jnp.float32),
         scratch_shapes=[
-            pltpu.VMEM((epochs, kinds, tiles + 2, height + 2 * MAXS, LANES), jnp.float32),
-            pltpu.VMEM((epochs * (tiles + 1) * height, LANES), jnp.float32),
+            pltpu.VMEM((kinds, 2, depth, LANES), jnp.float32),
+            pltpu.VMEM((kinds, 2, depth, LANES), jnp.bfloat16),
+            pltpu.VMEM((kinds, 2, depth, LANES), jnp.bfloat16),
+            pltpu.VMEM((height * members, LANES), jnp.float32),
         ],
         compiler_params=pltpu.CompilerParams(vmem_limit_bytes=VMEM),
         cost_estimate=pl.CostEstimate(flops=flops, bytes_accessed=12 << 20, transcendentals=0),
-    )(place, wide, border, high, both)
+    )(place, own, before, border, corner, bands)
 
 
 def stack_kernel(place, shifts, floor, *refs, group, parts, blocks):
@@ -258,8 +334,6 @@
 def local(images, variance, spread_kernel, shifts, epoch_owner, valid_rows):
     exposure, noise_var = images[0], variance[0]
     height, columns = exposure.shape
-    ksize = spread_kernel.shape[0]
-    epochs = epoch_owner.shape[0]
     blocks = lax.axis_size("vel")
     width = columns // blocks
     me, lower = lax.axis_index("vel"), lax.axis_index("rows")
@@ -273,46 +347,25 @@
         return jnp.where(index % 2 == 0, index // 2, blocks - 1 - index // 2)
 
     mine = position(me)
-    kernel_norm = spread_kernel / jnp.sum(spread_kernel)
-    kernel_sq = kernel_norm * kernel_norm
-    floor = (0.5 * jnp.sum(kernel_sq)).reshape(1)
-    taps = jnp.stack([kernel_norm, kernel_sq]).reshape(-1)
-
-    chunks = []
-    for step in range(blocks):
-        start = position(me ^ step) * width
-        chunk = jnp.stack(
-            [
-                lax.dynamic_slice_in_dim(exposure, start, width, 1),
-                lax.dynamic_slice_in_dim(noise_var, start, width, 1),
-            ]
-        )
-        if step:
-            chunk = lax.ppermute(chunk, "vel", [(i, i ^ step) for i in range(blocks)])
-        if step == 1:
-            chunk, taps = lax.optimization_barrier((chunk, taps))
-        chunks.append(chunk)
-    high, both = bands(taps, ksize)
-    chunks[-1], high, both = lax.optimization_barrier((chunks[-1], high, both))
-    row_ids = lower * height + jnp.arange(height, dtype=jnp.int32)[:, None]
-    fields = []
-    for epoch in range(epochs):
-        key = epoch_owner[epoch] ^ me
-        chosen = chunks[0]
-        for step in range(1, blocks):
-            chosen = jnp.where(key == step, chunks[step], chosen)
-        usable = (row_ids >= valid_rows[epoch, 0]) & (row_ids < valid_rows[epoch, 1])
-        fields.append(
-            jnp.stack([jnp.where(usable, chosen[0] / chosen[1], 0.0), jnp.where(usable, 1.0 / chosen[1], 0.0)])
-        )
-    field = jnp.stack(fields)
-    before = lax.ppermute(field[..., width - LANES :], "vel", right)
-    wide = jnp.concatenate([before, field], axis=3)
-    border = lax.ppermute(jnp.where(lower == 0, wide[:, :, height - MAXS :], wide[:, :, :MAXS]), "rows", swap)
     place = jnp.stack([mine, lower]).astype(jnp.int32)
-    payload = correlate(place, wide, border, high, both)
-
-    flat_shifts = shifts.reshape(-1)
+
+    starts = position(me ^ jnp.arange(blocks, dtype=jnp.int32)) * width
+    chunks = list(cut(starts, exposure, noise_var, blocks))
+    for step in range(1, blocks):
+        chunks[step] = lax.ppermute(chunks[step], "vel", [(i, i ^ step) for i in range(blocks)])
+    chunks[1], spread_kernel = lax.optimization_barrier((chunks[1], spread_kernel))
+    bands, floor = make_bands(spread_kernel)
+    chunks[-1], bands = lax.optimization_barrier((chunks[-1], bands))
+    spot = jnp.stack([me, lower]).astype(jnp.int32)
+    own, last, edges, corner = pick(spot, epoch_owner, valid_rows, chunks)
+    pairs = lax.axis_size("rows")
+    diagonal = [(a * pairs + r, b * pairs + 1 - r) for a, b in right for r in range(pairs)]
+    before = lax.ppermute(last, "vel", right)
+    corner = lax.ppermute(corner, ("vel", "rows"), diagonal)
+    border = lax.ppermute(edges, "rows", swap)
+    payload = correlate(place, own, before, border, corner, bands)
+
+    flat_shifts, floor = shifts.reshape(-1), floor[0, :1]
     out_shape = jax.ShapeDtypeStruct((shifts.shape[0], height, columns), jnp.float32)
     border = lax.ppermute(payload[:1], "rows", swap)
     have = {0: ((payload, 0), (payload, 1), (border, 0))}

time: 125 us -> 108 us (0.86)
  other arithmetic: 14.9 us -> 0.55 us
  Pallas kernels: 58.4 us -> 49 us
  local copies, waits for them, and re-layouts: 6.12 us -> 11.6 us
  starting transfers between devices: 24.2 us -> 27.2 us
  between operations: 2.93 us -> 0.3 us
    unnamed x5 -> x16, local copies, waits for them, and re-layouts: 0.13 us -> 9.33 us
    pallas_call x1, Pallas kernels: 15.3 us -> 7.53 us  [correlate(): pl.pallas_call(correlate_kernel, in_specs=[pl.BlockSpec(memory_space=pltp...]
    another operation x13 -> x1, other arithmetic: 5.4 us -> 0.07 us  [local(): spot = jnp.stack([me, lower]).astype(jnp.int32)]
    pallas_call x1 -> x3, Pallas kernels: 9.72 us -> 6.03 us  [the longest x1 4.59 us: make_bands(): pl.pallas_call(band_kernel, in_specs=[pl.BlockSpec(memory_space=pltpu.SME...]
    and x2 -> x0, other arithmetic: 3.62 us -> none  [local(): (row_ids >= valid_rows[epoch, 0]) & (row_ids < valid_rows[epoch, 1])]
    ppermute x9 -> x10, starting transfers between devices: 15.2 us -> 18.6 us  [the longest x7 15.7 us: local(): lax.ppermute(chunks[step], 'vel', [(i, i ^ step) for i in range(blocks)])]
    select_n x7 -> x0, other arithmetic: 3.19 us -> none  [the longest x3 2.92 us: local(): chosen = jnp.where(key == step, chunks[step], chosen)]
    ppermute x9 -> x10, waiting for transfers between devices: 3.65 us -> 6.24 us  [the longest x7 2.84 us: local(): lax.ppermute(chunks[step], 'vel', [(i, i ^ step) for i in range(blocks)])]
  transfers between devices with their start and end apart: 22 -> 23, of which waited for: 8 -> 11; matrix products, arithmetic and copies ran while one was open for 11% -> 3% of each run, Pallas kernels for 28% -> 29%
where the time goes in v4:
time: 108 us; the launch traced here: 107 us
  Pallas kernels  49 us (45%)
  starting transfers between devices  27.2 us (25%)
  waiting for transfers between devices  18.5 us (17%)
  local copies, waits for them, and re-layouts  11.6 us (11%)
    pallas_call x4, Pallas kernels, stack_blocks(): pl.pallas_call(functools.partial(stack_kernel, group=group, parts=parts,...  35.5 us
    ppermute x7, starting transfers between devices, local(): lax.ppermute(chunks[step], 'vel', [(i, i ^ step) for i in range(blocks)])  15.7 us
    unnamed x16, local copies, waits for them, and re-layouts  9.33 us
    ppermute x3, waiting for transfers between devices, local(): lax.ppermute(ahead, 'vel', left)  8.89 us
    pallas_call x1, Pallas kernels, correlate(): pl.pallas_call(correlate_kernel, in_specs=[pl.BlockSpec(memory_space=pltp...  7.53 us
    pallas_call x1, Pallas kernels, make_bands(): pl.pallas_call(band_kernel, in_specs=[pl.BlockSpec(memory_space=pltpu.SME...  4.59 us
    ppermute x3, starting transfers between devices, local(): lax.ppermute(ahead, 'vel', left)  3.92 us
    ppermute x7, waiting for transfers between devices, local(): lax.ppermute(chunks[step], 'vel', [(i, i ^ step) for i in range(blocks)])  2.84 us
  transfers between devices with their start and end apart: 23, of which 11 were waited for; matrix products, arithmetic and copies ran while one was open for 3% of the time, Pallas kernels for 29%

profile of v4, /device:TPU:0, one launch (start us, length us, event | category | flops | bytes accessed | tf_op | source)
XLA Modules:
  0.0 107.3 jit_solution(11190968198199514287)
XLA Ops:
  1.1 1.0 copy-done.1
  2.7 3.0 %collective-permute-start = (f32[2,32,512]{2,1,0:T(8,128)S(1)}, f32[2,32,512]{2,1,0:T(8,128)S(1)}, u32[]{:S(2)}, u32[]{:S(2)}) collective-permute-start(f32[2,32,512]{2,1,0:T(8,128)S(1)} %get-tuple-element.32), channel_id=1, source_target_pairs={{0,2},{2,0},{4,6},{6,4},{8,10},{10,8},{12,14},{14,12},{1,3},{3,1},... | collective-permute-start | bytes 393224 | tf_op jit(solution)/shard_map/ppermute | solution.py:355
  5.8 3.5 %collective-permute-start.6 = (f32[2,32,512]{2,1,0:T(8,128)S(1)}, f32[2,32,512]{2,1,0:T(8,128)S(1)}, u32[]{:S(2)}, u32[]{:S(2)}) collective-permute-start(f32[2,32,512]{2,1,0:T(8,128)S(1)} %get-tuple-element.42), channel_id=1, source_target_pairs={{0,14},{2,12},{4,10},{6,8},{8,6},{10,4},{12,2},{14,0},{1,15},{3,13... | collective-permute-start | bytes 393224 | tf_op jit(solution)/shard_map/ppermute | solution.py:355
  9.3 3.0 %collective-permute-start.2 = (f32[2,32,512]{2,1,0:T(8,128)S(1)}, f32[2,32,512]{2,1,0:T(8,128)S(1)}, u32[]{:S(2)}, u32[]{:S(2)}) collective-permute-start(f32[2,32,512]{2,1,0:T(8,128)S(1)} %get-tuple-element.38), channel_id=1, source_target_pairs={{0,6},{2,4},{4,2},{6,0},{8,14},{10,12},{12,10},{14,8},{1,7},{3,5},... | collective-permute-start | bytes 393224 | tf_op jit(solution)/shard_map/ppermute | solution.py:355
  12.3 2.9 %collective-permute-start.4 = (f32[2,32,512]{2,1,0:T(8,128)S(1)}, f32[2,32,512]{2,1,0:T(8,128)S(1)}, u32[]{:S(2)}, u32[]{:S(2)}) collective-permute-start(f32[2,32,512]{2,1,0:T(8,128)S(1)} %get-tuple-element.40), channel_id=1, source_target_pairs={{0,10},{2,8},{4,14},{6,12},{8,2},{10,0},{12,6},{14,4},{1,11},{3,9}... | collective-permute-start | bytes 393224 | tf_op jit(solution)/shard_map/ppermute | solution.py:355
  15.2 3.3 %collective-permute-start.5 = (f32[2,32,512]{2,1,0:T(8,128)S(1)}, f32[2,32,512]{2,1,0:T(8,128)S(1)}, u32[]{:S(2)}, u32[]{:S(2)}) collective-permute-start(f32[2,32,512]{2,1,0:T(8,128)S(1)} %get-tuple-element.41), channel_id=1, source_target_pairs={{0,12},{2,14},{4,8},{6,10},{8,4},{10,6},{12,0},{14,2},{1,13},{3,15... | collective-permute-start | bytes 393224 | tf_op jit(solution)/shard_map/ppermute | solution.py:355
  20.9 4.6 %shard_map.65 = (bf16[2,21,256,256]{3,2,1,0:T(8,128)(2,1)S(1)}, f32[8,128]{1,0:T(8,128)S(1)}) custom-call(f32[441]{0:T(512)S(1)} %reshape.10.taps, f32[21,21]{1,0:T(8,128)S(1)} %copy-done.2), custom_call_target="tpu_custom_call" | custom-call | bytes 20971520 | tf_op jit(solution)/shard_map/pallas_call | solution.py:41
  25.5 2.4 %copy-done.4 = bf16[2,21,256,256]{3,2,1,0:T(8,128)(2,1)} copy-done((bf16[2,21,256,256]{3,2,1,0:T(8,128)(2,1)}, bf16[2,21,256,256]{3,2,1,0:T(8,128)(2,1)S(1)}, u32[]{:S(2)}) %copy-start.4) | copy-done | bytes 5505048
  28.0 2.8 %collective-permute-done.4.refs_5_ = f32[2,32,512]{2,1,0:T(8,128)S(1)} collective-permute-done((f32[2,32,512]{2,1,0:T(8,128)S(1)}, f32[2,32,512]{2,1,0:T(8,128)S(1)}, u32[]{:S(2)}, u32[]{:S(2)}) %collective-permute-start.4) | collective-permute-done | bytes 131104 | tf_op jit(solution)/shard_map/ppermute | solution.py:355
  32.4 1.2 %collective-permute-start.9 = (f32[3,2,16,128]{3,2,1,0:T(8,128)S(1)}, f32[3,2,16,128]{3,2,1,0:T(8,128)S(1)}, u32[]{:S(2)}, u32[]{:S(2)}) collective-permute-start(f32[3,2,16,128]{3,2,1,0:T(8,128)S(1)} %get-tuple-element.48), channel_id=1, source_target_pairs={{0,5},{1,4},{4,9},{5,8},{8,13},{9,12},{12,15},{13,14},{14,11},{15,... | collective-permute-start | bytes 147464 | tf_op jit(solution)/shard_map/ppermute | solution.py:364
  33.6 1.6 %collective-permute-start.7 = (f32[3,2,32,128]{3,2,1,0:T(8,128)S(1)}, f32[3,2,32,128]{3,2,1,0:T(8,128)S(1)}, u32[]{:S(2)}, u32[]{:S(2)}) collective-permute-start(f32[3,2,32,128]{3,2,1,0:T(8,128)S(1)} %get-tuple-element.46), channel_id=1, source_target_pairs={{0,4},{4,8},{8,12},{12,14},{14,10},{10,6},{6,2},{2,0},{1,5},{5,9},... | collective-permute-start | bytes 294920 | tf_op jit(solution)/shard_map/ppermute | solution.py:363
  36.0 2.7 %collective-permute-done.7.before = f32[3,2,32,128]{3,2,1,0:T(8,128)S(1)} collective-permute-done((f32[3,2,32,128]{3,2,1,0:T(8,128)S(1)}, f32[3,2,32,128]{3,2,1,0:T(8,128)S(1)}, u32[]{:S(2)}, u32[]{:S(2)}) %collective-permute-start.7) | collective-permute-done | bytes 98336 | tf_op jit(solution)/shard_map/ppermute | solution.py:363
  38.7 2.6 %copy-done.5 = bf16[2,21,256,256]{3,2,1,0:T(8,128)(2,1)S(1)} copy-done((bf16[2,21,256,256]{3,2,1,0:T(8,128)(2,1)S(1)}, bf16[2,21,256,256]{3,2,1,0:T(8,128)(2,1)}, u32[]{:S(2)}) %copy-start.5) | copy-done | bytes 5505048
  41.2 7.5 %shard_map.67.refs_0_.refs_1_.refs_9_.refs_10_ = f32[2,3,2,4,16,128]{5,4,3,2,1,0:T(8,128)S(1)} custom-call(s32[2]{0:T(128)S(1)} %pad_add_fusion.place, f32[3,2,4,32,128]{4,3,2,1,0:T(8,128)S(1)} %get-tuple-element.45.own, f32[3,2,32,128]{3,2,1,0:T(8,128)S(1)} %collective-permute-done.7.before, f32[3,2,4,16,128]{4,3,2,1,0:T(8,128)S(1)} %collective-permute-done.8.border, ...), custom_call_target="tpu_custom_call" | custom-call | flops 5637144576 | bytes 12582912 | tf_op jit(solution)/shard_map/pallas_call | solution.py:181
  49.6 1.2 %collective-permute-start.10 = (f32[2,3,2,4,16,128]{5,4,3,2,1,0:T(8,128)S(1)}, f32[2,3,2,4,16,128]{5,4,3,2,1,0:T(8,128)S(1)}, u32[]{:S(2)}, u32[]{:S(2)}) collective-permute-start(f32[2,3,2,4,16,128]{5,4,3,2,1,0:T(8,128)S(1)} %shard_map.67.refs_0_.refs_1_.refs_9_.refs_10_), channel_id=1, source_target_pairs={{0,4},{4,8},{8,12},{12,14},{14,10},{10,6},{6,2},{2,0},{1,5},{5,9},... | collective-permute-start | bytes 1179656 | tf_op jit(solution)/shard_map/ppermute | solution.py:377
  50.9 8.5 %collective-permute-done.12.refs_3_.refs_4_.refs_0_.refs_1_ = f32[2,3,2,4,16,128]{5,4,3,2,1,0:T(8,128)S(1)} collective-permute-done((f32[2,3,2,4,16,128]{5,4,3,2,1,0:T(8,128)S(1)}, f32[2,3,2,4,16,128]{5,4,3,2,1,0:T(8,128)S(1)}, u32[]{:S(2)}, u32[]{:S(2)}) %collective-permute-start.12) | collective-permute-done | bytes 393248 | tf_op jit(solution)/shard_map/ppermute | solution.py:377
  60.0 1.8 %collective-permute-start.13 = (f32[2,3,2,4,16,128]{5,4,3,2,1,0:T(8,128)S(1)}, f32[2,3,2,4,16,128]{5,4,3,2,1,0:T(8,128)S(1)}, u32[]{:S(2)}, u32[]{:S(2)}) collective-permute-start(f32[2,3,2,4,16,128]{5,4,3,2,1,0:T(8,128)S(1)} %collective-permute-done.12.refs_3_.refs_4_.refs_0_.refs_1_), channel_id=1, source_target_pairs={{4,0},{8,4},{12,8},{14,12},{10,14},{6,10},{2,6},{0,2},{5,1},{9,5},... | collective-permute-start | bytes 1179656 | tf_op jit(solution)/shard_map/ppermute | solution.py:377
  63.6 8.9 %shard_map.68.refs_12_ = f32[36,32,4096]{2,1,0:T(8,128)} custom-call(s32[3]{0:T(128)S(1)} %add_add_fusion.1.place, s32[216]{0:T(256)S(1)} %reshape.9.shifts, f32[1]{0:T(128)} %bitcast.5.floor, f32[2,3,2,4,16,128]{5,4,3,2,1,0:T(8,128)S(1)} %shard_map.67.refs_0_.refs_1_.refs_9_.refs_10_, ...), custom_call_target="tpu_custom_call" | custom-call | flops 18874368 | bytes 28311552 | tf_op jit(solution)/shard_map/pallas_call | solution.py:312
  74.0 1.3 %collective-permute-start.17 = (f32[2,3,2,4,16,128]{5,4,3,2,1,0:T(8,128)S(1)}, f32[2,3,2,4,16,128]{5,4,3,2,1,0:T(8,128)S(1)}, u32[]{:S(2)}, u32[]{:S(2)}) collective-permute-start(f32[2,3,2,4,16,128]{5,4,3,2,1,0:T(8,128)S(1)} %collective-permute-done.13.refs_3_.refs_4_.refs_0_.refs_1_), channel_id=1, source_target_pairs={{4,0},{8,4},{12,8},{14,12},{10,14},{6,10},{2,6},{0,2},{5,1},{9,5},... | collective-permute-start | bytes 1179656 | tf_op jit(solution)/shard_map/ppermute | solution.py:377
  75.3 8.9 %shard_map.69.refs_12_ = f32[36,32,4096]{2,1,0:T(8,128)} custom-call(s32[3]{0:T(128)S(1)} %add_add_fusion.2.place, s32[216]{0:T(256)S(1)} %reshape.9.shifts, f32[1]{0:T(128)} %bitcast.5.floor, f32[2,3,2,4,16,128]{5,4,3,2,1,0:T(8,128)S(1)} %collective-permute-done.12.refs_3_.refs_4_.refs_0_.refs_1_, ...), custom_call_target="tpu_custom_call", output_to_operand_aliasing={{}: (15, {})} | custom-call | flops 18874368 | bytes 28311552 | tf_op jit(solution)/shard_map/pallas_call | solution.py:312
  85.9 1.1 collective-permute-start.20
  88.1 8.9 %shard_map.70.refs_12_ = f32[36,32,4096]{2,1,0:T(8,128)} custom-call(s32[3]{0:T(128)S(1)} %add_add_fusion.3.place, s32[216]{0:T(256)S(1)} %reshape.9.shifts, f32[1]{0:T(128)} %bitcast.5.floor, f32[2,3,2,4,16,128]{5,4,3,2,1,0:T(8,128)S(1)} %collective-permute-done.13.refs_3_.refs_4_.refs_0_.refs_1_, ...), custom_call_target="tpu_custom_call", output_to_operand_aliasing={{}: (15, {})} | custom-call | flops 18874368 | bytes 28311552 | tf_op jit(solution)/shard_map/pallas_call | solution.py:312
  97.1 1.3 %collective-permute-done.22.refs_5_.refs_8_ = f32[1,3,2,4,16,128]{5,4,3,2,1,0:T(8,128)S(1)} collective-permute-done((f32[1,3,2,4,16,128]{5,4,3,2,1,0:T(8,128)S(1)}, f32[1,3,2,4,16,128]{5,4,3,2,1,0:T(8,128)S(1)}, u32[]{:S(2)}, u32[]{:S(2)}) %collective-permute-start.22) | collective-permute-done | bytes 196640 | tf_op jit(solution)/shard_map/ppermute | solution.py:387
  98.4 8.9 %shard_map.71 = f32[36,32,4096]{2,1,0:T(8,128)} custom-call(s32[3]{0:T(128)S(1)} %add_add_fusion.place, s32[216]{0:T(256)S(1)} %reshape.9.shifts, f32[1]{0:T(128)} %bitcast.5.floor, f32[2,3,2,4,16,128]{5,4,3,2,1,0:T(8,128)S(1)} %collective-permute-done.17.refs_3_.refs_4_.refs_0_.refs_1_, ...), custom_call_target="tpu_custom_call", output_to_operand_aliasing={{}: (15, {})} | custom-call | flops 18874368 | bytes 28311552 | tf_op jit(solution)/shard_map/pallas_call | solution.py:312
  (67 shorter events, 14.1 us)
Async XLA Ops:
  0.0 62.2 %copy-start.6 = (s32[36,3,2]{0,2,1:T(2,128)S(1)}, s32[36,3,2]{0,2,1:T(2,128)}, u32[]{:S(2)}) copy-start(s32[36,3,2]{0,2,1:T(2,128)} %param.9) | copy-start | bytes 2596
  2.7 9.6 %collective-permute-start = (f32[2,32,512]{2,1,0:T(8,128)S(1)}, f32[2,32,512]{2,1,0:T(8,128)S(1)}, u32[]{:S(2)}, u32[]{:S(2)}) collective-permute-start(f32[2,32,512]{2,1,0:T(8,128)S(1)} %get-tuple-element.32), channel_id=1, source_target_pairs={{0,2},{2,0},{4,6},{6,4},{8,10},{10,8},{12,14},{14,12},{1,3},{3,1},... | collective-permute-start | bytes 393224 | tf_op jit(solution)/shard_map/ppermute | solution.py:355
  5.8 9.4 %collective-permute-start.6 = (f32[2,32,512]{2,1,0:T(8,128)S(1)}, f32[2,32,512]{2,1,0:T(8,128)S(1)}, u32[]{:S(2)}, u32[]{:S(2)}) collective-permute-start(f32[2,32,512]{2,1,0:T(8,128)S(1)} %get-tuple-element.42), channel_id=1, source_target_pairs={{0,14},{2,12},{4,10},{6,8},{8,6},{10,4},{12,2},{14,0},{1,15},{3,13... | collective-permute-start | bytes 393224 | tf_op jit(solution)/shard_map/ppermute | solution.py:355
  9.3 18.7 %collective-permute-start.1 = (f32[2,32,512]{2,1,0:T(8,128)S(1)}, f32[2,32,512]{2,1,0:T(8,128)S(1)}, u32[]{:S(2)}, u32[]{:S(2)}) collective-permute-start(f32[2,32,512]{2,1,0:T(8,128)S(1)} %get-tuple-element.37), channel_id=1, source_target_pairs={{0,4},{2,6},{4,0},{6,2},{8,12},{10,14},{12,8},{14,10},{1,5},{3,7},... | collective-permute-start | bytes 393224 | tf_op jit(solution)/shard_map/ppermute | solution.py:355
  9.3 18.7 %collective-permute-start.2 = (f32[2,32,512]{2,1,0:T(8,128)S(1)}, f32[2,32,512]{2,1,0:T(8,128)S(1)}, u32[]{:S(2)}, u32[]{:S(2)}) collective-permute-start(f32[2,32,512]{2,1,0:T(8,128)S(1)} %get-tuple-element.38), channel_id=1, source_target_pairs={{0,6},{2,4},{4,2},{6,0},{8,14},{10,12},{12,10},{14,8},{1,7},{3,5},... | collective-permute-start | bytes 393224 | tf_op jit(solution)/shard_map/ppermute | solution.py:355
  12.3 15.8 %collective-permute-start.3 = (f32[2,32,512]{2,1,0:T(8,128)S(1)}, f32[2,32,512]{2,1,0:T(8,128)S(1)}, u32[]{:S(2)}, u32[]{:S(2)}) collective-permute-start(f32[2,32,512]{2,1,0:T(8,128)S(1)} %get-tuple-element.39), channel_id=1, source_target_pairs={{0,8},{2,10},{4,12},{6,14},{8,0},{10,2},{12,4},{14,6},{1,9},{3,11}... | collective-permute-start | bytes 393224 | tf_op jit(solution)/shard_map/ppermute | solution.py:355
  12.3 18.5 %collective-permute-start.4 = (f32[2,32,512]{2,1,0:T(8,128)S(1)}, f32[2,32,512]{2,1,0:T(8,128)S(1)}, u32[]{:S(2)}, u32[]{:S(2)}) collective-permute-start(f32[2,32,512]{2,1,0:T(8,128)S(1)} %get-tuple-element.40), channel_id=1, source_target_pairs={{0,10},{2,8},{4,14},{6,12},{8,2},{10,0},{12,6},{14,4},{1,11},{3,9}... | collective-permute-start | bytes 393224 | tf_op jit(solution)/shard_map/ppermute | solution.py:355
  15.2 15.6 %collective-permute-start.5 = (f32[2,32,512]{2,1,0:T(8,128)S(1)}, f32[2,32,512]{2,1,0:T(8,128)S(1)}, u32[]{:S(2)}, u32[]{:S(2)}) collective-permute-start(f32[2,32,512]{2,1,0:T(8,128)S(1)} %get-tuple-element.41), channel_id=1, source_target_pairs={{0,12},{2,14},{4,8},{6,10},{8,4},{10,6},{12,0},{14,2},{1,13},{3,15... | collective-permute-start | bytes 393224 | tf_op jit(solution)/shard_map/ppermute | solution.py:355
  32.3 6.4 %collective-permute-start.8 = (f32[3,2,4,16,128]{4,3,2,1,0:T(8,128)S(1)}, f32[3,2,4,16,128]{4,3,2,1,0:T(8,128)S(1)}, u32[]{:S(2)}, u32[]{:S(2)}) collective-permute-start(f32[3,2,4,16,128]{4,3,2,1,0:T(8,128)S(1)} %get-tuple-element.47), channel_id=1, source_target_pairs={{0,1},{1,0},{2,3},{3,2},{4,5},{5,4},{6,7},{7,6},{8,9},{9,8},{10,11... | collective-permute-start | bytes 589832 | tf_op jit(solution)/shard_map/ppermute | solution.py:365
  32.4 3.6 %collective-permute-start.9 = (f32[3,2,16,128]{3,2,1,0:T(8,128)S(1)}, f32[3,2,16,128]{3,2,1,0:T(8,128)S(1)}, u32[]{:S(2)}, u32[]{:S(2)}) collective-permute-start(f32[3,2,16,128]{3,2,1,0:T(8,128)S(1)} %get-tuple-element.48), channel_id=1, source_target_pairs={{0,5},{1,4},{4,9},{5,8},{8,13},{9,12},{12,15},{13,14},{14,11},{15,... | collective-permute-start | bytes 147464 | tf_op jit(solution)/shard_map/ppermute | solution.py:364
  33.6 5.0 %collective-permute-start.7 = (f32[3,2,32,128]{3,2,1,0:T(8,128)S(1)}, f32[3,2,32,128]{3,2,1,0:T(8,128)S(1)}, u32[]{:S(2)}, u32[]{:S(2)}) collective-permute-start(f32[3,2,32,128]{3,2,1,0:T(8,128)S(1)} %get-tuple-element.46), channel_id=1, source_target_pairs={{0,4},{4,8},{8,12},{12,14},{14,10},{10,6},{6,2},{2,0},{1,5},{5,9},... | collective-permute-start | bytes 294920 | tf_op jit(solution)/shard_map/ppermute | solution.py:363
  48.8 10.6 %collective-permute-start.12 = (f32[2,3,2,4,16,128]{5,4,3,2,1,0:T(8,128)S(1)}, f32[2,3,2,4,16,128]{5,4,3,2,1,0:T(8,128)S(1)}, u32[]{:S(2)}, u32[]{:S(2)}) collective-permute-start(f32[2,3,2,4,16,128]{5,4,3,2,1,0:T(8,128)S(1)} %shard_map.67.refs_0_.refs_1_.refs_9_.refs_10_), channel_id=1, source_target_pairs={{4,0},{8,4},{12,8},{14,12},{10,14},{6,10},{2,6},{0,2},{5,1},{9,5},... | collective-permute-start | bytes 1179656 | tf_op jit(solution)/shard_map/ppermute | solution.py:377
  49.6 10.3 %collective-permute-start.10 = (f32[2,3,2,4,16,128]{5,4,3,2,1,0:T(8,128)S(1)}, f32[2,3,2,4,16,128]{5,4,3,2,1,0:T(8,128)S(1)}, u32[]{:S(2)}, u32[]{:S(2)}) collective-permute-start(f32[2,3,2,4,16,128]{5,4,3,2,1,0:T(8,128)S(1)} %shard_map.67.refs_0_.refs_1_.refs_9_.refs_10_), channel_id=1, source_target_pairs={{0,4},{4,8},{8,12},{12,14},{14,10},{10,6},{6,2},{2,0},{1,5},{5,9},... | collective-permute-start | bytes 1179656 | tf_op jit(solution)/shard_map/ppermute | solution.py:377
  60.0 3.7 %collective-permute-start.15 = (f32[2,3,2,4,16,128]{5,4,3,2,1,0:T(8,128)S(1)}, f32[2,3,2,4,16,128]{5,4,3,2,1,0:T(8,128)S(1)}, u32[]{:S(2)}, u32[]{:S(2)}) collective-permute-start(f32[2,3,2,4,16,128]{5,4,3,2,1,0:T(8,128)S(1)} %pad_maximum_fusion), channel_id=1, source_target_pairs={{0,1},{1,0},{2,3},{3,2},{4,5},{5,4},{6,7},{7,6},{8,9},{9,8},{10,11... | collective-permute-start | bytes 1179656 | tf_op jit(solution)/shard_map/ppermute | solution.py:380
  60.0 12.5 %collective-permute-start.13 = (f32[2,3,2,4,16,128]{5,4,3,2,1,0:T(8,128)S(1)}, f32[2,3,2,4,16,128]{5,4,3,2,1,0:T(8,128)S(1)}, u32[]{:S(2)}, u32[]{:S(2)}) collective-permute-start(f32[2,3,2,4,16,128]{5,4,3,2,1,0:T(8,128)S(1)} %collective-permute-done.12.refs_3_.refs_4_.refs_0_.refs_1_), channel_id=1, source_target_pairs={{4,0},{8,4},{12,8},{14,12},{10,14},{6,10},{2,6},{0,2},{5,1},{9,5},... | collective-permute-start | bytes 1179656 | tf_op jit(solution)/shard_map/ppermute | solution.py:377
  61.8 11.2 %collective-permute-start.11 = (f32[2,3,2,4,16,128]{5,4,3,2,1,0:T(8,128)S(1)}, f32[2,3,2,4,16,128]{5,4,3,2,1,0:T(8,128)S(1)}, u32[]{:S(2)}, u32[]{:S(2)}) collective-permute-start(f32[2,3,2,4,16,128]{5,4,3,2,1,0:T(8,128)S(1)} %collective-permute-done.10.refs_6_.refs_7_.refs_9_.refs_10_), channel_id=1, source_target_pairs={{0,4},{4,8},{8,12},{12,14},{14,10},{10,6},{6,2},{2,0},{1,5},{5,9},... | collective-permute-start | bytes 1179656 | tf_op jit(solution)/shard_map/ppermute | solution.py:377
  62.1 1.5 %collective-permute-start.14 = (f32[1,3,2,4,16,128]{5,4,3,2,1,0:T(8,128)S(1)}, f32[1,3,2,4,16,128]{5,4,3,2,1,0:T(8,128)S(1)}, u32[]{:S(2)}, u32[]{:S(2)}) collective-permute-start(f32[1,3,2,4,16,128]{5,4,3,2,1,0:T(8,128)S(1)} %slice.37), channel_id=1, source_target_pairs={{0,1},{1,0},{2,3},{3,2},{4,5},{5,4},{6,7},{7,6},{8,9},{9,8},{10,11... | collective-permute-start | bytes 589832 | tf_op jit(solution)/shard_map/ppermute | solution.py:370
  73.1 2.2 %collective-permute-start.18 = (f32[2,3,2,4,16,128]{5,4,3,2,1,0:T(8,128)S(1)}, f32[2,3,2,4,16,128]{5,4,3,2,1,0:T(8,128)S(1)}, u32[]{:S(2)}, u32[]{:S(2)}) collective-permute-start(f32[2,3,2,4,16,128]{5,4,3,2,1,0:T(8,128)S(1)} %pad_maximum_fusion.1), channel_id=1, source_target_pairs={{0,1},{1,0},{2,3},{3,2},{4,5},{5,4},{6,7},{7,6},{8,9},{9,8},{10,11... | collective-permute-start | bytes 1179656 | tf_op jit(solution)/shard_map/ppermute | solution.py:380
  73.2 11.5 %collective-permute-start.16 = (f32[2,3,2,4,16,128]{5,4,3,2,1,0:T(8,128)S(1)}, f32[2,3,2,4,16,128]{5,4,3,2,1,0:T(8,128)S(1)}, u32[]{:S(2)}, u32[]{:S(2)}) collective-permute-start(f32[2,3,2,4,16,128]{5,4,3,2,1,0:T(8,128)S(1)} %collective-permute-done.11.refs_6_.refs_7_.refs_9_.refs_10_), channel_id=1, source_target_pairs={{0,4},{4,8},{8,12},{12,14},{14,10},{10,6},{6,2},{2,0},{1,5},{5,9},... | collective-permute-start | bytes 1179656 | tf_op jit(solution)/shard_map/ppermute | solution.py:377
  74.0 11.1 %collective-permute-start.17 = (f32[2,3,2,4,16,128]{5,4,3,2,1,0:T(8,128)S(1)}, f32[2,3,2,4,16,128]{5,4,3,2,1,0:T(8,128)S(1)}, u32[]{:S(2)}, u32[]{:S(2)}) collective-permute-start(f32[2,3,2,4,16,128]{5,4,3,2,1,0:T(8,128)S(1)} %collective-permute-done.13.refs_3_.refs_4_.refs_0_.refs_1_), channel_id=1, source_target_pairs={{4,0},{8,4},{12,8},{14,12},{10,14},{6,10},{2,6},{0,2},{5,1},{9,5},... | collective-permute-start | bytes 1179656 | tf_op jit(solution)/shard_map/ppermute | solution.py:377
  85.8 2.2 %collective-permute-start.19 = (f32[2,3,2,4,16,128]{5,4,3,2,1,0:T(8,128)S(1)}, f32[2,3,2,4,16,128]{5,4,3,2,1,0:T(8,128)S(1)}, u32[]{:S(2)}, u32[]{:S(2)}) collective-permute-start(f32[2,3,2,4,16,128]{5,4,3,2,1,0:T(8,128)S(1)} %pad_maximum_fusion.2), channel_id=1, source_target_pairs={{0,1},{1,0},{2,3},{3,2},{4,5},{5,4},{6,7},{7,6},{8,9},{9,8},{10,11... | collective-permute-start | bytes 1179656 | tf_op jit(solution)/shard_map/ppermute | solution.py:380
  85.9 11.0 %collective-permute-start.20 = (f32[1,3,2,4,16,128]{5,4,3,2,1,0:T(8,128)S(1)}, f32[1,3,2,4,16,128]{5,4,3,2,1,0:T(8,128)S(1)}, u32[]{:S(2)}, u32[]{:S(2)}) collective-permute-start(f32[1,3,2,4,16,128]{5,4,3,2,1,0:T(8,128)S(1)} %slice.34), channel_id=1, source_target_pairs={{0,4},{4,8},{8,12},{12,14},{14,10},{10,6},{6,2},{2,0},{1,5},{5,9},... | collective-permute-start | bytes 589832 | tf_op jit(solution)/shard_map/ppermute | solution.py:384
  87.0 10.0 %collective-permute-start.21 = (f32[1,3,2,4,16,128]{5,4,3,2,1,0:T(8,128)}, f32[1,3,2,4,16,128]{5,4,3,2,1,0:T(8,128)S(1)}, u32[]{:S(2)}, u32[]{:S(2)}) collective-permute-start(f32[1,3,2,4,16,128]{5,4,3,2,1,0:T(8,128)} %get-tuple-element.59), channel_id=1, source_target_pairs={{4,0},{8,4},{12,8},{14,12},{10,14},{6,10},{2,6},{0,2},{5,1},{9,5},... | collective-permute-start | bytes 589832 | tf_op jit(solution)/shard_map/ppermute | solution.py:384
  97.0 1.4 %collective-permute-start.22 = (f32[1,3,2,4,16,128]{5,4,3,2,1,0:T(8,128)S(1)}, f32[1,3,2,4,16,128]{5,4,3,2,1,0:T(8,128)S(1)}, u32[]{:S(2)}, u32[]{:S(2)}) collective-permute-start(f32[1,3,2,4,16,128]{5,4,3,2,1,0:T(8,128)S(1)} %collective-permute-done.20.refs_3_.refs_6_), channel_id=1, source_target_pairs={{0,1},{1,0},{2,3},{3,2},{4,5},{5,4},{6,7},{7,6},{8,9},{9,8},{10,11... | collective-permute-start | bytes 589832 | tf_op jit(solution)/shard_map/ppermute | solution.py:387
  (6 other events, 8.5 us)

commit v5 on v4

--- a/solution.py
+++ b/solution.py
@@ -8,6 +8,7 @@
 
 LANES = 128
 MAXS = 16
+HALO = 32
 VMEM = 24 << 20
 
 
@@ -51,28 +52,55 @@
     )(spread_kernel.reshape(-1), spread_kernel)
 
 
-def cut_kernel(starts, exposure, noise_var, *chunk_refs):
+def cut_kernel(starts, exposure, noise_var, *refs):
+    chunk_refs, (held, arrived) = refs[:-2], refs[-2:]
+    _, height, columns = held.shape
+    tiles = columns // len(chunk_refs) // LANES
+    copies = []
+    for kind, source in enumerate((exposure, noise_var)):
+        for top in range(0, height, 8):
+            copies.append(
+                pltpu.make_async_copy(
+                    source.at[pl.ds(top, 8)], held.at[kind, pl.ds(top, 8)], arrived.at[kind, top // 8]
+                )
+            )
+            copies[-1].start()
+    for copy in copies:
+        copy.wait()
+    lane = lax.broadcasted_iota(jnp.int32, (8, LANES), 1)
     for index, ref in enumerate(chunk_refs):
-        columns = pl.ds(pl.multiple_of(starts[index], LANES), ref.shape[2])
-        ref[0] = exposure[:, columns]
-        ref[1] = noise_var[:, columns]
+        start = starts[index]
+        ahead = jnp.where(start == 0, columns, start) - LANES
+        for kind in range(2):
+            for tile in range(tiles):
+                at = pl.multiple_of(start + tile * LANES, LANES)
+                ref[kind, tile * height : (tile + 1) * height] = held[kind, :, pl.ds(at, LANES)]
+            halo = jnp.zeros((8, LANES), jnp.float32)
+            for group in range(LANES // HALO):
+                rows = held[kind, 8 * group : 8 * group + 8, pl.ds(pl.multiple_of(ahead, LANES), LANES)]
+                moved = pltpu.roll(rows, (group + 1) * HALO % LANES, 1)
+                halo = jnp.where(lane // HALO == group, moved, halo)
+            ref[kind, tiles * height :] = halo
 
 
 def cut(starts, exposure, noise_var, blocks):
     height, columns = exposure.shape
+    rows = columns // blocks // LANES * height + height * HALO // LANES
     return pl.pallas_call(
         cut_kernel,
-        in_specs=[pl.BlockSpec(memory_space=pltpu.SMEM)] + [pl.BlockSpec(memory_space=pltpu.VMEM)] * 2,
+        in_specs=[pl.BlockSpec(memory_space=pltpu.SMEM)] + [pl.BlockSpec(memory_space=pltpu.HBM)] * 2,
         out_specs=[pl.BlockSpec(memory_space=pltpu.VMEM)] * blocks,
-        out_shape=[jax.ShapeDtypeStruct((2, height, columns // blocks), jnp.float32)] * blocks,
+        out_shape=[jax.ShapeDtypeStruct((2, rows, LANES), jnp.float32)] * blocks,
+        scratch_shapes=[pltpu.VMEM((2, height, columns), jnp.float32), pltpu.SemaphoreType.DMA((2, height // 8))],
         compiler_params=pltpu.CompilerParams(vmem_limit_bytes=VMEM),
         cost_estimate=pl.CostEstimate(flops=0, bytes_accessed=16 * height * columns, transcendentals=0),
     )(starts, exposure, noise_var)
 
 
 def pick_kernel(place, owner, valid, *refs):
-    chunks, (own, last, edges, corner, chosen) = refs[:-5], refs[-5:]
-    epochs, _, tiles, height, _ = own.shape
+    chunks, (own, edges, chosen) = refs[:-3], refs[-3:]
+    epochs, _, count, height, _ = own.shape
+    tiles = count - 1
     me, lower = place[0], place[1]
     for epoch in range(epochs):
         for step, chunk in enumerate(chunks):
@@ -82,37 +110,49 @@
                 chosen[epoch] = chunk[...]
 
     row_ids = lower * height + lax.broadcasted_iota(jnp.int32, (height, LANES), 0)
+    behind = lax.broadcasted_iota(jnp.int32, (8, LANES), 1) >= LANES - HALO
     for epoch in range(epochs):
         usable = jnp.logical_and(row_ids >= valid[2 * epoch], row_ids < valid[2 * epoch + 1])
-        for tile in range(tiles):
-            columns = slice(tile * LANES, (tile + 1) * LANES)
-            inverse = jnp.where(usable, 1.0 / chosen[epoch, 1, :, columns], 0.0)
-            weighted = jnp.where(usable, chosen[epoch, 0, :, columns] / chosen[epoch, 1, :, columns], 0.0)
-            own[epoch, 0, tile] = weighted
-            own[epoch, 1, tile] = inverse
-    rows = pl.ds(pl.multiple_of((1 - lower) * (height - MAXS), MAXS), MAXS)
-    edges[...] = own[:, :, :, rows]
-    last[...] = own[:, :, tiles - 1]
-    corner[...] = own[:, :, tiles - 1, rows]
-
-
-def pick(place, owner, valid, chunks):
-    _, height, width = chunks[0].shape
-    epochs, tiles = owner.shape[0], width // LANES
-    shapes = [(tiles, height), (height,), (tiles, MAXS), (MAXS,)]
+        for tile in range(count):
+            if tile:
+                value, noise = (chosen[epoch, kind, (tile - 1) * height : tile * height] for kind in range(2))
+            else:
+                packed = [chosen[epoch, kind, tiles * height :] for kind in range(2)]
+                spread = [
+                    jnp.concatenate(
+                        [
+                            jnp.where(behind, pltpu.roll(rows, (LANES - (group + 1) * HALO) % LANES, 1), fill)
+                            for group in range(LANES // HALO)
+                        ],
+                        axis=0,
+                    )
+                    for rows, fill in zip(packed, (0.0, 1.0))
+                ]
+                value, noise = spread
+            own[epoch, 0, tile] = jnp.where(usable, value / noise, 0.0)
+            own[epoch, 1, tile] = jnp.where(usable, 1.0 / noise, 0.0)
+    edges[...] = own[:, :, :, pl.ds(pl.multiple_of((1 - lower) * (height - MAXS), MAXS), MAXS)]
+
+
+def pick(place, owner, valid, chunks, height):
+    rows = chunks[0].shape[1]
+    epochs, tiles = owner.shape[0], (rows - height * HALO // LANES) // height
     return pl.pallas_call(
         pick_kernel,
         in_specs=[pl.BlockSpec(memory_space=pltpu.SMEM)] * 3 + [pl.BlockSpec(memory_space=pltpu.VMEM)] * len(chunks),
-        out_specs=[pl.BlockSpec(memory_space=pltpu.VMEM)] * 4,
-        out_shape=[jax.ShapeDtypeStruct((epochs, 2) + shape + (LANES,), jnp.float32) for shape in shapes],
-        scratch_shapes=[pltpu.VMEM((epochs, 2, height, width), jnp.float32)],
+        out_specs=[pl.BlockSpec(memory_space=pltpu.VMEM)] * 2,
+        out_shape=[
+            jax.ShapeDtypeStruct((epochs, 2, tiles + 1, depth, LANES), jnp.float32) for depth in (height, MAXS)
+        ],
+        scratch_shapes=[pltpu.VMEM((epochs, 2, rows, LANES), jnp.float32)],
         compiler_params=pltpu.CompilerParams(vmem_limit_bytes=VMEM),
         cost_estimate=pl.CostEstimate(flops=0, bytes_accessed=4 << 20, transcendentals=0),
     )(place, owner, valid.reshape(-1), *chunks)
 
 
-def correlate_kernel(place, own, before, border, corner, bands_ref, rows_ref, ext, high, low, summed):
-    epochs, kinds, tiles, height, _ = own.shape
+def correlate_kernel(place, own, border, bands_ref, rows_ref, ext, high, low, summed):
+    epochs, kinds, count, height, _ = own.shape
+    tiles = count - 1
     ksize = bands_ref.shape[1]
     members = high.shape[2] // (height + 2 * MAXS)
     first, lower = place[0] == 0, place[1]
@@ -130,12 +170,12 @@
     for epoch in range(epochs):
         base = epoch * (tiles + 1)
         for kind in range(kinds):
-            for tile in range(tiles):
-                put(kind, 1, base + tile, own[epoch, kind, tile], border[epoch, kind, tile])
-                if tile + 1 < tiles:
-                    put(kind, 0, base + tile + 1, own[epoch, kind, tile], border[epoch, kind, tile])
-            put(kind, 0, base, before[epoch, kind] * keep, corner[epoch, kind] * keep)
-            put(kind, 0, base + tiles, before[epoch, kind], corner[epoch, kind])
+            for tile in range(1, count):
+                put(kind, 1, base + tile - 1, own[epoch, kind, tile], border[epoch, kind, tile])
+                if tile < tiles:
+                    put(kind, 0, base + tile, own[epoch, kind, tile], border[epoch, kind, tile])
+            put(kind, 0, base, own[epoch, kind, 0] * keep, border[epoch, kind, 0] * keep)
+            put(kind, 0, base + tiles, own[epoch, kind, 0], border[epoch, kind, 0])
             put(kind, 1, base + tiles, nothing, nothing[:MAXS])
 
     def split(index, _):
@@ -173,14 +213,15 @@
                     rows_ref[half, epoch, kind, tile] = rows_of(tile)
 
 
-def correlate(place, own, before, border, corner, bands):
-    epochs, kinds, tiles, height, _ = own.shape
+def correlate(place, own, border, bands):
+    epochs, kinds, count, height, _ = own.shape
+    tiles = count - 1
     members = -(-epochs * (tiles + 1) // 16) * 16
     depth = (height + 2 * MAXS) * members
     flops = 2 * 2 * kinds * members * height * bands.shape[1] * 4 * LANES * LANES
     return pl.pallas_call(
         correlate_kernel,
-        in_specs=[pl.BlockSpec(memory_space=pltpu.SMEM)] + [pl.BlockSpec(memory_space=pltpu.VMEM)] * 5,
+        in_specs=[pl.BlockSpec(memory_space=pltpu.SMEM)] + [pl.BlockSpec(memory_space=pltpu.VMEM)] * 3,
         out_specs=pl.BlockSpec(memory_space=pltpu.VMEM),
         out_shape=jax.ShapeDtypeStruct((2, epochs, kinds, tiles, MAXS, LANES), jnp.float32),
         scratch_shapes=[
@@ -191,7 +232,7 @@
         ],
         compiler_params=pltpu.CompilerParams(vmem_limit_bytes=VMEM),
         cost_estimate=pl.CostEstimate(flops=flops, bytes_accessed=12 << 20, transcendentals=0),
-    )(place, own, before, border, corner, bands)
+    )(place, own, border, bands)
 
 
 def stack_kernel(place, shifts, floor, *refs, group, parts, blocks):
@@ -258,7 +299,7 @@
                     near_packed[epoch, rows] = nearby
                 return 0
 
-            lax.fori_loop(0, reach // 8, quantize, 0)
+            lax.fori_loop(0, reach // 8, quantize, 0, unroll=4)
 
     height = out_ref.shape[1]
     across = lax.broadcasted_iota(jnp.int32, (8, LANES), 1)
@@ -294,13 +335,16 @@
 def stack_blocks(place, shifts, floor, sources, out, out_shape, parts, blocks):
     epochs, kinds, tiles = sources[0][0].shape[1:4]
     velocities, height, columns = out_shape.shape
-    group = next(size for size in (12, 9, 8, 6, 4, 3, 2, 1) if velocities % size == 0)
+    group = next(size for size in (18, 12, 9, 8, 6, 4, 3, 2, 1) if velocities % size == 0)
     width, reach = tiles * LANES, height + 2 * MAXS
     in_specs, operands = [], []
-    for index, (array, slot) in enumerate(sources):
+    for index, (array, slot, tile) in enumerate(sources):
         depth = tiles if index % 6 < 3 else 1
         in_specs.append(
-            pl.BlockSpec((1, epochs, kinds, depth, MAXS, LANES), functools.partial(lambda at, *_: (at, 0, 0, 0, 0, 0), slot))
+            pl.BlockSpec(
+                (1, epochs, kinds, depth, MAXS, LANES),
+                functools.partial(lambda slot, tile, *_: (slot, 0, 0, tile, 0, 0), slot, tile),
+            )
         )
         operands.append(array)
     aliases = {}
@@ -355,43 +399,43 @@
         chunks[step] = lax.ppermute(chunks[step], "vel", [(i, i ^ step) for i in range(blocks)])
     chunks[1], spread_kernel = lax.optimization_barrier((chunks[1], spread_kernel))
     bands, floor = make_bands(spread_kernel)
-    chunks[-1], bands = lax.optimization_barrier((chunks[-1], bands))
+    chunks[-1], floor = lax.optimization_barrier((chunks[-1], floor))
     spot = jnp.stack([me, lower]).astype(jnp.int32)
-    own, last, edges, corner = pick(spot, epoch_owner, valid_rows, chunks)
-    pairs = lax.axis_size("rows")
-    diagonal = [(a * pairs + r, b * pairs + 1 - r) for a, b in right for r in range(pairs)]
-    before = lax.ppermute(last, "vel", right)
-    corner = lax.ppermute(corner, ("vel", "rows"), diagonal)
-    border = lax.ppermute(edges, "rows", swap)
-    payload = correlate(place, own, before, border, corner, bands)
+    own, edges = pick(spot, epoch_owner, valid_rows, chunks, height)
+    payload = correlate(place, own, lax.ppermute(edges, "rows", swap), bands)
 
     flat_shifts, floor = shifts.reshape(-1), floor[0, :1]
     out_shape = jax.ShapeDtypeStruct((shifts.shape[0], height, columns), jnp.float32)
-    border = lax.ppermute(payload[:1], "rows", swap)
-    have = {0: ((payload, 0), (payload, 1), (border, 0))}
-    behind = ahead = payload
+
+    def stack_now(offsets, out):
+        sources = []
+        for offset in offsets:
+            sources += list(have[offset]) + list(front if offset == 0 else have[offset + 1])
+        spots = jnp.stack([(mine + offset) % blocks for offset in offsets] + [lower]).astype(jnp.int32)
+        return stack_blocks(spots, flat_shifts, floor, sources, out, out_shape, len(offsets), blocks)
+
+    tiles = payload.shape[3]
+    front = lax.ppermute(payload[:, :, :, :1], "vel", left)
+    behind, ahead = lax.ppermute(payload, "vel", right), lax.ppermute(payload, "vel", left)
+    border = lax.ppermute(jnp.concatenate([payload[:1], front[:1]], axis=3), "rows", swap)
+    front = ((front, 0, 0), (front, 1, 0), (border, 0, tiles))
+    have = {0: ((payload, 0, 0), (payload, 1, 0), (border, 0, 0))}
+    out = stack_now([0], None)
     half = blocks // 2
-    out = None
     for step in range(1, half + 1):
         if step < half:
-            behind, ahead = lax.ppermute(behind, "vel", right), lax.ppermute(ahead, "vel", left)
-            if out is not None:
-                behind, ahead, out = lax.optimization_barrier((behind, ahead, out))
+            if step > 1:
+                behind, ahead = lax.ppermute(behind, "vel", right), lax.ppermute(ahead, "vel", left)
+            behind, ahead, out = lax.optimization_barrier((behind, ahead, out))
             border = lax.ppermute(jnp.concatenate([behind[:1], ahead[:1]]), "rows", swap)
-            have[-step] = ((behind, 0), (behind, 1), (border, 0))
-            have[step] = ((ahead, 0), (ahead, 1), (border, 1))
+            have[-step] = ((behind, 0, 0), (behind, 1, 0), (border, 0, 0))
+            have[step] = ((ahead, 0, 0), (ahead, 1, 0), (border, 1, 0))
         else:
             edge, inner = lax.ppermute(behind[:1], "vel", right), lax.ppermute(ahead[1:], "vel", left)
-            if out is not None:
-                edge, inner, out = lax.optimization_barrier((edge, inner, out))
+            edge, inner, out = lax.optimization_barrier((edge, inner, out))
             border = lax.ppermute(edge, "rows", swap)
-            have[step] = have[-step] = ((edge, 0), (inner, 0), (border, 0))
-        now = [step - 1, -step]
-        sources = []
-        for offset in now:
-            sources += list(have[offset]) + list(have[offset + 1])
-        place = jnp.stack([(mine + offset) % blocks for offset in now] + [lower]).astype(jnp.int32)
-        out = stack_blocks(place, flat_shifts, floor, sources, out, out_shape, len(now), blocks)
+            have[step] = have[-step] = ((edge, 0, 0), (inner, 0, 0), (border, 0, 0))
+        out = stack_now([step - 1, -step] if step > 1 else [-step], out)
     return out
 
 

time: 108 us -> 107 us (level)
  Pallas kernels: 49 us -> 52.4 us
  starting transfers between devices: 27.2 us -> 24.8 us
  waiting for transfers between devices: 18.5 us -> 16.5 us
    ppermute x3 -> x2, waiting for transfers between devices: 8.89 us -> 4.5 us  [local(): lax.ppermute(ahead, 'vel', left)]
    pallas_call x4 -> x5, Pallas kernels: 35.5 us -> 37.2 us  [stack_blocks(): pl.pallas_call(functools.partial(stack_kernel, group=group, parts=parts,...]
    pallas_call x1, Pallas kernels: 0.61 us -> 2.22 us  [cut(): pl.pallas_call(cut_kernel, in_specs=[pl.BlockSpec(memory_space=pltpu.SMEM...]
    ppermute x3 -> x2, starting transfers between devices: 3.92 us -> 2.35 us  [local(): lax.ppermute(ahead, 'vel', left)]
    ppermute x7, waiting for transfers between devices: 2.84 us -> 4.22 us  [local(): lax.ppermute(chunks[step], 'vel', [(i, i ^ step) for i in range(blocks)])]
    ppermute x4 -> x5, waiting for transfers between devices: 3.94 us -> 4.94 us  [the longest x1 2.15 us: local(): front = lax.ppermute(payload[:, :, :, :1], 'vel', left)]
    ppermute x4 -> x5, starting transfers between devices: 2.95 us -> 3.63 us  [the longest x1 1.46 us: local(): front = lax.ppermute(payload[:, :, :, :1], 'vel', left)]
    ppermute x3 -> x2, starting transfers between devices: 2.31 us -> 1.8 us  [local(): lax.ppermute(behind, 'vel', right)]
  transfers between devices with their start and end apart: 23 -> 22, of which waited for: 11 -> 12; matrix products, arithmetic and copies ran while one was open for 3% -> 3% of each run, Pallas kernels for 29% -> 31%
where the time goes in v5:
time: 107 us; the launch traced here: 106 us
  Pallas kernels  52.4 us (49%)
  starting transfers between devices  24.8 us (23%)
  waiting for transfers between devices  16.5 us (15%)
  local copies, waits for them, and re-layouts  11.7 us (11%)
    pallas_call x5, Pallas kernels, stack_blocks(): pl.pallas_call(functools.partial(stack_kernel, group=group, parts=parts,...  37.2 us
    ppermute x7, starting transfers between devices, local(): lax.ppermute(chunks[step], 'vel', [(i, i ^ step) for i in range(blocks)])  14.7 us
    unnamed x16, local copies, waits for them, and re-layouts  9.33 us
    pallas_call x1, Pallas kernels, correlate(): pl.pallas_call(correlate_kernel, in_specs=[pl.BlockSpec(memory_space=pltp...  7.52 us
    pallas_call x1, Pallas kernels, make_bands(): pl.pallas_call(band_kernel, in_specs=[pl.BlockSpec(memory_space=pltpu.SME...  4.59 us
    ppermute x2, waiting for transfers between devices, local(): lax.ppermute(ahead, 'vel', left)  4.5 us
    ppermute x7, waiting for transfers between devices, local(): lax.ppermute(chunks[step], 'vel', [(i, i ^ step) for i in range(blocks)])  4.22 us
    ppermute x2, starting transfers between devices, local(): lax.ppermute(ahead, 'vel', left)  2.35 us
  transfers between devices with their start and end apart: 22, of which 12 were waited for; matrix products, arithmetic and copies ran while one was open for 3% of the time, Pallas kernels for 31%

profile of v5, /device:TPU:0, one launch (start us, length us, event | category | flops | bytes accessed | tf_op | source)
XLA Modules:
  0.0 106.3 jit_solution(17617269135025842455)
XLA Ops:
  2.1 2.2 %shard_map.64 = (f32[2,136,128]{2,1,0:T(8,128)S(1)}, f32[2,136,128]{2,1,0:T(8,128)S(1)}, f32[2,136,128]{2,1,0:T(8,128)S(1)}, f32[2,136,128]{2,1,0:T(8,128)S(1)},...) custom-call(s32[8]{0:T(128)S(1)} %fusion.starts, ...), custom_call_target="tpu_custom_call" | custom-call | bytes 2097152 | tf_op jit(solution)/shard_map/pallas_call | solution.py:89
  4.3 6.1 %collective-permute-start = (f32[2,136,128]{2,1,0:T(8,128)S(1)}, f32[2,136,128]{2,1,0:T(8,128)S(1)}, u32[]{:S(2)}, u32[]{:S(2)}) collective-permute-start(f32[2,136,128]{2,1,0:T(8,128)S(1)} %get-tuple-element.33), channel_id=1, source_target_pairs={{0,14},{2,12},{4,10},{6,8},{8,6},{10,4},{12,2},{14,0},{1,15},{3,13... | collective-permute-start | bytes 417800 | tf_op jit(solution)/shard_map/ppermute | solution.py:399
  10.9 3.0 %collective-permute-start.3 = (f32[2,136,128]{2,1,0:T(8,128)S(1)}, f32[2,136,128]{2,1,0:T(8,128)S(1)}, u32[]{:S(2)}, u32[]{:S(2)}) collective-permute-start(f32[2,136,128]{2,1,0:T(8,128)S(1)} %get-tuple-element.41), channel_id=1, source_target_pairs={{0,6},{2,4},{4,2},{6,0},{8,14},{10,12},{12,10},{14,8},{1,7},{3,5},... | collective-permute-start | bytes 417800 | tf_op jit(solution)/shard_map/ppermute | solution.py:399
  13.9 1.1 collective-permute-done.refs_7_
  14.9 4.8 %collective-permute-start.5 = (f32[2,136,128]{2,1,0:T(8,128)S(1)}, f32[2,136,128]{2,1,0:T(8,128)S(1)}, u32[]{:S(2)}, u32[]{:S(2)}) collective-permute-start(f32[2,136,128]{2,1,0:T(8,128)S(1)} %get-tuple-element.43), channel_id=1, source_target_pairs={{0,10},{2,8},{4,14},{6,12},{8,2},{10,0},{12,6},{14,4},{1,11},{3,9}... | collective-permute-start | bytes 417800 | tf_op jit(solution)/shard_map/ppermute | solution.py:399
  22.5 4.6 %shard_map.65 = (bf16[2,21,256,256]{3,2,1,0:T(8,128)(2,1)S(1)}, f32[8,128]{1,0:T(8,128)S(1)}) custom-call(f32[441]{0:T(512)S(1)} %reshape.10.taps, f32[21,21]{1,0:T(8,128)S(1)} %copy-done.2), custom_call_target="tpu_custom_call" | custom-call | bytes 20971520 | tf_op jit(solution)/shard_map/pallas_call | solution.py:42
  27.1 2.4 %copy-done.4 = bf16[2,21,256,256]{3,2,1,0:T(8,128)(2,1)} copy-done((bf16[2,21,256,256]{3,2,1,0:T(8,128)(2,1)}, bf16[2,21,256,256]{3,2,1,0:T(8,128)(2,1)S(1)}, u32[]{:S(2)}) %copy-start.4) | copy-done | bytes 5505048
  30.4 2.4 %collective-permute-done.5.refs_5_ = f32[2,136,128]{2,1,0:T(8,128)S(1)} collective-permute-done((f32[2,136,128]{2,1,0:T(8,128)S(1)}, f32[2,136,128]{2,1,0:T(8,128)S(1)}, u32[]{:S(2)}, u32[]{:S(2)}) %collective-permute-start.5) | collective-permute-done | bytes 139296 | tf_op jit(solution)/shard_map/ppermute | solution.py:399
  34.4 1.4 %collective-permute-done.7.border = f32[3,2,5,16,128]{4,3,2,1,0:T(8,128)S(1)} collective-permute-done((f32[3,2,5,16,128]{4,3,2,1,0:T(8,128)S(1)}, f32[3,2,5,16,128]{4,3,2,1,0:T(8,128)S(1)}, u32[]{:S(2)}, u32[]{:S(2)}) %collective-permute-start.7) | collective-permute-done | bytes 245792 | tf_op jit(solution)/shard_map/ppermute | solution.py:405
  35.8 2.6 %copy-done.5 = bf16[2,21,256,256]{3,2,1,0:T(8,128)(2,1)S(1)} copy-done((bf16[2,21,256,256]{3,2,1,0:T(8,128)(2,1)S(1)}, bf16[2,21,256,256]{3,2,1,0:T(8,128)(2,1)}, u32[]{:S(2)}) %copy-start.5) | copy-done | bytes 5505048
  38.4 7.5 %shard_map.67.refs_0_.refs_1_.refs_3_.refs_4_ = f32[2,3,2,4,16,128]{5,4,3,2,1,0:T(8,128)S(1)} custom-call(s32[2]{0:T(128)S(1)} %pad_add_fusion.place, f32[3,2,5,32,128]{4,3,2,1,0:T(8,128)S(1)} %get-tuple-element.46.own, f32[3,2,5,16,128]{4,3,2,1,0:T(8,128)S(1)} %collective-permute-done.7.border, bf16[2,21,256,256]{3,2,1,0:T(8,128)(2,1)S(1)} %copy-done.5), custom_call_target="tpu_custom_call" | custom-call | flops 5637144576 | bytes 12582912 | tf_op jit(solution)/shard_map/pallas_call | solution.py:222
  45.9 1.5 %collective-permute-start.10 = (f32[2,3,2,1,16,128]{5,4,3,2,1,0:T(8,128)S(1)}, f32[2,3,2,1,16,128]{5,4,3,2,1,0:T(8,128)S(1)}, u32[]{:S(2)}, u32[]{:S(2)}) collective-permute-start(f32[2,3,2,1,16,128]{5,4,3,2,1,0:T(8,128)S(1)} %slice.46), channel_id=1, source_target_pairs={{4,0},{8,4},{12,8},{14,12},{10,14},{6,10},{2,6},{0,2},{5,1},{9,5},... | collective-permute-start | bytes 294920 | tf_op jit(solution)/shard_map/ppermute | solution.py:418
  47.4 1.2 %collective-permute-start.9 = (f32[2,3,2,4,16,128]{5,4,3,2,1,0:T(8,128)S(1)}, f32[2,3,2,4,16,128]{5,4,3,2,1,0:T(8,128)S(1)}, u32[]{:S(2)}, u32[]{:S(2)}) collective-permute-start(f32[2,3,2,4,16,128]{5,4,3,2,1,0:T(8,128)S(1)} %shard_map.67.refs_0_.refs_1_.refs_3_.refs_4_), channel_id=1, source_target_pairs={{4,0},{8,4},{12,8},{14,12},{10,14},{6,10},{2,6},{0,2},{5,1},{9,5},... | collective-permute-start | bytes 1179656 | tf_op jit(solution)/shard_map/ppermute | solution.py:419
  49.5 2.2 %collective-permute-done.10.refs_3_.refs_4_ = f32[2,3,2,1,16,128]{5,4,3,2,1,0:T(8,128)S(1)} collective-permute-done((f32[2,3,2,1,16,128]{5,4,3,2,1,0:T(8,128)S(1)}, f32[2,3,2,1,16,128]{5,4,3,2,1,0:T(8,128)S(1)}, u32[]{:S(2)}, u32[]{:S(2)}) %collective-permute-start.10) | collective-permute-done | bytes 98336 | tf_op jit(solution)/shard_map/ppermute | solution.py:418
  53.2 5.5 %shard_map.68.refs_6_ = f32[36,32,4096]{2,1,0:T(8,128)} custom-call(s32[2]{0:T(128)S(1)} %pad_add_fusion.2.place, s32[216]{0:T(256)S(1)} %reshape.9.shifts, f32[1]{0:T(128)} %bitcast.5.floor, f32[2,3,2,4,16,128]{5,4,3,2,1,0:T(8,128)S(1)} %shard_map.67.refs_0_.refs_1_.refs_3_.refs_4_, f32[2,3,2,4,16,128]{5,4,3,2,1,0:T(8,128)S(1)} %shard_map.67.refs_0_.refs_1_.refs_3_.refs_4_, ...), custom_call_target="tpu_custom_call" | custom-call | flops 9437184 | bytes 14155776 | tf_op jit(solution)/shard_map/pallas_call | solution.py:356
  59.7 1.2 %collective-permute-start.13 = (f32[2,3,2,4,16,128]{5,4,3,2,1,0:T(8,128)S(1)}, f32[2,3,2,4,16,128]{5,4,3,2,1,0:T(8,128)S(1)}, u32[]{:S(2)}, u32[]{:S(2)}) collective-permute-start(f32[2,3,2,4,16,128]{5,4,3,2,1,0:T(8,128)S(1)} %collective-permute-done.9.refs_0_.refs_1_), channel_id=1, source_target_pairs={{4,0},{8,4},{12,8},{14,12},{10,14},{6,10},{2,6},{0,2},{5,1},{9,5},... | collective-permute-start | bytes 1179656 | tf_op jit(solution)/shard_map/ppermute | solution.py:428
  61.8 5.5 %shard_map.69.refs_12_ = f32[36,32,4096]{2,1,0:T(8,128)} custom-call(s32[2]{0:T(128)S(1)} %pad_add_fusion.3.place, s32[216]{0:T(256)S(1)} %reshape.9.shifts, f32[1]{0:T(128)} %bitcast.5.floor, f32[2,3,2,4,16,128]{5,4,3,2,1,0:T(8,128)S(1)} %collective-permute-done.8.refs_0_.refs_1_.refs_9_.refs_10_, ...), custom_call_target="tpu_custom_call", output_to_operand_aliasing={{}: (9, {})} | custom-call | flops 9437184 | bytes 14155776 | tf_op jit(solution)/shard_map/pallas_call | solution.py:356
  67.3 3.9 %collective-permute-done.13.refs_3_.refs_4_.refs_0_.refs_1_ = f32[2,3,2,4,16,128]{5,4,3,2,1,0:T(8,128)S(1)} collective-permute-done((f32[2,3,2,4,16,128]{5,4,3,2,1,0:T(8,128)S(1)}, f32[2,3,2,4,16,128]{5,4,3,2,1,0:T(8,128)S(1)}, u32[]{:S(2)}, u32[]{:S(2)}) %collective-permute-start.13) | collective-permute-done | bytes 393248 | tf_op jit(solution)/shard_map/ppermute | solution.py:428
  73.2 1.2 %collective-permute-start.16 = (f32[2,3,2,4,16,128]{5,4,3,2,1,0:T(8,128)S(1)}, f32[2,3,2,4,16,128]{5,4,3,2,1,0:T(8,128)S(1)}, u32[]{:S(2)}, u32[]{:S(2)}) collective-permute-start(f32[2,3,2,4,16,128]{5,4,3,2,1,0:T(8,128)S(1)} %collective-permute-done.13.refs_3_.refs_4_.refs_0_.refs_1_), channel_id=1, source_target_pairs={{4,0},{8,4},{12,8},{14,12},{10,14},{6,10},{2,6},{0,2},{5,1},{9,5},... | collective-permute-start | bytes 1179656 | tf_op jit(solution)/shard_map/ppermute | solution.py:428
  74.4 8.8 %shard_map.70.refs_12_ = f32[36,32,4096]{2,1,0:T(8,128)} custom-call(s32[3]{0:T(128)S(1)} %add_add_fusion.1.place, s32[216]{0:T(256)S(1)} %reshape.9.shifts, f32[1]{0:T(128)} %bitcast.5.floor, f32[2,3,2,4,16,128]{5,4,3,2,1,0:T(8,128)S(1)} %collective-permute-done.9.refs_0_.refs_1_, ...), custom_call_target="tpu_custom_call", output_to_operand_aliasing={{}: (15, {})} | custom-call | flops 18874368 | bytes 28311552 | tf_op jit(solution)/shard_map/pallas_call | solution.py:356
  85.2 1.8 %collective-permute-start.19 = (f32[1,3,2,4,16,128]{5,4,3,2,1,0:T(8,128)S(1)}, f32[1,3,2,4,16,128]{5,4,3,2,1,0:T(8,128)S(1)}, u32[]{:S(2)}, u32[]{:S(2)}) collective-permute-start(f32[1,3,2,4,16,128]{5,4,3,2,1,0:T(8,128)S(1)} %slice.42), channel_id=1, source_target_pairs={{0,4},{4,8},{8,12},{12,14},{14,10},{10,6},{6,2},{2,0},{1,5},{5,9},... | collective-permute-start | bytes 589832 | tf_op jit(solution)/shard_map/ppermute | solution.py:434
  87.3 8.8 %shard_map.71.refs_12_ = f32[36,32,4096]{2,1,0:T(8,128)} custom-call(s32[3]{0:T(128)S(1)} %add_add_fusion.2.place, s32[216]{0:T(256)S(1)} %reshape.9.shifts, f32[1]{0:T(128)} %bitcast.5.floor, f32[2,3,2,4,16,128]{5,4,3,2,1,0:T(8,128)S(1)} %collective-permute-done.13.refs_3_.refs_4_.refs_0_.refs_1_, ...), custom_call_target="tpu_custom_call", output_to_operand_aliasing={{}: (15, {})} | custom-call | flops 18874368 | bytes 28311552 | tf_op jit(solution)/shard_map/pallas_call | solution.py:356
  96.2 1.3 %collective-permute-done.21.refs_5_.refs_8_ = f32[1,3,2,4,16,128]{5,4,3,2,1,0:T(8,128)S(1)} collective-permute-done((f32[1,3,2,4,16,128]{5,4,3,2,1,0:T(8,128)S(1)}, f32[1,3,2,4,16,128]{5,4,3,2,1,0:T(8,128)S(1)}, u32[]{:S(2)}, u32[]{:S(2)}) %collective-permute-start.21) | collective-permute-done | bytes 196640 | tf_op jit(solution)/shard_map/ppermute | solution.py:436
  97.5 8.8 %shard_map.72 = f32[36,32,4096]{2,1,0:T(8,128)} custom-call(s32[3]{0:T(128)S(1)} %add_add_fusion.place, s32[216]{0:T(256)S(1)} %reshape.9.shifts, f32[1]{0:T(128)} %bitcast.5.floor, f32[2,3,2,4,16,128]{5,4,3,2,1,0:T(8,128)S(1)} %collective-permute-done.16.refs_3_.refs_4_.refs_0_.refs_1_, ...), custom_call_target="tpu_custom_call", output_to_operand_aliasing={{}: (15, {})} | custom-call | flops 18874368 | bytes 28311552 | tf_op jit(solution)/shard_map/pallas_call | solution.py:356
  (70 shorter events, 16.7 us)
Async XLA Ops:
  0.0 51.7 %copy-start.6 = (s32[36,3,2]{0,2,1:T(2,128)S(1)}, s32[36,3,2]{0,2,1:T(2,128)}, u32[]{:S(2)}) copy-start(s32[36,3,2]{0,2,1:T(2,128)} %param.9) | copy-start | bytes 2596
  4.3 10.6 %collective-permute-start = (f32[2,136,128]{2,1,0:T(8,128)S(1)}, f32[2,136,128]{2,1,0:T(8,128)S(1)}, u32[]{:S(2)}, u32[]{:S(2)}) collective-permute-start(f32[2,136,128]{2,1,0:T(8,128)S(1)} %get-tuple-element.33), channel_id=1, source_target_pairs={{0,14},{2,12},{4,10},{6,8},{8,6},{10,4},{12,2},{14,0},{1,15},{3,13... | collective-permute-start | bytes 417800 | tf_op jit(solution)/shard_map/ppermute | solution.py:399
  10.4 9.3 %collective-permute-start.1 = (f32[2,136,128]{2,1,0:T(8,128)S(1)}, f32[2,136,128]{2,1,0:T(8,128)S(1)}, u32[]{:S(2)}, u32[]{:S(2)}) collective-permute-start(f32[2,136,128]{2,1,0:T(8,128)S(1)} %get-tuple-element.34), channel_id=1, source_target_pairs={{0,2},{2,0},{4,6},{6,4},{8,10},{10,8},{12,14},{14,12},{1,3},{3,1},... | collective-permute-start | bytes 417800 | tf_op jit(solution)/shard_map/ppermute | solution.py:399
  10.9 18.7 %collective-permute-start.2 = (f32[2,136,128]{2,1,0:T(8,128)S(1)}, f32[2,136,128]{2,1,0:T(8,128)S(1)}, u32[]{:S(2)}, u32[]{:S(2)}) collective-permute-start(f32[2,136,128]{2,1,0:T(8,128)S(1)} %get-tuple-element.40), channel_id=1, source_target_pairs={{0,4},{2,6},{4,0},{6,2},{8,12},{10,14},{12,8},{14,10},{1,5},{3,7},... | collective-permute-start | bytes 417800 | tf_op jit(solution)/shard_map/ppermute | solution.py:399
  10.9 18.7 %collective-permute-start.3 = (f32[2,136,128]{2,1,0:T(8,128)S(1)}, f32[2,136,128]{2,1,0:T(8,128)S(1)}, u32[]{:S(2)}, u32[]{:S(2)}) collective-permute-start(f32[2,136,128]{2,1,0:T(8,128)S(1)} %get-tuple-element.41), channel_id=1, source_target_pairs={{0,6},{2,4},{4,2},{6,0},{8,14},{10,12},{12,10},{14,8},{1,7},{3,5},... | collective-permute-start | bytes 417800 | tf_op jit(solution)/shard_map/ppermute | solution.py:399
  13.9 16.5 %collective-permute-start.4 = (f32[2,136,128]{2,1,0:T(8,128)S(1)}, f32[2,136,128]{2,1,0:T(8,128)S(1)}, u32[]{:S(2)}, u32[]{:S(2)}) collective-permute-start(f32[2,136,128]{2,1,0:T(8,128)S(1)} %get-tuple-element.42), channel_id=1, source_target_pairs={{0,8},{2,10},{4,12},{6,14},{8,0},{10,2},{12,4},{14,6},{1,9},{3,11}... | collective-permute-start | bytes 417800 | tf_op jit(solution)/shard_map/ppermute | solution.py:399
  14.9 17.8 %collective-permute-start.5 = (f32[2,136,128]{2,1,0:T(8,128)S(1)}, f32[2,136,128]{2,1,0:T(8,128)S(1)}, u32[]{:S(2)}, u32[]{:S(2)}) collective-permute-start(f32[2,136,128]{2,1,0:T(8,128)S(1)} %get-tuple-element.43), channel_id=1, source_target_pairs={{0,10},{2,8},{4,14},{6,12},{8,2},{10,0},{12,6},{14,4},{1,11},{3,9}... | collective-permute-start | bytes 417800 | tf_op jit(solution)/shard_map/ppermute | solution.py:399
  19.7 13.0 %collective-permute-start.6 = (f32[2,136,128]{2,1,0:T(8,128)S(1)}, f32[2,136,128]{2,1,0:T(8,128)S(1)}, u32[]{:S(2)}, u32[]{:S(2)}) collective-permute-start(f32[2,136,128]{2,1,0:T(8,128)S(1)} %get-tuple-element.44), channel_id=1, source_target_pairs={{0,12},{2,14},{4,8},{6,10},{8,4},{10,6},{12,0},{14,2},{1,13},{3,15... | collective-permute-start | bytes 417800 | tf_op jit(solution)/shard_map/ppermute | solution.py:399
  34.3 1.6 %collective-permute-start.7 = (f32[3,2,5,16,128]{4,3,2,1,0:T(8,128)S(1)}, f32[3,2,5,16,128]{4,3,2,1,0:T(8,128)S(1)}, u32[]{:S(2)}, u32[]{:S(2)}) collective-permute-start(f32[3,2,5,16,128]{4,3,2,1,0:T(8,128)S(1)} %get-tuple-element.47), channel_id=1, source_target_pairs={{0,1},{1,0},{2,3},{3,2},{4,5},{5,4},{6,7},{7,6},{8,9},{9,8},{10,11... | collective-permute-start | bytes 737288 | tf_op jit(solution)/shard_map/ppermute | solution.py:405
  35.8 2.6 %copy-start.5 = (bf16[2,21,256,256]{3,2,1,0:T(8,128)(2,1)S(1)}, bf16[2,21,256,256]{3,2,1,0:T(8,128)(2,1)}, u32[]{:S(2)}) copy-start(bf16[2,21,256,256]{3,2,1,0:T(8,128)(2,1)} %copy-done.4) | copy-start | bytes 16515076
  45.9 5.7 %collective-permute-start.10 = (f32[2,3,2,1,16,128]{5,4,3,2,1,0:T(8,128)S(1)}, f32[2,3,2,1,16,128]{5,4,3,2,1,0:T(8,128)S(1)}, u32[]{:S(2)}, u32[]{:S(2)}) collective-permute-start(f32[2,3,2,1,16,128]{5,4,3,2,1,0:T(8,128)S(1)} %slice.46), channel_id=1, source_target_pairs={{4,0},{8,4},{12,8},{14,12},{10,14},{6,10},{2,6},{0,2},{5,1},{9,5},... | collective-permute-start | bytes 294920 | tf_op jit(solution)/shard_map/ppermute | solution.py:418
  47.4 12.1 %collective-permute-start.9 = (f32[2,3,2,4,16,128]{5,4,3,2,1,0:T(8,128)S(1)}, f32[2,3,2,4,16,128]{5,4,3,2,1,0:T(8,128)S(1)}, u32[]{:S(2)}, u32[]{:S(2)}) collective-permute-start(f32[2,3,2,4,16,128]{5,4,3,2,1,0:T(8,128)S(1)} %shard_map.67.refs_0_.refs_1_.refs_3_.refs_4_), channel_id=1, source_target_pairs={{4,0},{8,4},{12,8},{14,12},{10,14},{6,10},{2,6},{0,2},{5,1},{9,5},... | collective-permute-start | bytes 1179656 | tf_op jit(solution)/shard_map/ppermute | solution.py:419
  48.6 10.9 %collective-permute-start.8 = (f32[2,3,2,4,16,128]{5,4,3,2,1,0:T(8,128)S(1)}, f32[2,3,2,4,16,128]{5,4,3,2,1,0:T(8,128)S(1)}, u32[]{:S(2)}, u32[]{:S(2)}) collective-permute-start(f32[2,3,2,4,16,128]{5,4,3,2,1,0:T(8,128)S(1)} %shard_map.67.refs_0_.refs_1_.refs_3_.refs_4_), channel_id=1, source_target_pairs={{0,4},{4,8},{8,12},{12,14},{14,10},{10,6},{6,2},{2,0},{1,5},{5,9},... | collective-permute-start | bytes 1179656 | tf_op jit(solution)/shard_map/ppermute | solution.py:419
  51.6 1.6 %collective-permute-start.11 = (f32[1,3,2,5,16,128]{5,4,3,2,1,0:T(8,128)S(1)}, f32[1,3,2,5,16,128]{5,4,3,2,1,0:T(8,128)S(1)}, u32[]{:S(2)}, u32[]{:S(2)}) collective-permute-start(f32[1,3,2,5,16,128]{5,4,3,2,1,0:T(8,128)S(1)} %pad_maximum_fusion.3), channel_id=1, source_target_pairs={{0,1},{1,0},{2,3},{3,2},{4,5},{5,4},{6,7},{7,6},{8,9},{9,8},{10,11... | collective-permute-start | bytes 737288 | tf_op jit(solution)/shard_map/ppermute | solution.py:420
  59.6 2.2 %collective-permute-start.14 = (f32[2,3,2,4,16,128]{5,4,3,2,1,0:T(8,128)S(1)}, f32[2,3,2,4,16,128]{5,4,3,2,1,0:T(8,128)S(1)}, u32[]{:S(2)}, u32[]{:S(2)}) collective-permute-start(f32[2,3,2,4,16,128]{5,4,3,2,1,0:T(8,128)S(1)} %pad_maximum_fusion), channel_id=1, source_target_pairs={{0,1},{1,0},{2,3},{3,2},{4,5},{5,4},{6,7},{7,6},{8,9},{9,8},{10,11... | collective-permute-start | bytes 1179656 | tf_op jit(solution)/shard_map/ppermute | solution.py:430
  59.7 11.5 %collective-permute-start.13 = (f32[2,3,2,4,16,128]{5,4,3,2,1,0:T(8,128)S(1)}, f32[2,3,2,4,16,128]{5,4,3,2,1,0:T(8,128)S(1)}, u32[]{:S(2)}, u32[]{:S(2)}) collective-permute-start(f32[2,3,2,4,16,128]{5,4,3,2,1,0:T(8,128)S(1)} %collective-permute-done.9.refs_0_.refs_1_), channel_id=1, source_target_pairs={{4,0},{8,4},{12,8},{14,12},{10,14},{6,10},{2,6},{0,2},{5,1},{9,5},... | collective-permute-start | bytes 1179656 | tf_op jit(solution)/shard_map/ppermute | solution.py:428
  60.9 11.2 %collective-permute-start.12 = (f32[2,3,2,4,16,128]{5,4,3,2,1,0:T(8,128)S(1)}, f32[2,3,2,4,16,128]{5,4,3,2,1,0:T(8,128)S(1)}, u32[]{:S(2)}, u32[]{:S(2)}) collective-permute-start(f32[2,3,2,4,16,128]{5,4,3,2,1,0:T(8,128)S(1)} %collective-permute-done.8.refs_0_.refs_1_.refs_9_.refs_10_), channel_id=1, source_target_pairs={{0,4},{4,8},{8,12},{12,14},{14,10},{10,6},{6,2},{2,0},{1,5},{5,9},... | collective-permute-start | bytes 1179656 | tf_op jit(solution)/shard_map/ppermute | solution.py:428
  72.1 2.2 %collective-permute-start.17 = (f32[2,3,2,4,16,128]{5,4,3,2,1,0:T(8,128)S(1)}, f32[2,3,2,4,16,128]{5,4,3,2,1,0:T(8,128)S(1)}, u32[]{:S(2)}, u32[]{:S(2)}) collective-permute-start(f32[2,3,2,4,16,128]{5,4,3,2,1,0:T(8,128)S(1)} %pad_maximum_fusion.1), channel_id=1, source_target_pairs={{0,1},{1,0},{2,3},{3,2},{4,5},{5,4},{6,7},{7,6},{8,9},{9,8},{10,11... | collective-permute-start | bytes 1179656 | tf_op jit(solution)/shard_map/ppermute | solution.py:430
  72.2 11.5 %collective-permute-start.15 = (f32[2,3,2,4,16,128]{5,4,3,2,1,0:T(8,128)S(1)}, f32[2,3,2,4,16,128]{5,4,3,2,1,0:T(8,128)S(1)}, u32[]{:S(2)}, u32[]{:S(2)}) collective-permute-start(f32[2,3,2,4,16,128]{5,4,3,2,1,0:T(8,128)S(1)} %collective-permute-done.12.refs_6_.refs_7_.refs_9_.refs_10_), channel_id=1, source_target_pairs={{0,4},{4,8},{8,12},{12,14},{14,10},{10,6},{6,2},{2,0},{1,5},{5,9},... | collective-permute-start | bytes 1179656 | tf_op jit(solution)/shard_map/ppermute | solution.py:428
  73.2 11.2 %collective-permute-start.16 = (f32[2,3,2,4,16,128]{5,4,3,2,1,0:T(8,128)S(1)}, f32[2,3,2,4,16,128]{5,4,3,2,1,0:T(8,128)S(1)}, u32[]{:S(2)}, u32[]{:S(2)}) collective-permute-start(f32[2,3,2,4,16,128]{5,4,3,2,1,0:T(8,128)S(1)} %collective-permute-done.13.refs_3_.refs_4_.refs_0_.refs_1_), channel_id=1, source_target_pairs={{4,0},{8,4},{12,8},{14,12},{10,14},{6,10},{2,6},{0,2},{5,1},{9,5},... | collective-permute-start | bytes 1179656 | tf_op jit(solution)/shard_map/ppermute | solution.py:428
  85.1 2.2 %collective-permute-start.18 = (f32[2,3,2,4,16,128]{5,4,3,2,1,0:T(8,128)S(1)}, f32[2,3,2,4,16,128]{5,4,3,2,1,0:T(8,128)S(1)}, u32[]{:S(2)}, u32[]{:S(2)}) collective-permute-start(f32[2,3,2,4,16,128]{5,4,3,2,1,0:T(8,128)S(1)} %pad_maximum_fusion.2), channel_id=1, source_target_pairs={{0,1},{1,0},{2,3},{3,2},{4,5},{5,4},{6,7},{7,6},{8,9},{9,8},{10,11... | collective-permute-start | bytes 1179656 | tf_op jit(solution)/shard_map/ppermute | solution.py:430
  85.2 10.9 %collective-permute-start.19 = (f32[1,3,2,4,16,128]{5,4,3,2,1,0:T(8,128)S(1)}, f32[1,3,2,4,16,128]{5,4,3,2,1,0:T(8,128)S(1)}, u32[]{:S(2)}, u32[]{:S(2)}) collective-permute-start(f32[1,3,2,4,16,128]{5,4,3,2,1,0:T(8,128)S(1)} %slice.42), channel_id=1, source_target_pairs={{0,4},{4,8},{8,12},{12,14},{14,10},{10,6},{6,2},{2,0},{1,5},{5,9},... | collective-permute-start | bytes 589832 | tf_op jit(solution)/shard_map/ppermute | solution.py:434
  87.0 9.1 %collective-permute-start.20 = (f32[1,3,2,4,16,128]{5,4,3,2,1,0:T(8,128)}, f32[1,3,2,4,16,128]{5,4,3,2,1,0:T(8,128)S(1)}, u32[]{:S(2)}, u32[]{:S(2)}) collective-permute-start(f32[1,3,2,4,16,128]{5,4,3,2,1,0:T(8,128)} %get-tuple-element.61), channel_id=1, source_target_pairs={{4,0},{8,4},{12,8},{14,12},{10,14},{6,10},{2,6},{0,2},{5,1},{9,5},... | collective-permute-start | bytes 589832 | tf_op jit(solution)/shard_map/ppermute | solution.py:434
  96.1 1.4 %collective-permute-start.21 = (f32[1,3,2,4,16,128]{5,4,3,2,1,0:T(8,128)S(1)}, f32[1,3,2,4,16,128]{5,4,3,2,1,0:T(8,128)S(1)}, u32[]{:S(2)}, u32[]{:S(2)}) collective-permute-start(f32[1,3,2,4,16,128]{5,4,3,2,1,0:T(8,128)S(1)} %collective-permute-done.19.refs_3_.refs_6_), channel_id=1, source_target_pairs={{0,1},{1,0},{2,3},{3,2},{4,5},{5,4},{6,7},{7,6},{8,9},{9,8},{10,11... | collective-permute-start | bytes 589832 | tf_op jit(solution)/shard_map/ppermute | solution.py:436
  (5 other events, 5.9 us)

commit v6 on v5

--- a/solution.py
+++ b/solution.py
@@ -10,6 +10,7 @@
 MAXS = 16
 HALO = 32
 VMEM = 24 << 20
+LARGE = 56 << 20
 
 
 def band_kernel(taps, kernel, bands_ref, floor_ref):
@@ -47,7 +48,7 @@
             jax.ShapeDtypeStruct((2, ksize, 2 * LANES, 2 * LANES), jnp.bfloat16),
             jax.ShapeDtypeStruct((8, LANES), jnp.float32),
         ],
-        compiler_params=pltpu.CompilerParams(vmem_limit_bytes=VMEM),
+        compiler_params=pltpu.CompilerParams(vmem_limit_bytes=LARGE),
         cost_estimate=pl.CostEstimate(flops=0, bytes_accessed=20 << 20, transcendentals=0),
     )(spread_kernel.reshape(-1), spread_kernel)
 
@@ -92,7 +93,7 @@
         out_specs=[pl.BlockSpec(memory_space=pltpu.VMEM)] * blocks,
         out_shape=[jax.ShapeDtypeStruct((2, rows, LANES), jnp.float32)] * blocks,
         scratch_shapes=[pltpu.VMEM((2, height, columns), jnp.float32), pltpu.SemaphoreType.DMA((2, height // 8))],
-        compiler_params=pltpu.CompilerParams(vmem_limit_bytes=VMEM),
+        compiler_params=pltpu.CompilerParams(vmem_limit_bytes=LARGE),
         cost_estimate=pl.CostEstimate(flops=0, bytes_accessed=16 * height * columns, transcendentals=0),
     )(starts, exposure, noise_var)
 
@@ -150,11 +151,14 @@
     )(place, owner, valid.reshape(-1), *chunks)
 
 
-def correlate_kernel(place, own, border, bands_ref, rows_ref, ext, high, low, summed):
+def correlate_kernel(place, own, border, bands_hbm, rows_ref, ext, high, low, summed, bands_ref, arrived):
     epochs, kinds, count, height, _ = own.shape
     tiles = count - 1
     ksize = bands_ref.shape[1]
     members = high.shape[2] // (height + 2 * MAXS)
+    copies = [pltpu.make_async_copy(bands_hbm.at[kind], bands_ref.at[kind], arrived.at[kind]) for kind in range(kinds)]
+    for copy in copies:
+        copy.start()
     first, lower = place[0] == 0, place[1]
     at_border = (1 - lower) * (MAXS + height)
     summed_rows = height * members
@@ -196,6 +200,7 @@
         offsets = [pl.ds((row + MAXS - ksize // 2) * members, summed_rows) for row in range(ksize)]
         upper = jnp.concatenate([high[kind, half, rows] for rows in offsets for half in range(2)], axis=1)
         rest = jnp.concatenate([low[kind, half, rows] for rows in offsets for half in range(2)], axis=1)
+        copies[kind].wait()
         weights = bands_ref[kind].reshape(ksize * 2 * LANES, 2 * LANES)
         pair = jnp.dot(upper, weights, preferred_element_type=jnp.float32)
         more = jnp.dot(rest, weights[:, :LANES], preferred_element_type=jnp.float32)
@@ -221,7 +226,8 @@
     flops = 2 * 2 * kinds * members * height * bands.shape[1] * 4 * LANES * LANES
     return pl.pallas_call(
         correlate_kernel,
-        in_specs=[pl.BlockSpec(memory_space=pltpu.SMEM)] + [pl.BlockSpec(memory_space=pltpu.VMEM)] * 3,
+        in_specs=[pl.BlockSpec(memory_space=pltpu.SMEM)] + [pl.BlockSpec(memory_space=pltpu.VMEM)] * 2
+        + [pl.BlockSpec(memory_space=pltpu.HBM)],
         out_specs=pl.BlockSpec(memory_space=pltpu.VMEM),
         out_shape=jax.ShapeDtypeStruct((2, epochs, kinds, tiles, MAXS, LANES), jnp.float32),
         scratch_shapes=[
@@ -229,8 +235,10 @@
             pltpu.VMEM((kinds, 2, depth, LANES), jnp.bfloat16),
             pltpu.VMEM((kinds, 2, depth, LANES), jnp.bfloat16),
             pltpu.VMEM((height * members, LANES), jnp.float32),
+            pltpu.VMEM(bands.shape, bands.dtype),
+            pltpu.SemaphoreType.DMA((kinds,)),
         ],
-        compiler_params=pltpu.CompilerParams(vmem_limit_bytes=VMEM),
+        compiler_params=pltpu.CompilerParams(vmem_limit_bytes=LARGE),
         cost_estimate=pl.CostEstimate(flops=flops, bytes_accessed=12 << 20, transcendentals=0),
     )(place, own, border, bands)
 
@@ -395,11 +403,11 @@
 
     starts = position(me ^ jnp.arange(blocks, dtype=jnp.int32)) * width
     chunks = list(cut(starts, exposure, noise_var, blocks))
-    for step in range(1, blocks):
+    for step in range(blocks - 1, 0, -1):
         chunks[step] = lax.ppermute(chunks[step], "vel", [(i, i ^ step) for i in range(blocks)])
-    chunks[1], spread_kernel = lax.optimization_barrier((chunks[1], spread_kernel))
+    chunks[-1], spread_kernel = lax.optimization_barrier((chunks[-1], spread_kernel))
     bands, floor = make_bands(spread_kernel)
-    chunks[-1], floor = lax.optimization_barrier((chunks[-1], floor))
+    chunks[1], floor = lax.optimization_barrier((chunks[1], floor))
     spot = jnp.stack([me, lower]).astype(jnp.int32)
     own, edges = pick(spot, epoch_owner, valid_rows, chunks, height)
     payload = correlate(place, own, lax.ppermute(edges, "rows", swap), bands)

time: 107 us -> 110 us (1.028)
  Pallas kernels: 52.4 us -> 58.2 us
  waiting for transfers between devices: 16.5 us -> 13 us
  starting transfers between devices: 24.8 us -> 26.1 us
  other arithmetic: 0.64 us -> 1.8 us
    unnamed x16, local copies, waits for them, and re-layouts: 9.33 us -> 4.95 us
    pallas_call x1, Pallas kernels: 4.59 us -> 7.2 us  [make_bands(): pl.pallas_call(band_kernel, in_specs=[pl.BlockSpec(memory_space=pltpu.SME...]
    pallas_call x1, Pallas kernels: 7.52 us -> 9.86 us  [correlate(): pl.pallas_call(correlate_kernel, in_specs=[pl.BlockSpec(memory_space=pltp...]
    ppermute x7, starting transfers between devices: 14.7 us -> 16.1 us  [local(): lax.ppermute(chunks[step], 'vel', [(i, i ^ step) for i in range(blocks)])]
  transfers between devices with their start and end apart: 22 -> 22, of which waited for: 12 -> 10; matrix products, arithmetic and copies ran while one was open for 3% -> 5% of each run, Pallas kernels for 31% -> 32%
where the time goes in v6:
time: 110 us
  Pallas kernels  58.2 us (53%)
  starting transfers between devices  26.1 us (24%)
  waiting for transfers between devices  13 us (12%)
  local copies, waits for them, and re-layouts  10.6 us (10%)
  other arithmetic  1.8 us (2%)
    pallas_call x5, Pallas kernels, stack_blocks(): pl.pallas_call(functools.partial(stack_kernel, group=group, parts=parts,...  37.1 us
    ppermute x7, starting transfers between devices, local(): lax.ppermute(chunks[step], 'vel', [(i, i ^ step) for i in range(blocks)])  16.1 us
    pallas_call x1, Pallas kernels, correlate(): pl.pallas_call(correlate_kernel, in_specs=[pl.BlockSpec(memory_space=pltp...  9.86 us
    pallas_call x1, Pallas kernels, make_bands(): pl.pallas_call(band_kernel, in_specs=[pl.BlockSpec(memory_space=pltpu.SME...  7.2 us
    unnamed x16, local copies, waits for them, and re-layouts  4.95 us
    ppermute x2, waiting for transfers between devices, local(): lax.ppermute(ahead, 'vel', left)  3.76 us
    ppermute x7, waiting for transfers between devices, local(): lax.ppermute(chunks[step], 'vel', [(i, i ^ step) for i in range(blocks)])  3.48 us
    pallas_call x1, Pallas kernels, cut(): pl.pallas_call(cut_kernel, in_specs=[pl.BlockSpec(memory_space=pltpu.SMEM...  3.16 us
  transfers between devices with their start and end apart: 22, of which 10 were waited for; matrix products, arithmetic and copies ran while one was open for 5% of the time, Pallas kernels for 32%

profile of v6, /device:TPU:0, one launch (start us, length us, event | category | flops | bytes accessed | tf_op | source)
XLA Modules:
  0.0 109.9 jit_solution(6361144832666448375)
XLA Ops:
  0.6 3.2 %shard_map.64 = (f32[2,136,128]{2,1,0:T(8,128)}, f32[2,136,128]{2,1,0:T(8,128)}, f32[2,136,128]{2,1,0:T(8,128)}, f32[2,136,128]{2,1,0:T(8,128)}, f32[2,136,128]{...) custom-call(s32[8]{0:T(128)} %fusion.starts, f32[32,4096]{1,0:T(8,128)} %bitcast.14, ...), custom_call_target="tpu_custom_call" | custom-call | bytes 2097152 | tf_op jit(solution)/shard_map/pallas_call | solution.py:90
  3.8 3.0 %collective-permute-start = (f32[2,136,128]{2,1,0:T(8,128)}, f32[2,136,128]{2,1,0:T(8,128)S(1)}, u32[]{:S(2)}, u32[]{:S(2)}) collective-permute-start(f32[2,136,128]{2,1,0:T(8,128)} %get-tuple-element.33), channel_id=1, source_target_pairs={{0,2},{2,0},{4,6},{6,4},{8,10},{10,8},{12,14},{14,12},{1,3},{3,1},... | collective-permute-start | bytes 417800 | tf_op jit(solution)/shard_map/ppermute | solution.py:407
  6.8 3.5 %collective-permute-start.1 = (f32[2,136,128]{2,1,0:T(8,128)}, f32[2,136,128]{2,1,0:T(8,128)S(1)}, u32[]{:S(2)}, u32[]{:S(2)}) collective-permute-start(f32[2,136,128]{2,1,0:T(8,128)} %get-tuple-element.34), channel_id=1, source_target_pairs={{0,14},{2,12},{4,10},{6,8},{8,6},{10,4},{12,2},{14,0},{1,15},{3,13... | collective-permute-start | bytes 417800 | tf_op jit(solution)/shard_map/ppermute | solution.py:407
  10.3 3.0 %collective-permute-start.3 = (f32[2,136,128]{2,1,0:T(8,128)}, f32[2,136,128]{2,1,0:T(8,128)S(1)}, u32[]{:S(2)}, u32[]{:S(2)}) collective-permute-start(f32[2,136,128]{2,1,0:T(8,128)} %get-tuple-element.41), channel_id=1, source_target_pairs={{0,6},{2,4},{4,2},{6,0},{8,14},{10,12},{12,10},{14,8},{1,7},{3,5},... | collective-permute-start | bytes 417800 | tf_op jit(solution)/shard_map/ppermute | solution.py:407
  13.3 3.2 %collective-permute-start.5 = (f32[2,136,128]{2,1,0:T(8,128)}, f32[2,136,128]{2,1,0:T(8,128)S(1)}, u32[]{:S(2)}, u32[]{:S(2)}) collective-permute-start(f32[2,136,128]{2,1,0:T(8,128)} %get-tuple-element.43), channel_id=1, source_target_pairs={{0,10},{2,8},{4,14},{6,12},{8,2},{10,0},{12,6},{14,4},{1,11},{3,9}... | collective-permute-start | bytes 417800 | tf_op jit(solution)/shard_map/ppermute | solution.py:407
  16.5 3.4 %collective-permute-start.6 = (f32[2,136,128]{2,1,0:T(8,128)}, f32[2,136,128]{2,1,0:T(8,128)S(1)}, u32[]{:S(2)}, u32[]{:S(2)}) collective-permute-start(f32[2,136,128]{2,1,0:T(8,128)} %get-tuple-element.44), channel_id=1, source_target_pairs={{0,12},{2,14},{4,8},{6,10},{8,4},{10,6},{12,0},{14,2},{1,13},{3,15... | collective-permute-start | bytes 417800 | tf_op jit(solution)/shard_map/ppermute | solution.py:407
  20.8 1.4 %reshape.10.taps = f32[441]{0:T(512)} reshape(f32[21,21]{1,0:T(8,128)} %kernel) | data formatting | bytes 3528 | tf_op jit(solution)/shard_map/reshape | solution.py:53
  22.2 7.2 %shard_map.65 = (bf16[2,21,256,256]{3,2,1,0:T(8,128)(2,1)}, f32[8,128]{1,0:T(8,128)}) custom-call(f32[441]{0:T(512)} %reshape.10.taps, f32[21,21]{1,0:T(8,128)} %kernel), custom_call_target="tpu_custom_call" | custom-call | bytes 20971520 | tf_op jit(solution)/shard_map/pallas_call | solution.py:43
  30.0 2.9 %collective-permute-done.5.refs_5_ = f32[2,136,128]{2,1,0:T(8,128)S(1)} collective-permute-done((f32[2,136,128]{2,1,0:T(8,128)}, f32[2,136,128]{2,1,0:T(8,128)S(1)}, u32[]{:S(2)}, u32[]{:S(2)}) %collective-permute-start.5) | collective-permute-done | bytes 139296 | tf_op jit(solution)/shard_map/ppermute | solution.py:407
  38.4 9.9 %shard_map.67.refs_0_.refs_1_.refs_3_.refs_4_ = f32[2,3,2,4,16,128]{5,4,3,2,1,0:T(8,128)} custom-call(s32[2]{0:T(128)} %pad_add_fusion.place, f32[3,2,5,32,128]{4,3,2,1,0:T(8,128)} %copy-done.4, f32[3,2,5,16,128]{4,3,2,1,0:T(8,128)} %copy-done.6, bf16[2,21,256,256]{3,2,1,0:T(8,128)(2,1)} %get-tuple-element.48.bands_hbm), custom_call_target="tpu_custom_call" | custom-call | flops 5637144576 | bytes 12582912 | tf_op jit(solution)/shard_map/pallas_call | solution.py:227
  50.3 2.1 %collective-permute-start.9 = (f32[2,3,2,4,16,128]{5,4,3,2,1,0:T(8,128)}, f32[2,3,2,4,16,128]{5,4,3,2,1,0:T(8,128)S(1)}, u32[]{:S(2)}, u32[]{:S(2)}) collective-permute-start(f32[2,3,2,4,16,128]{5,4,3,2,1,0:T(8,128)} %shard_map.67.refs_0_.refs_1_.refs_3_.refs_4_), channel_id=1, source_target_pairs={{4,0},{8,4},{12,8},{14,12},{10,14},{6,10},{2,6},{0,2},{5,1},{9,5},... | collective-permute-start | bytes 1179656 | tf_op jit(solution)/shard_map/ppermute | solution.py:427
  53.4 1.5 %collective-permute-done.10.refs_3_.refs_4_ = f32[2,3,2,1,16,128]{5,4,3,2,1,0:T(8,128)S(1)} collective-permute-done((f32[2,3,2,1,16,128]{5,4,3,2,1,0:T(8,128)S(1)}, f32[2,3,2,1,16,128]{5,4,3,2,1,0:T(8,128)S(1)}, u32[]{:S(2)}, u32[]{:S(2)}) %collective-permute-start.10) | collective-permute-done | bytes 98336 | tf_op jit(solution)/shard_map/ppermute | solution.py:426
  55.3 1.3 %slice.34 = f32[1,1]{1,0:T(1,128)} slice(f32[8,128]{1,0:T(8,128)} %get-tuple-element.37), slice={[0:1], [0:1]} | slice | bytes 8 | tf_op jit(solution)/shard_map/slice | solution.py:415
  57.6 5.4 %shard_map.68.refs_6_ = f32[36,32,4096]{2,1,0:T(8,128)} custom-call(s32[2]{0:T(128)S(1)} %pad_add_fusion.2.place, s32[216]{0:T(256)S(1)} %reshape.9.shifts, f32[1]{0:T(128)} %bitcast.5.floor, f32[2,3,2,4,16,128]{5,4,3,2,1,0:T(8,128)S(1)} %copy-done, f32[2,3,2,4,16,128]{5,4,3,2,1,0:T(8,128)S(1)} %copy-done, ...), custom_call_target="tpu_custom_call" | custom-call | flops 9437184 | bytes 14155776 | tf_op jit(solution)/shard_map/pallas_call | solution.py:364
  63.7 1.3 %collective-permute-start.13 = (f32[2,3,2,4,16,128]{5,4,3,2,1,0:T(8,128)S(1)}, f32[2,3,2,4,16,128]{5,4,3,2,1,0:T(8,128)S(1)}, u32[]{:S(2)}, u32[]{:S(2)}) collective-permute-start(f32[2,3,2,4,16,128]{5,4,3,2,1,0:T(8,128)S(1)} %collective-permute-done.9.refs_0_.refs_1_), channel_id=1, source_target_pairs={{4,0},{8,4},{12,8},{14,12},{10,14},{6,10},{2,6},{0,2},{5,1},{9,5},... | collective-permute-start | bytes 1179656 | tf_op jit(solution)/shard_map/ppermute | solution.py:436
  65.8 5.4 %shard_map.69.refs_12_ = f32[36,32,4096]{2,1,0:T(8,128)} custom-call(s32[2]{0:T(128)S(1)} %pad_add_fusion.3.place, s32[216]{0:T(256)S(1)} %reshape.9.shifts, f32[1]{0:T(128)} %bitcast.5.floor, f32[2,3,2,4,16,128]{5,4,3,2,1,0:T(8,128)S(1)} %collective-permute-done.8.refs_0_.refs_1_.refs_9_.refs_10_, ...), custom_call_target="tpu_custom_call", output_to_operand_aliasing={{}: (9, {})} | custom-call | flops 9437184 | bytes 14155776 | tf_op jit(solution)/shard_map/pallas_call | solution.py:364
  71.2 3.6 %collective-permute-done.13.refs_3_.refs_4_.refs_0_.refs_1_ = f32[2,3,2,4,16,128]{5,4,3,2,1,0:T(8,128)S(1)} collective-permute-done((f32[2,3,2,4,16,128]{5,4,3,2,1,0:T(8,128)S(1)}, f32[2,3,2,4,16,128]{5,4,3,2,1,0:T(8,128)S(1)}, u32[]{:S(2)}, u32[]{:S(2)}) %collective-permute-start.13) | collective-permute-done | bytes 393248 | tf_op jit(solution)/shard_map/ppermute | solution.py:436
  74.9 1.3 %collective-permute-done.12.refs_6_.refs_7_.refs_9_.refs_10_ = f32[2,3,2,4,16,128]{5,4,3,2,1,0:T(8,128)S(1)} collective-permute-done((f32[2,3,2,4,16,128]{5,4,3,2,1,0:T(8,128)S(1)}, f32[2,3,2,4,16,128]{5,4,3,2,1,0:T(8,128)S(1)}, u32[]{:S(2)}, u32[]{:S(2)}) %collective-permute-start.12) | collective-permute-done | bytes 393248 | tf_op jit(solution)/shard_map/ppermute | solution.py:436
  76.8 1.6 %collective-permute-start.16 = (f32[2,3,2,4,16,128]{5,4,3,2,1,0:T(8,128)S(1)}, f32[2,3,2,4,16,128]{5,4,3,2,1,0:T(8,128)S(1)}, u32[]{:S(2)}, u32[]{:S(2)}) collective-permute-start(f32[2,3,2,4,16,128]{5,4,3,2,1,0:T(8,128)S(1)} %collective-permute-done.13.refs_3_.refs_4_.refs_0_.refs_1_), channel_id=1, source_target_pairs={{4,0},{8,4},{12,8},{14,12},{10,14},{6,10},{2,6},{0,2},{5,1},{9,5},... | collective-permute-start | bytes 1179656 | tf_op jit(solution)/shard_map/ppermute | solution.py:436
  78.5 8.7 %shard_map.70.refs_12_ = f32[36,32,4096]{2,1,0:T(8,128)} custom-call(s32[3]{0:T(128)S(1)} %add_add_fusion.1.place, s32[216]{0:T(256)S(1)} %reshape.9.shifts, f32[1]{0:T(128)} %bitcast.5.floor, f32[2,3,2,4,16,128]{5,4,3,2,1,0:T(8,128)S(1)} %collective-permute-done.9.refs_0_.refs_1_, ...), custom_call_target="tpu_custom_call", output_to_operand_aliasing={{}: (15, {})} | custom-call | flops 18874368 | bytes 28311552 | tf_op jit(solution)/shard_map/pallas_call | solution.py:364
  88.8 1.6 %collective-permute-start.19 = (f32[1,3,2,4,16,128]{5,4,3,2,1,0:T(8,128)S(1)}, f32[1,3,2,4,16,128]{5,4,3,2,1,0:T(8,128)S(1)}, u32[]{:S(2)}, u32[]{:S(2)}) collective-permute-start(f32[1,3,2,4,16,128]{5,4,3,2,1,0:T(8,128)S(1)} %slice.42), channel_id=1, source_target_pairs={{0,4},{4,8},{8,12},{12,14},{14,10},{10,6},{6,2},{2,0},{1,5},{5,9},... | collective-permute-start | bytes 589832 | tf_op jit(solution)/shard_map/ppermute | solution.py:442
  91.0 8.7 %shard_map.71.refs_12_ = f32[36,32,4096]{2,1,0:T(8,128)} custom-call(s32[3]{0:T(128)S(1)} %add_add_fusion.2.place, s32[216]{0:T(256)S(1)} %reshape.9.shifts, f32[1]{0:T(128)} %bitcast.5.floor, f32[2,3,2,4,16,128]{5,4,3,2,1,0:T(8,128)S(1)} %collective-permute-done.13.refs_3_.refs_4_.refs_0_.refs_1_, ...), custom_call_target="tpu_custom_call", output_to_operand_aliasing={{}: (15, {})} | custom-call | flops 18874368 | bytes 28311552 | tf_op jit(solution)/shard_map/pallas_call | solution.py:364
  99.9 1.3 %collective-permute-done.21.refs_5_.refs_8_ = f32[1,3,2,4,16,128]{5,4,3,2,1,0:T(8,128)S(1)} collective-permute-done((f32[1,3,2,4,16,128]{5,4,3,2,1,0:T(8,128)S(1)}, f32[1,3,2,4,16,128]{5,4,3,2,1,0:T(8,128)S(1)}, u32[]{:S(2)}, u32[]{:S(2)}) %collective-permute-start.21) | collective-permute-done | bytes 196640 | tf_op jit(solution)/shard_map/ppermute | solution.py:444
  101.2 8.7 %shard_map.72 = f32[36,32,4096]{2,1,0:T(8,128)} custom-call(s32[3]{0:T(128)S(1)} %add_add_fusion.place, s32[216]{0:T(256)S(1)} %reshape.9.shifts, f32[1]{0:T(128)} %bitcast.5.floor, f32[2,3,2,4,16,128]{5,4,3,2,1,0:T(8,128)S(1)} %collective-permute-done.16.refs_3_.refs_4_.refs_0_.refs_1_, ...), custom_call_target="tpu_custom_call", output_to_operand_aliasing={{}: (15, {})} | custom-call | flops 18874368 | bytes 28311552 | tf_op jit(solution)/shard_map/pallas_call | solution.py:364
  (70 shorter events, 16.3 us)
Async XLA Ops:
  0.0 55.0 %copy-start.5 = (s32[36,3,2]{0,2,1:T(2,128)S(1)}, s32[36,3,2]{0,2,1:T(2,128)}, u32[]{:S(2)}) copy-start(s32[36,3,2]{0,2,1:T(2,128)} %param.9) | copy-start | bytes 2596
  3.8 9.6 %collective-permute-start = (f32[2,136,128]{2,1,0:T(8,128)}, f32[2,136,128]{2,1,0:T(8,128)S(1)}, u32[]{:S(2)}, u32[]{:S(2)}) collective-permute-start(f32[2,136,128]{2,1,0:T(8,128)} %get-tuple-element.33), channel_id=1, source_target_pairs={{0,2},{2,0},{4,6},{6,4},{8,10},{10,8},{12,14},{14,12},{1,3},{3,1},... | collective-permute-start | bytes 417800 | tf_op jit(solution)/shard_map/ppermute | solution.py:407
  6.8 9.7 %collective-permute-start.1 = (f32[2,136,128]{2,1,0:T(8,128)}, f32[2,136,128]{2,1,0:T(8,128)S(1)}, u32[]{:S(2)}, u32[]{:S(2)}) collective-permute-start(f32[2,136,128]{2,1,0:T(8,128)} %get-tuple-element.34), channel_id=1, source_target_pairs={{0,14},{2,12},{4,10},{6,8},{8,6},{10,4},{12,2},{14,0},{1,15},{3,13... | collective-permute-start | bytes 417800 | tf_op jit(solution)/shard_map/ppermute | solution.py:407
  10.3 19.1 %collective-permute-start.2 = (f32[2,136,128]{2,1,0:T(8,128)}, f32[2,136,128]{2,1,0:T(8,128)S(1)}, u32[]{:S(2)}, u32[]{:S(2)}) collective-permute-start(f32[2,136,128]{2,1,0:T(8,128)} %get-tuple-element.40), channel_id=1, source_target_pairs={{0,4},{2,6},{4,0},{6,2},{8,12},{10,14},{12,8},{14,10},{1,5},{3,7},... | collective-permute-start | bytes 417800 | tf_op jit(solution)/shard_map/ppermute | solution.py:407
  10.3 19.1 %collective-permute-start.3 = (f32[2,136,128]{2,1,0:T(8,128)}, f32[2,136,128]{2,1,0:T(8,128)S(1)}, u32[]{:S(2)}, u32[]{:S(2)}) collective-permute-start(f32[2,136,128]{2,1,0:T(8,128)} %get-tuple-element.41), channel_id=1, source_target_pairs={{0,6},{2,4},{4,2},{6,0},{8,14},{10,12},{12,10},{14,8},{1,7},{3,5},... | collective-permute-start | bytes 417800 | tf_op jit(solution)/shard_map/ppermute | solution.py:407
  13.3 16.7 %collective-permute-start.4 = (f32[2,136,128]{2,1,0:T(8,128)}, f32[2,136,128]{2,1,0:T(8,128)S(1)}, u32[]{:S(2)}, u32[]{:S(2)}) collective-permute-start(f32[2,136,128]{2,1,0:T(8,128)} %get-tuple-element.42), channel_id=1, source_target_pairs={{0,8},{2,10},{4,12},{6,14},{8,0},{10,2},{12,4},{14,6},{1,9},{3,11}... | collective-permute-start | bytes 417800 | tf_op jit(solution)/shard_map/ppermute | solution.py:407
  13.3 19.6 %collective-permute-start.5 = (f32[2,136,128]{2,1,0:T(8,128)}, f32[2,136,128]{2,1,0:T(8,128)S(1)}, u32[]{:S(2)}, u32[]{:S(2)}) collective-permute-start(f32[2,136,128]{2,1,0:T(8,128)} %get-tuple-element.43), channel_id=1, source_target_pairs={{0,10},{2,8},{4,14},{6,12},{8,2},{10,0},{12,6},{14,4},{1,11},{3,9}... | collective-permute-start | bytes 417800 | tf_op jit(solution)/shard_map/ppermute | solution.py:407
  16.5 16.4 %collective-permute-start.6 = (f32[2,136,128]{2,1,0:T(8,128)}, f32[2,136,128]{2,1,0:T(8,128)S(1)}, u32[]{:S(2)}, u32[]{:S(2)}) collective-permute-start(f32[2,136,128]{2,1,0:T(8,128)} %get-tuple-element.44), channel_id=1, source_target_pairs={{0,12},{2,14},{4,8},{6,10},{8,4},{10,6},{12,0},{14,2},{1,13},{3,15... | collective-permute-start | bytes 417800 | tf_op jit(solution)/shard_map/ppermute | solution.py:407
  36.2 1.5 %collective-permute-start.7 = (f32[3,2,5,16,128]{4,3,2,1,0:T(8,128)S(1)}, f32[3,2,5,16,128]{4,3,2,1,0:T(8,128)S(1)}, u32[]{:S(2)}, u32[]{:S(2)}) collective-permute-start(f32[3,2,5,16,128]{4,3,2,1,0:T(8,128)S(1)} %get-tuple-element.47), channel_id=1, source_target_pairs={{0,1},{1,0},{2,3},{3,2},{4,5},{5,4},{6,7},{7,6},{8,9},{9,8},{10,11... | collective-permute-start | bytes 737288 | tf_op jit(solution)/shard_map/ppermute | solution.py:413
  48.2 17.5 %copy-start.1 = (f32[2,3,2,4,16,128]{5,4,3,2,1,0:T(8,128)S(1)}, f32[2,3,2,4,16,128]{5,4,3,2,1,0:T(8,128)}, u32[]{:S(2)}) copy-start(f32[2,3,2,4,16,128]{5,4,3,2,1,0:T(8,128)} %shard_map.67.refs_0_.refs_1_.refs_3_.refs_4_) | copy-start | bytes 1179652
  49.2 5.6 %collective-permute-start.10 = (f32[2,3,2,1,16,128]{5,4,3,2,1,0:T(8,128)S(1)}, f32[2,3,2,1,16,128]{5,4,3,2,1,0:T(8,128)S(1)}, u32[]{:S(2)}, u32[]{:S(2)}) collective-permute-start(f32[2,3,2,1,16,128]{5,4,3,2,1,0:T(8,128)S(1)} %slice.46), channel_id=1, source_target_pairs={{4,0},{8,4},{12,8},{14,12},{10,14},{6,10},{2,6},{0,2},{5,1},{9,5},... | collective-permute-start | bytes 294920 | tf_op jit(solution)/shard_map/ppermute | solution.py:426
  50.3 12.7 %collective-permute-start.9 = (f32[2,3,2,4,16,128]{5,4,3,2,1,0:T(8,128)}, f32[2,3,2,4,16,128]{5,4,3,2,1,0:T(8,128)S(1)}, u32[]{:S(2)}, u32[]{:S(2)}) collective-permute-start(f32[2,3,2,4,16,128]{5,4,3,2,1,0:T(8,128)} %shard_map.67.refs_0_.refs_1_.refs_3_.refs_4_), channel_id=1, source_target_pairs={{4,0},{8,4},{12,8},{14,12},{10,14},{6,10},{2,6},{0,2},{5,1},{9,5},... | collective-permute-start | bytes 1179656 | tf_op jit(solution)/shard_map/ppermute | solution.py:427
  52.4 10.8 %collective-permute-start.8 = (f32[2,3,2,4,16,128]{5,4,3,2,1,0:T(8,128)}, f32[2,3,2,4,16,128]{5,4,3,2,1,0:T(8,128)S(1)}, u32[]{:S(2)}, u32[]{:S(2)}) collective-permute-start(f32[2,3,2,4,16,128]{5,4,3,2,1,0:T(8,128)} %shard_map.67.refs_0_.refs_1_.refs_3_.refs_4_), channel_id=1, source_target_pairs={{0,4},{4,8},{8,12},{12,14},{14,10},{10,6},{6,2},{2,0},{1,5},{5,9},... | collective-permute-start | bytes 1179656 | tf_op jit(solution)/shard_map/ppermute | solution.py:427
  54.9 1.7 %collective-permute-start.11 = (f32[1,3,2,5,16,128]{5,4,3,2,1,0:T(8,128)S(1)}, f32[1,3,2,5,16,128]{5,4,3,2,1,0:T(8,128)S(1)}, u32[]{:S(2)}, u32[]{:S(2)}) collective-permute-start(f32[1,3,2,5,16,128]{5,4,3,2,1,0:T(8,128)S(1)} %pad_maximum_fusion.3), channel_id=1, source_target_pairs={{0,1},{1,0},{2,3},{3,2},{4,5},{5,4},{6,7},{7,6},{8,9},{9,8},{10,11... | collective-permute-start | bytes 737288 | tf_op jit(solution)/shard_map/ppermute | solution.py:428
  63.3 2.5 %collective-permute-start.14 = (f32[2,3,2,4,16,128]{5,4,3,2,1,0:T(8,128)S(1)}, f32[2,3,2,4,16,128]{5,4,3,2,1,0:T(8,128)S(1)}, u32[]{:S(2)}, u32[]{:S(2)}) collective-permute-start(f32[2,3,2,4,16,128]{5,4,3,2,1,0:T(8,128)S(1)} %pad_maximum_fusion), channel_id=1, source_target_pairs={{0,1},{1,0},{2,3},{3,2},{4,5},{5,4},{6,7},{7,6},{8,9},{9,8},{10,11... | collective-permute-start | bytes 1179656 | tf_op jit(solution)/shard_map/ppermute | solution.py:438
  63.7 11.2 %collective-permute-start.13 = (f32[2,3,2,4,16,128]{5,4,3,2,1,0:T(8,128)S(1)}, f32[2,3,2,4,16,128]{5,4,3,2,1,0:T(8,128)S(1)}, u32[]{:S(2)}, u32[]{:S(2)}) collective-permute-start(f32[2,3,2,4,16,128]{5,4,3,2,1,0:T(8,128)S(1)} %collective-permute-done.9.refs_0_.refs_1_), channel_id=1, source_target_pairs={{4,0},{8,4},{12,8},{14,12},{10,14},{6,10},{2,6},{0,2},{5,1},{9,5},... | collective-permute-start | bytes 1179656 | tf_op jit(solution)/shard_map/ppermute | solution.py:436
  65.0 11.2 %collective-permute-start.12 = (f32[2,3,2,4,16,128]{5,4,3,2,1,0:T(8,128)S(1)}, f32[2,3,2,4,16,128]{5,4,3,2,1,0:T(8,128)S(1)}, u32[]{:S(2)}, u32[]{:S(2)}) collective-permute-start(f32[2,3,2,4,16,128]{5,4,3,2,1,0:T(8,128)S(1)} %collective-permute-done.8.refs_0_.refs_1_.refs_9_.refs_10_), channel_id=1, source_target_pairs={{0,4},{4,8},{8,12},{12,14},{14,10},{10,6},{6,2},{2,0},{1,5},{5,9},... | collective-permute-start | bytes 1179656 | tf_op jit(solution)/shard_map/ppermute | solution.py:436
  76.3 2.2 %collective-permute-start.17 = (f32[2,3,2,4,16,128]{5,4,3,2,1,0:T(8,128)S(1)}, f32[2,3,2,4,16,128]{5,4,3,2,1,0:T(8,128)S(1)}, u32[]{:S(2)}, u32[]{:S(2)}) collective-permute-start(f32[2,3,2,4,16,128]{5,4,3,2,1,0:T(8,128)S(1)} %pad_maximum_fusion.1), channel_id=1, source_target_pairs={{0,1},{1,0},{2,3},{3,2},{4,5},{5,4},{6,7},{7,6},{8,9},{9,8},{10,11... | collective-permute-start | bytes 1179656 | tf_op jit(solution)/shard_map/ppermute | solution.py:438
  76.4 11.5 %collective-permute-start.15 = (f32[2,3,2,4,16,128]{5,4,3,2,1,0:T(8,128)S(1)}, f32[2,3,2,4,16,128]{5,4,3,2,1,0:T(8,128)S(1)}, u32[]{:S(2)}, u32[]{:S(2)}) collective-permute-start(f32[2,3,2,4,16,128]{5,4,3,2,1,0:T(8,128)S(1)} %collective-permute-done.12.refs_6_.refs_7_.refs_9_.refs_10_), channel_id=1, source_target_pairs={{0,4},{4,8},{8,12},{12,14},{14,10},{10,6},{6,2},{2,0},{1,5},{5,9},... | collective-permute-start | bytes 1179656 | tf_op jit(solution)/shard_map/ppermute | solution.py:436
  76.8 11.2 %collective-permute-start.16 = (f32[2,3,2,4,16,128]{5,4,3,2,1,0:T(8,128)S(1)}, f32[2,3,2,4,16,128]{5,4,3,2,1,0:T(8,128)S(1)}, u32[]{:S(2)}, u32[]{:S(2)}) collective-permute-start(f32[2,3,2,4,16,128]{5,4,3,2,1,0:T(8,128)S(1)} %collective-permute-done.13.refs_3_.refs_4_.refs_0_.refs_1_), channel_id=1, source_target_pairs={{4,0},{8,4},{12,8},{14,12},{10,14},{6,10},{2,6},{0,2},{5,1},{9,5},... | collective-permute-start | bytes 1179656 | tf_op jit(solution)/shard_map/ppermute | solution.py:436
  88.8 2.2 %collective-permute-start.18 = (f32[2,3,2,4,16,128]{5,4,3,2,1,0:T(8,128)S(1)}, f32[2,3,2,4,16,128]{5,4,3,2,1,0:T(8,128)S(1)}, u32[]{:S(2)}, u32[]{:S(2)}) collective-permute-start(f32[2,3,2,4,16,128]{5,4,3,2,1,0:T(8,128)S(1)} %pad_maximum_fusion.2), channel_id=1, source_target_pairs={{0,1},{1,0},{2,3},{3,2},{4,5},{5,4},{6,7},{7,6},{8,9},{9,8},{10,11... | collective-permute-start | bytes 1179656 | tf_op jit(solution)/shard_map/ppermute | solution.py:438
  88.8 10.9 %collective-permute-start.19 = (f32[1,3,2,4,16,128]{5,4,3,2,1,0:T(8,128)S(1)}, f32[1,3,2,4,16,128]{5,4,3,2,1,0:T(8,128)S(1)}, u32[]{:S(2)}, u32[]{:S(2)}) collective-permute-start(f32[1,3,2,4,16,128]{5,4,3,2,1,0:T(8,128)S(1)} %slice.42), channel_id=1, source_target_pairs={{0,4},{4,8},{8,12},{12,14},{14,10},{10,6},{6,2},{2,0},{1,5},{5,9},... | collective-permute-start | bytes 589832 | tf_op jit(solution)/shard_map/ppermute | solution.py:442
  90.5 9.3 %collective-permute-start.20 = (f32[1,3,2,4,16,128]{5,4,3,2,1,0:T(8,128)}, f32[1,3,2,4,16,128]{5,4,3,2,1,0:T(8,128)S(1)}, u32[]{:S(2)}, u32[]{:S(2)}) collective-permute-start(f32[1,3,2,4,16,128]{5,4,3,2,1,0:T(8,128)} %get-tuple-element.61), channel_id=1, source_target_pairs={{4,0},{8,4},{12,8},{14,12},{10,14},{6,10},{2,6},{0,2},{5,1},{9,5},... | collective-permute-start | bytes 589832 | tf_op jit(solution)/shard_map/ppermute | solution.py:442
  99.7 1.4 %collective-permute-start.21 = (f32[1,3,2,4,16,128]{5,4,3,2,1,0:T(8,128)S(1)}, f32[1,3,2,4,16,128]{5,4,3,2,1,0:T(8,128)S(1)}, u32[]{:S(2)}, u32[]{:S(2)}) collective-permute-start(f32[1,3,2,4,16,128]{5,4,3,2,1,0:T(8,128)S(1)} %collective-permute-done.19.refs_3_.refs_6_), channel_id=1, source_target_pairs={{0,1},{1,0},{2,3},{3,2},{4,5},{5,4},{6,7},{7,6},{8,9},{9,8},{10,11... | collective-permute-start | bytes 589832 | tf_op jit(solution)/shard_map/ppermute | solution.py:444
  (5 other events, 4.1 us)

commit v7 on v5

--- a/solution.py
+++ b/solution.py
@@ -52,32 +52,20 @@
     )(spread_kernel.reshape(-1), spread_kernel)
 
 
-def cut_kernel(starts, exposure, noise_var, *refs):
-    chunk_refs, (held, arrived) = refs[:-2], refs[-2:]
-    _, height, columns = held.shape
+def cut_kernel(starts, exposure, noise_var, *chunk_refs):
+    height, columns = exposure.shape
     tiles = columns // len(chunk_refs) // LANES
-    copies = []
-    for kind, source in enumerate((exposure, noise_var)):
-        for top in range(0, height, 8):
-            copies.append(
-                pltpu.make_async_copy(
-                    source.at[pl.ds(top, 8)], held.at[kind, pl.ds(top, 8)], arrived.at[kind, top // 8]
-                )
-            )
-            copies[-1].start()
-    for copy in copies:
-        copy.wait()
     lane = lax.broadcasted_iota(jnp.int32, (8, LANES), 1)
     for index, ref in enumerate(chunk_refs):
         start = starts[index]
         ahead = jnp.where(start == 0, columns, start) - LANES
-        for kind in range(2):
+        for kind, held in enumerate((exposure, noise_var)):
             for tile in range(tiles):
                 at = pl.multiple_of(start + tile * LANES, LANES)
-                ref[kind, tile * height : (tile + 1) * height] = held[kind, :, pl.ds(at, LANES)]
+                ref[kind, tile * height : (tile + 1) * height] = held[:, pl.ds(at, LANES)]
             halo = jnp.zeros((8, LANES), jnp.float32)
             for group in range(LANES // HALO):
-                rows = held[kind, 8 * group : 8 * group + 8, pl.ds(pl.multiple_of(ahead, LANES), LANES)]
+                rows = held[8 * group : 8 * group + 8, pl.ds(pl.multiple_of(ahead, LANES), LANES)]
                 moved = pltpu.roll(rows, (group + 1) * HALO % LANES, 1)
                 halo = jnp.where(lane // HALO == group, moved, halo)
             ref[kind, tiles * height :] = halo
@@ -88,10 +76,9 @@
     rows = columns // blocks // LANES * height + height * HALO // LANES
     return pl.pallas_call(
         cut_kernel,
-        in_specs=[pl.BlockSpec(memory_space=pltpu.SMEM)] + [pl.BlockSpec(memory_space=pltpu.HBM)] * 2,
+        in_specs=[pl.BlockSpec(memory_space=pltpu.SMEM)] + [pl.BlockSpec(memory_space=pltpu.VMEM)] * 2,
         out_specs=[pl.BlockSpec(memory_space=pltpu.VMEM)] * blocks,
         out_shape=[jax.ShapeDtypeStruct((2, rows, LANES), jnp.float32)] * blocks,
-        scratch_shapes=[pltpu.VMEM((2, height, columns), jnp.float32), pltpu.SemaphoreType.DMA((2, height // 8))],
         compiler_params=pltpu.CompilerParams(vmem_limit_bytes=VMEM),
         cost_estimate=pl.CostEstimate(flops=0, bytes_accessed=16 * height * columns, transcendentals=0),
     )(starts, exposure, noise_var)
@@ -235,136 +222,144 @@
     )(place, own, border, bands)
 
 
-def stack_kernel(place, shifts, floor, *refs, group, parts, blocks):
-    sources, out_ref = refs[: 6 * parts], refs[-6]
-    raw, whole, packed, near_packed, scale = refs[-5:]
-    part, base = pl.program_id(0), pl.program_id(1) * group
-    epochs, count, reach = whole.shape[:3]
-    tiles = count - 1
-    lower = place[parts]
-    lane = lax.broadcasted_iota(jnp.int32, (1, LANES), 1)
+def stack_kernel(place, shifts, floor, *refs, segments, sources, total, together):
+    operands, out_ref = refs[:sources], refs[-6]
+    raw, whole, lows, packed, scale = refs[-5:]
+    step = pl.program_id(0)
+    epochs, slots, reach = whole.shape[:3]
+    velocities, height = out_ref.shape[:2]
+    fold = height // 8
+    steps = sum(len(held) - 1 for held in segments)
+    lower = place[steps]
     at = [pl.multiple_of(row, MAXS) for row in (32 - 16 * lower, 16 + 16 * lower, 48 - 48 * lower)]
     blank = pl.multiple_of(48 * lower, MAXS)
     most_psi = ((1 << 23) - 1) // epochs
-    most_high = 255 // epochs
-    most_phi = most_high * 64 + 63
-
-    for index in range(parts):
-
-        @pl.when(jnp.logical_and(part == index, pl.program_id(1) == 0))
-        def _():
-            block = place[index]
-            keep_first = jnp.where(jnp.logical_and(block == 0, lane < MAXS), 0.0, 1.0) > 0.5
-            keep_last = jnp.where(jnp.logical_and(block == blocks - 1, lane >= MAXS), 0.0, 1.0) > 0.5
+    most_phi = 255 // epochs * 64 + 63
+    lane = lax.broadcasted_iota(jnp.int32, (8, LANES), 1)
+
+    def assemble(first, held):
+        tops = [jnp.zeros((MAXS, LANES), jnp.float32) for _ in range(2)]
+        for slot, pieces in enumerate(held):
             for epoch in range(epochs):
                 for kind in range(2):
-                    for tile in range(count):
-                        raw[epoch, kind, tile, pl.ds(blank, MAXS)] = jnp.zeros((MAXS, LANES), jnp.float32)
-            tops = [jnp.zeros((MAXS, LANES), jnp.float32) for _ in range(2)]
-            for piece in range(3):
-                own, nearby = sources[6 * index + piece], sources[6 * index + 3 + piece]
-                rows = pl.ds(at[piece], MAXS)
-                for epoch in range(epochs):
-                    for kind in range(2):
-                        for tile in range(count):
-                            if tile == tiles:
-                                value = jnp.where(keep_last, nearby[0, epoch, kind, 0], 0.0)
-                            elif tile == 0:
-                                value = jnp.where(keep_first, own[0, epoch, kind, 0], 0.0)
-                            else:
-                                value = own[0, epoch, kind, tile]
-                            tops[kind] = jnp.maximum(tops[kind], jnp.abs(value))
-                            raw[epoch, kind, tile, rows] = value
-            tops = [jnp.full((8, LANES), jnp.maximum(jnp.max(top), 1e-30), jnp.float32) for top in tops]
-            per_psi, per_phi = most_psi / tops[0], most_phi / tops[1]
-            scale[0] = floor[0] * per_phi
-            scale[1] = jnp.sqrt(per_phi) / per_psi
-
-            def quantize(index, _):
-                rows = pl.ds(pl.multiple_of(index * 8, 8), 8)
-                for epoch in range(epochs):
-                    lows = []
-                    for tile in range(count):
-                        psi = jnp.floor(raw[epoch, 0, tile, rows] * per_psi + 0.5).astype(jnp.int32)
-                        phi = jnp.floor(jnp.maximum(raw[epoch, 1, tile, rows], 0.0) * per_phi + 0.5).astype(jnp.int32)
-                        psi = jnp.clip(psi, -most_psi, most_psi)
-                        phi = jnp.minimum(phi, most_phi)
-                        whole[epoch, tile, rows] = psi * 256 + (phi >> 6)
-                        lows.append(phi & 63)
-                    here, nearby = lows[0], lows[1]
-                    for tile in range(1, tiles):
-                        here = here + (lows[tile] << (8 * tile))
-                        nearby = nearby + (lows[tile + 1] << (8 * tile))
-                    packed[epoch, rows] = here
-                    near_packed[epoch, rows] = nearby
-                return 0
-
-            lax.fori_loop(0, reach // 8, quantize, 0, unroll=4)
-
-    height = out_ref.shape[1]
-    across = lax.broadcasted_iota(jnp.int32, (8, LANES), 1)
+                    raw[epoch, kind, slot, pl.ds(blank, MAXS)] = jnp.zeros((MAXS, LANES), jnp.float32)
+                    for start, (source, index, tile) in zip(at, pieces):
+                        value = operands[source][index, epoch, kind, tile]
+                        tops[kind] = jnp.maximum(tops[kind], jnp.abs(value))
+                        raw[epoch, kind, slot, pl.ds(start, MAXS)] = value
+        tops = [jnp.full((8, LANES), jnp.maximum(jnp.max(top), 1e-30), jnp.float32) for top in tops]
+        per_psi, per_phi = most_psi / tops[0], most_phi / tops[1]
+        scale[0] = floor[0] * per_phi
+        scale[1] = jnp.sqrt(per_phi) / per_psi
+
+        def quantize(index, _):
+            rows = pl.ds(pl.multiple_of(index * 8, 8), 8)
+            for epoch in range(epochs):
+                for slot in range(len(held)):
+                    psi = jnp.floor(raw[epoch, 0, slot, rows] * per_psi + 0.5).astype(jnp.int32)
+                    phi = jnp.floor(jnp.maximum(raw[epoch, 1, slot, rows], 0.0) * per_phi + 0.5).astype(jnp.int32)
+                    psi = jnp.clip(psi, -most_psi, most_psi)
+                    phi = jnp.minimum(phi, most_phi)
+                    whole[epoch, slot, rows] = psi * 256 + (phi >> 6)
+                    lows[epoch, slot, rows] = phi & 63
+            return 0
+
+        lax.fori_loop(0, reach // 8, quantize, 0, unroll=4)
+        for epoch in range(epochs):
+            for slot in range(len(held)):
+                for top in range(0, reach - 8 * (fold - 1), 8):
+                    word = lows[epoch, slot, top : top + 8]
+                    for part in range(1, fold):
+                        word = word + (lows[epoch, slot, top + 8 * part : top + 8 * part + 8] << (8 * part))
+                    packed[epoch, slot, top : top + 8] = word
+        for slot in range(len(held)):
+            number = place[first + slot] if slot < len(held) - 1 else (place[first + slot - 1] + 1) % total
+            for spot, keep in ((slots - 2, lane >= MAXS), (slots - 1, lane < MAXS)):
+
+                @pl.when(number == 0)
+                def _():
+                    for epoch in range(epochs):
+                        for ref in (whole, packed):
+                            for top in range(0, ref.shape[2], 8):
+                                rows = slice(top, top + 8)
+                                ref[epoch, spot, rows] = jnp.where(keep, ref[epoch, slot, rows], 0)
+
+    first, begin = 0, 0
+    for held in segments:
+        pl.when(step == first)(functools.partial(assemble, first, held))
+        begin = jnp.where(step >= first, first, begin)
+        first += len(held) - 1
+
+    number = place[step]
+    left = jnp.where(number == 0, slots - 2, step - begin)
+    right = jnp.where(number == total - 1, slots - 1, step - begin + 1)
     least, unit = scale[0], scale[1]
 
-    def one_velocity(local_index, _):
-        start = (base + local_index) * epochs * 2
-        rows = [shifts[start + 2 * epoch] + MAXS for epoch in range(epochs)]
-        cols = [shifts[start + 2 * epoch + 1] + MAXS for epoch in range(epochs)]
-        beyond = [across < col for col in cols]
-        turn = [jnp.where(col == 0, 0, LANES - col) for col in cols]
-        for top in range(0, height, 8):
-            totals, low_total = [None] * tiles, None
-            for epoch in range(epochs):
-                here = pl.ds(rows[epoch] + top, 8)
-                loaded = [whole[epoch, tile, here] for tile in range(count)]
-                for tile in range(tiles):
-                    moved = pltpu.roll(jnp.where(beyond[epoch], loaded[tile + 1], loaded[tile]), turn[epoch], 1)
-                    totals[tile] = moved if epoch == 0 else totals[tile] + moved
-                moved = pltpu.roll(jnp.where(beyond[epoch], near_packed[epoch, here], packed[epoch, here]), turn[epoch], 1)
-                low_total = moved if epoch == 0 else low_total + moved
-            for tile in range(tiles):
-                psi = (totals[tile] >> 8).astype(jnp.float32)
-                phi = (((totals[tile] & 255) << 6) + ((low_total >> (8 * tile)) & 255)).astype(jnp.float32)
-                out_ref[local_index, top : top + 8, tile * LANES : (tile + 1) * LANES] = (
-                    psi * unit * lax.rsqrt(jnp.maximum(phi, least))
-                )
+    def one_velocity(velocity, _):
+        start = velocity * epochs * 2
+        totals, low_total = [None] * fold, None
+        for epoch in range(epochs):
+            row, col = shifts[start + 2 * epoch] + MAXS, shifts[start + 2 * epoch + 1] + MAXS
+            beyond, turn = lane < col, jnp.where(col == 0, 0, LANES - col)
+
+            def moved(ref, top):
+                rows = pl.ds(row + top, 8)
+                return pltpu.roll(jnp.where(beyond, ref[epoch, right, rows], ref[epoch, left, rows]), turn, 1)
+
+            for part in range(fold):
+                word = moved(whole, 8 * part)
+                totals[part] = word if epoch == 0 else totals[part] + word
+            word = moved(packed, 0)
+            low_total = word if epoch == 0 else low_total + word
+        for part in range(fold):
+            psi = (totals[part] >> 8).astype(jnp.float32)
+            phi = (((totals[part] & 255) << 6) + ((low_total >> (8 * part)) & 255)).astype(jnp.float32)
+            out_ref[velocity, 8 * part : 8 * part + 8] = psi * unit * lax.rsqrt(jnp.maximum(phi, least))
         return 0
 
-    lax.fori_loop(0, group, one_velocity, 0, unroll=True)
-
-
-def stack_blocks(place, shifts, floor, sources, out, out_shape, parts, blocks):
-    epochs, kinds, tiles = sources[0][0].shape[1:4]
+    lax.fori_loop(0, velocities, one_velocity, 0, unroll=together)
+
+
+def stack_tiles(numbers, lower, shifts, floor, segments, out, out_shape):
     velocities, height, columns = out_shape.shape
-    group = next(size for size in (18, 12, 9, 8, 6, 4, 3, 2, 1) if velocities % size == 0)
-    width, reach = tiles * LANES, height + 2 * MAXS
-    in_specs, operands = [], []
-    for index, (array, slot, tile) in enumerate(sources):
-        depth = tiles if index % 6 < 3 else 1
-        in_specs.append(
-            pl.BlockSpec(
-                (1, epochs, kinds, depth, MAXS, LANES),
-                functools.partial(lambda slot, tile, *_: (slot, 0, 0, tile, 0, 0), slot, tile),
-            )
-        )
-        operands.append(array)
+    operands, described = [], []
+    for held in segments:
+        tiles = []
+        for pieces, tile in held:
+            spots = []
+            for array, index in pieces:
+                source = next((i for i, other in enumerate(operands) if other is array), len(operands))
+                operands += [array] if source == len(operands) else []
+                spots.append((source, index, tile))
+            tiles.append(spots)
+        described.append(tiles)
+    sources, epochs = len(operands), operands[0].shape[1]
+    in_specs = [pl.BlockSpec(memory_space=pltpu.VMEM)] * sources
     aliases = {}
     if out is not None:
         in_specs.append(pl.BlockSpec(memory_space=pl.ANY))
         operands.append(out)
-        aliases = {3 + len(sources): 0}
-    work = parts * velocities * height * width
+        aliases = {3 + sources: 0}
+    steps, longest, reach = len(numbers), max(len(held) for held in segments), height + 2 * MAXS
+    work = steps * velocities * height * LANES
     return pl.pallas_call(
-        functools.partial(stack_kernel, group=group, parts=parts, blocks=blocks),
+        functools.partial(
+            stack_kernel,
+            segments=described,
+            sources=sources,
+            total=columns // LANES,
+            together=next(size for size in (36, 18, 12, 9, 8, 6, 4, 3, 2, 1) if velocities % size == 0),
+        ),
         grid_spec=pltpu.PrefetchScalarGridSpec(
             num_scalar_prefetch=3,
-            grid=(parts, velocities // group),
+            grid=(steps,),
             in_specs=in_specs,
-            out_specs=pl.BlockSpec((group, height, width), lambda part, chunk, place, *_: (chunk, 0, place[part])),
+            out_specs=pl.BlockSpec((velocities, height, LANES), lambda step, place, *_: (0, 0, place[step])),
             scratch_shapes=[
-                pltpu.VMEM((epochs, kinds, tiles + 1, reach, LANES), jnp.float32),
-                pltpu.VMEM((epochs, tiles + 1, reach, LANES), jnp.int32),
-                pltpu.VMEM((epochs, reach, LANES), jnp.int32),
-                pltpu.VMEM((epochs, reach, LANES), jnp.int32),
+                pltpu.VMEM((epochs, 2, longest, reach, LANES), jnp.float32),
+                pltpu.VMEM((epochs, longest + 2, reach, LANES), jnp.int32),
+                pltpu.VMEM((epochs, longest, reach, LANES), jnp.int32),
+                pltpu.VMEM((epochs, longest + 2, reach - height + 8, LANES), jnp.int32),
                 pltpu.VMEM((2, 8, LANES), jnp.float32),
             ],
         ),
@@ -372,7 +367,7 @@
         input_output_aliases=aliases,
         compiler_params=pltpu.CompilerParams(vmem_limit_bytes=VMEM),
         cost_estimate=pl.CostEstimate(flops=16 * work, bytes_accessed=24 * work, transcendentals=work),
-    )(place, shifts, floor, *operands)
+    )(jnp.stack(numbers + [lower]).astype(jnp.int32), shifts, floor, *operands)
 
 
 def local(images, variance, spread_kernel, shifts, epoch_owner, valid_rows):
@@ -407,35 +402,38 @@
     flat_shifts, floor = shifts.reshape(-1), floor[0, :1]
     out_shape = jax.ShapeDtypeStruct((shifts.shape[0], height, columns), jnp.float32)
 
-    def stack_now(offsets, out):
-        sources = []
-        for offset in offsets:
-            sources += list(have[offset]) + list(front if offset == 0 else have[offset + 1])
-        spots = jnp.stack([(mine + offset) % blocks for offset in offsets] + [lower]).astype(jnp.int32)
-        return stack_blocks(spots, flat_shifts, floor, sources, out, out_shape, len(offsets), blocks)
-
-    tiles = payload.shape[3]
-    front = lax.ppermute(payload[:, :, :, :1], "vel", left)
+    tiles, half = payload.shape[3], blocks // 2
+
+    def stack_now(segments, out):
+        numbers = [
+            (mine + offset) % blocks * tiles + tile for held in segments for offset, tile in held[:-1]
+        ]
+        held = [[(have[offset], tile) for offset, tile in segment] for segment in segments]
+        return stack_tiles(numbers, lower, flat_shifts, floor, held, out, out_shape)
+
+    def block(offset):
+        return [(offset, tile) for tile in range(tiles)]
+
     behind, ahead = lax.ppermute(payload, "vel", right), lax.ppermute(payload, "vel", left)
-    border = lax.ppermute(jnp.concatenate([payload[:1], front[:1]], axis=3), "rows", swap)
-    front = ((front, 0, 0), (front, 1, 0), (border, 0, tiles))
-    have = {0: ((payload, 0, 0), (payload, 1, 0), (border, 0, 0))}
-    out = stack_now([0], None)
-    half = blocks // 2
+    border = lax.ppermute(payload[:1], "rows", swap)
+    have = {0: ((payload, 0), (payload, 1), (border, 0))}
+    out = stack_now([block(0)], None)
     for step in range(1, half + 1):
         if step < half:
             if step > 1:
                 behind, ahead = lax.ppermute(behind, "vel", right), lax.ppermute(ahead, "vel", left)
             behind, ahead, out = lax.optimization_barrier((behind, ahead, out))
             border = lax.ppermute(jnp.concatenate([behind[:1], ahead[:1]]), "rows", swap)
-            have[-step] = ((behind, 0, 0), (behind, 1, 0), (border, 0, 0))
-            have[step] = ((ahead, 0, 0), (ahead, 1, 0), (border, 1, 0))
+            have[-step] = ((behind, 0), (behind, 1), (border, 0))
+            have[step] = ((ahead, 0), (ahead, 1), (border, 1))
+            segments = [block(-step) + [(1 - step, 0)], [(step - 1, tiles - 1)] + block(step)]
         else:
             edge, inner = lax.ppermute(behind[:1], "vel", right), lax.ppermute(ahead[1:], "vel", left)
             edge, inner, out = lax.optimization_barrier((edge, inner, out))
             border = lax.ppermute(edge, "rows", swap)
-            have[step] = have[-step] = ((edge, 0, 0), (inner, 0, 0), (border, 0, 0))
-        out = stack_now([step - 1, -step] if step > 1 else [-step], out)
+            have[step] = ((edge, 0), (inner, 0), (border, 0))
+            segments = [[(step - 1, tiles - 1)] + block(step) + [(1 - step, 0)]]
+        out = stack_now(segments, out)
     return out
 
 

time: 107 us -> 103 us (0.963)
  waiting for transfers between devices: 16.5 us -> 13.6 us
  starting transfers between devices: 24.8 us -> 23.4 us
    ppermute x2, waiting for transfers between devices: 4.5 us -> 2.06 us  [local(): lax.ppermute(ahead, 'vel', left)]
    ppermute x1, waiting for transfers between devices: 0.85 us -> 3.03 us  [local(): lax.ppermute(payload, 'vel', left)]
    ppermute x2 -> x1, waiting for transfers between devices: 2.69 us -> 0.52 us  [local(): border = lax.ppermute(payload[:1], 'rows', swap)]
    pallas_call x5, Pallas kernels: 37.2 us -> 39.1 us  [stack_tiles(): pl.pallas_call(functools.partial(stack_kernel, segments=described, source...]
    ppermute x2 -> x1, starting transfers between devices: 1.53 us -> 0.07 us  [local(): border = lax.ppermute(payload[:1], 'rows', swap)]
    pallas_call x1, Pallas kernels: 2.22 us -> 0.78 us  [cut(): pl.pallas_call(cut_kernel, in_specs=[pl.BlockSpec(memory_space=pltpu.SMEM...]
    ppermute x2, waiting for transfers between devices: 1.47 us -> 0.16 us  [local(): lax.ppermute(behind, 'vel', right)]
  transfers between devices with their start and end apart: 22 -> 21, of which waited for: 12 -> 12; matrix products, arithmetic and copies ran while one was open for 3% -> 3% of each run, Pallas kernels for 31% -> 36%
where the time goes in v7:
time: 103 us; the launch traced here: 102 us
  Pallas kernels  52.9 us (51%)
  starting transfers between devices  23.4 us (23%)
  waiting for transfers between devices  13.6 us (13%)
  local copies, waits for them, and re-layouts  12 us (12%)
    pallas_call x5, Pallas kernels, stack_tiles(): pl.pallas_call(functools.partial(stack_kernel, segments=described, source...  39.1 us
    ppermute x7, starting transfers between devices, local(): lax.ppermute(chunks[step], 'vel', [(i, i ^ step) for i in range(blocks)])  14.7 us
    unnamed x16, local copies, waits for them, and re-layouts  9.33 us
    pallas_call x1, Pallas kernels, correlate(): pl.pallas_call(correlate_kernel, in_specs=[pl.BlockSpec(memory_space=pltp...  7.52 us
    pallas_call x1, Pallas kernels, make_bands(): pl.pallas_call(band_kernel, in_specs=[pl.BlockSpec(memory_space=pltpu.SME...  4.59 us
    ppermute x7, waiting for transfers between devices, local(): lax.ppermute(chunks[step], 'vel', [(i, i ^ step) for i in range(blocks)])  4.22 us
    ppermute x1, waiting for transfers between devices, local(): lax.ppermute(payload, 'vel', left)  3.03 us
    ppermute x2, starting transfers between devices, local(): lax.ppermute(behind, 'vel', right)  2.72 us
  transfers between devices with their start and end apart: 21, of which 12 were waited for; matrix products, arithmetic and copies ran while one was open for 3% of the time, Pallas kernels for 36%

profile of v7, /device:TPU:0, one launch (start us, length us, event | category | flops | bytes accessed | tf_op | source)
XLA Modules:
  0.0 102.4 jit_solution(14383009967761826776)
XLA Ops:
  0.0 1.0 %copy-done = f32[1,32,4096]{2,1,0:T(8,128)S(1)} copy-done((f32[1,32,4096]{2,1,0:T(8,128)S(1)}, f32[1,32,4096]{2,1,0:T(8,128)}, u32[]{:S(2)}) %copy-start) | copy-done | bytes 524312
  1.1 1.0 %copy-done.1 = f32[1,32,4096]{2,1,0:T(8,128)S(1)} copy-done((f32[1,32,4096]{2,1,0:T(8,128)S(1)}, f32[1,32,4096]{2,1,0:T(8,128)}, u32[]{:S(2)}) %copy-start.1) | copy-done | bytes 524312
  2.9 6.1 %collective-permute-start = (f32[2,136,128]{2,1,0:T(8,128)S(1)}, f32[2,136,128]{2,1,0:T(8,128)S(1)}, u32[]{:S(2)}, u32[]{:S(2)}) collective-permute-start(f32[2,136,128]{2,1,0:T(8,128)S(1)} %get-tuple-element.33), channel_id=1, source_target_pairs={{0,14},{2,12},{4,10},{6,8},{8,6},{10,4},{12,2},{14,0},{1,15},{3,13... | collective-permute-start | bytes 417800 | tf_op jit(solution)/shard_map/ppermute | solution.py:394
  9.5 3.0 %collective-permute-start.3 = (f32[2,136,128]{2,1,0:T(8,128)S(1)}, f32[2,136,128]{2,1,0:T(8,128)S(1)}, u32[]{:S(2)}, u32[]{:S(2)}) collective-permute-start(f32[2,136,128]{2,1,0:T(8,128)S(1)} %get-tuple-element.41), channel_id=1, source_target_pairs={{0,6},{2,4},{4,2},{6,0},{8,14},{10,12},{12,10},{14,8},{1,7},{3,5},... | collective-permute-start | bytes 417800 | tf_op jit(solution)/shard_map/ppermute | solution.py:394
  12.5 1.1 %collective-permute-done.refs_7_ = f32[2,136,128]{2,1,0:T(8,128)S(1)} collective-permute-done((f32[2,136,128]{2,1,0:T(8,128)S(1)}, f32[2,136,128]{2,1,0:T(8,128)S(1)}, u32[]{:S(2)}, u32[]{:S(2)}) %collective-permute-start) | collective-permute-done | bytes 139296 | tf_op jit(solution)/shard_map/ppermute | solution.py:394
  13.5 4.8 %collective-permute-start.5 = (f32[2,136,128]{2,1,0:T(8,128)S(1)}, f32[2,136,128]{2,1,0:T(8,128)S(1)}, u32[]{:S(2)}, u32[]{:S(2)}) collective-permute-start(f32[2,136,128]{2,1,0:T(8,128)S(1)} %get-tuple-element.43), channel_id=1, source_target_pairs={{0,10},{2,8},{4,14},{6,12},{8,2},{10,0},{12,6},{14,4},{1,11},{3,9}... | collective-permute-start | bytes 417800 | tf_op jit(solution)/shard_map/ppermute | solution.py:394
  21.1 4.6 %shard_map.65 = (bf16[2,21,256,256]{3,2,1,0:T(8,128)(2,1)S(1)}, f32[8,128]{1,0:T(8,128)S(1)}) custom-call(f32[441]{0:T(512)S(1)} %reshape.10.taps, f32[21,21]{1,0:T(8,128)S(1)} %copy-done.2), custom_call_target="tpu_custom_call" | custom-call | bytes 20971520 | tf_op jit(solution)/shard_map/pallas_call | solution.py:42
  25.7 2.4 %copy-done.4 = bf16[2,21,256,256]{3,2,1,0:T(8,128)(2,1)} copy-done((bf16[2,21,256,256]{3,2,1,0:T(8,128)(2,1)}, bf16[2,21,256,256]{3,2,1,0:T(8,128)(2,1)S(1)}, u32[]{:S(2)}) %copy-start.4) | copy-done | bytes 5505048
  28.9 2.4 %collective-permute-done.5.refs_5_ = f32[2,136,128]{2,1,0:T(8,128)S(1)} collective-permute-done((f32[2,136,128]{2,1,0:T(8,128)S(1)}, f32[2,136,128]{2,1,0:T(8,128)S(1)}, u32[]{:S(2)}, u32[]{:S(2)}) %collective-permute-start.5) | collective-permute-done | bytes 139296 | tf_op jit(solution)/shard_map/ppermute | solution.py:394
  33.0 1.4 %collective-permute-done.7.border = f32[3,2,5,16,128]{4,3,2,1,0:T(8,128)S(1)} collective-permute-done((f32[3,2,5,16,128]{4,3,2,1,0:T(8,128)S(1)}, f32[3,2,5,16,128]{4,3,2,1,0:T(8,128)S(1)}, u32[]{:S(2)}, u32[]{:S(2)}) %collective-permute-start.7) | collective-permute-done | bytes 245792 | tf_op jit(solution)/shard_map/ppermute | solution.py:400
  34.4 2.6 %copy-done.5 = bf16[2,21,256,256]{3,2,1,0:T(8,128)(2,1)S(1)} copy-done((bf16[2,21,256,256]{3,2,1,0:T(8,128)(2,1)S(1)}, bf16[2,21,256,256]{3,2,1,0:T(8,128)(2,1)}, u32[]{:S(2)}) %copy-start.5) | copy-done | bytes 5505048
  37.0 7.5 %shard_map.67.refs_0_.refs_2_ = f32[2,3,2,4,16,128]{5,4,3,2,1,0:T(8,128)S(1)} custom-call(s32[2]{0:T(128)S(1)} %pad_add_fusion.place, f32[3,2,5,32,128]{4,3,2,1,0:T(8,128)S(1)} %get-tuple-element.46.own, f32[3,2,5,16,128]{4,3,2,1,0:T(8,128)S(1)} %collective-permute-done.7.border, bf16[2,21,256,256]{3,2,1,0:T(8,128)(2,1)S(1)} %copy-done.5), custom_call_target="tpu_custom_call" | custom-call | flops 5637144576 | bytes 12582912 | tf_op jit(solution)/shard_map/pallas_call | solution.py:209
  44.5 1.5 %collective-permute-start.9 = (f32[2,3,2,4,16,128]{5,4,3,2,1,0:T(8,128)S(1)}, f32[2,3,2,4,16,128]{5,4,3,2,1,0:T(8,128)S(1)}, u32[]{:S(2)}, u32[]{:S(2)}) collective-permute-start(f32[2,3,2,4,16,128]{5,4,3,2,1,0:T(8,128)S(1)} %shard_map.67.refs_0_.refs_2_), channel_id=1, source_target_pairs={{4,0},{8,4},{12,8},{14,12},{10,14},{6,10},{2,6},{0,2},{5,1},{9,5},... | collective-permute-start | bytes 1179656 | tf_op jit(solution)/shard_map/ppermute | solution.py:417
  48.1 4.8 %shard_map.68.refs_5_ = f32[36,32,4096]{2,1,0:T(8,128)} custom-call(s32[4]{0:T(128)S(1)} %pad_add_fusion.2.place, s32[216]{0:T(256)S(1)} %reshape.9.shifts, f32[1]{0:T(128)} %bitcast.8.floor, f32[2,3,2,4,16,128]{5,4,3,2,1,0:T(8,128)S(1)} %shard_map.67.refs_0_.refs_2_, f32[1,3,2,4,16,128]{5,4,3,2,1,0:T(8,128)S(1)} %collective-permute-done.10.refs_1_.refs_3_), custom_call_target="tpu_custom_call" | custom-call | flops 7077888 | bytes 10616832 | tf_op jit(solution)/shard_map/pallas_call | solution.py:345
  52.9 3.0 %collective-permute-done.9.refs_4_ = f32[2,3,2,4,16,128]{5,4,3,2,1,0:T(8,128)S(1)} collective-permute-done((f32[2,3,2,4,16,128]{5,4,3,2,1,0:T(8,128)S(1)}, f32[2,3,2,4,16,128]{5,4,3,2,1,0:T(8,128)S(1)}, u32[]{:S(2)}, u32[]{:S(2)}) %collective-permute-start.9) | collective-permute-done | bytes 393248 | tf_op jit(solution)/shard_map/ppermute | solution.py:417
  58.0 1.1 %collective-permute-start.12 = (f32[2,3,2,4,16,128]{5,4,3,2,1,0:T(8,128)S(1)}, f32[2,3,2,4,16,128]{5,4,3,2,1,0:T(8,128)S(1)}, u32[]{:S(2)}, u32[]{:S(2)}) collective-permute-start(f32[2,3,2,4,16,128]{5,4,3,2,1,0:T(8,128)S(1)} %collective-permute-done.9.refs_4_), channel_id=1, source_target_pairs={{4,0},{8,4},{12,8},{14,12},{10,14},{6,10},{2,6},{0,2},{5,1},{9,5},... | collective-permute-start | bytes 1179656 | tf_op jit(solution)/shard_map/ppermute | solution.py:424
  59.2 9.3 %shard_map.69.refs_6_ = f32[36,32,4096]{2,1,0:T(8,128)} custom-call(s32[9]{0:T(128)S(1)} %stack.155.place, s32[216]{0:T(256)S(1)} %reshape.9.shifts, f32[1]{0:T(128)} %bitcast.8.floor, f32[2,3,2,4,16,128]{5,4,3,2,1,0:T(8,128)S(1)} %collective-permute-done.8.refs_0_.refs_2_, ...), custom_call_target="tpu_custom_call", output_to_operand_aliasing={{}: (8, {})} | custom-call | flops 18874368 | bytes 28311552 | tf_op jit(solution)/shard_map/pallas_call | solution.py:345
  69.3 1.7 %collective-permute-start.14 = (f32[2,3,2,4,16,128]{5,4,3,2,1,0:T(8,128)S(1)}, f32[2,3,2,4,16,128]{5,4,3,2,1,0:T(8,128)S(1)}, u32[]{:S(2)}, u32[]{:S(2)}) collective-permute-start(f32[2,3,2,4,16,128]{5,4,3,2,1,0:T(8,128)S(1)} %collective-permute-done.11.refs_0_.refs_2_), channel_id=1, source_target_pairs={{0,4},{4,8},{8,12},{12,14},{14,10},{10,6},{6,2},{2,0},{1,5},{5,9},... | collective-permute-start | bytes 1179656 | tf_op jit(solution)/shard_map/ppermute | solution.py:424
  71.5 9.3 %shard_map.70.refs_6_ = f32[36,32,4096]{2,1,0:T(8,128)} custom-call(s32[9]{0:T(128)S(1)} %stack.164.place, s32[216]{0:T(256)S(1)} %reshape.9.shifts, f32[1]{0:T(128)} %bitcast.8.floor, f32[2,3,2,4,16,128]{5,4,3,2,1,0:T(8,128)S(1)} %collective-permute-done.11.refs_0_.refs_2_, ...), custom_call_target="tpu_custom_call", output_to_operand_aliasing={{}: (9, {})} | custom-call | flops 18874368 | bytes 28311552 | tf_op jit(solution)/shard_map/pallas_call | solution.py:345
  80.8 1.4 %collective-permute-done.15.refs_5_.refs_0_ = f32[2,3,2,4,16,128]{5,4,3,2,1,0:T(8,128)S(1)} collective-permute-done((f32[2,3,2,4,16,128]{5,4,3,2,1,0:T(8,128)S(1)}, f32[2,3,2,4,16,128]{5,4,3,2,1,0:T(8,128)S(1)}, u32[]{:S(2)}, u32[]{:S(2)}) %collective-permute-start.15) | collective-permute-done | bytes 393248 | tf_op jit(solution)/shard_map/ppermute | solution.py:424
  83.1 1.6 %collective-permute-start.18 = (f32[1,3,2,4,16,128]{5,4,3,2,1,0:T(8,128)S(1)}, f32[1,3,2,4,16,128]{5,4,3,2,1,0:T(8,128)S(1)}, u32[]{:S(2)}, u32[]{:S(2)}) collective-permute-start(f32[1,3,2,4,16,128]{5,4,3,2,1,0:T(8,128)S(1)} %slice.34), channel_id=1, source_target_pairs={{0,4},{4,8},{8,12},{12,14},{14,10},{10,6},{6,2},{2,0},{1,5},{5,9},... | collective-permute-start | bytes 589832 | tf_op jit(solution)/shard_map/ppermute | solution.py:431
  85.2 9.3 %shard_map.71.refs_6_ = f32[36,32,4096]{2,1,0:T(8,128)} custom-call(s32[9]{0:T(128)S(1)} %stack.173.place, s32[216]{0:T(256)S(1)} %reshape.9.shifts, f32[1]{0:T(128)} %bitcast.8.floor, f32[2,3,2,4,16,128]{5,4,3,2,1,0:T(8,128)S(1)} %collective-permute-done.14.refs_0_.refs_5_, ...), custom_call_target="tpu_custom_call", output_to_operand_aliasing={{}: (9, {})} | custom-call | flops 18874368 | bytes 28311552 | tf_op jit(solution)/shard_map/pallas_call | solution.py:345
  94.6 1.3 %collective-permute-done.20.refs_4_ = f32[1,3,2,4,16,128]{5,4,3,2,1,0:T(8,128)S(1)} collective-permute-done((f32[1,3,2,4,16,128]{5,4,3,2,1,0:T(8,128)S(1)}, f32[1,3,2,4,16,128]{5,4,3,2,1,0:T(8,128)S(1)}, u32[]{:S(2)}, u32[]{:S(2)}) %collective-permute-start.20) | collective-permute-done | bytes 196640 | tf_op jit(solution)/shard_map/ppermute | solution.py:433
  95.9 6.5 %shard_map.72 = f32[36,32,4096]{2,1,0:T(8,128)} custom-call(s32[6]{0:T(128)S(1)} %stack.138.place, s32[216]{0:T(256)S(1)} %reshape.9.shifts, f32[1]{0:T(128)} %bitcast.8.floor, f32[2,3,2,4,16,128]{5,4,3,2,1,0:T(8,128)S(1)} %collective-permute-done.15.refs_5_.refs_0_, ...), custom_call_target="tpu_custom_call", output_to_operand_aliasing={{}: (9, {})} | custom-call | flops 11796480 | bytes 17694720 | tf_op jit(solution)/shard_map/pallas_call | solution.py:345
  (65 shorter events, 13.6 us)
Async XLA Ops:
  0.0 46.7 %copy-start.6 = (s32[36,3,2]{0,2,1:T(2,128)S(1)}, s32[36,3,2]{0,2,1:T(2,128)}, u32[]{:S(2)}) copy-start(s32[36,3,2]{0,2,1:T(2,128)} %param.9) | copy-start | bytes 2596
  2.9 10.6 %collective-permute-start = (f32[2,136,128]{2,1,0:T(8,128)S(1)}, f32[2,136,128]{2,1,0:T(8,128)S(1)}, u32[]{:S(2)}, u32[]{:S(2)}) collective-permute-start(f32[2,136,128]{2,1,0:T(8,128)S(1)} %get-tuple-element.33), channel_id=1, source_target_pairs={{0,14},{2,12},{4,10},{6,8},{8,6},{10,4},{12,2},{14,0},{1,15},{3,13... | collective-permute-start | bytes 417800 | tf_op jit(solution)/shard_map/ppermute | solution.py:394
  9.0 9.3 %collective-permute-start.1 = (f32[2,136,128]{2,1,0:T(8,128)S(1)}, f32[2,136,128]{2,1,0:T(8,128)S(1)}, u32[]{:S(2)}, u32[]{:S(2)}) collective-permute-start(f32[2,136,128]{2,1,0:T(8,128)S(1)} %get-tuple-element.34), channel_id=1, source_target_pairs={{0,2},{2,0},{4,6},{6,4},{8,10},{10,8},{12,14},{14,12},{1,3},{3,1},... | collective-permute-start | bytes 417800 | tf_op jit(solution)/shard_map/ppermute | solution.py:394
  9.5 18.7 %collective-permute-start.2 = (f32[2,136,128]{2,1,0:T(8,128)S(1)}, f32[2,136,128]{2,1,0:T(8,128)S(1)}, u32[]{:S(2)}, u32[]{:S(2)}) collective-permute-start(f32[2,136,128]{2,1,0:T(8,128)S(1)} %get-tuple-element.40), channel_id=1, source_target_pairs={{0,4},{2,6},{4,0},{6,2},{8,12},{10,14},{12,8},{14,10},{1,5},{3,7},... | collective-permute-start | bytes 417800 | tf_op jit(solution)/shard_map/ppermute | solution.py:394
  9.5 18.7 %collective-permute-start.3 = (f32[2,136,128]{2,1,0:T(8,128)S(1)}, f32[2,136,128]{2,1,0:T(8,128)S(1)}, u32[]{:S(2)}, u32[]{:S(2)}) collective-permute-start(f32[2,136,128]{2,1,0:T(8,128)S(1)} %get-tuple-element.41), channel_id=1, source_target_pairs={{0,6},{2,4},{4,2},{6,0},{8,14},{10,12},{12,10},{14,8},{1,7},{3,5},... | collective-permute-start | bytes 417800 | tf_op jit(solution)/shard_map/ppermute | solution.py:394
  12.5 16.5 %collective-permute-start.4 = (f32[2,136,128]{2,1,0:T(8,128)S(1)}, f32[2,136,128]{2,1,0:T(8,128)S(1)}, u32[]{:S(2)}, u32[]{:S(2)}) collective-permute-start(f32[2,136,128]{2,1,0:T(8,128)S(1)} %get-tuple-element.42), channel_id=1, source_target_pairs={{0,8},{2,10},{4,12},{6,14},{8,0},{10,2},{12,4},{14,6},{1,9},{3,11}... | collective-permute-start | bytes 417800 | tf_op jit(solution)/shard_map/ppermute | solution.py:394
  13.5 17.8 %collective-permute-start.5 = (f32[2,136,128]{2,1,0:T(8,128)S(1)}, f32[2,136,128]{2,1,0:T(8,128)S(1)}, u32[]{:S(2)}, u32[]{:S(2)}) collective-permute-start(f32[2,136,128]{2,1,0:T(8,128)S(1)} %get-tuple-element.43), channel_id=1, source_target_pairs={{0,10},{2,8},{4,14},{6,12},{8,2},{10,0},{12,6},{14,4},{1,11},{3,9}... | collective-permute-start | bytes 417800 | tf_op jit(solution)/shard_map/ppermute | solution.py:394
  18.3 13.0 %collective-permute-start.6 = (f32[2,136,128]{2,1,0:T(8,128)S(1)}, f32[2,136,128]{2,1,0:T(8,128)S(1)}, u32[]{:S(2)}, u32[]{:S(2)}) collective-permute-start(f32[2,136,128]{2,1,0:T(8,128)S(1)} %get-tuple-element.44), channel_id=1, source_target_pairs={{0,12},{2,14},{4,8},{6,10},{8,4},{10,6},{12,0},{14,2},{1,13},{3,15... | collective-permute-start | bytes 417800 | tf_op jit(solution)/shard_map/ppermute | solution.py:394
  25.7 2.4 %copy-start.4 = (bf16[2,21,256,256]{3,2,1,0:T(8,128)(2,1)}, bf16[2,21,256,256]{3,2,1,0:T(8,128)(2,1)S(1)}, u32[]{:S(2)}) copy-start(bf16[2,21,256,256]{3,2,1,0:T(8,128)(2,1)S(1)} %get-tuple-element.48.bands_ref) | copy-start | bytes 16515076
  32.8 1.6 %collective-permute-start.7 = (f32[3,2,5,16,128]{4,3,2,1,0:T(8,128)S(1)}, f32[3,2,5,16,128]{4,3,2,1,0:T(8,128)S(1)}, u32[]{:S(2)}, u32[]{:S(2)}) collective-permute-start(f32[3,2,5,16,128]{4,3,2,1,0:T(8,128)S(1)} %get-tuple-element.47), channel_id=1, source_target_pairs={{0,1},{1,0},{2,3},{3,2},{4,5},{5,4},{6,7},{7,6},{8,9},{9,8},{10,11... | collective-permute-start | bytes 737288 | tf_op jit(solution)/shard_map/ppermute | solution.py:400
  34.4 2.6 %copy-start.5 = (bf16[2,21,256,256]{3,2,1,0:T(8,128)(2,1)S(1)}, bf16[2,21,256,256]{3,2,1,0:T(8,128)(2,1)}, u32[]{:S(2)}) copy-start(bf16[2,21,256,256]{3,2,1,0:T(8,128)(2,1)} %copy-done.4) | copy-start | bytes 16515076
  44.5 11.5 %collective-permute-start.9 = (f32[2,3,2,4,16,128]{5,4,3,2,1,0:T(8,128)S(1)}, f32[2,3,2,4,16,128]{5,4,3,2,1,0:T(8,128)S(1)}, u32[]{:S(2)}, u32[]{:S(2)}) collective-permute-start(f32[2,3,2,4,16,128]{5,4,3,2,1,0:T(8,128)S(1)} %shard_map.67.refs_0_.refs_2_), channel_id=1, source_target_pairs={{4,0},{8,4},{12,8},{14,12},{10,14},{6,10},{2,6},{0,2},{5,1},{9,5},... | collective-permute-start | bytes 1179656 | tf_op jit(solution)/shard_map/ppermute | solution.py:417
  46.0 10.9 %collective-permute-start.8 = (f32[2,3,2,4,16,128]{5,4,3,2,1,0:T(8,128)S(1)}, f32[2,3,2,4,16,128]{5,4,3,2,1,0:T(8,128)S(1)}, u32[]{:S(2)}, u32[]{:S(2)}) collective-permute-start(f32[2,3,2,4,16,128]{5,4,3,2,1,0:T(8,128)S(1)} %shard_map.67.refs_0_.refs_2_), channel_id=1, source_target_pairs={{0,4},{4,8},{8,12},{12,14},{14,10},{10,6},{6,2},{2,0},{1,5},{5,9},... | collective-permute-start | bytes 1179656 | tf_op jit(solution)/shard_map/ppermute | solution.py:417
  46.6 1.5 %collective-permute-start.10 = (f32[1,3,2,4,16,128]{5,4,3,2,1,0:T(8,128)S(1)}, f32[1,3,2,4,16,128]{5,4,3,2,1,0:T(8,128)S(1)}, u32[]{:S(2)}, u32[]{:S(2)}) collective-permute-start(f32[1,3,2,4,16,128]{5,4,3,2,1,0:T(8,128)S(1)} %slice.37), channel_id=1, source_target_pairs={{0,1},{1,0},{2,3},{3,2},{4,5},{5,4},{6,7},{7,6},{8,9},{9,8},{10,11... | collective-permute-start | bytes 589832 | tf_op jit(solution)/shard_map/ppermute | solution.py:418
  56.9 2.2 %collective-permute-start.13 = (f32[2,3,2,4,16,128]{5,4,3,2,1,0:T(8,128)S(1)}, f32[2,3,2,4,16,128]{5,4,3,2,1,0:T(8,128)S(1)}, u32[]{:S(2)}, u32[]{:S(2)}) collective-permute-start(f32[2,3,2,4,16,128]{5,4,3,2,1,0:T(8,128)S(1)} %pad_maximum_fusion), channel_id=1, source_target_pairs={{0,1},{1,0},{2,3},{3,2},{4,5},{5,4},{6,7},{7,6},{8,9},{9,8},{10,11... | collective-permute-start | bytes 1179656 | tf_op jit(solution)/shard_map/ppermute | solution.py:426
  57.0 11.5 %collective-permute-start.11 = (f32[2,3,2,4,16,128]{5,4,3,2,1,0:T(8,128)S(1)}, f32[2,3,2,4,16,128]{5,4,3,2,1,0:T(8,128)S(1)}, u32[]{:S(2)}, u32[]{:S(2)}) collective-permute-start(f32[2,3,2,4,16,128]{5,4,3,2,1,0:T(8,128)S(1)} %collective-permute-done.8.refs_0_.refs_2_), channel_id=1, source_target_pairs={{0,4},{4,8},{8,12},{12,14},{14,10},{10,6},{6,2},{2,0},{1,5},{5,9},... | collective-permute-start | bytes 1179656 | tf_op jit(solution)/shard_map/ppermute | solution.py:424
  58.0 11.2 %collective-permute-start.12 = (f32[2,3,2,4,16,128]{5,4,3,2,1,0:T(8,128)S(1)}, f32[2,3,2,4,16,128]{5,4,3,2,1,0:T(8,128)S(1)}, u32[]{:S(2)}, u32[]{:S(2)}) collective-permute-start(f32[2,3,2,4,16,128]{5,4,3,2,1,0:T(8,128)S(1)} %collective-permute-done.9.refs_4_), channel_id=1, source_target_pairs={{4,0},{8,4},{12,8},{14,12},{10,14},{6,10},{2,6},{0,2},{5,1},{9,5},... | collective-permute-start | bytes 1179656 | tf_op jit(solution)/shard_map/ppermute | solution.py:424
  69.2 2.2 %collective-permute-start.16 = (f32[2,3,2,4,16,128]{5,4,3,2,1,0:T(8,128)S(1)}, f32[2,3,2,4,16,128]{5,4,3,2,1,0:T(8,128)S(1)}, u32[]{:S(2)}, u32[]{:S(2)}) collective-permute-start(f32[2,3,2,4,16,128]{5,4,3,2,1,0:T(8,128)S(1)} %pad_maximum_fusion.1), channel_id=1, source_target_pairs={{0,1},{1,0},{2,3},{3,2},{4,5},{5,4},{6,7},{7,6},{8,9},{9,8},{10,11... | collective-permute-start | bytes 1179656 | tf_op jit(solution)/shard_map/ppermute | solution.py:426
  69.3 11.5 %collective-permute-start.14 = (f32[2,3,2,4,16,128]{5,4,3,2,1,0:T(8,128)S(1)}, f32[2,3,2,4,16,128]{5,4,3,2,1,0:T(8,128)S(1)}, u32[]{:S(2)}, u32[]{:S(2)}) collective-permute-start(f32[2,3,2,4,16,128]{5,4,3,2,1,0:T(8,128)S(1)} %collective-permute-done.11.refs_0_.refs_2_), channel_id=1, source_target_pairs={{0,4},{4,8},{8,12},{12,14},{14,10},{10,6},{6,2},{2,0},{1,5},{5,9},... | collective-permute-start | bytes 1179656 | tf_op jit(solution)/shard_map/ppermute | solution.py:424
  71.0 11.2 %collective-permute-start.15 = (f32[2,3,2,4,16,128]{5,4,3,2,1,0:T(8,128)S(1)}, f32[2,3,2,4,16,128]{5,4,3,2,1,0:T(8,128)S(1)}, u32[]{:S(2)}, u32[]{:S(2)}) collective-permute-start(f32[2,3,2,4,16,128]{5,4,3,2,1,0:T(8,128)S(1)} %collective-permute-done.12.refs_5_.refs_4_), channel_id=1, source_target_pairs={{4,0},{8,4},{12,8},{14,12},{10,14},{6,10},{2,6},{0,2},{5,1},{9,5},... | collective-permute-start | bytes 1179656 | tf_op jit(solution)/shard_map/ppermute | solution.py:424
  83.0 2.2 %collective-permute-start.17 = (f32[2,3,2,4,16,128]{5,4,3,2,1,0:T(8,128)S(1)}, f32[2,3,2,4,16,128]{5,4,3,2,1,0:T(8,128)S(1)}, u32[]{:S(2)}, u32[]{:S(2)}) collective-permute-start(f32[2,3,2,4,16,128]{5,4,3,2,1,0:T(8,128)S(1)} %pad_maximum_fusion.2), channel_id=1, source_target_pairs={{0,1},{1,0},{2,3},{3,2},{4,5},{5,4},{6,7},{7,6},{8,9},{9,8},{10,11... | collective-permute-start | bytes 1179656 | tf_op jit(solution)/shard_map/ppermute | solution.py:426
  83.1 11.4 %collective-permute-start.18 = (f32[1,3,2,4,16,128]{5,4,3,2,1,0:T(8,128)S(1)}, f32[1,3,2,4,16,128]{5,4,3,2,1,0:T(8,128)S(1)}, u32[]{:S(2)}, u32[]{:S(2)}) collective-permute-start(f32[1,3,2,4,16,128]{5,4,3,2,1,0:T(8,128)S(1)} %slice.34), channel_id=1, source_target_pairs={{0,4},{4,8},{8,12},{12,14},{14,10},{10,6},{6,2},{2,0},{1,5},{5,9},... | collective-permute-start | bytes 589832 | tf_op jit(solution)/shard_map/ppermute | solution.py:431
  84.7 9.8 %collective-permute-start.19 = (f32[1,3,2,4,16,128]{5,4,3,2,1,0:T(8,128)}, f32[1,3,2,4,16,128]{5,4,3,2,1,0:T(8,128)S(1)}, u32[]{:S(2)}, u32[]{:S(2)}) collective-permute-start(f32[1,3,2,4,16,128]{5,4,3,2,1,0:T(8,128)} %get-tuple-element.61), channel_id=1, source_target_pairs={{4,0},{8,4},{12,8},{14,12},{10,14},{6,10},{2,6},{0,2},{5,1},{9,5},... | collective-permute-start | bytes 589832 | tf_op jit(solution)/shard_map/ppermute | solution.py:431
  94.5 1.4 %collective-permute-start.20 = (f32[1,3,2,4,16,128]{5,4,3,2,1,0:T(8,128)S(1)}, f32[1,3,2,4,16,128]{5,4,3,2,1,0:T(8,128)S(1)}, u32[]{:S(2)}, u32[]{:S(2)}) collective-permute-start(f32[1,3,2,4,16,128]{5,4,3,2,1,0:T(8,128)S(1)} %collective-permute-done.18.refs_2_), channel_id=1, source_target_pairs={{0,1},{1,0},{2,3},{3,2},{4,5},{5,4},{6,7},{7,6},{8,9},{9,8},{10,11... | collective-permute-start | bytes 589832 | tf_op jit(solution)/shard_map/ppermute | solution.py:433
  (4 other events, 3.5 us)

commit v8 on v7

--- a/solution.py
+++ b/solution.py
@@ -84,22 +84,23 @@
     )(starts, exposure, noise_var)
 
 
-def pick_kernel(place, owner, valid, *refs):
+def pick_kernel(numbers, *refs):
     chunks, (own, edges, chosen) = refs[:-3], refs[-3:]
     epochs, _, count, height, _ = own.shape
     tiles = count - 1
-    me, lower = place[0], place[1]
+    me, lower, valid = numbers[0], numbers[1], 2 + epochs
     for epoch in range(epochs):
         for step, chunk in enumerate(chunks):
 
-            @pl.when(owner[epoch] ^ me == step)
+            @pl.when(numbers[2 + epoch] ^ me == step)
             def _():
                 chosen[epoch] = chunk[...]
 
     row_ids = lower * height + lax.broadcasted_iota(jnp.int32, (height, LANES), 0)
     behind = lax.broadcasted_iota(jnp.int32, (8, LANES), 1) >= LANES - HALO
     for epoch in range(epochs):
-        usable = jnp.logical_and(row_ids >= valid[2 * epoch], row_ids < valid[2 * epoch + 1])
+        first, last = numbers[valid + 2 * epoch], numbers[valid + 2 * epoch + 1]
+        usable = jnp.logical_and(row_ids >= first, row_ids < last)
         for tile in range(count):
             if tile:
                 value, noise = (chosen[epoch, kind, (tile - 1) * height : tile * height] for kind in range(2))
@@ -121,12 +122,12 @@
     edges[...] = own[:, :, :, pl.ds(pl.multiple_of((1 - lower) * (height - MAXS), MAXS), MAXS)]
 
 
-def pick(place, owner, valid, chunks, height):
+def pick(numbers, epochs, chunks, height):
     rows = chunks[0].shape[1]
-    epochs, tiles = owner.shape[0], (rows - height * HALO // LANES) // height
+    tiles = (rows - height * HALO // LANES) // height
     return pl.pallas_call(
         pick_kernel,
-        in_specs=[pl.BlockSpec(memory_space=pltpu.SMEM)] * 3 + [pl.BlockSpec(memory_space=pltpu.VMEM)] * len(chunks),
+        in_specs=[pl.BlockSpec(memory_space=pltpu.SMEM)] + [pl.BlockSpec(memory_space=pltpu.VMEM)] * len(chunks),
         out_specs=[pl.BlockSpec(memory_space=pltpu.VMEM)] * 2,
         out_shape=[
             jax.ShapeDtypeStruct((epochs, 2, tiles + 1, depth, LANES), jnp.float32) for depth in (height, MAXS)
@@ -134,7 +135,7 @@
         scratch_shapes=[pltpu.VMEM((epochs, 2, rows, LANES), jnp.float32)],
         compiler_params=pltpu.CompilerParams(vmem_limit_bytes=VMEM),
         cost_estimate=pl.CostEstimate(flops=0, bytes_accessed=4 << 20, transcendentals=0),
-    )(place, owner, valid.reshape(-1), *chunks)
+    )(numbers, *chunks)
 
 
 def correlate_kernel(place, own, border, bands_ref, rows_ref, ext, high, low, summed):
@@ -245,26 +246,24 @@
                     raw[epoch, kind, slot, pl.ds(blank, MAXS)] = jnp.zeros((MAXS, LANES), jnp.float32)
                     for start, (source, index, tile) in zip(at, pieces):
                         value = operands[source][index, epoch, kind, tile]
-                        tops[kind] = jnp.maximum(tops[kind], jnp.abs(value))
+                        tops[kind] = jnp.maximum(tops[kind], value if kind else jnp.abs(value))
                         raw[epoch, kind, slot, pl.ds(start, MAXS)] = value
         tops = [jnp.full((8, LANES), jnp.maximum(jnp.max(top), 1e-30), jnp.float32) for top in tops]
-        per_psi, per_phi = most_psi / tops[0], most_phi / tops[1]
+        per_psi, per_phi = (most_psi - 1) / tops[0], (most_phi - 1) / tops[1]
         scale[0] = floor[0] * per_phi
-        scale[1] = jnp.sqrt(per_phi) / per_psi
+        scale[1] = jnp.sqrt(per_phi) / (per_psi * 256.0)
 
         def quantize(index, _):
             rows = pl.ds(pl.multiple_of(index * 8, 8), 8)
             for epoch in range(epochs):
                 for slot in range(len(held)):
                     psi = jnp.floor(raw[epoch, 0, slot, rows] * per_psi + 0.5).astype(jnp.int32)
-                    phi = jnp.floor(jnp.maximum(raw[epoch, 1, slot, rows], 0.0) * per_phi + 0.5).astype(jnp.int32)
-                    psi = jnp.clip(psi, -most_psi, most_psi)
-                    phi = jnp.minimum(phi, most_phi)
+                    phi = (raw[epoch, 1, slot, rows] * per_phi + 0.5).astype(jnp.int32)
                     whole[epoch, slot, rows] = psi * 256 + (phi >> 6)
                     lows[epoch, slot, rows] = phi & 63
             return 0
 
-        lax.fori_loop(0, reach // 8, quantize, 0, unroll=4)
+        lax.fori_loop(0, reach // 8, quantize, 0, unroll=8)
         for epoch in range(epochs):
             for slot in range(len(held)):
                 for top in range(0, reach - 8 * (fold - 1), 8):
@@ -299,8 +298,8 @@
         start = velocity * epochs * 2
         totals, low_total = [None] * fold, None
         for epoch in range(epochs):
-            row, col = shifts[start + 2 * epoch] + MAXS, shifts[start + 2 * epoch + 1] + MAXS
-            beyond, turn = lane < col, jnp.where(col == 0, 0, LANES - col)
+            row, col = shifts[start + 2 * epoch], shifts[start + 2 * epoch + 1]
+            beyond, turn = lane < col, (LANES - col) & (LANES - 1)
 
             def moved(ref, top):
                 rows = pl.ds(row + top, 8)
@@ -312,7 +311,7 @@
             word = moved(packed, 0)
             low_total = word if epoch == 0 else low_total + word
         for part in range(fold):
-            psi = (totals[part] >> 8).astype(jnp.float32)
+            psi = totals[part].astype(jnp.float32)
             phi = (((totals[part] & 255) << 6) + ((low_total >> (8 * part)) & 255)).astype(jnp.float32)
             out_ref[velocity, 8 * part : 8 * part + 8] = psi * unit * lax.rsqrt(jnp.maximum(phi, least))
         return 0
@@ -367,7 +366,7 @@
         input_output_aliases=aliases,
         compiler_params=pltpu.CompilerParams(vmem_limit_bytes=VMEM),
         cost_estimate=pl.CostEstimate(flops=16 * work, bytes_accessed=24 * work, transcendentals=work),
-    )(jnp.stack(numbers + [lower]).astype(jnp.int32), shifts, floor, *operands)
+    )(jnp.stack(numbers + [lower]).astype(jnp.int32), shifts + MAXS, floor, *operands)
 
 
 def local(images, variance, spread_kernel, shifts, epoch_owner, valid_rows):
@@ -388,15 +387,15 @@
     mine = position(me)
     place = jnp.stack([mine, lower]).astype(jnp.int32)
 
+    numbers = jnp.concatenate([jnp.stack([me, lower]).astype(jnp.int32), epoch_owner, valid_rows.reshape(-1)])
     starts = position(me ^ jnp.arange(blocks, dtype=jnp.int32)) * width
     chunks = list(cut(starts, exposure, noise_var, blocks))
     for step in range(1, blocks):
         chunks[step] = lax.ppermute(chunks[step], "vel", [(i, i ^ step) for i in range(blocks)])
-    chunks[1], spread_kernel = lax.optimization_barrier((chunks[1], spread_kernel))
+    chunks[1], spread_kernel, numbers = lax.optimization_barrier((chunks[1], spread_kernel, numbers))
     bands, floor = make_bands(spread_kernel)
     chunks[-1], floor = lax.optimization_barrier((chunks[-1], floor))
-    spot = jnp.stack([me, lower]).astype(jnp.int32)
-    own, edges = pick(spot, epoch_owner, valid_rows, chunks, height)
+    own, edges = pick(numbers, epoch_owner.shape[0], chunks, height)
     payload = correlate(place, own, lax.ppermute(edges, "rows", swap), bands)
 
     flat_shifts, floor = shifts.reshape(-1), floor[0, :1]
@@ -428,10 +427,10 @@
             have[step] = ((ahead, 0), (ahead, 1), (border, 1))
             segments = [block(-step) + [(1 - step, 0)], [(step - 1, tiles - 1)] + block(step)]
         else:
-            edge, inner = lax.ppermute(behind[:1], "vel", right), lax.ppermute(ahead[1:], "vel", left)
-            edge, inner, out = lax.optimization_barrier((edge, inner, out))
-            border = lax.ppermute(edge, "rows", swap)
-            have[step] = ((edge, 0), (inner, 0), (border, 0))
+            behind = lax.ppermute(behind, "vel", right)
+            behind, out = lax.optimization_barrier((behind, out))
+            border = lax.ppermute(behind[:1], "rows", swap)
+            have[step] = ((behind, 0), (behind, 1), (border, 0))
             segments = [[(step - 1, tiles - 1)] + block(step) + [(1 - step, 0)]]
         out = stack_now(segments, out)
     return out

time: 103 us -> 101 us (0.981)
  local copies, waits for them, and re-layouts: 12 us -> 10.7 us
  Pallas kernels: 52.9 us -> 51.8 us
    unnamed x16 -> x13, local copies, waits for them, and re-layouts: 9.33 us -> 8.55 us
    ppermute x3 -> x2, waiting for transfers between devices: 1.33 us -> 2.11 us  [the longest x1 1.32 us: local(): border = lax.ppermute(behind[:1], 'rows', swap)]
    ppermute x3 -> x2, starting transfers between devices: 2.08 us -> 1.7 us  [the longest x1 1.63 us: local(): behind = lax.ppermute(behind, 'vel', right)]
  transfers between devices with their start and end apart: 21 -> 20, of which waited for: 12 -> 13; matrix products, arithmetic and copies ran while one was open for 3% -> 4% of each run, Pallas kernels for 36% -> 36%
where the time goes in v8:
time: 101 us
  Pallas kernels  51.8 us (51%)
  starting transfers between devices  23 us (23%)
  waiting for transfers between devices  14.3 us (14%)
  local copies, waits for them, and re-layouts  10.7 us (11%)
    pallas_call x5, Pallas kernels, stack_tiles(): pl.pallas_call(functools.partial(stack_kernel, segments=described, source...  38.1 us
    ppermute x7, starting transfers between devices, local(): lax.ppermute(chunks[step], 'vel', [(i, i ^ step) for i in range(blocks)])  14.7 us
    unnamed x13, local copies, waits for them, and re-layouts  8.55 us
    pallas_call x1, Pallas kernels, correlate(): pl.pallas_call(correlate_kernel, in_specs=[pl.BlockSpec(memory_space=pltp...  7.52 us
    pallas_call x1, Pallas kernels, make_bands(): pl.pallas_call(band_kernel, in_specs=[pl.BlockSpec(memory_space=pltpu.SME...  4.59 us
    ppermute x7, waiting for transfers between devices, local(): lax.ppermute(chunks[step], 'vel', [(i, i ^ step) for i in range(blocks)])  3.56 us
    ppermute x1, waiting for transfers between devices, local(): lax.ppermute(payload, 'vel', left)  3.15 us
    ppermute x2, starting transfers between devices, local(): lax.ppermute(behind, 'vel', right)  2.72 us
  transfers between devices with their start and end apart: 20, of which 13 were waited for; matrix products, arithmetic and copies ran while one was open for 4% of the time, Pallas kernels for 36%

profile of v8, /device:TPU:0, one launch (start us, length us, event | category | flops | bytes accessed | tf_op | source)
XLA Modules:
  0.0 101.1 jit_solution(9388701603711018897)
XLA Ops:
  0.0 1.0 %copy-done = f32[1,32,4096]{2,1,0:T(8,128)S(1)} copy-done((f32[1,32,4096]{2,1,0:T(8,128)S(1)}, f32[1,32,4096]{2,1,0:T(8,128)}, u32[]{:S(2)}) %copy-start) | copy-done | bytes 524312
  1.1 1.0 %copy-done.1 = f32[1,32,4096]{2,1,0:T(8,128)S(1)} copy-done((f32[1,32,4096]{2,1,0:T(8,128)S(1)}, f32[1,32,4096]{2,1,0:T(8,128)}, u32[]{:S(2)}) %copy-start.1) | copy-done | bytes 524312
  2.9 6.1 %collective-permute-start = (f32[2,136,128]{2,1,0:T(8,128)S(1)}, f32[2,136,128]{2,1,0:T(8,128)S(1)}, u32[]{:S(2)}, u32[]{:S(2)}) collective-permute-start(f32[2,136,128]{2,1,0:T(8,128)S(1)} %get-tuple-element.33), channel_id=1, source_target_pairs={{0,14},{2,12},{4,10},{6,8},{8,6},{10,4},{12,2},{14,0},{1,15},{3,13... | collective-permute-start | bytes 417800 | tf_op jit(solution)/shard_map/ppermute | solution.py:394
  9.5 3.0 %collective-permute-start.3 = (f32[2,136,128]{2,1,0:T(8,128)S(1)}, f32[2,136,128]{2,1,0:T(8,128)S(1)}, u32[]{:S(2)}, u32[]{:S(2)}) collective-permute-start(f32[2,136,128]{2,1,0:T(8,128)S(1)} %get-tuple-element.42), channel_id=1, source_target_pairs={{0,6},{2,4},{4,2},{6,0},{8,14},{10,12},{12,10},{14,8},{1,7},{3,5},... | collective-permute-start | bytes 417800 | tf_op jit(solution)/shard_map/ppermute | solution.py:394
  12.5 1.1 %collective-permute-done.refs_7_ = f32[2,136,128]{2,1,0:T(8,128)S(1)} collective-permute-done((f32[2,136,128]{2,1,0:T(8,128)S(1)}, f32[2,136,128]{2,1,0:T(8,128)S(1)}, u32[]{:S(2)}, u32[]{:S(2)}) %collective-permute-start) | collective-permute-done | bytes 139296 | tf_op jit(solution)/shard_map/ppermute | solution.py:394
  13.5 4.8 %collective-permute-start.5 = (f32[2,136,128]{2,1,0:T(8,128)S(1)}, f32[2,136,128]{2,1,0:T(8,128)S(1)}, u32[]{:S(2)}, u32[]{:S(2)}) collective-permute-start(f32[2,136,128]{2,1,0:T(8,128)S(1)} %get-tuple-element.44), channel_id=1, source_target_pairs={{0,10},{2,8},{4,14},{6,12},{8,2},{10,0},{12,6},{14,4},{1,11},{3,9}... | collective-permute-start | bytes 417800 | tf_op jit(solution)/shard_map/ppermute | solution.py:394
  21.7 4.6 %shard_map.65 = (bf16[2,21,256,256]{3,2,1,0:T(8,128)(2,1)S(1)}, f32[8,128]{1,0:T(8,128)S(1)}) custom-call(f32[441]{0:T(512)S(1)} %reshape.10.taps, f32[21,21]{1,0:T(8,128)S(1)} %copy-done.2), custom_call_target="tpu_custom_call" | custom-call | bytes 20971520 | tf_op jit(solution)/shard_map/pallas_call | solution.py:42
  26.3 2.4 %copy-done.3 = bf16[2,21,256,256]{3,2,1,0:T(8,128)(2,1)} copy-done((bf16[2,21,256,256]{3,2,1,0:T(8,128)(2,1)}, bf16[2,21,256,256]{3,2,1,0:T(8,128)(2,1)S(1)}, u32[]{:S(2)}) %copy-start.3) | copy-done | bytes 5505048
  28.9 2.4 %collective-permute-done.5.refs_5_ = f32[2,136,128]{2,1,0:T(8,128)S(1)} collective-permute-done((f32[2,136,128]{2,1,0:T(8,128)S(1)}, f32[2,136,128]{2,1,0:T(8,128)S(1)}, u32[]{:S(2)}, u32[]{:S(2)}) %collective-permute-start.5) | collective-permute-done | bytes 139296 | tf_op jit(solution)/shard_map/ppermute | solution.py:394
  32.3 1.4 %collective-permute-done.7.border = f32[3,2,5,16,128]{4,3,2,1,0:T(8,128)S(1)} collective-permute-done((f32[3,2,5,16,128]{4,3,2,1,0:T(8,128)S(1)}, f32[3,2,5,16,128]{4,3,2,1,0:T(8,128)S(1)}, u32[]{:S(2)}, u32[]{:S(2)}) %collective-permute-start.7) | collective-permute-done | bytes 245792 | tf_op jit(solution)/shard_map/ppermute | solution.py:399
  33.7 2.6 %copy-done.4 = bf16[2,21,256,256]{3,2,1,0:T(8,128)(2,1)S(1)} copy-done((bf16[2,21,256,256]{3,2,1,0:T(8,128)(2,1)S(1)}, bf16[2,21,256,256]{3,2,1,0:T(8,128)(2,1)}, u32[]{:S(2)}) %copy-start.4) | copy-done | bytes 5505048
  36.3 7.5 %shard_map.67.refs_0_.refs_2_ = f32[2,3,2,4,16,128]{5,4,3,2,1,0:T(8,128)S(1)} custom-call(s32[2]{0:T(128)S(1)} %pad_add_fusion.1.place, f32[3,2,5,32,128]{4,3,2,1,0:T(8,128)S(1)} %get-tuple-element.47.own, f32[3,2,5,16,128]{4,3,2,1,0:T(8,128)S(1)} %collective-permute-done.7.border, bf16[2,21,256,256]{3,2,1,0:T(8,128)(2,1)S(1)} %copy-done.4), custom_call_target="tpu_custom_call" | custom-call | flops 5637144576 | bytes 12582912 | tf_op jit(solution)/shard_map/pallas_call | solution.py:210
  43.8 1.5 %collective-permute-start.9 = (f32[2,3,2,4,16,128]{5,4,3,2,1,0:T(8,128)S(1)}, f32[2,3,2,4,16,128]{5,4,3,2,1,0:T(8,128)S(1)}, u32[]{:S(2)}, u32[]{:S(2)}) collective-permute-start(f32[2,3,2,4,16,128]{5,4,3,2,1,0:T(8,128)S(1)} %shard_map.67.refs_0_.refs_2_), channel_id=1, source_target_pairs={{4,0},{8,4},{12,8},{14,12},{10,14},{6,10},{2,6},{0,2},{5,1},{9,5},... | collective-permute-start | bytes 1179656 | tf_op jit(solution)/shard_map/ppermute | solution.py:416
  47.5 4.7 %shard_map.68.refs_5_ = f32[36,32,4096]{2,1,0:T(8,128)} custom-call(s32[4]{0:T(128)S(1)} %pad_add_fusion.2.place, s32[216]{0:T(256)S(1)} %add.193.shifts, f32[1]{0:T(128)} %bitcast.9.floor, f32[2,3,2,4,16,128]{5,4,3,2,1,0:T(8,128)S(1)} %shard_map.67.refs_0_.refs_2_, f32[1,3,2,4,16,128]{5,4,3,2,1,0:T(8,128)S(1)} %collective-permute-done.10.refs_1_.refs_3_), custom_call_target="tpu_custom_call" | custom-call | flops 7077888 | bytes 10616832 | tf_op jit(solution)/shard_map/pallas_call | solution.py:344
  52.1 3.1 %collective-permute-done.9.refs_4_ = f32[2,3,2,4,16,128]{5,4,3,2,1,0:T(8,128)S(1)} collective-permute-done((f32[2,3,2,4,16,128]{5,4,3,2,1,0:T(8,128)S(1)}, f32[2,3,2,4,16,128]{5,4,3,2,1,0:T(8,128)S(1)}, u32[]{:S(2)}, u32[]{:S(2)}) %collective-permute-start.9) | collective-permute-done | bytes 393248 | tf_op jit(solution)/shard_map/ppermute | solution.py:416
  57.3 1.1 %collective-permute-start.12 = (f32[2,3,2,4,16,128]{5,4,3,2,1,0:T(8,128)S(1)}, f32[2,3,2,4,16,128]{5,4,3,2,1,0:T(8,128)S(1)}, u32[]{:S(2)}, u32[]{:S(2)}) collective-permute-start(f32[2,3,2,4,16,128]{5,4,3,2,1,0:T(8,128)S(1)} %collective-permute-done.9.refs_4_), channel_id=1, source_target_pairs={{4,0},{8,4},{12,8},{14,12},{10,14},{6,10},{2,6},{0,2},{5,1},{9,5},... | collective-permute-start | bytes 1179656 | tf_op jit(solution)/shard_map/ppermute | solution.py:423
  58.5 9.1 %shard_map.69.refs_6_ = f32[36,32,4096]{2,1,0:T(8,128)} custom-call(s32[9]{0:T(128)S(1)} %stack.151.place, s32[216]{0:T(256)S(1)} %add.193.shifts, f32[1]{0:T(128)} %bitcast.9.floor, f32[2,3,2,4,16,128]{5,4,3,2,1,0:T(8,128)S(1)} %collective-permute-done.8.refs_0_.refs_2_, ...), custom_call_target="tpu_custom_call", output_to_operand_aliasing={{}: (8, {})} | custom-call | flops 18874368 | bytes 28311552 | tf_op jit(solution)/shard_map/pallas_call | solution.py:344
  68.6 1.7 %collective-permute-start.14 = (f32[2,3,2,4,16,128]{5,4,3,2,1,0:T(8,128)S(1)}, f32[2,3,2,4,16,128]{5,4,3,2,1,0:T(8,128)S(1)}, u32[]{:S(2)}, u32[]{:S(2)}) collective-permute-start(f32[2,3,2,4,16,128]{5,4,3,2,1,0:T(8,128)S(1)} %collective-permute-done.11.refs_0_.refs_2_), channel_id=1, source_target_pairs={{0,4},{4,8},{8,12},{12,14},{14,10},{10,6},{6,2},{2,0},{1,5},{5,9},... | collective-permute-start | bytes 1179656 | tf_op jit(solution)/shard_map/ppermute | solution.py:423
  70.8 9.0 %shard_map.70.refs_6_ = f32[36,32,4096]{2,1,0:T(8,128)} custom-call(s32[9]{0:T(128)S(1)} %stack.160.place, s32[216]{0:T(256)S(1)} %add.193.shifts, f32[1]{0:T(128)} %bitcast.9.floor, f32[2,3,2,4,16,128]{5,4,3,2,1,0:T(8,128)S(1)} %collective-permute-done.11.refs_0_.refs_2_, ...), custom_call_target="tpu_custom_call", output_to_operand_aliasing={{}: (9, {})} | custom-call | flops 18874368 | bytes 28311552 | tf_op jit(solution)/shard_map/pallas_call | solution.py:344
  80.2 1.4 %collective-permute-done.15.refs_5_.refs_0_ = f32[2,3,2,4,16,128]{5,4,3,2,1,0:T(8,128)S(1)} collective-permute-done((f32[2,3,2,4,16,128]{5,4,3,2,1,0:T(8,128)S(1)}, f32[2,3,2,4,16,128]{5,4,3,2,1,0:T(8,128)S(1)}, u32[]{:S(2)}, u32[]{:S(2)}) %collective-permute-start.15) | collective-permute-done | bytes 393248 | tf_op jit(solution)/shard_map/ppermute | solution.py:423
  81.7 1.6 %collective-permute-start.18 = (f32[2,3,2,4,16,128]{5,4,3,2,1,0:T(8,128)S(1)}, f32[2,3,2,4,16,128]{5,4,3,2,1,0:T(8,128)S(1)}, u32[]{:S(2)}, u32[]{:S(2)}) collective-permute-start(f32[2,3,2,4,16,128]{5,4,3,2,1,0:T(8,128)S(1)} %collective-permute-done.14.refs_0_.refs_4_), channel_id=1, source_target_pairs={{0,4},{4,8},{8,12},{12,14},{14,10},{10,6},{6,2},{2,0},{1,5},{5,9},... | collective-permute-start | bytes 1179656 | tf_op jit(solution)/shard_map/ppermute | solution.py:430
  83.4 9.0 %shard_map.71.refs_5_ = f32[36,32,4096]{2,1,0:T(8,128)} custom-call(s32[9]{0:T(128)S(1)} %stack.169.place, s32[216]{0:T(256)S(1)} %add.193.shifts, f32[1]{0:T(128)} %bitcast.9.floor, f32[2,3,2,4,16,128]{5,4,3,2,1,0:T(8,128)S(1)} %collective-permute-done.14.refs_0_.refs_4_, ...), custom_call_target="tpu_custom_call", output_to_operand_aliasing={{}: (9, {})} | custom-call | flops 18874368 | bytes 28311552 | tf_op jit(solution)/shard_map/pallas_call | solution.py:344
  93.4 1.3 %collective-permute-done.19.refs_3_ = f32[1,3,2,4,16,128]{5,4,3,2,1,0:T(8,128)S(1)} collective-permute-done((f32[1,3,2,4,16,128]{5,4,3,2,1,0:T(8,128)S(1)}, f32[1,3,2,4,16,128]{5,4,3,2,1,0:T(8,128)S(1)}, u32[]{:S(2)}, u32[]{:S(2)}) %collective-permute-start.19) | collective-permute-done | bytes 196640 | tf_op jit(solution)/shard_map/ppermute | solution.py:432
  94.8 6.3 %shard_map.72 = f32[36,32,4096]{2,1,0:T(8,128)} custom-call(s32[6]{0:T(128)S(1)} %stack.135.place, s32[216]{0:T(256)S(1)} %add.193.shifts, f32[1]{0:T(128)} %bitcast.9.floor, f32[2,3,2,4,16,128]{5,4,3,2,1,0:T(8,128)S(1)} %collective-permute-done.15.refs_5_.refs_0_, ...), custom_call_target="tpu_custom_call", output_to_operand_aliasing={{}: (8, {})} | custom-call | flops 11796480 | bytes 17694720 | tf_op jit(solution)/shard_map/pallas_call | solution.py:344
  (63 shorter events, 13.1 us)
Async XLA Ops:
  0.0 46.0 %copy-start.5 = (s32[36,3,2]{0,2,1:T(2,128)S(1)}, s32[36,3,2]{0,2,1:T(2,128)}, u32[]{:S(2)}) copy-start(s32[36,3,2]{0,2,1:T(2,128)} %param.9) | copy-start | bytes 2596
  0.0 1.0 %copy-start = (f32[1,32,4096]{2,1,0:T(8,128)S(1)}, f32[1,32,4096]{2,1,0:T(8,128)}, u32[]{:S(2)}) copy-start(f32[1,32,4096]{2,1,0:T(8,128)} %param.6) | copy-start | bytes 1572868
  2.9 10.6 %collective-permute-start = (f32[2,136,128]{2,1,0:T(8,128)S(1)}, f32[2,136,128]{2,1,0:T(8,128)S(1)}, u32[]{:S(2)}, u32[]{:S(2)}) collective-permute-start(f32[2,136,128]{2,1,0:T(8,128)S(1)} %get-tuple-element.33), channel_id=1, source_target_pairs={{0,14},{2,12},{4,10},{6,8},{8,6},{10,4},{12,2},{14,0},{1,15},{3,13... | collective-permute-start | bytes 417800 | tf_op jit(solution)/shard_map/ppermute | solution.py:394
  9.0 9.3 %collective-permute-start.1 = (f32[2,136,128]{2,1,0:T(8,128)S(1)}, f32[2,136,128]{2,1,0:T(8,128)S(1)}, u32[]{:S(2)}, u32[]{:S(2)}) collective-permute-start(f32[2,136,128]{2,1,0:T(8,128)S(1)} %get-tuple-element.34), channel_id=1, source_target_pairs={{0,2},{2,0},{4,6},{6,4},{8,10},{10,8},{12,14},{14,12},{1,3},{3,1},... | collective-permute-start | bytes 417800 | tf_op jit(solution)/shard_map/ppermute | solution.py:394
  9.5 19.3 %collective-permute-start.2 = (f32[2,136,128]{2,1,0:T(8,128)S(1)}, f32[2,136,128]{2,1,0:T(8,128)S(1)}, u32[]{:S(2)}, u32[]{:S(2)}) collective-permute-start(f32[2,136,128]{2,1,0:T(8,128)S(1)} %get-tuple-element.41), channel_id=1, source_target_pairs={{0,4},{2,6},{4,0},{6,2},{8,12},{10,14},{12,8},{14,10},{1,5},{3,7},... | collective-permute-start | bytes 417800 | tf_op jit(solution)/shard_map/ppermute | solution.py:394
  9.5 19.3 %collective-permute-start.3 = (f32[2,136,128]{2,1,0:T(8,128)S(1)}, f32[2,136,128]{2,1,0:T(8,128)S(1)}, u32[]{:S(2)}, u32[]{:S(2)}) collective-permute-start(f32[2,136,128]{2,1,0:T(8,128)S(1)} %get-tuple-element.42), channel_id=1, source_target_pairs={{0,6},{2,4},{4,2},{6,0},{8,14},{10,12},{12,10},{14,8},{1,7},{3,5},... | collective-permute-start | bytes 417800 | tf_op jit(solution)/shard_map/ppermute | solution.py:394
  12.5 16.5 %collective-permute-start.4 = (f32[2,136,128]{2,1,0:T(8,128)S(1)}, f32[2,136,128]{2,1,0:T(8,128)S(1)}, u32[]{:S(2)}, u32[]{:S(2)}) collective-permute-start(f32[2,136,128]{2,1,0:T(8,128)S(1)} %get-tuple-element.43), channel_id=1, source_target_pairs={{0,8},{2,10},{4,12},{6,14},{8,0},{10,2},{12,4},{14,6},{1,9},{3,11}... | collective-permute-start | bytes 417800 | tf_op jit(solution)/shard_map/ppermute | solution.py:394
  13.5 17.8 %collective-permute-start.5 = (f32[2,136,128]{2,1,0:T(8,128)S(1)}, f32[2,136,128]{2,1,0:T(8,128)S(1)}, u32[]{:S(2)}, u32[]{:S(2)}) collective-permute-start(f32[2,136,128]{2,1,0:T(8,128)S(1)} %get-tuple-element.44), channel_id=1, source_target_pairs={{0,10},{2,8},{4,14},{6,12},{8,2},{10,0},{12,6},{14,4},{1,11},{3,9}... | collective-permute-start | bytes 417800 | tf_op jit(solution)/shard_map/ppermute | solution.py:394
  18.3 13.0 %collective-permute-start.6 = (f32[2,136,128]{2,1,0:T(8,128)S(1)}, f32[2,136,128]{2,1,0:T(8,128)S(1)}, u32[]{:S(2)}, u32[]{:S(2)}) collective-permute-start(f32[2,136,128]{2,1,0:T(8,128)S(1)} %get-tuple-element.45), channel_id=1, source_target_pairs={{0,12},{2,14},{4,8},{6,10},{8,4},{10,6},{12,0},{14,2},{1,13},{3,15... | collective-permute-start | bytes 417800 | tf_op jit(solution)/shard_map/ppermute | solution.py:394
  26.3 2.4 %copy-start.3 = (bf16[2,21,256,256]{3,2,1,0:T(8,128)(2,1)}, bf16[2,21,256,256]{3,2,1,0:T(8,128)(2,1)S(1)}, u32[]{:S(2)}) copy-start(bf16[2,21,256,256]{3,2,1,0:T(8,128)(2,1)S(1)} %get-tuple-element.49.bands_ref) | copy-start | bytes 16515076
  32.2 1.6 %collective-permute-start.7 = (f32[3,2,5,16,128]{4,3,2,1,0:T(8,128)S(1)}, f32[3,2,5,16,128]{4,3,2,1,0:T(8,128)S(1)}, u32[]{:S(2)}, u32[]{:S(2)}) collective-permute-start(f32[3,2,5,16,128]{4,3,2,1,0:T(8,128)S(1)} %get-tuple-element.48), channel_id=1, source_target_pairs={{0,1},{1,0},{2,3},{3,2},{4,5},{5,4},{6,7},{7,6},{8,9},{9,8},{10,11... | collective-permute-start | bytes 737288 | tf_op jit(solution)/shard_map/ppermute | solution.py:399
  33.7 2.6 %copy-start.4 = (bf16[2,21,256,256]{3,2,1,0:T(8,128)(2,1)S(1)}, bf16[2,21,256,256]{3,2,1,0:T(8,128)(2,1)}, u32[]{:S(2)}) copy-start(bf16[2,21,256,256]{3,2,1,0:T(8,128)(2,1)} %copy-done.3) | copy-start | bytes 16515076
  43.8 11.5 %collective-permute-start.9 = (f32[2,3,2,4,16,128]{5,4,3,2,1,0:T(8,128)S(1)}, f32[2,3,2,4,16,128]{5,4,3,2,1,0:T(8,128)S(1)}, u32[]{:S(2)}, u32[]{:S(2)}) collective-permute-start(f32[2,3,2,4,16,128]{5,4,3,2,1,0:T(8,128)S(1)} %shard_map.67.refs_0_.refs_2_), channel_id=1, source_target_pairs={{4,0},{8,4},{12,8},{14,12},{10,14},{6,10},{2,6},{0,2},{5,1},{9,5},... | collective-permute-start | bytes 1179656 | tf_op jit(solution)/shard_map/ppermute | solution.py:416
  45.3 10.9 %collective-permute-start.8 = (f32[2,3,2,4,16,128]{5,4,3,2,1,0:T(8,128)S(1)}, f32[2,3,2,4,16,128]{5,4,3,2,1,0:T(8,128)S(1)}, u32[]{:S(2)}, u32[]{:S(2)}) collective-permute-start(f32[2,3,2,4,16,128]{5,4,3,2,1,0:T(8,128)S(1)} %shard_map.67.refs_0_.refs_2_), channel_id=1, source_target_pairs={{0,4},{4,8},{8,12},{12,14},{14,10},{10,6},{6,2},{2,0},{1,5},{5,9},... | collective-permute-start | bytes 1179656 | tf_op jit(solution)/shard_map/ppermute | solution.py:416
  46.0 1.5 %collective-permute-start.10 = (f32[1,3,2,4,16,128]{5,4,3,2,1,0:T(8,128)S(1)}, f32[1,3,2,4,16,128]{5,4,3,2,1,0:T(8,128)S(1)}, u32[]{:S(2)}, u32[]{:S(2)}) collective-permute-start(f32[1,3,2,4,16,128]{5,4,3,2,1,0:T(8,128)S(1)} %slice.36), channel_id=1, source_target_pairs={{0,1},{1,0},{2,3},{3,2},{4,5},{5,4},{6,7},{7,6},{8,9},{9,8},{10,11... | collective-permute-start | bytes 589832 | tf_op jit(solution)/shard_map/ppermute | solution.py:417
  56.2 2.2 %collective-permute-start.13 = (f32[2,3,2,4,16,128]{5,4,3,2,1,0:T(8,128)S(1)}, f32[2,3,2,4,16,128]{5,4,3,2,1,0:T(8,128)S(1)}, u32[]{:S(2)}, u32[]{:S(2)}) collective-permute-start(f32[2,3,2,4,16,128]{5,4,3,2,1,0:T(8,128)S(1)} %pad_maximum_fusion), channel_id=1, source_target_pairs={{0,1},{1,0},{2,3},{3,2},{4,5},{5,4},{6,7},{7,6},{8,9},{9,8},{10,11... | collective-permute-start | bytes 1179656 | tf_op jit(solution)/shard_map/ppermute | solution.py:425
  56.3 11.5 %collective-permute-start.11 = (f32[2,3,2,4,16,128]{5,4,3,2,1,0:T(8,128)S(1)}, f32[2,3,2,4,16,128]{5,4,3,2,1,0:T(8,128)S(1)}, u32[]{:S(2)}, u32[]{:S(2)}) collective-permute-start(f32[2,3,2,4,16,128]{5,4,3,2,1,0:T(8,128)S(1)} %collective-permute-done.8.refs_0_.refs_2_), channel_id=1, source_target_pairs={{0,4},{4,8},{8,12},{12,14},{14,10},{10,6},{6,2},{2,0},{1,5},{5,9},... | collective-permute-start | bytes 1179656 | tf_op jit(solution)/shard_map/ppermute | solution.py:423
  57.3 11.2 %collective-permute-start.12 = (f32[2,3,2,4,16,128]{5,4,3,2,1,0:T(8,128)S(1)}, f32[2,3,2,4,16,128]{5,4,3,2,1,0:T(8,128)S(1)}, u32[]{:S(2)}, u32[]{:S(2)}) collective-permute-start(f32[2,3,2,4,16,128]{5,4,3,2,1,0:T(8,128)S(1)} %collective-permute-done.9.refs_4_), channel_id=1, source_target_pairs={{4,0},{8,4},{12,8},{14,12},{10,14},{6,10},{2,6},{0,2},{5,1},{9,5},... | collective-permute-start | bytes 1179656 | tf_op jit(solution)/shard_map/ppermute | solution.py:423
  68.6 2.2 %collective-permute-start.16 = (f32[2,3,2,4,16,128]{5,4,3,2,1,0:T(8,128)S(1)}, f32[2,3,2,4,16,128]{5,4,3,2,1,0:T(8,128)S(1)}, u32[]{:S(2)}, u32[]{:S(2)}) collective-permute-start(f32[2,3,2,4,16,128]{5,4,3,2,1,0:T(8,128)S(1)} %pad_maximum_fusion.1), channel_id=1, source_target_pairs={{0,1},{1,0},{2,3},{3,2},{4,5},{5,4},{6,7},{7,6},{8,9},{9,8},{10,11... | collective-permute-start | bytes 1179656 | tf_op jit(solution)/shard_map/ppermute | solution.py:425
  68.6 11.5 %collective-permute-start.14 = (f32[2,3,2,4,16,128]{5,4,3,2,1,0:T(8,128)S(1)}, f32[2,3,2,4,16,128]{5,4,3,2,1,0:T(8,128)S(1)}, u32[]{:S(2)}, u32[]{:S(2)}) collective-permute-start(f32[2,3,2,4,16,128]{5,4,3,2,1,0:T(8,128)S(1)} %collective-permute-done.11.refs_0_.refs_2_), channel_id=1, source_target_pairs={{0,4},{4,8},{8,12},{12,14},{14,10},{10,6},{6,2},{2,0},{1,5},{5,9},... | collective-permute-start | bytes 1179656 | tf_op jit(solution)/shard_map/ppermute | solution.py:423
  70.4 11.2 %collective-permute-start.15 = (f32[2,3,2,4,16,128]{5,4,3,2,1,0:T(8,128)S(1)}, f32[2,3,2,4,16,128]{5,4,3,2,1,0:T(8,128)S(1)}, u32[]{:S(2)}, u32[]{:S(2)}) collective-permute-start(f32[2,3,2,4,16,128]{5,4,3,2,1,0:T(8,128)S(1)} %collective-permute-done.12.refs_5_.refs_4_), channel_id=1, source_target_pairs={{4,0},{8,4},{12,8},{14,12},{10,14},{6,10},{2,6},{0,2},{5,1},{9,5},... | collective-permute-start | bytes 1179656 | tf_op jit(solution)/shard_map/ppermute | solution.py:423
  81.6 1.8 %collective-permute-start.17 = (f32[2,3,2,4,16,128]{5,4,3,2,1,0:T(8,128)S(1)}, f32[2,3,2,4,16,128]{5,4,3,2,1,0:T(8,128)S(1)}, u32[]{:S(2)}, u32[]{:S(2)}) collective-permute-start(f32[2,3,2,4,16,128]{5,4,3,2,1,0:T(8,128)S(1)} %pad_maximum_fusion.2), channel_id=1, source_target_pairs={{0,1},{1,0},{2,3},{3,2},{4,5},{5,4},{6,7},{7,6},{8,9},{9,8},{10,11... | collective-permute-start | bytes 1179656 | tf_op jit(solution)/shard_map/ppermute | solution.py:425
  81.7 11.5 %collective-permute-start.18 = (f32[2,3,2,4,16,128]{5,4,3,2,1,0:T(8,128)S(1)}, f32[2,3,2,4,16,128]{5,4,3,2,1,0:T(8,128)S(1)}, u32[]{:S(2)}, u32[]{:S(2)}) collective-permute-start(f32[2,3,2,4,16,128]{5,4,3,2,1,0:T(8,128)S(1)} %collective-permute-done.14.refs_0_.refs_4_), channel_id=1, source_target_pairs={{0,4},{4,8},{8,12},{12,14},{14,10},{10,6},{6,2},{2,0},{1,5},{5,9},... | collective-permute-start | bytes 1179656 | tf_op jit(solution)/shard_map/ppermute | solution.py:430
  93.3 1.5 %collective-permute-start.19 = (f32[1,3,2,4,16,128]{5,4,3,2,1,0:T(8,128)S(1)}, f32[1,3,2,4,16,128]{5,4,3,2,1,0:T(8,128)S(1)}, u32[]{:S(2)}, u32[]{:S(2)}) collective-permute-start(f32[1,3,2,4,16,128]{5,4,3,2,1,0:T(8,128)S(1)} %slice.35), channel_id=1, source_target_pairs={{0,1},{1,0},{2,3},{3,2},{4,5},{5,4},{6,7},{7,6},{8,9},{9,8},{10,11... | collective-permute-start | bytes 589832 | tf_op jit(solution)/shard_map/ppermute | solution.py:432
  (2 other events, 1.8 us)

commit v9 on v8

--- a/solution.py
+++ b/solution.py
@@ -10,6 +10,7 @@
 MAXS = 16
 HALO = 32
 VMEM = 24 << 20
+LARGE = 50 << 20
 
 
 def band_kernel(taps, kernel, bands_ref, floor_ref):
@@ -138,11 +139,14 @@
     )(numbers, *chunks)
 
 
-def correlate_kernel(place, own, border, bands_ref, rows_ref, ext, high, low, summed):
+def correlate_kernel(place, own, border, bands_hbm, rows_ref, ext, high, low, summed, bands_ref, arrived):
     epochs, kinds, count, height, _ = own.shape
     tiles = count - 1
     ksize = bands_ref.shape[1]
     members = high.shape[2] // (height + 2 * MAXS)
+    copies = [pltpu.make_async_copy(bands_hbm.at[kind], bands_ref.at[kind], arrived.at[kind]) for kind in range(kinds)]
+    for copy in copies:
+        copy.start()
     first, lower = place[0] == 0, place[1]
     at_border = (1 - lower) * (MAXS + height)
     summed_rows = height * members
@@ -184,6 +188,7 @@
         offsets = [pl.ds((row + MAXS - ksize // 2) * members, summed_rows) for row in range(ksize)]
         upper = jnp.concatenate([high[kind, half, rows] for rows in offsets for half in range(2)], axis=1)
         rest = jnp.concatenate([low[kind, half, rows] for rows in offsets for half in range(2)], axis=1)
+        copies[kind].wait()
         weights = bands_ref[kind].reshape(ksize * 2 * LANES, 2 * LANES)
         pair = jnp.dot(upper, weights, preferred_element_type=jnp.float32)
         more = jnp.dot(rest, weights[:, :LANES], preferred_element_type=jnp.float32)
@@ -209,7 +214,8 @@
     flops = 2 * 2 * kinds * members * height * bands.shape[1] * 4 * LANES * LANES
     return pl.pallas_call(
         correlate_kernel,
-        in_specs=[pl.BlockSpec(memory_space=pltpu.SMEM)] + [pl.BlockSpec(memory_space=pltpu.VMEM)] * 3,
+        in_specs=[pl.BlockSpec(memory_space=pltpu.SMEM)] + [pl.BlockSpec(memory_space=pltpu.VMEM)] * 2
+        + [pl.BlockSpec(memory_space=pltpu.HBM)],
         out_specs=pl.BlockSpec(memory_space=pltpu.VMEM),
         out_shape=jax.ShapeDtypeStruct((2, epochs, kinds, tiles, MAXS, LANES), jnp.float32),
         scratch_shapes=[
@@ -217,8 +223,10 @@
             pltpu.VMEM((kinds, 2, depth, LANES), jnp.bfloat16),
             pltpu.VMEM((kinds, 2, depth, LANES), jnp.bfloat16),
             pltpu.VMEM((height * members, LANES), jnp.float32),
+            pltpu.VMEM(bands.shape, bands.dtype),
+            pltpu.SemaphoreType.DMA((kinds,)),
         ],
-        compiler_params=pltpu.CompilerParams(vmem_limit_bytes=VMEM),
+        compiler_params=pltpu.CompilerParams(vmem_limit_bytes=LARGE),
         cost_estimate=pl.CostEstimate(flops=flops, bytes_accessed=12 << 20, transcendentals=0),
     )(place, own, border, bands)
 

time: 101 us -> 100 us (0.990)
  local copies, waits for them, and re-layouts: 10.7 us -> 8.18 us
  Pallas kernels: 51.8 us -> 53.2 us
    unnamed x13 -> x11, local copies, waits for them, and re-layouts: 8.55 us -> 5.99 us
    pallas_call x1, Pallas kernels: 7.52 us -> 8.55 us  [correlate(): pl.pallas_call(correlate_kernel, in_specs=[pl.BlockSpec(memory_space=pltp...]
  transfers between devices with their start and end apart: 20 -> 20, of which waited for: 13 -> 13; matrix products, arithmetic and copies ran while one was open for 4% -> 4% of each run, Pallas kernels for 36% -> 37%
where the time goes in v9:
time: 100 us; the launch traced here: 99.6 us
  Pallas kernels  53.2 us (53%)
  starting transfers between devices  23 us (23%)
  waiting for transfers between devices  13.9 us (14%)
  local copies, waits for them, and re-layouts  8.18 us (8%)
    pallas_call x5, Pallas kernels, stack_tiles(): pl.pallas_call(functools.partial(stack_kernel, segments=described, source...  38.4 us
    ppermute x7, starting transfers between devices, local(): lax.ppermute(chunks[step], 'vel', [(i, i ^ step) for i in range(blocks)])  14.7 us
    pallas_call x1, Pallas kernels, correlate(): pl.pallas_call(correlate_kernel, in_specs=[pl.BlockSpec(memory_space=pltp...  8.55 us
    unnamed x11, local copies, waits for them, and re-layouts  5.99 us
    pallas_call x1, Pallas kernels, make_bands(): pl.pallas_call(band_kernel, in_specs=[pl.BlockSpec(memory_space=pltpu.SME...  4.59 us
    ppermute x7, waiting for transfers between devices, local(): lax.ppermute(chunks[step], 'vel', [(i, i ^ step) for i in range(blocks)])  3.56 us
    ppermute x1, waiting for transfers between devices, local(): lax.ppermute(payload, 'vel', left)  3.08 us
    ppermute x2, starting transfers between devices, local(): lax.ppermute(behind, 'vel', right)  2.72 us
  transfers between devices with their start and end apart: 20, of which 13 were waited for; matrix products, arithmetic and copies ran while one was open for 4% of the time, Pallas kernels for 37%

profile of v9, /device:TPU:0, one launch (start us, length us, event | category | flops | bytes accessed | tf_op | source)
XLA Modules:
  0.0 99.6 jit_solution(3409102754630467570)
XLA Ops:
  0.0 1.0 %copy-done = f32[1,32,4096]{2,1,0:T(8,128)S(1)} copy-done((f32[1,32,4096]{2,1,0:T(8,128)S(1)}, f32[1,32,4096]{2,1,0:T(8,128)}, u32[]{:S(2)}) %copy-start) | copy-done | bytes 524312
  1.1 1.0 %copy-done.1 = f32[1,32,4096]{2,1,0:T(8,128)S(1)} copy-done((f32[1,32,4096]{2,1,0:T(8,128)S(1)}, f32[1,32,4096]{2,1,0:T(8,128)}, u32[]{:S(2)}) %copy-start.1) | copy-done | bytes 524312
  2.9 6.1 %collective-permute-start = (f32[2,136,128]{2,1,0:T(8,128)S(1)}, f32[2,136,128]{2,1,0:T(8,128)S(1)}, u32[]{:S(2)}, u32[]{:S(2)}) collective-permute-start(f32[2,136,128]{2,1,0:T(8,128)S(1)} %get-tuple-element.33), channel_id=1, source_target_pairs={{0,14},{2,12},{4,10},{6,8},{8,6},{10,4},{12,2},{14,0},{1,15},{3,13... | collective-permute-start | bytes 417800 | tf_op jit(solution)/shard_map/ppermute | solution.py:402
  9.5 3.0 %collective-permute-start.3 = (f32[2,136,128]{2,1,0:T(8,128)S(1)}, f32[2,136,128]{2,1,0:T(8,128)S(1)}, u32[]{:S(2)}, u32[]{:S(2)}) collective-permute-start(f32[2,136,128]{2,1,0:T(8,128)S(1)} %get-tuple-element.42), channel_id=1, source_target_pairs={{0,6},{2,4},{4,2},{6,0},{8,14},{10,12},{12,10},{14,8},{1,7},{3,5},... | collective-permute-start | bytes 417800 | tf_op jit(solution)/shard_map/ppermute | solution.py:402
  12.5 1.1 %collective-permute-done.refs_7_ = f32[2,136,128]{2,1,0:T(8,128)S(1)} collective-permute-done((f32[2,136,128]{2,1,0:T(8,128)S(1)}, f32[2,136,128]{2,1,0:T(8,128)S(1)}, u32[]{:S(2)}, u32[]{:S(2)}) %collective-permute-start) | collective-permute-done | bytes 139296 | tf_op jit(solution)/shard_map/ppermute | solution.py:402
  13.5 4.8 %collective-permute-start.5 = (f32[2,136,128]{2,1,0:T(8,128)S(1)}, f32[2,136,128]{2,1,0:T(8,128)S(1)}, u32[]{:S(2)}, u32[]{:S(2)}) collective-permute-start(f32[2,136,128]{2,1,0:T(8,128)S(1)} %get-tuple-element.44), channel_id=1, source_target_pairs={{0,10},{2,8},{4,14},{6,12},{8,2},{10,0},{12,6},{14,4},{1,11},{3,9}... | collective-permute-start | bytes 417800 | tf_op jit(solution)/shard_map/ppermute | solution.py:402
  21.7 4.6 %shard_map.65 = (bf16[2,21,256,256]{3,2,1,0:T(8,128)(2,1)S(1)}, f32[8,128]{1,0:T(8,128)S(1)}) custom-call(f32[441]{0:T(512)S(1)} %reshape.10.taps, f32[21,21]{1,0:T(8,128)S(1)} %copy-done.2), custom_call_target="tpu_custom_call" | custom-call | bytes 20971520 | tf_op jit(solution)/shard_map/pallas_call | solution.py:43
  26.3 2.4 %copy-done.3 = bf16[2,21,256,256]{3,2,1,0:T(8,128)(2,1)} copy-done((bf16[2,21,256,256]{3,2,1,0:T(8,128)(2,1)}, bf16[2,21,256,256]{3,2,1,0:T(8,128)(2,1)S(1)}, u32[]{:S(2)}) %copy-start.3) | copy-done | bytes 5505048
  28.9 2.4 %collective-permute-done.5.refs_5_ = f32[2,136,128]{2,1,0:T(8,128)S(1)} collective-permute-done((f32[2,136,128]{2,1,0:T(8,128)S(1)}, f32[2,136,128]{2,1,0:T(8,128)S(1)}, u32[]{:S(2)}, u32[]{:S(2)}) %collective-permute-start.5) | collective-permute-done | bytes 139296 | tf_op jit(solution)/shard_map/ppermute | solution.py:402
  32.3 1.4 %collective-permute-done.7.border = f32[3,2,5,16,128]{4,3,2,1,0:T(8,128)S(1)} collective-permute-done((f32[3,2,5,16,128]{4,3,2,1,0:T(8,128)S(1)}, f32[3,2,5,16,128]{4,3,2,1,0:T(8,128)S(1)}, u32[]{:S(2)}, u32[]{:S(2)}) %collective-permute-start.7) | collective-permute-done | bytes 245792 | tf_op jit(solution)/shard_map/ppermute | solution.py:407
  33.7 8.5 %shard_map.67.refs_0_.refs_2_ = f32[2,3,2,4,16,128]{5,4,3,2,1,0:T(8,128)S(1)} custom-call(s32[2]{0:T(128)S(1)} %pad_add_fusion.1.place, f32[3,2,5,32,128]{4,3,2,1,0:T(8,128)S(1)} %get-tuple-element.47.own, f32[3,2,5,16,128]{4,3,2,1,0:T(8,128)S(1)} %collective-permute-done.7.border, bf16[2,21,256,256]{3,2,1,0:T(8,128)(2,1)} %copy-done.3), custom_call_target="tpu_custom_call" | custom-call | flops 5637144576 | bytes 12582912 | tf_op jit(solution)/shard_map/pallas_call | solution.py:215
  42.3 1.5 %collective-permute-start.9 = (f32[2,3,2,4,16,128]{5,4,3,2,1,0:T(8,128)S(1)}, f32[2,3,2,4,16,128]{5,4,3,2,1,0:T(8,128)S(1)}, u32[]{:S(2)}, u32[]{:S(2)}) collective-permute-start(f32[2,3,2,4,16,128]{5,4,3,2,1,0:T(8,128)S(1)} %shard_map.67.refs_0_.refs_2_), channel_id=1, source_target_pairs={{4,0},{8,4},{12,8},{14,12},{10,14},{6,10},{2,6},{0,2},{5,1},{9,5},... | collective-permute-start | bytes 1179656 | tf_op jit(solution)/shard_map/ppermute | solution.py:424
  45.9 4.7 %shard_map.68.refs_5_ = f32[36,32,4096]{2,1,0:T(8,128)} custom-call(s32[4]{0:T(128)S(1)} %pad_add_fusion.2.place, s32[216]{0:T(256)S(1)} %add.193.shifts, f32[1]{0:T(128)} %bitcast.9.floor, f32[2,3,2,4,16,128]{5,4,3,2,1,0:T(8,128)S(1)} %shard_map.67.refs_0_.refs_2_, f32[1,3,2,4,16,128]{5,4,3,2,1,0:T(8,128)S(1)} %collective-permute-done.10.refs_1_.refs_3_), custom_call_target="tpu_custom_call" | custom-call | flops 7077888 | bytes 10616832 | tf_op jit(solution)/shard_map/pallas_call | solution.py:352
  50.7 3.1 %collective-permute-done.9.refs_4_ = f32[2,3,2,4,16,128]{5,4,3,2,1,0:T(8,128)S(1)} collective-permute-done((f32[2,3,2,4,16,128]{5,4,3,2,1,0:T(8,128)S(1)}, f32[2,3,2,4,16,128]{5,4,3,2,1,0:T(8,128)S(1)}, u32[]{:S(2)}, u32[]{:S(2)}) %collective-permute-start.9) | collective-permute-done | bytes 393248 | tf_op jit(solution)/shard_map/ppermute | solution.py:424
  54.8 1.0 collective-permute-start.11
  55.8 1.1 %collective-permute-start.12 = (f32[2,3,2,4,16,128]{5,4,3,2,1,0:T(8,128)S(1)}, f32[2,3,2,4,16,128]{5,4,3,2,1,0:T(8,128)S(1)}, u32[]{:S(2)}, u32[]{:S(2)}) collective-permute-start(f32[2,3,2,4,16,128]{5,4,3,2,1,0:T(8,128)S(1)} %collective-permute-done.9.refs_4_), channel_id=1, source_target_pairs={{4,0},{8,4},{12,8},{14,12},{10,14},{6,10},{2,6},{0,2},{5,1},{9,5},... | collective-permute-start | bytes 1179656 | tf_op jit(solution)/shard_map/ppermute | solution.py:431
  57.0 9.1 %shard_map.69.refs_6_ = f32[36,32,4096]{2,1,0:T(8,128)} custom-call(s32[9]{0:T(128)S(1)} %stack.151.place, s32[216]{0:T(256)S(1)} %add.193.shifts, f32[1]{0:T(128)} %bitcast.9.floor, f32[2,3,2,4,16,128]{5,4,3,2,1,0:T(8,128)S(1)} %collective-permute-done.8.refs_0_.refs_2_, ...), custom_call_target="tpu_custom_call", output_to_operand_aliasing={{}: (8, {})} | custom-call | flops 18874368 | bytes 28311552 | tf_op jit(solution)/shard_map/pallas_call | solution.py:352
  67.1 1.7 %collective-permute-start.14 = (f32[2,3,2,4,16,128]{5,4,3,2,1,0:T(8,128)S(1)}, f32[2,3,2,4,16,128]{5,4,3,2,1,0:T(8,128)S(1)}, u32[]{:S(2)}, u32[]{:S(2)}) collective-permute-start(f32[2,3,2,4,16,128]{5,4,3,2,1,0:T(8,128)S(1)} %collective-permute-done.11.refs_0_.refs_2_), channel_id=1, source_target_pairs={{0,4},{4,8},{8,12},{12,14},{14,10},{10,6},{6,2},{2,0},{1,5},{5,9},... | collective-permute-start | bytes 1179656 | tf_op jit(solution)/shard_map/ppermute | solution.py:431
  69.3 9.1 %shard_map.70.refs_6_ = f32[36,32,4096]{2,1,0:T(8,128)} custom-call(s32[9]{0:T(128)S(1)} %stack.160.place, s32[216]{0:T(256)S(1)} %add.193.shifts, f32[1]{0:T(128)} %bitcast.9.floor, f32[2,3,2,4,16,128]{5,4,3,2,1,0:T(8,128)S(1)} %collective-permute-done.11.refs_0_.refs_2_, ...), custom_call_target="tpu_custom_call", output_to_operand_aliasing={{}: (9, {})} | custom-call | flops 18874368 | bytes 28311552 | tf_op jit(solution)/shard_map/pallas_call | solution.py:352
  78.6 1.4 %collective-permute-done.15.refs_5_.refs_0_ = f32[2,3,2,4,16,128]{5,4,3,2,1,0:T(8,128)S(1)} collective-permute-done((f32[2,3,2,4,16,128]{5,4,3,2,1,0:T(8,128)S(1)}, f32[2,3,2,4,16,128]{5,4,3,2,1,0:T(8,128)S(1)}, u32[]{:S(2)}, u32[]{:S(2)}) %collective-permute-start.15) | collective-permute-done | bytes 393248 | tf_op jit(solution)/shard_map/ppermute | solution.py:431
  80.2 1.6 %collective-permute-start.18 = (f32[2,3,2,4,16,128]{5,4,3,2,1,0:T(8,128)S(1)}, f32[2,3,2,4,16,128]{5,4,3,2,1,0:T(8,128)S(1)}, u32[]{:S(2)}, u32[]{:S(2)}) collective-permute-start(f32[2,3,2,4,16,128]{5,4,3,2,1,0:T(8,128)S(1)} %collective-permute-done.14.refs_0_.refs_4_), channel_id=1, source_target_pairs={{0,4},{4,8},{8,12},{12,14},{14,10},{10,6},{6,2},{2,0},{1,5},{5,9},... | collective-permute-start | bytes 1179656 | tf_op jit(solution)/shard_map/ppermute | solution.py:438
  81.9 9.1 %shard_map.71.refs_5_ = f32[36,32,4096]{2,1,0:T(8,128)} custom-call(s32[9]{0:T(128)S(1)} %stack.169.place, s32[216]{0:T(256)S(1)} %add.193.shifts, f32[1]{0:T(128)} %bitcast.9.floor, f32[2,3,2,4,16,128]{5,4,3,2,1,0:T(8,128)S(1)} %collective-permute-done.14.refs_0_.refs_4_, ...), custom_call_target="tpu_custom_call", output_to_operand_aliasing={{}: (9, {})} | custom-call | flops 18874368 | bytes 28311552 | tf_op jit(solution)/shard_map/pallas_call | solution.py:352
  91.9 1.3 %collective-permute-done.19.refs_3_ = f32[1,3,2,4,16,128]{5,4,3,2,1,0:T(8,128)S(1)} collective-permute-done((f32[1,3,2,4,16,128]{5,4,3,2,1,0:T(8,128)S(1)}, f32[1,3,2,4,16,128]{5,4,3,2,1,0:T(8,128)S(1)}, u32[]{:S(2)}, u32[]{:S(2)}) %collective-permute-start.19) | collective-permute-done | bytes 196640 | tf_op jit(solution)/shard_map/ppermute | solution.py:440
  93.2 6.4 %shard_map.72 = f32[36,32,4096]{2,1,0:T(8,128)} custom-call(s32[6]{0:T(128)S(1)} %stack.135.place, s32[216]{0:T(256)S(1)} %add.193.shifts, f32[1]{0:T(128)} %bitcast.9.floor, f32[2,3,2,4,16,128]{5,4,3,2,1,0:T(8,128)S(1)} %collective-permute-done.15.refs_5_.refs_0_, ...), custom_call_target="tpu_custom_call", output_to_operand_aliasing={{}: (8, {})} | custom-call | flops 11796480 | bytes 17694720 | tf_op jit(solution)/shard_map/pallas_call | solution.py:352
  (61 shorter events, 11.9 us)
Async XLA Ops:
  0.0 44.5 %copy-start.4 = (s32[36,3,2]{0,2,1:T(2,128)S(1)}, s32[36,3,2]{0,2,1:T(2,128)}, u32[]{:S(2)}) copy-start(s32[36,3,2]{0,2,1:T(2,128)} %param.9) | copy-start | bytes 2596
  0.0 1.0 %copy-start = (f32[1,32,4096]{2,1,0:T(8,128)S(1)}, f32[1,32,4096]{2,1,0:T(8,128)}, u32[]{:S(2)}) copy-start(f32[1,32,4096]{2,1,0:T(8,128)} %param.6) | copy-start | bytes 1572868
  1.1 1.0 %copy-start.1 = (f32[1,32,4096]{2,1,0:T(8,128)S(1)}, f32[1,32,4096]{2,1,0:T(8,128)}, u32[]{:S(2)}) copy-start(f32[1,32,4096]{2,1,0:T(8,128)} %param.7) | copy-start | bytes 1572868
  2.9 10.6 %collective-permute-start = (f32[2,136,128]{2,1,0:T(8,128)S(1)}, f32[2,136,128]{2,1,0:T(8,128)S(1)}, u32[]{:S(2)}, u32[]{:S(2)}) collective-permute-start(f32[2,136,128]{2,1,0:T(8,128)S(1)} %get-tuple-element.33), channel_id=1, source_target_pairs={{0,14},{2,12},{4,10},{6,8},{8,6},{10,4},{12,2},{14,0},{1,15},{3,13... | collective-permute-start | bytes 417800 | tf_op jit(solution)/shard_map/ppermute | solution.py:402
  9.0 9.3 %collective-permute-start.1 = (f32[2,136,128]{2,1,0:T(8,128)S(1)}, f32[2,136,128]{2,1,0:T(8,128)S(1)}, u32[]{:S(2)}, u32[]{:S(2)}) collective-permute-start(f32[2,136,128]{2,1,0:T(8,128)S(1)} %get-tuple-element.34), channel_id=1, source_target_pairs={{0,2},{2,0},{4,6},{6,4},{8,10},{10,8},{12,14},{14,12},{1,3},{3,1},... | collective-permute-start | bytes 417800 | tf_op jit(solution)/shard_map/ppermute | solution.py:402
  9.5 19.3 %collective-permute-start.2 = (f32[2,136,128]{2,1,0:T(8,128)S(1)}, f32[2,136,128]{2,1,0:T(8,128)S(1)}, u32[]{:S(2)}, u32[]{:S(2)}) collective-permute-start(f32[2,136,128]{2,1,0:T(8,128)S(1)} %get-tuple-element.41), channel_id=1, source_target_pairs={{0,4},{2,6},{4,0},{6,2},{8,12},{10,14},{12,8},{14,10},{1,5},{3,7},... | collective-permute-start | bytes 417800 | tf_op jit(solution)/shard_map/ppermute | solution.py:402
  9.5 19.3 %collective-permute-start.3 = (f32[2,136,128]{2,1,0:T(8,128)S(1)}, f32[2,136,128]{2,1,0:T(8,128)S(1)}, u32[]{:S(2)}, u32[]{:S(2)}) collective-permute-start(f32[2,136,128]{2,1,0:T(8,128)S(1)} %get-tuple-element.42), channel_id=1, source_target_pairs={{0,6},{2,4},{4,2},{6,0},{8,14},{10,12},{12,10},{14,8},{1,7},{3,5},... | collective-permute-start | bytes 417800 | tf_op jit(solution)/shard_map/ppermute | solution.py:402
  12.5 16.5 %collective-permute-start.4 = (f32[2,136,128]{2,1,0:T(8,128)S(1)}, f32[2,136,128]{2,1,0:T(8,128)S(1)}, u32[]{:S(2)}, u32[]{:S(2)}) collective-permute-start(f32[2,136,128]{2,1,0:T(8,128)S(1)} %get-tuple-element.43), channel_id=1, source_target_pairs={{0,8},{2,10},{4,12},{6,14},{8,0},{10,2},{12,4},{14,6},{1,9},{3,11}... | collective-permute-start | bytes 417800 | tf_op jit(solution)/shard_map/ppermute | solution.py:402
  13.5 17.8 %collective-permute-start.5 = (f32[2,136,128]{2,1,0:T(8,128)S(1)}, f32[2,136,128]{2,1,0:T(8,128)S(1)}, u32[]{:S(2)}, u32[]{:S(2)}) collective-permute-start(f32[2,136,128]{2,1,0:T(8,128)S(1)} %get-tuple-element.44), channel_id=1, source_target_pairs={{0,10},{2,8},{4,14},{6,12},{8,2},{10,0},{12,6},{14,4},{1,11},{3,9}... | collective-permute-start | bytes 417800 | tf_op jit(solution)/shard_map/ppermute | solution.py:402
  18.3 13.0 %collective-permute-start.6 = (f32[2,136,128]{2,1,0:T(8,128)S(1)}, f32[2,136,128]{2,1,0:T(8,128)S(1)}, u32[]{:S(2)}, u32[]{:S(2)}) collective-permute-start(f32[2,136,128]{2,1,0:T(8,128)S(1)} %get-tuple-element.45), channel_id=1, source_target_pairs={{0,12},{2,14},{4,8},{6,10},{8,4},{10,6},{12,0},{14,2},{1,13},{3,15... | collective-permute-start | bytes 417800 | tf_op jit(solution)/shard_map/ppermute | solution.py:402
  26.3 2.4 %copy-start.3 = (bf16[2,21,256,256]{3,2,1,0:T(8,128)(2,1)}, bf16[2,21,256,256]{3,2,1,0:T(8,128)(2,1)S(1)}, u32[]{:S(2)}) copy-start(bf16[2,21,256,256]{3,2,1,0:T(8,128)(2,1)S(1)} %get-tuple-element.49.bands_hbm) | copy-start | bytes 16515076
  32.2 1.6 %collective-permute-start.7 = (f32[3,2,5,16,128]{4,3,2,1,0:T(8,128)S(1)}, f32[3,2,5,16,128]{4,3,2,1,0:T(8,128)S(1)}, u32[]{:S(2)}, u32[]{:S(2)}) collective-permute-start(f32[3,2,5,16,128]{4,3,2,1,0:T(8,128)S(1)} %get-tuple-element.48), channel_id=1, source_target_pairs={{0,1},{1,0},{2,3},{3,2},{4,5},{5,4},{6,7},{7,6},{8,9},{9,8},{10,11... | collective-permute-start | bytes 737288 | tf_op jit(solution)/shard_map/ppermute | solution.py:407
  42.3 11.5 %collective-permute-start.9 = (f32[2,3,2,4,16,128]{5,4,3,2,1,0:T(8,128)S(1)}, f32[2,3,2,4,16,128]{5,4,3,2,1,0:T(8,128)S(1)}, u32[]{:S(2)}, u32[]{:S(2)}) collective-permute-start(f32[2,3,2,4,16,128]{5,4,3,2,1,0:T(8,128)S(1)} %shard_map.67.refs_0_.refs_2_), channel_id=1, source_target_pairs={{4,0},{8,4},{12,8},{14,12},{10,14},{6,10},{2,6},{0,2},{5,1},{9,5},... | collective-permute-start | bytes 1179656 | tf_op jit(solution)/shard_map/ppermute | solution.py:424
  43.8 10.9 %collective-permute-start.8 = (f32[2,3,2,4,16,128]{5,4,3,2,1,0:T(8,128)S(1)}, f32[2,3,2,4,16,128]{5,4,3,2,1,0:T(8,128)S(1)}, u32[]{:S(2)}, u32[]{:S(2)}) collective-permute-start(f32[2,3,2,4,16,128]{5,4,3,2,1,0:T(8,128)S(1)} %shard_map.67.refs_0_.refs_2_), channel_id=1, source_target_pairs={{0,4},{4,8},{8,12},{12,14},{14,10},{10,6},{6,2},{2,0},{1,5},{5,9},... | collective-permute-start | bytes 1179656 | tf_op jit(solution)/shard_map/ppermute | solution.py:424
  44.4 1.5 %collective-permute-start.10 = (f32[1,3,2,4,16,128]{5,4,3,2,1,0:T(8,128)S(1)}, f32[1,3,2,4,16,128]{5,4,3,2,1,0:T(8,128)S(1)}, u32[]{:S(2)}, u32[]{:S(2)}) collective-permute-start(f32[1,3,2,4,16,128]{5,4,3,2,1,0:T(8,128)S(1)} %slice.36), channel_id=1, source_target_pairs={{0,1},{1,0},{2,3},{3,2},{4,5},{5,4},{6,7},{7,6},{8,9},{9,8},{10,11... | collective-permute-start | bytes 589832 | tf_op jit(solution)/shard_map/ppermute | solution.py:425
  54.7 2.2 %collective-permute-start.13 = (f32[2,3,2,4,16,128]{5,4,3,2,1,0:T(8,128)S(1)}, f32[2,3,2,4,16,128]{5,4,3,2,1,0:T(8,128)S(1)}, u32[]{:S(2)}, u32[]{:S(2)}) collective-permute-start(f32[2,3,2,4,16,128]{5,4,3,2,1,0:T(8,128)S(1)} %pad_maximum_fusion), channel_id=1, source_target_pairs={{0,1},{1,0},{2,3},{3,2},{4,5},{5,4},{6,7},{7,6},{8,9},{9,8},{10,11... | collective-permute-start | bytes 1179656 | tf_op jit(solution)/shard_map/ppermute | solution.py:433
  54.8 11.5 %collective-permute-start.11 = (f32[2,3,2,4,16,128]{5,4,3,2,1,0:T(8,128)S(1)}, f32[2,3,2,4,16,128]{5,4,3,2,1,0:T(8,128)S(1)}, u32[]{:S(2)}, u32[]{:S(2)}) collective-permute-start(f32[2,3,2,4,16,128]{5,4,3,2,1,0:T(8,128)S(1)} %collective-permute-done.8.refs_0_.refs_2_), channel_id=1, source_target_pairs={{0,4},{4,8},{8,12},{12,14},{14,10},{10,6},{6,2},{2,0},{1,5},{5,9},... | collective-permute-start | bytes 1179656 | tf_op jit(solution)/shard_map/ppermute | solution.py:431
  55.8 11.2 %collective-permute-start.12 = (f32[2,3,2,4,16,128]{5,4,3,2,1,0:T(8,128)S(1)}, f32[2,3,2,4,16,128]{5,4,3,2,1,0:T(8,128)S(1)}, u32[]{:S(2)}, u32[]{:S(2)}) collective-permute-start(f32[2,3,2,4,16,128]{5,4,3,2,1,0:T(8,128)S(1)} %collective-permute-done.9.refs_4_), channel_id=1, source_target_pairs={{4,0},{8,4},{12,8},{14,12},{10,14},{6,10},{2,6},{0,2},{5,1},{9,5},... | collective-permute-start | bytes 1179656 | tf_op jit(solution)/shard_map/ppermute | solution.py:431
  67.0 2.2 %collective-permute-start.16 = (f32[2,3,2,4,16,128]{5,4,3,2,1,0:T(8,128)S(1)}, f32[2,3,2,4,16,128]{5,4,3,2,1,0:T(8,128)S(1)}, u32[]{:S(2)}, u32[]{:S(2)}) collective-permute-start(f32[2,3,2,4,16,128]{5,4,3,2,1,0:T(8,128)S(1)} %pad_maximum_fusion.1), channel_id=1, source_target_pairs={{0,1},{1,0},{2,3},{3,2},{4,5},{5,4},{6,7},{7,6},{8,9},{9,8},{10,11... | collective-permute-start | bytes 1179656 | tf_op jit(solution)/shard_map/ppermute | solution.py:433
  67.1 11.5 %collective-permute-start.14 = (f32[2,3,2,4,16,128]{5,4,3,2,1,0:T(8,128)S(1)}, f32[2,3,2,4,16,128]{5,4,3,2,1,0:T(8,128)S(1)}, u32[]{:S(2)}, u32[]{:S(2)}) collective-permute-start(f32[2,3,2,4,16,128]{5,4,3,2,1,0:T(8,128)S(1)} %collective-permute-done.11.refs_0_.refs_2_), channel_id=1, source_target_pairs={{0,4},{4,8},{8,12},{12,14},{14,10},{10,6},{6,2},{2,0},{1,5},{5,9},... | collective-permute-start | bytes 1179656 | tf_op jit(solution)/shard_map/ppermute | solution.py:431
  68.8 11.2 %collective-permute-start.15 = (f32[2,3,2,4,16,128]{5,4,3,2,1,0:T(8,128)S(1)}, f32[2,3,2,4,16,128]{5,4,3,2,1,0:T(8,128)S(1)}, u32[]{:S(2)}, u32[]{:S(2)}) collective-permute-start(f32[2,3,2,4,16,128]{5,4,3,2,1,0:T(8,128)S(1)} %collective-permute-done.12.refs_5_.refs_4_), channel_id=1, source_target_pairs={{4,0},{8,4},{12,8},{14,12},{10,14},{6,10},{2,6},{0,2},{5,1},{9,5},... | collective-permute-start | bytes 1179656 | tf_op jit(solution)/shard_map/ppermute | solution.py:431
  80.1 1.8 %collective-permute-start.17 = (f32[2,3,2,4,16,128]{5,4,3,2,1,0:T(8,128)S(1)}, f32[2,3,2,4,16,128]{5,4,3,2,1,0:T(8,128)S(1)}, u32[]{:S(2)}, u32[]{:S(2)}) collective-permute-start(f32[2,3,2,4,16,128]{5,4,3,2,1,0:T(8,128)S(1)} %pad_maximum_fusion.2), channel_id=1, source_target_pairs={{0,1},{1,0},{2,3},{3,2},{4,5},{5,4},{6,7},{7,6},{8,9},{9,8},{10,11... | collective-permute-start | bytes 1179656 | tf_op jit(solution)/shard_map/ppermute | solution.py:433
  80.2 11.5 %collective-permute-start.18 = (f32[2,3,2,4,16,128]{5,4,3,2,1,0:T(8,128)S(1)}, f32[2,3,2,4,16,128]{5,4,3,2,1,0:T(8,128)S(1)}, u32[]{:S(2)}, u32[]{:S(2)}) collective-permute-start(f32[2,3,2,4,16,128]{5,4,3,2,1,0:T(8,128)S(1)} %collective-permute-done.14.refs_0_.refs_4_), channel_id=1, source_target_pairs={{0,4},{4,8},{8,12},{12,14},{14,10},{10,6},{6,2},{2,0},{1,5},{5,9},... | collective-permute-start | bytes 1179656 | tf_op jit(solution)/shard_map/ppermute | solution.py:438
  91.7 1.5 %collective-permute-start.19 = (f32[1,3,2,4,16,128]{5,4,3,2,1,0:T(8,128)S(1)}, f32[1,3,2,4,16,128]{5,4,3,2,1,0:T(8,128)S(1)}, u32[]{:S(2)}, u32[]{:S(2)}) collective-permute-start(f32[1,3,2,4,16,128]{5,4,3,2,1,0:T(8,128)S(1)} %slice.35), channel_id=1, source_target_pairs={{0,1},{1,0},{2,3},{3,2},{4,5},{5,4},{6,7},{7,6},{8,9},{9,8},{10,11... | collective-permute-start | bytes 589832 | tf_op jit(solution)/shard_map/ppermute | solution.py:440
  (1 other events, 0.7 us)

commit v10 on v9

--- a/solution.py
+++ b/solution.py
@@ -13,16 +13,25 @@
 LARGE = 50 << 20
 
 
+FOLD = LANES // HALO
+
+
+def band_row(row, ksize):
+    group, place = row // FOLD, row % FOLD
+    base = group * (FOLD + 1) * LANES
+    count = min(FOLD, ksize - group * FOLD) if isinstance(row, int) else jnp.minimum(FOLD, ksize - group * FOLD)
+    return base + place * LANES, base + count * LANES + place * HALO
+
+
 def band_kernel(taps, kernel, bands_ref, floor_ref):
     ksize = kernel.shape[0]
-    skip = LANES - MAXS - ksize // 2
-    top = skip // 8 * 8
-    shape = (2 * LANES - top, LANES)
-    offset = lax.broadcasted_iota(jnp.int32, shape, 0) - lax.broadcasted_iota(jnp.int32, shape, 1) + (top - skip)
+    skip = HALO - MAXS - ksize // 2
+    shape = (HALO + LANES, LANES)
+    offset = lax.broadcasted_iota(jnp.int32, shape, 0) - lax.broadcasted_iota(jnp.int32, shape, 1) - skip
     total = jnp.full((8, LANES), jnp.sum(kernel[...]), jnp.float32)
     norm = kernel[...] / total[:1, :1]
     floor_ref[...] = jnp.full(floor_ref.shape, 0.5 * jnp.sum(norm * norm), jnp.float32)
-    bands_ref[:, :, :top] = jnp.zeros(bands_ref.shape[:2] + (top, 2 * LANES), jnp.bfloat16)
+    bands_ref[:, -LANES:] = jnp.zeros((2, LANES, 2 * LANES), jnp.bfloat16)
 
     def one(row, _):
         band = jnp.zeros(shape, jnp.float32)
@@ -31,8 +40,10 @@
         band = band / total[:1]
         for kind, value in enumerate((band, band * band)):
             high = value.astype(jnp.bfloat16)
-            bands_ref[kind, row, top:, :LANES] = high
-            bands_ref[kind, row, top:, LANES:] = (value - high.astype(jnp.float32)).astype(jnp.bfloat16)
+            both = jnp.concatenate([high, (value - high.astype(jnp.float32)).astype(jnp.bfloat16)], axis=1)
+            main, halo = (pl.multiple_of(at, HALO) for at in band_row(row, ksize))
+            bands_ref[kind, pl.ds(main, LANES)] = both[HALO:]
+            bands_ref[kind, pl.ds(halo, HALO)] = both[:HALO]
         return 0
 
     lax.fori_loop(0, ksize, one, 0)
@@ -45,7 +56,7 @@
         in_specs=[pl.BlockSpec(memory_space=pltpu.SMEM), pl.BlockSpec(memory_space=pltpu.VMEM)],
         out_specs=[pl.BlockSpec(memory_space=pltpu.VMEM)] * 2,
         out_shape=[
-            jax.ShapeDtypeStruct((2, ksize, 2 * LANES, 2 * LANES), jnp.bfloat16),
+            jax.ShapeDtypeStruct((2, (ksize - (-ksize // FOLD)) * LANES, 2 * LANES), jnp.bfloat16),
             jax.ShapeDtypeStruct((8, LANES), jnp.float32),
         ],
         compiler_params=pltpu.CompilerParams(vmem_limit_bytes=VMEM),
@@ -139,10 +150,9 @@
     )(numbers, *chunks)
 
 
-def correlate_kernel(place, own, border, bands_hbm, rows_ref, ext, high, low, summed, bands_ref, arrived):
+def correlate_kernel(place, own, border, bands_hbm, rows_ref, ext, high, low, summed, bands_ref, arrived, *, ksize):
     epochs, kinds, count, height, _ = own.shape
     tiles = count - 1
-    ksize = bands_ref.shape[1]
     members = high.shape[2] // (height + 2 * MAXS)
     copies = [pltpu.make_async_copy(bands_hbm.at[kind], bands_ref.at[kind], arrived.at[kind]) for kind in range(kinds)]
     for copy in copies:
@@ -170,26 +180,34 @@
             put(kind, 0, base + tiles, own[epoch, kind, 0], border[epoch, kind, 0])
             put(kind, 1, base + tiles, nothing, nothing[:MAXS])
 
+    lanes = lax.broadcasted_iota(jnp.int32, (128, LANES), 1)
+
     def split(index, _):
         rows = pl.ds(pl.multiple_of(index * 128, 128), 128)
         for kind in range(kinds):
-            for half in range(2):
-                value = ext[kind, half, rows]
+            halo = jnp.zeros((128, LANES), jnp.float32)
+            for fold in range(FOLD):
+                ahead = ext[kind, 0, pl.ds(pl.multiple_of(index * 128 + fold * members, 16), 128)]
+                halo = jnp.where(lanes // HALO == fold, pltpu.roll(ahead, (fold + 1) * HALO % LANES, 1), halo)
+            for half, value in enumerate((halo, ext[kind, 1, rows])):
                 part = value.astype(jnp.bfloat16)
                 high[kind, half, rows] = part
                 low[kind, half, rows] = (value - part.astype(jnp.float32)).astype(jnp.bfloat16)
         return 0
 
-    lax.fori_loop(0, ext.shape[2] // 128, split, 0)
+    lax.fori_loop(0, high.shape[2] // 128, split, 0, unroll=4)
 
     lane = lax.broadcasted_iota(jnp.int32, (MAXS, LANES), 1)
     wrapped = jnp.logical_and(first, lane < MAXS)
     for kind in range(kinds):
         offsets = [pl.ds((row + MAXS - ksize // 2) * members, summed_rows) for row in range(ksize)]
-        upper = jnp.concatenate([high[kind, half, rows] for rows in offsets for half in range(2)], axis=1)
-        rest = jnp.concatenate([low[kind, half, rows] for rows in offsets for half in range(2)], axis=1)
+        parts = []
+        for base in range(0, ksize, FOLD):
+            parts += [(1, rows) for rows in offsets[base : base + FOLD]] + [(0, offsets[base])]
+        upper = jnp.concatenate([high[kind, half, rows] for half, rows in parts], axis=1)
+        rest = jnp.concatenate([low[kind, half, rows] for half, rows in parts], axis=1)
         copies[kind].wait()
-        weights = bands_ref[kind].reshape(ksize * 2 * LANES, 2 * LANES)
+        weights = bands_ref[kind]
         pair = jnp.dot(upper, weights, preferred_element_type=jnp.float32)
         more = jnp.dot(rest, weights[:, :LANES], preferred_element_type=jnp.float32)
         summed[...] = pair[:, :LANES] + (pair[:, LANES:] + more)
@@ -206,20 +224,20 @@
                     rows_ref[half, epoch, kind, tile] = rows_of(tile)
 
 
-def correlate(place, own, border, bands):
+def correlate(place, own, border, bands, ksize):
     epochs, kinds, count, height, _ = own.shape
     tiles = count - 1
     members = -(-epochs * (tiles + 1) // 16) * 16
     depth = (height + 2 * MAXS) * members
-    flops = 2 * 2 * kinds * members * height * bands.shape[1] * 4 * LANES * LANES
+    flops = 2 * 2 * kinds * members * height * bands.shape[1] * 2 * LANES
     return pl.pallas_call(
-        correlate_kernel,
+        functools.partial(correlate_kernel, ksize=ksize),
         in_specs=[pl.BlockSpec(memory_space=pltpu.SMEM)] + [pl.BlockSpec(memory_space=pltpu.VMEM)] * 2
         + [pl.BlockSpec(memory_space=pltpu.HBM)],
         out_specs=pl.BlockSpec(memory_space=pltpu.VMEM),
         out_shape=jax.ShapeDtypeStruct((2, epochs, kinds, tiles, MAXS, LANES), jnp.float32),
         scratch_shapes=[
-            pltpu.VMEM((kinds, 2, depth, LANES), jnp.float32),
+            pltpu.VMEM((kinds, 2, depth + (FOLD - 1) * members, LANES), jnp.float32),
             pltpu.VMEM((kinds, 2, depth, LANES), jnp.bfloat16),
             pltpu.VMEM((kinds, 2, depth, LANES), jnp.bfloat16),
             pltpu.VMEM((height * members, LANES), jnp.float32),
@@ -404,7 +422,7 @@
     bands, floor = make_bands(spread_kernel)
     chunks[-1], floor = lax.optimization_barrier((chunks[-1], floor))
     own, edges = pick(numbers, epoch_owner.shape[0], chunks, height)
-    payload = correlate(place, own, lax.ppermute(edges, "rows", swap), bands)
+    payload = correlate(place, own, lax.ppermute(edges, "rows", swap), bands, spread_kernel.shape[0])
 
     flat_shifts, floor = shifts.reshape(-1), floor[0, :1]
     out_shape = jax.ShapeDtypeStruct((shifts.shape[0], height, columns), jnp.float32)

time: 100 us -> 98.1 us (0.981)
  Pallas kernels: 53.2 us -> 51 us
    pallas_call x1, Pallas kernels: 8.55 us -> 6.67 us  [correlate(): pl.pallas_call(functools.partial(correlate_kernel, ksize=ksize), in_specs...]
    unnamed x11 -> x9, local copies, waits for them, and re-layouts: 5.99 us -> 5.33 us
  transfers between devices with their start and end apart: 20 -> 20, of which waited for: 13 -> 12; matrix products, arithmetic and copies ran while one was open for 4% -> 5% of each run, Pallas kernels for 37% -> 37%
where the time goes in v10:
time: 98.1 us; the launch traced here: 97.7 us
  Pallas kernels  51 us (52%)
  starting transfers between devices  23.2 us (24%)
  waiting for transfers between devices  14 us (14%)
  local copies, waits for them, and re-layouts  7.51 us (8%)
  other arithmetic  1.68 us (2%)
    pallas_call x5, Pallas kernels, stack_tiles(): pl.pallas_call(functools.partial(stack_kernel, segments=described, source...  38.3 us
    ppermute x7, starting transfers between devices, local(): lax.ppermute(chunks[step], 'vel', [(i, i ^ step) for i in range(blocks)])  14.7 us
    pallas_call x1, Pallas kernels, correlate(): pl.pallas_call(functools.partial(correlate_kernel, ksize=ksize), in_specs...  6.67 us
    unnamed x9, local copies, waits for them, and re-layouts  5.33 us
    pallas_call x1, Pallas kernels, make_bands(): pl.pallas_call(band_kernel, in_specs=[pl.BlockSpec(memory_space=pltpu.SME...  4.41 us
    ppermute x7, waiting for transfers between devices, local(): lax.ppermute(chunks[step], 'vel', [(i, i ^ step) for i in range(blocks)])  4.39 us
    ppermute x1, waiting for transfers between devices, local(): lax.ppermute(payload, 'vel', left)  2.91 us
    ppermute x2, starting transfers between devices, local(): lax.ppermute(behind, 'vel', right)  2.72 us
  transfers between devices with their start and end apart: 20, of which 12 were waited for; matrix products, arithmetic and copies ran while one was open for 5% of the time, Pallas kernels for 37%

profile of v10, /device:TPU:0, one launch (start us, length us, event | category | flops | bytes accessed | tf_op | source)
XLA Modules:
  0.0 97.7 jit_solution(1519993161373626037)
XLA Ops:
  0.0 1.0 %copy-done = f32[1,32,4096]{2,1,0:T(8,128)S(1)} copy-done((f32[1,32,4096]{2,1,0:T(8,128)S(1)}, f32[1,32,4096]{2,1,0:T(8,128)}, u32[]{:S(2)}) %copy-start) | copy-done | bytes 524312
  1.1 1.0 %copy-done.1 = f32[1,32,4096]{2,1,0:T(8,128)S(1)} copy-done((f32[1,32,4096]{2,1,0:T(8,128)S(1)}, f32[1,32,4096]{2,1,0:T(8,128)}, u32[]{:S(2)}) %copy-start.1) | copy-done | bytes 524312
  2.9 6.1 %collective-permute-start = (f32[2,136,128]{2,1,0:T(8,128)S(1)}, f32[2,136,128]{2,1,0:T(8,128)S(1)}, u32[]{:S(2)}, u32[]{:S(2)}) collective-permute-start(f32[2,136,128]{2,1,0:T(8,128)S(1)} %get-tuple-element.33), channel_id=1, source_target_pairs={{0,14},{2,12},{4,10},{6,8},{8,6},{10,4},{12,2},{14,0},{1,15},{3,13... | collective-permute-start | bytes 417800 | tf_op jit(solution)/shard_map/ppermute | solution.py:420
  9.5 3.0 %collective-permute-start.3 = (f32[2,136,128]{2,1,0:T(8,128)S(1)}, f32[2,136,128]{2,1,0:T(8,128)S(1)}, u32[]{:S(2)}, u32[]{:S(2)}) collective-permute-start(f32[2,136,128]{2,1,0:T(8,128)S(1)} %get-tuple-element.42), channel_id=1, source_target_pairs={{0,6},{2,4},{4,2},{6,0},{8,14},{10,12},{12,10},{14,8},{1,7},{3,5},... | collective-permute-start | bytes 417800 | tf_op jit(solution)/shard_map/ppermute | solution.py:420
  12.5 1.1 %collective-permute-done.refs_7_ = f32[2,136,128]{2,1,0:T(8,128)S(1)} collective-permute-done((f32[2,136,128]{2,1,0:T(8,128)S(1)}, f32[2,136,128]{2,1,0:T(8,128)S(1)}, u32[]{:S(2)}, u32[]{:S(2)}) %collective-permute-start) | collective-permute-done | bytes 139296 | tf_op jit(solution)/shard_map/ppermute | solution.py:420
  13.5 4.8 %collective-permute-start.5 = (f32[2,136,128]{2,1,0:T(8,128)S(1)}, f32[2,136,128]{2,1,0:T(8,128)S(1)}, u32[]{:S(2)}, u32[]{:S(2)}) collective-permute-start(f32[2,136,128]{2,1,0:T(8,128)S(1)} %get-tuple-element.44), channel_id=1, source_target_pairs={{0,10},{2,8},{4,14},{6,12},{8,2},{10,0},{12,6},{14,4},{1,11},{3,9}... | collective-permute-start | bytes 417800 | tf_op jit(solution)/shard_map/ppermute | solution.py:420
  21.7 4.4 %shard_map.65 = (bf16[2,3456,256]{2,1,0:T(8,128)(2,1)S(1)}, f32[8,128]{1,0:T(8,128)S(1)}) custom-call(f32[441]{0:T(512)S(1)} %reshape.10.taps, f32[21,21]{1,0:T(8,128)S(1)} %copy-done.2), custom_call_target="tpu_custom_call" | custom-call | bytes 20971520 | tf_op jit(solution)/shard_map/pallas_call | solution.py:54
  26.2 1.8 %copy-done.3 = bf16[2,3456,256]{2,1,0:T(8,128)(2,1)} copy-done((bf16[2,3456,256]{2,1,0:T(8,128)(2,1)}, bf16[2,3456,256]{2,1,0:T(8,128)(2,1)S(1)}, u32[]{:S(2)}) %copy-start.3) | copy-done | bytes 3538968
  28.9 2.4 %collective-permute-done.5.refs_5_ = f32[2,136,128]{2,1,0:T(8,128)S(1)} collective-permute-done((f32[2,136,128]{2,1,0:T(8,128)S(1)}, f32[2,136,128]{2,1,0:T(8,128)S(1)}, u32[]{:S(2)}, u32[]{:S(2)}) %collective-permute-start.5) | collective-permute-done | bytes 139296 | tf_op jit(solution)/shard_map/ppermute | solution.py:420
  32.3 1.4 %collective-permute-done.7.border = f32[3,2,5,16,128]{4,3,2,1,0:T(8,128)S(1)} collective-permute-done((f32[3,2,5,16,128]{4,3,2,1,0:T(8,128)S(1)}, f32[3,2,5,16,128]{4,3,2,1,0:T(8,128)S(1)}, u32[]{:S(2)}, u32[]{:S(2)}) %collective-permute-start.7) | collective-permute-done | bytes 245792 | tf_op jit(solution)/shard_map/ppermute | solution.py:425
  33.7 6.7 %shard_map.67.refs_0_.refs_2_ = f32[2,3,2,4,16,128]{5,4,3,2,1,0:T(8,128)S(1)} custom-call(s32[2]{0:T(128)S(1)} %pad_add_fusion.1.place, f32[3,2,5,32,128]{4,3,2,1,0:T(8,128)S(1)} %get-tuple-element.47.own, f32[3,2,5,16,128]{4,3,2,1,0:T(8,128)S(1)} %collective-permute-done.7.border, bf16[2,3456,256]{2,1,0:T(8,128)(2,1)} %copy-done.3), custom_call_target="tpu_custom_call" | custom-call | flops 3623878656 | bytes 12582912 | tf_op jit(solution)/shard_map/pallas_call | solution.py:233
  40.4 1.5 %collective-permute-start.9 = (f32[2,3,2,4,16,128]{5,4,3,2,1,0:T(8,128)S(1)}, f32[2,3,2,4,16,128]{5,4,3,2,1,0:T(8,128)S(1)}, u32[]{:S(2)}, u32[]{:S(2)}) collective-permute-start(f32[2,3,2,4,16,128]{5,4,3,2,1,0:T(8,128)S(1)} %shard_map.67.refs_0_.refs_2_), channel_id=1, source_target_pairs={{4,0},{8,4},{12,8},{14,12},{10,14},{6,10},{2,6},{0,2},{5,1},{9,5},... | collective-permute-start | bytes 1179656 | tf_op jit(solution)/shard_map/ppermute | solution.py:442
  44.2 4.7 %shard_map.68.refs_5_ = f32[36,32,4096]{2,1,0:T(8,128)} custom-call(s32[4]{0:T(128)S(1)} %pad_add_fusion.2.place, s32[216]{0:T(256)S(1)} %add.193.shifts, f32[1]{0:T(128)} %bitcast.9.floor, f32[2,3,2,4,16,128]{5,4,3,2,1,0:T(8,128)S(1)} %shard_map.67.refs_0_.refs_2_, f32[1,3,2,4,16,128]{5,4,3,2,1,0:T(8,128)S(1)} %collective-permute-done.10.refs_1_.refs_3_), custom_call_target="tpu_custom_call" | custom-call | flops 7077888 | bytes 10616832 | tf_op jit(solution)/shard_map/pallas_call | solution.py:370
  49.0 2.9 %collective-permute-done.9.refs_4_ = f32[2,3,2,4,16,128]{5,4,3,2,1,0:T(8,128)S(1)} collective-permute-done((f32[2,3,2,4,16,128]{5,4,3,2,1,0:T(8,128)S(1)}, f32[2,3,2,4,16,128]{5,4,3,2,1,0:T(8,128)S(1)}, u32[]{:S(2)}, u32[]{:S(2)}) %collective-permute-start.9) | collective-permute-done | bytes 393248 | tf_op jit(solution)/shard_map/ppermute | solution.py:442
  52.9 1.0 %collective-permute-start.11 = (f32[2,3,2,4,16,128]{5,4,3,2,1,0:T(8,128)S(1)}, f32[2,3,2,4,16,128]{5,4,3,2,1,0:T(8,128)S(1)}, u32[]{:S(2)}, u32[]{:S(2)}) collective-permute-start(f32[2,3,2,4,16,128]{5,4,3,2,1,0:T(8,128)S(1)} %collective-permute-done.8.refs_0_.refs_2_), channel_id=1, source_target_pairs={{0,4},{4,8},{8,12},{12,14},{14,10},{10,6},{6,2},{2,0},{1,5},{5,9},... | collective-permute-start | bytes 1179656 | tf_op jit(solution)/shard_map/ppermute | solution.py:449
  53.9 1.1 %collective-permute-start.12 = (f32[2,3,2,4,16,128]{5,4,3,2,1,0:T(8,128)S(1)}, f32[2,3,2,4,16,128]{5,4,3,2,1,0:T(8,128)S(1)}, u32[]{:S(2)}, u32[]{:S(2)}) collective-permute-start(f32[2,3,2,4,16,128]{5,4,3,2,1,0:T(8,128)S(1)} %collective-permute-done.9.refs_4_), channel_id=1, source_target_pairs={{4,0},{8,4},{12,8},{14,12},{10,14},{6,10},{2,6},{0,2},{5,1},{9,5},... | collective-permute-start | bytes 1179656 | tf_op jit(solution)/shard_map/ppermute | solution.py:449
  55.1 9.1 %shard_map.69.refs_6_ = f32[36,32,4096]{2,1,0:T(8,128)} custom-call(s32[9]{0:T(128)S(1)} %stack.151.place, s32[216]{0:T(256)S(1)} %add.193.shifts, f32[1]{0:T(128)} %bitcast.9.floor, f32[2,3,2,4,16,128]{5,4,3,2,1,0:T(8,128)S(1)} %collective-permute-done.8.refs_0_.refs_2_, ...), custom_call_target="tpu_custom_call", output_to_operand_aliasing={{}: (8, {})} | custom-call | flops 18874368 | bytes 28311552 | tf_op jit(solution)/shard_map/pallas_call | solution.py:370
  65.2 1.7 %collective-permute-start.14 = (f32[2,3,2,4,16,128]{5,4,3,2,1,0:T(8,128)S(1)}, f32[2,3,2,4,16,128]{5,4,3,2,1,0:T(8,128)S(1)}, u32[]{:S(2)}, u32[]{:S(2)}) collective-permute-start(f32[2,3,2,4,16,128]{5,4,3,2,1,0:T(8,128)S(1)} %collective-permute-done.11.refs_0_.refs_2_), channel_id=1, source_target_pairs={{0,4},{4,8},{8,12},{12,14},{14,10},{10,6},{6,2},{2,0},{1,5},{5,9},... | collective-permute-start | bytes 1179656 | tf_op jit(solution)/shard_map/ppermute | solution.py:449
  67.4 9.1 %shard_map.70.refs_6_ = f32[36,32,4096]{2,1,0:T(8,128)} custom-call(s32[9]{0:T(128)S(1)} %stack.160.place, s32[216]{0:T(256)S(1)} %add.193.shifts, f32[1]{0:T(128)} %bitcast.9.floor, f32[2,3,2,4,16,128]{5,4,3,2,1,0:T(8,128)S(1)} %collective-permute-done.11.refs_0_.refs_2_, ...), custom_call_target="tpu_custom_call", output_to_operand_aliasing={{}: (9, {})} | custom-call | flops 18874368 | bytes 28311552 | tf_op jit(solution)/shard_map/pallas_call | solution.py:370
  76.7 1.4 %collective-permute-done.15.refs_5_.refs_0_ = f32[2,3,2,4,16,128]{5,4,3,2,1,0:T(8,128)S(1)} collective-permute-done((f32[2,3,2,4,16,128]{5,4,3,2,1,0:T(8,128)S(1)}, f32[2,3,2,4,16,128]{5,4,3,2,1,0:T(8,128)S(1)}, u32[]{:S(2)}, u32[]{:S(2)}) %collective-permute-start.15) | collective-permute-done | bytes 393248 | tf_op jit(solution)/shard_map/ppermute | solution.py:449
  78.3 1.8 %collective-permute-start.18 = (f32[2,3,2,4,16,128]{5,4,3,2,1,0:T(8,128)S(1)}, f32[2,3,2,4,16,128]{5,4,3,2,1,0:T(8,128)S(1)}, u32[]{:S(2)}, u32[]{:S(2)}) collective-permute-start(f32[2,3,2,4,16,128]{5,4,3,2,1,0:T(8,128)S(1)} %collective-permute-done.14.refs_0_.refs_4_), channel_id=1, source_target_pairs={{0,4},{4,8},{8,12},{12,14},{14,10},{10,6},{6,2},{2,0},{1,5},{5,9},... | collective-permute-start | bytes 1179656 | tf_op jit(solution)/shard_map/ppermute | solution.py:456
  80.2 9.1 %shard_map.71.refs_5_ = f32[36,32,4096]{2,1,0:T(8,128)} custom-call(s32[9]{0:T(128)S(1)} %stack.169.place, s32[216]{0:T(256)S(1)} %add.193.shifts, f32[1]{0:T(128)} %bitcast.9.floor, f32[2,3,2,4,16,128]{5,4,3,2,1,0:T(8,128)S(1)} %collective-permute-done.14.refs_0_.refs_4_, ...), custom_call_target="tpu_custom_call", output_to_operand_aliasing={{}: (9, {})} | custom-call | flops 18874368 | bytes 28311552 | tf_op jit(solution)/shard_map/pallas_call | solution.py:370
  90.0 1.3 %collective-permute-done.19.refs_3_ = f32[1,3,2,4,16,128]{5,4,3,2,1,0:T(8,128)S(1)} collective-permute-done((f32[1,3,2,4,16,128]{5,4,3,2,1,0:T(8,128)S(1)}, f32[1,3,2,4,16,128]{5,4,3,2,1,0:T(8,128)S(1)}, u32[]{:S(2)}, u32[]{:S(2)}) %collective-permute-start.19) | collective-permute-done | bytes 196640 | tf_op jit(solution)/shard_map/ppermute | solution.py:458
  91.3 6.4 %shard_map.72 = f32[36,32,4096]{2,1,0:T(8,128)} custom-call(s32[6]{0:T(128)S(1)} %stack.135.place, s32[216]{0:T(256)S(1)} %add.193.shifts, f32[1]{0:T(128)} %bitcast.9.floor, f32[2,3,2,4,16,128]{5,4,3,2,1,0:T(8,128)S(1)} %collective-permute-done.15.refs_5_.refs_0_, ...), custom_call_target="tpu_custom_call", output_to_operand_aliasing={{}: (8, {})} | custom-call | flops 11796480 | bytes 17694720 | tf_op jit(solution)/shard_map/pallas_call | solution.py:370
  (59 shorter events, 12.9 us)
Async XLA Ops:
  0.0 1.0 %copy-start = (f32[1,32,4096]{2,1,0:T(8,128)S(1)}, f32[1,32,4096]{2,1,0:T(8,128)}, u32[]{:S(2)}) copy-start(f32[1,32,4096]{2,1,0:T(8,128)} %param.6) | copy-start | bytes 1572868
  1.1 1.0 %copy-start.1 = (f32[1,32,4096]{2,1,0:T(8,128)S(1)}, f32[1,32,4096]{2,1,0:T(8,128)}, u32[]{:S(2)}) copy-start(f32[1,32,4096]{2,1,0:T(8,128)} %param.7) | copy-start | bytes 1572868
  2.9 10.6 %collective-permute-start = (f32[2,136,128]{2,1,0:T(8,128)S(1)}, f32[2,136,128]{2,1,0:T(8,128)S(1)}, u32[]{:S(2)}, u32[]{:S(2)}) collective-permute-start(f32[2,136,128]{2,1,0:T(8,128)S(1)} %get-tuple-element.33), channel_id=1, source_target_pairs={{0,14},{2,12},{4,10},{6,8},{8,6},{10,4},{12,2},{14,0},{1,15},{3,13... | collective-permute-start | bytes 417800 | tf_op jit(solution)/shard_map/ppermute | solution.py:420
  9.0 9.3 %collective-permute-start.1 = (f32[2,136,128]{2,1,0:T(8,128)S(1)}, f32[2,136,128]{2,1,0:T(8,128)S(1)}, u32[]{:S(2)}, u32[]{:S(2)}) collective-permute-start(f32[2,136,128]{2,1,0:T(8,128)S(1)} %get-tuple-element.34), channel_id=1, source_target_pairs={{0,2},{2,0},{4,6},{6,4},{8,10},{10,8},{12,14},{14,12},{1,3},{3,1},... | collective-permute-start | bytes 417800 | tf_op jit(solution)/shard_map/ppermute | solution.py:420
  9.5 18.5 %collective-permute-start.2 = (f32[2,136,128]{2,1,0:T(8,128)S(1)}, f32[2,136,128]{2,1,0:T(8,128)S(1)}, u32[]{:S(2)}, u32[]{:S(2)}) collective-permute-start(f32[2,136,128]{2,1,0:T(8,128)S(1)} %get-tuple-element.41), channel_id=1, source_target_pairs={{0,4},{2,6},{4,0},{6,2},{8,12},{10,14},{12,8},{14,10},{1,5},{3,7},... | collective-permute-start | bytes 417800 | tf_op jit(solution)/shard_map/ppermute | solution.py:420
  9.5 18.5 %collective-permute-start.3 = (f32[2,136,128]{2,1,0:T(8,128)S(1)}, f32[2,136,128]{2,1,0:T(8,128)S(1)}, u32[]{:S(2)}, u32[]{:S(2)}) collective-permute-start(f32[2,136,128]{2,1,0:T(8,128)S(1)} %get-tuple-element.42), channel_id=1, source_target_pairs={{0,6},{2,4},{4,2},{6,0},{8,14},{10,12},{12,10},{14,8},{1,7},{3,5},... | collective-permute-start | bytes 417800 | tf_op jit(solution)/shard_map/ppermute | solution.py:420
  12.5 16.5 %collective-permute-start.4 = (f32[2,136,128]{2,1,0:T(8,128)S(1)}, f32[2,136,128]{2,1,0:T(8,128)S(1)}, u32[]{:S(2)}, u32[]{:S(2)}) collective-permute-start(f32[2,136,128]{2,1,0:T(8,128)S(1)} %get-tuple-element.43), channel_id=1, source_target_pairs={{0,8},{2,10},{4,12},{6,14},{8,0},{10,2},{12,4},{14,6},{1,9},{3,11}... | collective-permute-start | bytes 417800 | tf_op jit(solution)/shard_map/ppermute | solution.py:420
  13.5 17.8 %collective-permute-start.5 = (f32[2,136,128]{2,1,0:T(8,128)S(1)}, f32[2,136,128]{2,1,0:T(8,128)S(1)}, u32[]{:S(2)}, u32[]{:S(2)}) collective-permute-start(f32[2,136,128]{2,1,0:T(8,128)S(1)} %get-tuple-element.44), channel_id=1, source_target_pairs={{0,10},{2,8},{4,14},{6,12},{8,2},{10,0},{12,6},{14,4},{1,11},{3,9}... | collective-permute-start | bytes 417800 | tf_op jit(solution)/shard_map/ppermute | solution.py:420
  18.3 13.0 %collective-permute-start.6 = (f32[2,136,128]{2,1,0:T(8,128)S(1)}, f32[2,136,128]{2,1,0:T(8,128)S(1)}, u32[]{:S(2)}, u32[]{:S(2)}) collective-permute-start(f32[2,136,128]{2,1,0:T(8,128)S(1)} %get-tuple-element.45), channel_id=1, source_target_pairs={{0,12},{2,14},{4,8},{6,10},{8,4},{10,6},{12,0},{14,2},{1,13},{3,15... | collective-permute-start | bytes 417800 | tf_op jit(solution)/shard_map/ppermute | solution.py:420
  21.0 0.7 copy-start.2
  26.2 1.8 %copy-start.3 = (bf16[2,3456,256]{2,1,0:T(8,128)(2,1)}, bf16[2,3456,256]{2,1,0:T(8,128)(2,1)S(1)}, u32[]{:S(2)}) copy-start(bf16[2,3456,256]{2,1,0:T(8,128)(2,1)S(1)} %get-tuple-element.49.bands_hbm) | copy-start | bytes 10616836
  32.2 1.6 %collective-permute-start.7 = (f32[3,2,5,16,128]{4,3,2,1,0:T(8,128)S(1)}, f32[3,2,5,16,128]{4,3,2,1,0:T(8,128)S(1)}, u32[]{:S(2)}, u32[]{:S(2)}) collective-permute-start(f32[3,2,5,16,128]{4,3,2,1,0:T(8,128)S(1)} %get-tuple-element.48), channel_id=1, source_target_pairs={{0,1},{1,0},{2,3},{3,2},{4,5},{5,4},{6,7},{7,6},{8,9},{9,8},{10,11... | collective-permute-start | bytes 737288 | tf_op jit(solution)/shard_map/ppermute | solution.py:425
  40.4 11.5 %collective-permute-start.9 = (f32[2,3,2,4,16,128]{5,4,3,2,1,0:T(8,128)S(1)}, f32[2,3,2,4,16,128]{5,4,3,2,1,0:T(8,128)S(1)}, u32[]{:S(2)}, u32[]{:S(2)}) collective-permute-start(f32[2,3,2,4,16,128]{5,4,3,2,1,0:T(8,128)S(1)} %shard_map.67.refs_0_.refs_2_), channel_id=1, source_target_pairs={{4,0},{8,4},{12,8},{14,12},{10,14},{6,10},{2,6},{0,2},{5,1},{9,5},... | collective-permute-start | bytes 1179656 | tf_op jit(solution)/shard_map/ppermute | solution.py:442
  41.9 10.9 %collective-permute-start.8 = (f32[2,3,2,4,16,128]{5,4,3,2,1,0:T(8,128)S(1)}, f32[2,3,2,4,16,128]{5,4,3,2,1,0:T(8,128)S(1)}, u32[]{:S(2)}, u32[]{:S(2)}) collective-permute-start(f32[2,3,2,4,16,128]{5,4,3,2,1,0:T(8,128)S(1)} %shard_map.67.refs_0_.refs_2_), channel_id=1, source_target_pairs={{0,4},{4,8},{8,12},{12,14},{14,10},{10,6},{6,2},{2,0},{1,5},{5,9},... | collective-permute-start | bytes 1179656 | tf_op jit(solution)/shard_map/ppermute | solution.py:442
  42.5 1.7 %collective-permute-start.10 = (f32[1,3,2,4,16,128]{5,4,3,2,1,0:T(8,128)S(1)}, f32[1,3,2,4,16,128]{5,4,3,2,1,0:T(8,128)S(1)}, u32[]{:S(2)}, u32[]{:S(2)}) collective-permute-start(f32[1,3,2,4,16,128]{5,4,3,2,1,0:T(8,128)S(1)} %slice.36), channel_id=1, source_target_pairs={{0,1},{1,0},{2,3},{3,2},{4,5},{5,4},{6,7},{7,6},{8,9},{9,8},{10,11... | collective-permute-start | bytes 589832 | tf_op jit(solution)/shard_map/ppermute | solution.py:443
  52.8 2.2 %collective-permute-start.13 = (f32[2,3,2,4,16,128]{5,4,3,2,1,0:T(8,128)S(1)}, f32[2,3,2,4,16,128]{5,4,3,2,1,0:T(8,128)S(1)}, u32[]{:S(2)}, u32[]{:S(2)}) collective-permute-start(f32[2,3,2,4,16,128]{5,4,3,2,1,0:T(8,128)S(1)} %pad_maximum_fusion), channel_id=1, source_target_pairs={{0,1},{1,0},{2,3},{3,2},{4,5},{5,4},{6,7},{7,6},{8,9},{9,8},{10,11... | collective-permute-start | bytes 1179656 | tf_op jit(solution)/shard_map/ppermute | solution.py:451
  52.9 11.5 %collective-permute-start.11 = (f32[2,3,2,4,16,128]{5,4,3,2,1,0:T(8,128)S(1)}, f32[2,3,2,4,16,128]{5,4,3,2,1,0:T(8,128)S(1)}, u32[]{:S(2)}, u32[]{:S(2)}) collective-permute-start(f32[2,3,2,4,16,128]{5,4,3,2,1,0:T(8,128)S(1)} %collective-permute-done.8.refs_0_.refs_2_), channel_id=1, source_target_pairs={{0,4},{4,8},{8,12},{12,14},{14,10},{10,6},{6,2},{2,0},{1,5},{5,9},... | collective-permute-start | bytes 1179656 | tf_op jit(solution)/shard_map/ppermute | solution.py:449
  53.9 11.2 %collective-permute-start.12 = (f32[2,3,2,4,16,128]{5,4,3,2,1,0:T(8,128)S(1)}, f32[2,3,2,4,16,128]{5,4,3,2,1,0:T(8,128)S(1)}, u32[]{:S(2)}, u32[]{:S(2)}) collective-permute-start(f32[2,3,2,4,16,128]{5,4,3,2,1,0:T(8,128)S(1)} %collective-permute-done.9.refs_4_), channel_id=1, source_target_pairs={{4,0},{8,4},{12,8},{14,12},{10,14},{6,10},{2,6},{0,2},{5,1},{9,5},... | collective-permute-start | bytes 1179656 | tf_op jit(solution)/shard_map/ppermute | solution.py:449
  65.1 2.2 %collective-permute-start.16 = (f32[2,3,2,4,16,128]{5,4,3,2,1,0:T(8,128)S(1)}, f32[2,3,2,4,16,128]{5,4,3,2,1,0:T(8,128)S(1)}, u32[]{:S(2)}, u32[]{:S(2)}) collective-permute-start(f32[2,3,2,4,16,128]{5,4,3,2,1,0:T(8,128)S(1)} %pad_maximum_fusion.1), channel_id=1, source_target_pairs={{0,1},{1,0},{2,3},{3,2},{4,5},{5,4},{6,7},{7,6},{8,9},{9,8},{10,11... | collective-permute-start | bytes 1179656 | tf_op jit(solution)/shard_map/ppermute | solution.py:451
  65.2 11.5 %collective-permute-start.14 = (f32[2,3,2,4,16,128]{5,4,3,2,1,0:T(8,128)S(1)}, f32[2,3,2,4,16,128]{5,4,3,2,1,0:T(8,128)S(1)}, u32[]{:S(2)}, u32[]{:S(2)}) collective-permute-start(f32[2,3,2,4,16,128]{5,4,3,2,1,0:T(8,128)S(1)} %collective-permute-done.11.refs_0_.refs_2_), channel_id=1, source_target_pairs={{0,4},{4,8},{8,12},{12,14},{14,10},{10,6},{6,2},{2,0},{1,5},{5,9},... | collective-permute-start | bytes 1179656 | tf_op jit(solution)/shard_map/ppermute | solution.py:449
  67.0 11.2 %collective-permute-start.15 = (f32[2,3,2,4,16,128]{5,4,3,2,1,0:T(8,128)S(1)}, f32[2,3,2,4,16,128]{5,4,3,2,1,0:T(8,128)S(1)}, u32[]{:S(2)}, u32[]{:S(2)}) collective-permute-start(f32[2,3,2,4,16,128]{5,4,3,2,1,0:T(8,128)S(1)} %collective-permute-done.12.refs_5_.refs_4_), channel_id=1, source_target_pairs={{4,0},{8,4},{12,8},{14,12},{10,14},{6,10},{2,6},{0,2},{5,1},{9,5},... | collective-permute-start | bytes 1179656 | tf_op jit(solution)/shard_map/ppermute | solution.py:449
  78.2 2.0 %collective-permute-start.17 = (f32[2,3,2,4,16,128]{5,4,3,2,1,0:T(8,128)S(1)}, f32[2,3,2,4,16,128]{5,4,3,2,1,0:T(8,128)S(1)}, u32[]{:S(2)}, u32[]{:S(2)}) collective-permute-start(f32[2,3,2,4,16,128]{5,4,3,2,1,0:T(8,128)S(1)} %pad_maximum_fusion.2), channel_id=1, source_target_pairs={{0,1},{1,0},{2,3},{3,2},{4,5},{5,4},{6,7},{7,6},{8,9},{9,8},{10,11... | collective-permute-start | bytes 1179656 | tf_op jit(solution)/shard_map/ppermute | solution.py:451
  78.3 11.5 %collective-permute-start.18 = (f32[2,3,2,4,16,128]{5,4,3,2,1,0:T(8,128)S(1)}, f32[2,3,2,4,16,128]{5,4,3,2,1,0:T(8,128)S(1)}, u32[]{:S(2)}, u32[]{:S(2)}) collective-permute-start(f32[2,3,2,4,16,128]{5,4,3,2,1,0:T(8,128)S(1)} %collective-permute-done.14.refs_0_.refs_4_), channel_id=1, source_target_pairs={{0,4},{4,8},{8,12},{12,14},{14,10},{10,6},{6,2},{2,0},{1,5},{5,9},... | collective-permute-start | bytes 1179656 | tf_op jit(solution)/shard_map/ppermute | solution.py:456
  89.8 1.5 %collective-permute-start.19 = (f32[1,3,2,4,16,128]{5,4,3,2,1,0:T(8,128)S(1)}, f32[1,3,2,4,16,128]{5,4,3,2,1,0:T(8,128)S(1)}, u32[]{:S(2)}, u32[]{:S(2)}) collective-permute-start(f32[1,3,2,4,16,128]{5,4,3,2,1,0:T(8,128)S(1)} %slice.35), channel_id=1, source_target_pairs={{0,1},{1,0},{2,3},{3,2},{4,5},{5,4},{6,7},{7,6},{8,9},{9,8},{10,11... | collective-permute-start | bytes 589832 | tf_op jit(solution)/shard_map/ppermute | solution.py:458

commit v11 on v10

--- a/solution.py
+++ b/solution.py
@@ -64,36 +64,36 @@
     )(spread_kernel.reshape(-1), spread_kernel)
 
 
-def cut_kernel(starts, exposure, noise_var, *chunk_refs):
-    height, columns = exposure.shape
+def cut_kernel(starts, pair, *chunk_refs):
+    _, height, columns = pair.shape
     tiles = columns // len(chunk_refs) // LANES
     lane = lax.broadcasted_iota(jnp.int32, (8, LANES), 1)
     for index, ref in enumerate(chunk_refs):
         start = starts[index]
         ahead = jnp.where(start == 0, columns, start) - LANES
-        for kind, held in enumerate((exposure, noise_var)):
+        for kind in range(2):
             for tile in range(tiles):
                 at = pl.multiple_of(start + tile * LANES, LANES)
-                ref[kind, tile * height : (tile + 1) * height] = held[:, pl.ds(at, LANES)]
+                ref[kind, tile * height : (tile + 1) * height] = pair[kind, :, pl.ds(at, LANES)]
             halo = jnp.zeros((8, LANES), jnp.float32)
             for group in range(LANES // HALO):
-                rows = held[8 * group : 8 * group + 8, pl.ds(pl.multiple_of(ahead, LANES), LANES)]
+                rows = pair[kind, 8 * group : 8 * group + 8, pl.ds(pl.multiple_of(ahead, LANES), LANES)]
                 moved = pltpu.roll(rows, (group + 1) * HALO % LANES, 1)
                 halo = jnp.where(lane // HALO == group, moved, halo)
             ref[kind, tiles * height :] = halo
 
 
-def cut(starts, exposure, noise_var, blocks):
-    height, columns = exposure.shape
+def cut(starts, pair, blocks):
+    _, height, columns = pair.shape
     rows = columns // blocks // LANES * height + height * HALO // LANES
     return pl.pallas_call(
         cut_kernel,
-        in_specs=[pl.BlockSpec(memory_space=pltpu.SMEM)] + [pl.BlockSpec(memory_space=pltpu.VMEM)] * 2,
+        in_specs=[pl.BlockSpec(memory_space=pltpu.SMEM), pl.BlockSpec(memory_space=pltpu.VMEM)],
         out_specs=[pl.BlockSpec(memory_space=pltpu.VMEM)] * blocks,
         out_shape=[jax.ShapeDtypeStruct((2, rows, LANES), jnp.float32)] * blocks,
         compiler_params=pltpu.CompilerParams(vmem_limit_bytes=VMEM),
         cost_estimate=pl.CostEstimate(flops=0, bytes_accessed=16 * height * columns, transcendentals=0),
-    )(starts, exposure, noise_var)
+    )(starts, pair)
 
 
 def pick_kernel(numbers, *refs):
@@ -396,8 +396,7 @@
 
 
 def local(images, variance, spread_kernel, shifts, epoch_owner, valid_rows):
-    exposure, noise_var = images[0], variance[0]
-    height, columns = exposure.shape
+    height, columns = images.shape[1:]
     blocks = lax.axis_size("vel")
     width = columns // blocks
     me, lower = lax.axis_index("vel"), lax.axis_index("rows")
@@ -415,7 +414,7 @@
 
     numbers = jnp.concatenate([jnp.stack([me, lower]).astype(jnp.int32), epoch_owner, valid_rows.reshape(-1)])
     starts = position(me ^ jnp.arange(blocks, dtype=jnp.int32)) * width
-    chunks = list(cut(starts, exposure, noise_var, blocks))
+    chunks = list(cut(starts, jnp.concatenate([images, variance]), blocks))
     for step in range(1, blocks):
         chunks[step] = lax.ppermute(chunks[step], "vel", [(i, i ^ step) for i in range(blocks)])
     chunks[1], spread_kernel, numbers = lax.optimization_barrier((chunks[1], spread_kernel, numbers))
@@ -453,9 +452,8 @@
             have[step] = ((ahead, 0), (ahead, 1), (border, 1))
             segments = [block(-step) + [(1 - step, 0)], [(step - 1, tiles - 1)] + block(step)]
         else:
-            behind = lax.ppermute(behind, "vel", right)
-            behind, out = lax.optimization_barrier((behind, out))
-            border = lax.ppermute(behind[:1], "rows", swap)
+            behind, border = lax.ppermute(behind, "vel", right), lax.ppermute(border[1:], "vel", left)
+            behind, border, out = lax.optimization_barrier((behind, border, out))
             have[step] = ((behind, 0), (behind, 1), (border, 0))
             segments = [[(step - 1, tiles - 1)] + block(step) + [(1 - step, 0)]]
         out = stack_now(segments, out)

time: 98.1 us -> 95.7 us (0.976)
  local copies, waits for them, and re-layouts: 7.51 us -> 5.38 us
  waiting for transfers between devices: 14 us -> 12.5 us
  other arithmetic: 1.68 us -> 2.95 us
    unnamed x9 -> x5, local copies, waits for them, and re-layouts: 5.33 us -> 3.26 us
    ppermute x2 -> x1, waiting for transfers between devices: 1.88 us -> 0.01 us  [local(): lax.ppermute(border[1:], 'vel', left)]
    ppermute x2 -> x3, starting transfers between devices: 2.72 us -> 4.35 us  [local(): lax.ppermute(behind, 'vel', right)]
    ppermute x2 -> x1, starting transfers between devices: 1.88 us -> 0.6 us  [local(): lax.ppermute(border[1:], 'vel', left)]
    concatenate x0 -> x1, other arithmetic: none -> 1.27 us  [local(): chunks = list(cut(starts, jnp.concatenate([images, variance]), blocks))]
  transfers between devices with their start and end apart: 20 -> 20, of which waited for: 12 -> 11; matrix products, arithmetic and copies ran while one was open for 5% -> 5% of each run, Pallas kernels for 37% -> 38%
where the time goes in v11:
time: 95.7 us; the launch traced here: 95.4 us
  Pallas kernels  50.7 us (53%)
  starting transfers between devices  23.6 us (25%)
  waiting for transfers between devices  12.5 us (13%)
  local copies, waits for them, and re-layouts  5.38 us (6%)
  other arithmetic  2.95 us (3%)
    pallas_call x5, Pallas kernels, stack_tiles(): pl.pallas_call(functools.partial(stack_kernel, segments=described, source...  38 us
    ppermute x7, starting transfers between devices, local(): lax.ppermute(chunks[step], 'vel', [(i, i ^ step) for i in range(blocks)])  14.7 us
    pallas_call x1, Pallas kernels, correlate(): pl.pallas_call(functools.partial(correlate_kernel, ksize=ksize), in_specs...  6.67 us
    pallas_call x1, Pallas kernels, make_bands(): pl.pallas_call(band_kernel, in_specs=[pl.BlockSpec(memory_space=pltpu.SME...  4.41 us
    ppermute x7, waiting for transfers between devices, local(): lax.ppermute(chunks[step], 'vel', [(i, i ^ step) for i in range(blocks)])  4.39 us
    ppermute x3, starting transfers between devices, local(): lax.ppermute(behind, 'vel', right)  4.35 us
    unnamed x5, local copies, waits for them, and re-layouts  3.26 us
    ppermute x1, waiting for transfers between devices, local(): lax.ppermute(payload, 'vel', left)  3.01 us
  transfers between devices with their start and end apart: 20, of which 11 were waited for; matrix products, arithmetic and copies ran while one was open for 5% of the time, Pallas kernels for 38%

profile of v11, /device:TPU:0, one launch (start us, length us, event | category | flops | bytes accessed | tf_op | source)
XLA Modules:
  0.0 95.4 jit_solution(16671971600495250811)
XLA Ops:
  0.0 1.3 %pad_maximum_fusion.pair = f32[2,32,4096]{2,1,0:T(8,128)S(1)} fusion(f32[1,32,4096]{2,1,0:T(8,128)} %param.7, f32[1,32,4096]{2,1,0:T(8,128)} %param.6), kind=kLoop, calls=%fused_computation | loop fusion | flops 262144 | bytes 2097152 | tf_op jit(solution)/shard_map/concatenate | solution.py:417
  2.1 6.1 %collective-permute-start = (f32[2,136,128]{2,1,0:T(8,128)S(1)}, f32[2,136,128]{2,1,0:T(8,128)S(1)}, u32[]{:S(2)}, u32[]{:S(2)}) collective-permute-start(f32[2,136,128]{2,1,0:T(8,128)S(1)} %get-tuple-element.34), channel_id=1, source_target_pairs={{0,14},{2,12},{4,10},{6,8},{8,6},{10,4},{12,2},{14,0},{1,15},{3,13... | collective-permute-start | bytes 417800 | tf_op jit(solution)/shard_map/ppermute | solution.py:419
  8.7 3.0 %collective-permute-start.3 = (f32[2,136,128]{2,1,0:T(8,128)S(1)}, f32[2,136,128]{2,1,0:T(8,128)S(1)}, u32[]{:S(2)}, u32[]{:S(2)}) collective-permute-start(f32[2,136,128]{2,1,0:T(8,128)S(1)} %get-tuple-element.43), channel_id=1, source_target_pairs={{0,6},{2,4},{4,2},{6,0},{8,14},{10,12},{12,10},{14,8},{1,7},{3,5},... | collective-permute-start | bytes 417800 | tf_op jit(solution)/shard_map/ppermute | solution.py:419
  11.7 1.1 %collective-permute-done.refs_7_ = f32[2,136,128]{2,1,0:T(8,128)S(1)} collective-permute-done((f32[2,136,128]{2,1,0:T(8,128)S(1)}, f32[2,136,128]{2,1,0:T(8,128)S(1)}, u32[]{:S(2)}, u32[]{:S(2)}) %collective-permute-start) | collective-permute-done | bytes 139296 | tf_op jit(solution)/shard_map/ppermute | solution.py:419
  12.7 4.8 %collective-permute-start.5 = (f32[2,136,128]{2,1,0:T(8,128)S(1)}, f32[2,136,128]{2,1,0:T(8,128)S(1)}, u32[]{:S(2)}, u32[]{:S(2)}) collective-permute-start(f32[2,136,128]{2,1,0:T(8,128)S(1)} %get-tuple-element.45), channel_id=1, source_target_pairs={{0,10},{2,8},{4,14},{6,12},{8,2},{10,0},{12,6},{14,4},{1,11},{3,9}... | collective-permute-start | bytes 417800 | tf_op jit(solution)/shard_map/ppermute | solution.py:419
  20.9 4.4 %shard_map.65 = (bf16[2,3456,256]{2,1,0:T(8,128)(2,1)S(1)}, f32[8,128]{1,0:T(8,128)S(1)}) custom-call(f32[441]{0:T(512)S(1)} %reshape.10.taps, f32[21,21]{1,0:T(8,128)S(1)} %copy-done), custom_call_target="tpu_custom_call" | custom-call | bytes 20971520 | tf_op jit(solution)/shard_map/pallas_call | solution.py:54
  25.4 1.8 %copy-done.1 = bf16[2,3456,256]{2,1,0:T(8,128)(2,1)} copy-done((bf16[2,3456,256]{2,1,0:T(8,128)(2,1)}, bf16[2,3456,256]{2,1,0:T(8,128)(2,1)S(1)}, u32[]{:S(2)}) %copy-start.1) | copy-done | bytes 3538968
  27.2 1.0 %collective-permute-done.4.refs_4_ = f32[2,136,128]{2,1,0:T(8,128)S(1)} collective-permute-done((f32[2,136,128]{2,1,0:T(8,128)S(1)}, f32[2,136,128]{2,1,0:T(8,128)S(1)}, u32[]{:S(2)}, u32[]{:S(2)}) %collective-permute-start.4) | collective-permute-done | bytes 139296 | tf_op jit(solution)/shard_map/ppermute | solution.py:419
  28.1 2.4 %collective-permute-done.5.refs_5_ = f32[2,136,128]{2,1,0:T(8,128)S(1)} collective-permute-done((f32[2,136,128]{2,1,0:T(8,128)S(1)}, f32[2,136,128]{2,1,0:T(8,128)S(1)}, u32[]{:S(2)}, u32[]{:S(2)}) %collective-permute-start.5) | collective-permute-done | bytes 139296 | tf_op jit(solution)/shard_map/ppermute | solution.py:419
  31.5 1.4 %collective-permute-done.7.border = f32[3,2,5,16,128]{4,3,2,1,0:T(8,128)S(1)} collective-permute-done((f32[3,2,5,16,128]{4,3,2,1,0:T(8,128)S(1)}, f32[3,2,5,16,128]{4,3,2,1,0:T(8,128)S(1)}, u32[]{:S(2)}, u32[]{:S(2)}) %collective-permute-start.7) | collective-permute-done | bytes 245792 | tf_op jit(solution)/shard_map/ppermute | solution.py:424
  32.9 6.7 %shard_map.67.refs_0_.refs_2_ = f32[2,3,2,4,16,128]{5,4,3,2,1,0:T(8,128)S(1)} custom-call(s32[2]{0:T(128)S(1)} %pad_add_fusion.1.place, f32[3,2,5,32,128]{4,3,2,1,0:T(8,128)S(1)} %get-tuple-element.48.own, f32[3,2,5,16,128]{4,3,2,1,0:T(8,128)S(1)} %collective-permute-done.7.border, bf16[2,3456,256]{2,1,0:T(8,128)(2,1)} %copy-done.1), custom_call_target="tpu_custom_call" | custom-call | flops 3623878656 | bytes 12582912 | tf_op jit(solution)/shard_map/pallas_call | solution.py:233
  39.6 1.5 %collective-permute-start.9 = (f32[2,3,2,4,16,128]{5,4,3,2,1,0:T(8,128)S(1)}, f32[2,3,2,4,16,128]{5,4,3,2,1,0:T(8,128)S(1)}, u32[]{:S(2)}, u32[]{:S(2)}) collective-permute-start(f32[2,3,2,4,16,128]{5,4,3,2,1,0:T(8,128)S(1)} %shard_map.67.refs_0_.refs_2_), channel_id=1, source_target_pairs={{4,0},{8,4},{12,8},{14,12},{10,14},{6,10},{2,6},{0,2},{5,1},{9,5},... | collective-permute-start | bytes 1179656 | tf_op jit(solution)/shard_map/ppermute | solution.py:441
  43.4 4.7 %shard_map.68.refs_5_ = f32[36,32,4096]{2,1,0:T(8,128)} custom-call(s32[4]{0:T(128)S(1)} %pad_add_fusion.2.place, s32[216]{0:T(256)S(1)} %add.193.shifts, f32[1]{0:T(128)} %bitcast.7.floor, f32[2,3,2,4,16,128]{5,4,3,2,1,0:T(8,128)S(1)} %shard_map.67.refs_0_.refs_2_, f32[1,3,2,4,16,128]{5,4,3,2,1,0:T(8,128)S(1)} %collective-permute-done.10.refs_1_.refs_3_), custom_call_target="tpu_custom_call" | custom-call | flops 7077888 | bytes 10616832 | tf_op jit(solution)/shard_map/pallas_call | solution.py:370
  48.1 3.0 %collective-permute-done.9.refs_4_ = f32[2,3,2,4,16,128]{5,4,3,2,1,0:T(8,128)S(1)} collective-permute-done((f32[2,3,2,4,16,128]{5,4,3,2,1,0:T(8,128)S(1)}, f32[2,3,2,4,16,128]{5,4,3,2,1,0:T(8,128)S(1)}, u32[]{:S(2)}, u32[]{:S(2)}) %collective-permute-start.9) | collective-permute-done | bytes 393248 | tf_op jit(solution)/shard_map/ppermute | solution.py:441
  51.1 0.9 collective-permute-done.8.refs_0_.refs_2_
  52.1 1.0 %collective-permute-start.11 = (f32[2,3,2,4,16,128]{5,4,3,2,1,0:T(8,128)S(1)}, f32[2,3,2,4,16,128]{5,4,3,2,1,0:T(8,128)S(1)}, u32[]{:S(2)}, u32[]{:S(2)}) collective-permute-start(f32[2,3,2,4,16,128]{5,4,3,2,1,0:T(8,128)S(1)} %collective-permute-done.8.refs_0_.refs_2_), channel_id=1, source_target_pairs={{0,4},{4,8},{8,12},{12,14},{14,10},{10,6},{6,2},{2,0},{1,5},{5,9},... | collective-permute-start | bytes 1179656 | tf_op jit(solution)/shard_map/ppermute | solution.py:448
  53.1 1.1 %collective-permute-start.12 = (f32[2,3,2,4,16,128]{5,4,3,2,1,0:T(8,128)S(1)}, f32[2,3,2,4,16,128]{5,4,3,2,1,0:T(8,128)S(1)}, u32[]{:S(2)}, u32[]{:S(2)}) collective-permute-start(f32[2,3,2,4,16,128]{5,4,3,2,1,0:T(8,128)S(1)} %collective-permute-done.9.refs_4_), channel_id=1, source_target_pairs={{4,0},{8,4},{12,8},{14,12},{10,14},{6,10},{2,6},{0,2},{5,1},{9,5},... | collective-permute-start | bytes 1179656 | tf_op jit(solution)/shard_map/ppermute | solution.py:448
  54.3 9.0 %shard_map.69.refs_6_ = f32[36,32,4096]{2,1,0:T(8,128)} custom-call(s32[9]{0:T(128)S(1)} %stack.151.place, s32[216]{0:T(256)S(1)} %add.193.shifts, f32[1]{0:T(128)} %bitcast.7.floor, f32[2,3,2,4,16,128]{5,4,3,2,1,0:T(8,128)S(1)} %collective-permute-done.8.refs_0_.refs_2_, ...), custom_call_target="tpu_custom_call", output_to_operand_aliasing={{}: (8, {})} | custom-call | flops 18874368 | bytes 28311552 | tf_op jit(solution)/shard_map/pallas_call | solution.py:370
  64.4 1.7 %collective-permute-start.14 = (f32[2,3,2,4,16,128]{5,4,3,2,1,0:T(8,128)S(1)}, f32[2,3,2,4,16,128]{5,4,3,2,1,0:T(8,128)S(1)}, u32[]{:S(2)}, u32[]{:S(2)}) collective-permute-start(f32[2,3,2,4,16,128]{5,4,3,2,1,0:T(8,128)S(1)} %collective-permute-done.11.refs_0_.refs_2_), channel_id=1, source_target_pairs={{0,4},{4,8},{8,12},{12,14},{14,10},{10,6},{6,2},{2,0},{1,5},{5,9},... | collective-permute-start | bytes 1179656 | tf_op jit(solution)/shard_map/ppermute | solution.py:448
  66.6 9.0 %shard_map.70.refs_6_ = f32[36,32,4096]{2,1,0:T(8,128)} custom-call(s32[9]{0:T(128)S(1)} %stack.160.place, s32[216]{0:T(256)S(1)} %add.193.shifts, f32[1]{0:T(128)} %bitcast.7.floor, f32[2,3,2,4,16,128]{5,4,3,2,1,0:T(8,128)S(1)} %collective-permute-done.11.refs_0_.refs_2_, ...), custom_call_target="tpu_custom_call", output_to_operand_aliasing={{}: (9, {})} | custom-call | flops 18874368 | bytes 28311552 | tf_op jit(solution)/shard_map/pallas_call | solution.py:370
  75.9 1.4 %collective-permute-done.15.refs_5_.refs_0_ = f32[2,3,2,4,16,128]{5,4,3,2,1,0:T(8,128)S(1)} collective-permute-done((f32[2,3,2,4,16,128]{5,4,3,2,1,0:T(8,128)S(1)}, f32[2,3,2,4,16,128]{5,4,3,2,1,0:T(8,128)S(1)}, u32[]{:S(2)}, u32[]{:S(2)}) %collective-permute-start.15) | collective-permute-done | bytes 393248 | tf_op jit(solution)/shard_map/ppermute | solution.py:448
  77.5 1.6 %collective-permute-start.18 = (f32[2,3,2,4,16,128]{5,4,3,2,1,0:T(8,128)S(1)}, f32[2,3,2,4,16,128]{5,4,3,2,1,0:T(8,128)S(1)}, u32[]{:S(2)}, u32[]{:S(2)}) collective-permute-start(f32[2,3,2,4,16,128]{5,4,3,2,1,0:T(8,128)S(1)} %collective-permute-done.14.refs_0_.refs_4_), channel_id=1, source_target_pairs={{0,4},{4,8},{8,12},{12,14},{14,10},{10,6},{6,2},{2,0},{1,5},{5,9},... | collective-permute-start | bytes 1179656 | tf_op jit(solution)/shard_map/ppermute | solution.py:455
  80.0 9.0 %shard_map.71.refs_5_ = f32[36,32,4096]{2,1,0:T(8,128)} custom-call(s32[9]{0:T(128)S(1)} %stack.169.place, s32[216]{0:T(256)S(1)} %add.193.shifts, f32[1]{0:T(128)} %bitcast.7.floor, f32[2,3,2,4,16,128]{5,4,3,2,1,0:T(8,128)S(1)} %collective-permute-done.14.refs_0_.refs_4_, ...), custom_call_target="tpu_custom_call", output_to_operand_aliasing={{}: (9, {})} | custom-call | flops 18874368 | bytes 28311552 | tf_op jit(solution)/shard_map/pallas_call | solution.py:370
  89.0 6.3 %shard_map.72 = f32[36,32,4096]{2,1,0:T(8,128)} custom-call(s32[6]{0:T(128)S(1)} %stack.135.place, s32[216]{0:T(256)S(1)} %add.193.shifts, f32[1]{0:T(128)} %bitcast.7.floor, f32[2,3,2,4,16,128]{5,4,3,2,1,0:T(8,128)S(1)} %collective-permute-done.15.refs_5_.refs_0_, ...), custom_call_target="tpu_custom_call", output_to_operand_aliasing={{}: (8, {})} | custom-call | flops 11796480 | bytes 17694720 | tf_op jit(solution)/shard_map/pallas_call | solution.py:370
  (56 shorter events, 11.2 us)
Async XLA Ops:
  2.1 10.6 %collective-permute-start = (f32[2,136,128]{2,1,0:T(8,128)S(1)}, f32[2,136,128]{2,1,0:T(8,128)S(1)}, u32[]{:S(2)}, u32[]{:S(2)}) collective-permute-start(f32[2,136,128]{2,1,0:T(8,128)S(1)} %get-tuple-element.34), channel_id=1, source_target_pairs={{0,14},{2,12},{4,10},{6,8},{8,6},{10,4},{12,2},{14,0},{1,15},{3,13... | collective-permute-start | bytes 417800 | tf_op jit(solution)/shard_map/ppermute | solution.py:419
  8.2 9.3 %collective-permute-start.1 = (f32[2,136,128]{2,1,0:T(8,128)S(1)}, f32[2,136,128]{2,1,0:T(8,128)S(1)}, u32[]{:S(2)}, u32[]{:S(2)}) collective-permute-start(f32[2,136,128]{2,1,0:T(8,128)S(1)} %get-tuple-element.35), channel_id=1, source_target_pairs={{0,2},{2,0},{4,6},{6,4},{8,10},{10,8},{12,14},{14,12},{1,3},{3,1},... | collective-permute-start | bytes 417800 | tf_op jit(solution)/shard_map/ppermute | solution.py:419
  8.7 18.5 %collective-permute-start.2 = (f32[2,136,128]{2,1,0:T(8,128)S(1)}, f32[2,136,128]{2,1,0:T(8,128)S(1)}, u32[]{:S(2)}, u32[]{:S(2)}) collective-permute-start(f32[2,136,128]{2,1,0:T(8,128)S(1)} %get-tuple-element.42), channel_id=1, source_target_pairs={{0,4},{2,6},{4,0},{6,2},{8,12},{10,14},{12,8},{14,10},{1,5},{3,7},... | collective-permute-start | bytes 417800 | tf_op jit(solution)/shard_map/ppermute | solution.py:419
  8.7 18.5 %collective-permute-start.3 = (f32[2,136,128]{2,1,0:T(8,128)S(1)}, f32[2,136,128]{2,1,0:T(8,128)S(1)}, u32[]{:S(2)}, u32[]{:S(2)}) collective-permute-start(f32[2,136,128]{2,1,0:T(8,128)S(1)} %get-tuple-element.43), channel_id=1, source_target_pairs={{0,6},{2,4},{4,2},{6,0},{8,14},{10,12},{12,10},{14,8},{1,7},{3,5},... | collective-permute-start | bytes 417800 | tf_op jit(solution)/shard_map/ppermute | solution.py:419
  11.7 16.5 %collective-permute-start.4 = (f32[2,136,128]{2,1,0:T(8,128)S(1)}, f32[2,136,128]{2,1,0:T(8,128)S(1)}, u32[]{:S(2)}, u32[]{:S(2)}) collective-permute-start(f32[2,136,128]{2,1,0:T(8,128)S(1)} %get-tuple-element.44), channel_id=1, source_target_pairs={{0,8},{2,10},{4,12},{6,14},{8,0},{10,2},{12,4},{14,6},{1,9},{3,11}... | collective-permute-start | bytes 417800 | tf_op jit(solution)/shard_map/ppermute | solution.py:419
  12.7 17.8 %collective-permute-start.5 = (f32[2,136,128]{2,1,0:T(8,128)S(1)}, f32[2,136,128]{2,1,0:T(8,128)S(1)}, u32[]{:S(2)}, u32[]{:S(2)}) collective-permute-start(f32[2,136,128]{2,1,0:T(8,128)S(1)} %get-tuple-element.45), channel_id=1, source_target_pairs={{0,10},{2,8},{4,14},{6,12},{8,2},{10,0},{12,6},{14,4},{1,11},{3,9}... | collective-permute-start | bytes 417800 | tf_op jit(solution)/shard_map/ppermute | solution.py:419
  17.5 13.0 %collective-permute-start.6 = (f32[2,136,128]{2,1,0:T(8,128)S(1)}, f32[2,136,128]{2,1,0:T(8,128)S(1)}, u32[]{:S(2)}, u32[]{:S(2)}) collective-permute-start(f32[2,136,128]{2,1,0:T(8,128)S(1)} %get-tuple-element.46), channel_id=1, source_target_pairs={{0,12},{2,14},{4,8},{6,10},{8,4},{10,6},{12,0},{14,2},{1,13},{3,15... | collective-permute-start | bytes 417800 | tf_op jit(solution)/shard_map/ppermute | solution.py:419
  20.2 0.7 copy-start
  25.4 1.8 %copy-start.1 = (bf16[2,3456,256]{2,1,0:T(8,128)(2,1)}, bf16[2,3456,256]{2,1,0:T(8,128)(2,1)S(1)}, u32[]{:S(2)}) copy-start(bf16[2,3456,256]{2,1,0:T(8,128)(2,1)S(1)} %get-tuple-element.50.bands_hbm) | copy-start | bytes 10616836
  31.4 1.6 %collective-permute-start.7 = (f32[3,2,5,16,128]{4,3,2,1,0:T(8,128)S(1)}, f32[3,2,5,16,128]{4,3,2,1,0:T(8,128)S(1)}, u32[]{:S(2)}, u32[]{:S(2)}) collective-permute-start(f32[3,2,5,16,128]{4,3,2,1,0:T(8,128)S(1)} %get-tuple-element.49), channel_id=1, source_target_pairs={{0,1},{1,0},{2,3},{3,2},{4,5},{5,4},{6,7},{7,6},{8,9},{9,8},{10,11... | collective-permute-start | bytes 737288 | tf_op jit(solution)/shard_map/ppermute | solution.py:424
  39.6 11.5 %collective-permute-start.9 = (f32[2,3,2,4,16,128]{5,4,3,2,1,0:T(8,128)S(1)}, f32[2,3,2,4,16,128]{5,4,3,2,1,0:T(8,128)S(1)}, u32[]{:S(2)}, u32[]{:S(2)}) collective-permute-start(f32[2,3,2,4,16,128]{5,4,3,2,1,0:T(8,128)S(1)} %shard_map.67.refs_0_.refs_2_), channel_id=1, source_target_pairs={{4,0},{8,4},{12,8},{14,12},{10,14},{6,10},{2,6},{0,2},{5,1},{9,5},... | collective-permute-start | bytes 1179656 | tf_op jit(solution)/shard_map/ppermute | solution.py:441
  41.1 10.9 %collective-permute-start.8 = (f32[2,3,2,4,16,128]{5,4,3,2,1,0:T(8,128)S(1)}, f32[2,3,2,4,16,128]{5,4,3,2,1,0:T(8,128)S(1)}, u32[]{:S(2)}, u32[]{:S(2)}) collective-permute-start(f32[2,3,2,4,16,128]{5,4,3,2,1,0:T(8,128)S(1)} %shard_map.67.refs_0_.refs_2_), channel_id=1, source_target_pairs={{0,4},{4,8},{8,12},{12,14},{14,10},{10,6},{6,2},{2,0},{1,5},{5,9},... | collective-permute-start | bytes 1179656 | tf_op jit(solution)/shard_map/ppermute | solution.py:441
  41.7 1.7 %collective-permute-start.10 = (f32[1,3,2,4,16,128]{5,4,3,2,1,0:T(8,128)S(1)}, f32[1,3,2,4,16,128]{5,4,3,2,1,0:T(8,128)S(1)}, u32[]{:S(2)}, u32[]{:S(2)}) collective-permute-start(f32[1,3,2,4,16,128]{5,4,3,2,1,0:T(8,128)S(1)} %slice.36), channel_id=1, source_target_pairs={{0,1},{1,0},{2,3},{3,2},{4,5},{5,4},{6,7},{7,6},{8,9},{9,8},{10,11... | collective-permute-start | bytes 589832 | tf_op jit(solution)/shard_map/ppermute | solution.py:442
  52.0 2.2 %collective-permute-start.13 = (f32[2,3,2,4,16,128]{5,4,3,2,1,0:T(8,128)S(1)}, f32[2,3,2,4,16,128]{5,4,3,2,1,0:T(8,128)S(1)}, u32[]{:S(2)}, u32[]{:S(2)}) collective-permute-start(f32[2,3,2,4,16,128]{5,4,3,2,1,0:T(8,128)S(1)} %pad_maximum_fusion.1), channel_id=1, source_target_pairs={{0,1},{1,0},{2,3},{3,2},{4,5},{5,4},{6,7},{7,6},{8,9},{9,8},{10,11... | collective-permute-start | bytes 1179656 | tf_op jit(solution)/shard_map/ppermute | solution.py:450
  52.1 11.5 %collective-permute-start.11 = (f32[2,3,2,4,16,128]{5,4,3,2,1,0:T(8,128)S(1)}, f32[2,3,2,4,16,128]{5,4,3,2,1,0:T(8,128)S(1)}, u32[]{:S(2)}, u32[]{:S(2)}) collective-permute-start(f32[2,3,2,4,16,128]{5,4,3,2,1,0:T(8,128)S(1)} %collective-permute-done.8.refs_0_.refs_2_), channel_id=1, source_target_pairs={{0,4},{4,8},{8,12},{12,14},{14,10},{10,6},{6,2},{2,0},{1,5},{5,9},... | collective-permute-start | bytes 1179656 | tf_op jit(solution)/shard_map/ppermute | solution.py:448
  53.1 11.2 %collective-permute-start.12 = (f32[2,3,2,4,16,128]{5,4,3,2,1,0:T(8,128)S(1)}, f32[2,3,2,4,16,128]{5,4,3,2,1,0:T(8,128)S(1)}, u32[]{:S(2)}, u32[]{:S(2)}) collective-permute-start(f32[2,3,2,4,16,128]{5,4,3,2,1,0:T(8,128)S(1)} %collective-permute-done.9.refs_4_), channel_id=1, source_target_pairs={{4,0},{8,4},{12,8},{14,12},{10,14},{6,10},{2,6},{0,2},{5,1},{9,5},... | collective-permute-start | bytes 1179656 | tf_op jit(solution)/shard_map/ppermute | solution.py:448
  64.3 2.2 %collective-permute-start.16 = (f32[2,3,2,4,16,128]{5,4,3,2,1,0:T(8,128)S(1)}, f32[2,3,2,4,16,128]{5,4,3,2,1,0:T(8,128)S(1)}, u32[]{:S(2)}, u32[]{:S(2)}) collective-permute-start(f32[2,3,2,4,16,128]{5,4,3,2,1,0:T(8,128)S(1)} %pad_maximum_fusion.2), channel_id=1, source_target_pairs={{0,1},{1,0},{2,3},{3,2},{4,5},{5,4},{6,7},{7,6},{8,9},{9,8},{10,11... | collective-permute-start | bytes 1179656 | tf_op jit(solution)/shard_map/ppermute | solution.py:450
  64.4 11.5 %collective-permute-start.14 = (f32[2,3,2,4,16,128]{5,4,3,2,1,0:T(8,128)S(1)}, f32[2,3,2,4,16,128]{5,4,3,2,1,0:T(8,128)S(1)}, u32[]{:S(2)}, u32[]{:S(2)}) collective-permute-start(f32[2,3,2,4,16,128]{5,4,3,2,1,0:T(8,128)S(1)} %collective-permute-done.11.refs_0_.refs_2_), channel_id=1, source_target_pairs={{0,4},{4,8},{8,12},{12,14},{14,10},{10,6},{6,2},{2,0},{1,5},{5,9},... | collective-permute-start | bytes 1179656 | tf_op jit(solution)/shard_map/ppermute | solution.py:448
  66.2 11.2 %collective-permute-start.15 = (f32[2,3,2,4,16,128]{5,4,3,2,1,0:T(8,128)S(1)}, f32[2,3,2,4,16,128]{5,4,3,2,1,0:T(8,128)S(1)}, u32[]{:S(2)}, u32[]{:S(2)}) collective-permute-start(f32[2,3,2,4,16,128]{5,4,3,2,1,0:T(8,128)S(1)} %collective-permute-done.12.refs_5_.refs_4_), channel_id=1, source_target_pairs={{4,0},{8,4},{12,8},{14,12},{10,14},{6,10},{2,6},{0,2},{5,1},{9,5},... | collective-permute-start | bytes 1179656 | tf_op jit(solution)/shard_map/ppermute | solution.py:448
  77.4 1.8 %collective-permute-start.17 = (f32[2,3,2,4,16,128]{5,4,3,2,1,0:T(8,128)S(1)}, f32[2,3,2,4,16,128]{5,4,3,2,1,0:T(8,128)S(1)}, u32[]{:S(2)}, u32[]{:S(2)}) collective-permute-start(f32[2,3,2,4,16,128]{5,4,3,2,1,0:T(8,128)S(1)} %pad_maximum_fusion.3), channel_id=1, source_target_pairs={{0,1},{1,0},{2,3},{3,2},{4,5},{5,4},{6,7},{7,6},{8,9},{9,8},{10,11... | collective-permute-start | bytes 1179656 | tf_op jit(solution)/shard_map/ppermute | solution.py:450
  77.5 11.5 %collective-permute-start.18 = (f32[2,3,2,4,16,128]{5,4,3,2,1,0:T(8,128)S(1)}, f32[2,3,2,4,16,128]{5,4,3,2,1,0:T(8,128)S(1)}, u32[]{:S(2)}, u32[]{:S(2)}) collective-permute-start(f32[2,3,2,4,16,128]{5,4,3,2,1,0:T(8,128)S(1)} %collective-permute-done.14.refs_0_.refs_4_), channel_id=1, source_target_pairs={{0,4},{4,8},{8,12},{12,14},{14,10},{10,6},{6,2},{2,0},{1,5},{5,9},... | collective-permute-start | bytes 1179656 | tf_op jit(solution)/shard_map/ppermute | solution.py:455
  79.2 9.8 %collective-permute-start.19 = (f32[1,3,2,4,16,128]{5,4,3,2,1,0:T(8,128)S(1)}, f32[1,3,2,4,16,128]{5,4,3,2,1,0:T(8,128)S(1)}, u32[]{:S(2)}, u32[]{:S(2)}) collective-permute-start(f32[1,3,2,4,16,128]{5,4,3,2,1,0:T(8,128)S(1)} %slice.37), channel_id=1, source_target_pairs={{4,0},{8,4},{12,8},{14,12},{10,14},{6,10},{2,6},{0,2},{5,1},{9,5},... | collective-permute-start | bytes 589832 | tf_op jit(solution)/shard_map/ppermute | solution.py:455

commit v12 on v11

--- a/solution.py
+++ b/solution.py
@@ -210,7 +210,7 @@
         weights = bands_ref[kind]
         pair = jnp.dot(upper, weights, preferred_element_type=jnp.float32)
         more = jnp.dot(rest, weights[:, :LANES], preferred_element_type=jnp.float32)
-        summed[...] = pair[:, :LANES] + (pair[:, LANES:] + more)
+        summed[:summed_rows] = pair[:, :LANES] + (pair[:, LANES:] + more)
         for half in range(2):
             start = (1 - lower if half == 0 else lower) * (height - MAXS)
             for epoch in range(epochs):
@@ -240,7 +240,7 @@
             pltpu.VMEM((kinds, 2, depth + (FOLD - 1) * members, LANES), jnp.float32),
             pltpu.VMEM((kinds, 2, depth, LANES), jnp.bfloat16),
             pltpu.VMEM((kinds, 2, depth, LANES), jnp.bfloat16),
-            pltpu.VMEM((height * members, LANES), jnp.float32),
+            pltpu.VMEM(((height + 1) * members, LANES), jnp.float32),
             pltpu.VMEM(bands.shape, bands.dtype),
             pltpu.SemaphoreType.DMA((kinds,)),
         ],
@@ -277,7 +277,7 @@
         tops = [jnp.full((8, LANES), jnp.maximum(jnp.max(top), 1e-30), jnp.float32) for top in tops]
         per_psi, per_phi = (most_psi - 1) / tops[0], (most_phi - 1) / tops[1]
         scale[0] = floor[0] * per_phi
-        scale[1] = jnp.sqrt(per_phi) / (per_psi * 256.0)
+        scale[1] = jnp.sqrt(per_phi) / per_psi / 256.0
 
         def quantize(index, _):
             rows = pl.ds(pl.multiple_of(index * 8, 8), 8)

time: 95.7 us -> 95.7 us (level)
  no operation moved by 1% of the time
where the time goes in v12:
time: 95.7 us; the launch traced here: 95.3 us
  Pallas kernels  50.8 us (53%)
  starting transfers between devices  23.6 us (25%)
  waiting for transfers between devices  12.4 us (13%)
  local copies, waits for them, and re-layouts  5.38 us (6%)
  other arithmetic  2.95 us (3%)
    pallas_call x5, Pallas kernels, stack_tiles(): pl.pallas_call(functools.partial(stack_kernel, segments=described, source...  38.1 us
    ppermute x7, starting transfers between devices, local(): lax.ppermute(chunks[step], 'vel', [(i, i ^ step) for i in range(blocks)])  14.7 us
    pallas_call x1, Pallas kernels, correlate(): pl.pallas_call(functools.partial(correlate_kernel, ksize=ksize), in_specs...  6.67 us
    pallas_call x1, Pallas kernels, make_bands(): pl.pallas_call(band_kernel, in_specs=[pl.BlockSpec(memory_space=pltpu.SME...  4.41 us
    ppermute x7, waiting for transfers between devices, local(): lax.ppermute(chunks[step], 'vel', [(i, i ^ step) for i in range(blocks)])  4.39 us
    ppermute x3, starting transfers between devices, local(): lax.ppermute(behind, 'vel', right)  4.35 us
    unnamed x5, local copies, waits for them, and re-layouts  3.26 us
    ppermute x1, waiting for transfers between devices, local(): lax.ppermute(payload, 'vel', left)  3.01 us
  transfers between devices with their start and end apart: 20, of which 11 were waited for; matrix products, arithmetic and copies ran while one was open for 5% of the time, Pallas kernels for 38%

profile of v12, /device:TPU:0, one launch (start us, length us, event | category | flops | bytes accessed | tf_op | source)
XLA Modules:
  0.0 95.3 jit_solution(6517096453476448763)
XLA Ops:
  0.0 1.3 %pad_maximum_fusion.pair = f32[2,32,4096]{2,1,0:T(8,128)S(1)} fusion(f32[1,32,4096]{2,1,0:T(8,128)} %param.7, f32[1,32,4096]{2,1,0:T(8,128)} %param.6), kind=kLoop, calls=%fused_computation | loop fusion | flops 262144 | bytes 2097152 | tf_op jit(solution)/shard_map/concatenate | solution.py:417
  2.1 6.1 %collective-permute-start = (f32[2,136,128]{2,1,0:T(8,128)S(1)}, f32[2,136,128]{2,1,0:T(8,128)S(1)}, u32[]{:S(2)}, u32[]{:S(2)}) collective-permute-start(f32[2,136,128]{2,1,0:T(8,128)S(1)} %get-tuple-element.34), channel_id=1, source_target_pairs={{0,14},{2,12},{4,10},{6,8},{8,6},{10,4},{12,2},{14,0},{1,15},{3,13... | collective-permute-start | bytes 417800 | tf_op jit(solution)/shard_map/ppermute | solution.py:419
  8.7 3.0 %collective-permute-start.3 = (f32[2,136,128]{2,1,0:T(8,128)S(1)}, f32[2,136,128]{2,1,0:T(8,128)S(1)}, u32[]{:S(2)}, u32[]{:S(2)}) collective-permute-start(f32[2,136,128]{2,1,0:T(8,128)S(1)} %get-tuple-element.43), channel_id=1, source_target_pairs={{0,6},{2,4},{4,2},{6,0},{8,14},{10,12},{12,10},{14,8},{1,7},{3,5},... | collective-permute-start | bytes 417800 | tf_op jit(solution)/shard_map/ppermute | solution.py:419
  11.7 1.1 %collective-permute-done.refs_7_ = f32[2,136,128]{2,1,0:T(8,128)S(1)} collective-permute-done((f32[2,136,128]{2,1,0:T(8,128)S(1)}, f32[2,136,128]{2,1,0:T(8,128)S(1)}, u32[]{:S(2)}, u32[]{:S(2)}) %collective-permute-start) | collective-permute-done | bytes 139296 | tf_op jit(solution)/shard_map/ppermute | solution.py:419
  12.7 4.8 %collective-permute-start.5 = (f32[2,136,128]{2,1,0:T(8,128)S(1)}, f32[2,136,128]{2,1,0:T(8,128)S(1)}, u32[]{:S(2)}, u32[]{:S(2)}) collective-permute-start(f32[2,136,128]{2,1,0:T(8,128)S(1)} %get-tuple-element.45), channel_id=1, source_target_pairs={{0,10},{2,8},{4,14},{6,12},{8,2},{10,0},{12,6},{14,4},{1,11},{3,9}... | collective-permute-start | bytes 417800 | tf_op jit(solution)/shard_map/ppermute | solution.py:419
  20.9 4.4 %shard_map.65 = (bf16[2,3456,256]{2,1,0:T(8,128)(2,1)S(1)}, f32[8,128]{1,0:T(8,128)S(1)}) custom-call(f32[441]{0:T(512)S(1)} %reshape.10.taps, f32[21,21]{1,0:T(8,128)S(1)} %copy-done), custom_call_target="tpu_custom_call" | custom-call | bytes 20971520 | tf_op jit(solution)/shard_map/pallas_call | solution.py:54
  25.4 1.8 %copy-done.1 = bf16[2,3456,256]{2,1,0:T(8,128)(2,1)} copy-done((bf16[2,3456,256]{2,1,0:T(8,128)(2,1)}, bf16[2,3456,256]{2,1,0:T(8,128)(2,1)S(1)}, u32[]{:S(2)}) %copy-start.1) | copy-done | bytes 3538968
  27.2 1.0 %collective-permute-done.4.refs_4_ = f32[2,136,128]{2,1,0:T(8,128)S(1)} collective-permute-done((f32[2,136,128]{2,1,0:T(8,128)S(1)}, f32[2,136,128]{2,1,0:T(8,128)S(1)}, u32[]{:S(2)}, u32[]{:S(2)}) %collective-permute-start.4) | collective-permute-done | bytes 139296 | tf_op jit(solution)/shard_map/ppermute | solution.py:419
  28.1 2.4 %collective-permute-done.5.refs_5_ = f32[2,136,128]{2,1,0:T(8,128)S(1)} collective-permute-done((f32[2,136,128]{2,1,0:T(8,128)S(1)}, f32[2,136,128]{2,1,0:T(8,128)S(1)}, u32[]{:S(2)}, u32[]{:S(2)}) %collective-permute-start.5) | collective-permute-done | bytes 139296 | tf_op jit(solution)/shard_map/ppermute | solution.py:419
  31.5 1.4 %collective-permute-done.7.border = f32[3,2,5,16,128]{4,3,2,1,0:T(8,128)S(1)} collective-permute-done((f32[3,2,5,16,128]{4,3,2,1,0:T(8,128)S(1)}, f32[3,2,5,16,128]{4,3,2,1,0:T(8,128)S(1)}, u32[]{:S(2)}, u32[]{:S(2)}) %collective-permute-start.7) | collective-permute-done | bytes 245792 | tf_op jit(solution)/shard_map/ppermute | solution.py:424
  32.9 6.7 %shard_map.67.refs_0_.refs_2_ = f32[2,3,2,4,16,128]{5,4,3,2,1,0:T(8,128)S(1)} custom-call(s32[2]{0:T(128)S(1)} %pad_add_fusion.1.place, f32[3,2,5,32,128]{4,3,2,1,0:T(8,128)S(1)} %get-tuple-element.48.own, f32[3,2,5,16,128]{4,3,2,1,0:T(8,128)S(1)} %collective-permute-done.7.border, bf16[2,3456,256]{2,1,0:T(8,128)(2,1)} %copy-done.1), custom_call_target="tpu_custom_call" | custom-call | flops 3623878656 | bytes 12582912 | tf_op jit(solution)/shard_map/pallas_call | solution.py:233
  39.6 1.5 %collective-permute-start.9 = (f32[2,3,2,4,16,128]{5,4,3,2,1,0:T(8,128)S(1)}, f32[2,3,2,4,16,128]{5,4,3,2,1,0:T(8,128)S(1)}, u32[]{:S(2)}, u32[]{:S(2)}) collective-permute-start(f32[2,3,2,4,16,128]{5,4,3,2,1,0:T(8,128)S(1)} %shard_map.67.refs_0_.refs_2_), channel_id=1, source_target_pairs={{4,0},{8,4},{12,8},{14,12},{10,14},{6,10},{2,6},{0,2},{5,1},{9,5},... | collective-permute-start | bytes 1179656 | tf_op jit(solution)/shard_map/ppermute | solution.py:441
  43.4 4.7 %shard_map.68.refs_5_ = f32[36,32,4096]{2,1,0:T(8,128)} custom-call(s32[4]{0:T(128)S(1)} %pad_add_fusion.2.place, s32[216]{0:T(256)S(1)} %add.193.shifts, f32[1]{0:T(128)} %bitcast.7.floor, f32[2,3,2,4,16,128]{5,4,3,2,1,0:T(8,128)S(1)} %shard_map.67.refs_0_.refs_2_, f32[1,3,2,4,16,128]{5,4,3,2,1,0:T(8,128)S(1)} %collective-permute-done.10.refs_1_.refs_3_), custom_call_target="tpu_custom_call" | custom-call | flops 7077888 | bytes 10616832 | tf_op jit(solution)/shard_map/pallas_call | solution.py:370
  48.1 3.0 %collective-permute-done.9.refs_4_ = f32[2,3,2,4,16,128]{5,4,3,2,1,0:T(8,128)S(1)} collective-permute-done((f32[2,3,2,4,16,128]{5,4,3,2,1,0:T(8,128)S(1)}, f32[2,3,2,4,16,128]{5,4,3,2,1,0:T(8,128)S(1)}, u32[]{:S(2)}, u32[]{:S(2)}) %collective-permute-start.9) | collective-permute-done | bytes 393248 | tf_op jit(solution)/shard_map/ppermute | solution.py:441
  51.1 0.9 collective-permute-done.8.refs_0_.refs_2_
  52.1 1.0 %collective-permute-start.11 = (f32[2,3,2,4,16,128]{5,4,3,2,1,0:T(8,128)S(1)}, f32[2,3,2,4,16,128]{5,4,3,2,1,0:T(8,128)S(1)}, u32[]{:S(2)}, u32[]{:S(2)}) collective-permute-start(f32[2,3,2,4,16,128]{5,4,3,2,1,0:T(8,128)S(1)} %collective-permute-done.8.refs_0_.refs_2_), channel_id=1, source_target_pairs={{0,4},{4,8},{8,12},{12,14},{14,10},{10,6},{6,2},{2,0},{1,5},{5,9},... | collective-permute-start | bytes 1179656 | tf_op jit(solution)/shard_map/ppermute | solution.py:448
  53.1 1.1 %collective-permute-start.12 = (f32[2,3,2,4,16,128]{5,4,3,2,1,0:T(8,128)S(1)}, f32[2,3,2,4,16,128]{5,4,3,2,1,0:T(8,128)S(1)}, u32[]{:S(2)}, u32[]{:S(2)}) collective-permute-start(f32[2,3,2,4,16,128]{5,4,3,2,1,0:T(8,128)S(1)} %collective-permute-done.9.refs_4_), channel_id=1, source_target_pairs={{4,0},{8,4},{12,8},{14,12},{10,14},{6,10},{2,6},{0,2},{5,1},{9,5},... | collective-permute-start | bytes 1179656 | tf_op jit(solution)/shard_map/ppermute | solution.py:448
  54.3 9.1 %shard_map.69.refs_6_ = f32[36,32,4096]{2,1,0:T(8,128)} custom-call(s32[9]{0:T(128)S(1)} %stack.151.place, s32[216]{0:T(256)S(1)} %add.193.shifts, f32[1]{0:T(128)} %bitcast.7.floor, f32[2,3,2,4,16,128]{5,4,3,2,1,0:T(8,128)S(1)} %collective-permute-done.8.refs_0_.refs_2_, ...), custom_call_target="tpu_custom_call", output_to_operand_aliasing={{}: (8, {})} | custom-call | flops 18874368 | bytes 28311552 | tf_op jit(solution)/shard_map/pallas_call | solution.py:370
  64.4 1.7 %collective-permute-start.14 = (f32[2,3,2,4,16,128]{5,4,3,2,1,0:T(8,128)S(1)}, f32[2,3,2,4,16,128]{5,4,3,2,1,0:T(8,128)S(1)}, u32[]{:S(2)}, u32[]{:S(2)}) collective-permute-start(f32[2,3,2,4,16,128]{5,4,3,2,1,0:T(8,128)S(1)} %collective-permute-done.11.refs_0_.refs_2_), channel_id=1, source_target_pairs={{0,4},{4,8},{8,12},{12,14},{14,10},{10,6},{6,2},{2,0},{1,5},{5,9},... | collective-permute-start | bytes 1179656 | tf_op jit(solution)/shard_map/ppermute | solution.py:448
  66.6 9.0 %shard_map.70.refs_6_ = f32[36,32,4096]{2,1,0:T(8,128)} custom-call(s32[9]{0:T(128)S(1)} %stack.160.place, s32[216]{0:T(256)S(1)} %add.193.shifts, f32[1]{0:T(128)} %bitcast.7.floor, f32[2,3,2,4,16,128]{5,4,3,2,1,0:T(8,128)S(1)} %collective-permute-done.11.refs_0_.refs_2_, ...), custom_call_target="tpu_custom_call", output_to_operand_aliasing={{}: (9, {})} | custom-call | flops 18874368 | bytes 28311552 | tf_op jit(solution)/shard_map/pallas_call | solution.py:370
  75.9 1.4 %collective-permute-done.15.refs_5_.refs_0_ = f32[2,3,2,4,16,128]{5,4,3,2,1,0:T(8,128)S(1)} collective-permute-done((f32[2,3,2,4,16,128]{5,4,3,2,1,0:T(8,128)S(1)}, f32[2,3,2,4,16,128]{5,4,3,2,1,0:T(8,128)S(1)}, u32[]{:S(2)}, u32[]{:S(2)}) %collective-permute-start.15) | collective-permute-done | bytes 393248 | tf_op jit(solution)/shard_map/ppermute | solution.py:448
  77.5 1.6 %collective-permute-start.18 = (f32[2,3,2,4,16,128]{5,4,3,2,1,0:T(8,128)S(1)}, f32[2,3,2,4,16,128]{5,4,3,2,1,0:T(8,128)S(1)}, u32[]{:S(2)}, u32[]{:S(2)}) collective-permute-start(f32[2,3,2,4,16,128]{5,4,3,2,1,0:T(8,128)S(1)} %collective-permute-done.14.refs_0_.refs_4_), channel_id=1, source_target_pairs={{0,4},{4,8},{8,12},{12,14},{14,10},{10,6},{6,2},{2,0},{1,5},{5,9},... | collective-permute-start | bytes 1179656 | tf_op jit(solution)/shard_map/ppermute | solution.py:455
  80.0 9.0 %shard_map.71.refs_5_ = f32[36,32,4096]{2,1,0:T(8,128)} custom-call(s32[9]{0:T(128)S(1)} %stack.169.place, s32[216]{0:T(256)S(1)} %add.193.shifts, f32[1]{0:T(128)} %bitcast.7.floor, f32[2,3,2,4,16,128]{5,4,3,2,1,0:T(8,128)S(1)} %collective-permute-done.14.refs_0_.refs_4_, ...), custom_call_target="tpu_custom_call", output_to_operand_aliasing={{}: (9, {})} | custom-call | flops 18874368 | bytes 28311552 | tf_op jit(solution)/shard_map/pallas_call | solution.py:370
  89.0 6.3 %shard_map.72 = f32[36,32,4096]{2,1,0:T(8,128)} custom-call(s32[6]{0:T(128)S(1)} %stack.135.place, s32[216]{0:T(256)S(1)} %add.193.shifts, f32[1]{0:T(128)} %bitcast.7.floor, f32[2,3,2,4,16,128]{5,4,3,2,1,0:T(8,128)S(1)} %collective-permute-done.15.refs_5_.refs_0_, ...), custom_call_target="tpu_custom_call", output_to_operand_aliasing={{}: (8, {})} | custom-call | flops 11796480 | bytes 17694720 | tf_op jit(solution)/shard_map/pallas_call | solution.py:370
  (56 shorter events, 11.1 us)
Async XLA Ops:
  2.1 10.6 %collective-permute-start = (f32[2,136,128]{2,1,0:T(8,128)S(1)}, f32[2,136,128]{2,1,0:T(8,128)S(1)}, u32[]{:S(2)}, u32[]{:S(2)}) collective-permute-start(f32[2,136,128]{2,1,0:T(8,128)S(1)} %get-tuple-element.34), channel_id=1, source_target_pairs={{0,14},{2,12},{4,10},{6,8},{8,6},{10,4},{12,2},{14,0},{1,15},{3,13... | collective-permute-start | bytes 417800 | tf_op jit(solution)/shard_map/ppermute | solution.py:419
  8.2 9.3 %collective-permute-start.1 = (f32[2,136,128]{2,1,0:T(8,128)S(1)}, f32[2,136,128]{2,1,0:T(8,128)S(1)}, u32[]{:S(2)}, u32[]{:S(2)}) collective-permute-start(f32[2,136,128]{2,1,0:T(8,128)S(1)} %get-tuple-element.35), channel_id=1, source_target_pairs={{0,2},{2,0},{4,6},{6,4},{8,10},{10,8},{12,14},{14,12},{1,3},{3,1},... | collective-permute-start | bytes 417800 | tf_op jit(solution)/shard_map/ppermute | solution.py:419
  8.7 18.5 %collective-permute-start.2 = (f32[2,136,128]{2,1,0:T(8,128)S(1)}, f32[2,136,128]{2,1,0:T(8,128)S(1)}, u32[]{:S(2)}, u32[]{:S(2)}) collective-permute-start(f32[2,136,128]{2,1,0:T(8,128)S(1)} %get-tuple-element.42), channel_id=1, source_target_pairs={{0,4},{2,6},{4,0},{6,2},{8,12},{10,14},{12,8},{14,10},{1,5},{3,7},... | collective-permute-start | bytes 417800 | tf_op jit(solution)/shard_map/ppermute | solution.py:419
  8.7 18.5 %collective-permute-start.3 = (f32[2,136,128]{2,1,0:T(8,128)S(1)}, f32[2,136,128]{2,1,0:T(8,128)S(1)}, u32[]{:S(2)}, u32[]{:S(2)}) collective-permute-start(f32[2,136,128]{2,1,0:T(8,128)S(1)} %get-tuple-element.43), channel_id=1, source_target_pairs={{0,6},{2,4},{4,2},{6,0},{8,14},{10,12},{12,10},{14,8},{1,7},{3,5},... | collective-permute-start | bytes 417800 | tf_op jit(solution)/shard_map/ppermute | solution.py:419
  11.7 16.5 %collective-permute-start.4 = (f32[2,136,128]{2,1,0:T(8,128)S(1)}, f32[2,136,128]{2,1,0:T(8,128)S(1)}, u32[]{:S(2)}, u32[]{:S(2)}) collective-permute-start(f32[2,136,128]{2,1,0:T(8,128)S(1)} %get-tuple-element.44), channel_id=1, source_target_pairs={{0,8},{2,10},{4,12},{6,14},{8,0},{10,2},{12,4},{14,6},{1,9},{3,11}... | collective-permute-start | bytes 417800 | tf_op jit(solution)/shard_map/ppermute | solution.py:419
  12.7 17.8 %collective-permute-start.5 = (f32[2,136,128]{2,1,0:T(8,128)S(1)}, f32[2,136,128]{2,1,0:T(8,128)S(1)}, u32[]{:S(2)}, u32[]{:S(2)}) collective-permute-start(f32[2,136,128]{2,1,0:T(8,128)S(1)} %get-tuple-element.45), channel_id=1, source_target_pairs={{0,10},{2,8},{4,14},{6,12},{8,2},{10,0},{12,6},{14,4},{1,11},{3,9}... | collective-permute-start | bytes 417800 | tf_op jit(solution)/shard_map/ppermute | solution.py:419
  17.5 13.0 %collective-permute-start.6 = (f32[2,136,128]{2,1,0:T(8,128)S(1)}, f32[2,136,128]{2,1,0:T(8,128)S(1)}, u32[]{:S(2)}, u32[]{:S(2)}) collective-permute-start(f32[2,136,128]{2,1,0:T(8,128)S(1)} %get-tuple-element.46), channel_id=1, source_target_pairs={{0,12},{2,14},{4,8},{6,10},{8,4},{10,6},{12,0},{14,2},{1,13},{3,15... | collective-permute-start | bytes 417800 | tf_op jit(solution)/shard_map/ppermute | solution.py:419
  20.2 0.7 copy-start
  25.4 1.8 %copy-start.1 = (bf16[2,3456,256]{2,1,0:T(8,128)(2,1)}, bf16[2,3456,256]{2,1,0:T(8,128)(2,1)S(1)}, u32[]{:S(2)}) copy-start(bf16[2,3456,256]{2,1,0:T(8,128)(2,1)S(1)} %get-tuple-element.50.bands_hbm) | copy-start | bytes 10616836
  31.4 1.6 %collective-permute-start.7 = (f32[3,2,5,16,128]{4,3,2,1,0:T(8,128)S(1)}, f32[3,2,5,16,128]{4,3,2,1,0:T(8,128)S(1)}, u32[]{:S(2)}, u32[]{:S(2)}) collective-permute-start(f32[3,2,5,16,128]{4,3,2,1,0:T(8,128)S(1)} %get-tuple-element.49), channel_id=1, source_target_pairs={{0,1},{1,0},{2,3},{3,2},{4,5},{5,4},{6,7},{7,6},{8,9},{9,8},{10,11... | collective-permute-start | bytes 737288 | tf_op jit(solution)/shard_map/ppermute | solution.py:424
  39.6 11.5 %collective-permute-start.9 = (f32[2,3,2,4,16,128]{5,4,3,2,1,0:T(8,128)S(1)}, f32[2,3,2,4,16,128]{5,4,3,2,1,0:T(8,128)S(1)}, u32[]{:S(2)}, u32[]{:S(2)}) collective-permute-start(f32[2,3,2,4,16,128]{5,4,3,2,1,0:T(8,128)S(1)} %shard_map.67.refs_0_.refs_2_), channel_id=1, source_target_pairs={{4,0},{8,4},{12,8},{14,12},{10,14},{6,10},{2,6},{0,2},{5,1},{9,5},... | collective-permute-start | bytes 1179656 | tf_op jit(solution)/shard_map/ppermute | solution.py:441
  41.1 10.9 %collective-permute-start.8 = (f32[2,3,2,4,16,128]{5,4,3,2,1,0:T(8,128)S(1)}, f32[2,3,2,4,16,128]{5,4,3,2,1,0:T(8,128)S(1)}, u32[]{:S(2)}, u32[]{:S(2)}) collective-permute-start(f32[2,3,2,4,16,128]{5,4,3,2,1,0:T(8,128)S(1)} %shard_map.67.refs_0_.refs_2_), channel_id=1, source_target_pairs={{0,4},{4,8},{8,12},{12,14},{14,10},{10,6},{6,2},{2,0},{1,5},{5,9},... | collective-permute-start | bytes 1179656 | tf_op jit(solution)/shard_map/ppermute | solution.py:441
  41.7 1.7 %collective-permute-start.10 = (f32[1,3,2,4,16,128]{5,4,3,2,1,0:T(8,128)S(1)}, f32[1,3,2,4,16,128]{5,4,3,2,1,0:T(8,128)S(1)}, u32[]{:S(2)}, u32[]{:S(2)}) collective-permute-start(f32[1,3,2,4,16,128]{5,4,3,2,1,0:T(8,128)S(1)} %slice.36), channel_id=1, source_target_pairs={{0,1},{1,0},{2,3},{3,2},{4,5},{5,4},{6,7},{7,6},{8,9},{9,8},{10,11... | collective-permute-start | bytes 589832 | tf_op jit(solution)/shard_map/ppermute | solution.py:442
  52.0 2.2 %collective-permute-start.13 = (f32[2,3,2,4,16,128]{5,4,3,2,1,0:T(8,128)S(1)}, f32[2,3,2,4,16,128]{5,4,3,2,1,0:T(8,128)S(1)}, u32[]{:S(2)}, u32[]{:S(2)}) collective-permute-start(f32[2,3,2,4,16,128]{5,4,3,2,1,0:T(8,128)S(1)} %pad_maximum_fusion.1), channel_id=1, source_target_pairs={{0,1},{1,0},{2,3},{3,2},{4,5},{5,4},{6,7},{7,6},{8,9},{9,8},{10,11... | collective-permute-start | bytes 1179656 | tf_op jit(solution)/shard_map/ppermute | solution.py:450
  52.1 11.5 %collective-permute-start.11 = (f32[2,3,2,4,16,128]{5,4,3,2,1,0:T(8,128)S(1)}, f32[2,3,2,4,16,128]{5,4,3,2,1,0:T(8,128)S(1)}, u32[]{:S(2)}, u32[]{:S(2)}) collective-permute-start(f32[2,3,2,4,16,128]{5,4,3,2,1,0:T(8,128)S(1)} %collective-permute-done.8.refs_0_.refs_2_), channel_id=1, source_target_pairs={{0,4},{4,8},{8,12},{12,14},{14,10},{10,6},{6,2},{2,0},{1,5},{5,9},... | collective-permute-start | bytes 1179656 | tf_op jit(solution)/shard_map/ppermute | solution.py:448
  53.1 11.2 %collective-permute-start.12 = (f32[2,3,2,4,16,128]{5,4,3,2,1,0:T(8,128)S(1)}, f32[2,3,2,4,16,128]{5,4,3,2,1,0:T(8,128)S(1)}, u32[]{:S(2)}, u32[]{:S(2)}) collective-permute-start(f32[2,3,2,4,16,128]{5,4,3,2,1,0:T(8,128)S(1)} %collective-permute-done.9.refs_4_), channel_id=1, source_target_pairs={{4,0},{8,4},{12,8},{14,12},{10,14},{6,10},{2,6},{0,2},{5,1},{9,5},... | collective-permute-start | bytes 1179656 | tf_op jit(solution)/shard_map/ppermute | solution.py:448
  64.3 2.2 %collective-permute-start.16 = (f32[2,3,2,4,16,128]{5,4,3,2,1,0:T(8,128)S(1)}, f32[2,3,2,4,16,128]{5,4,3,2,1,0:T(8,128)S(1)}, u32[]{:S(2)}, u32[]{:S(2)}) collective-permute-start(f32[2,3,2,4,16,128]{5,4,3,2,1,0:T(8,128)S(1)} %pad_maximum_fusion.2), channel_id=1, source_target_pairs={{0,1},{1,0},{2,3},{3,2},{4,5},{5,4},{6,7},{7,6},{8,9},{9,8},{10,11... | collective-permute-start | bytes 1179656 | tf_op jit(solution)/shard_map/ppermute | solution.py:450
  64.4 11.5 %collective-permute-start.14 = (f32[2,3,2,4,16,128]{5,4,3,2,1,0:T(8,128)S(1)}, f32[2,3,2,4,16,128]{5,4,3,2,1,0:T(8,128)S(1)}, u32[]{:S(2)}, u32[]{:S(2)}) collective-permute-start(f32[2,3,2,4,16,128]{5,4,3,2,1,0:T(8,128)S(1)} %collective-permute-done.11.refs_0_.refs_2_), channel_id=1, source_target_pairs={{0,4},{4,8},{8,12},{12,14},{14,10},{10,6},{6,2},{2,0},{1,5},{5,9},... | collective-permute-start | bytes 1179656 | tf_op jit(solution)/shard_map/ppermute | solution.py:448
  66.2 11.2 %collective-permute-start.15 = (f32[2,3,2,4,16,128]{5,4,3,2,1,0:T(8,128)S(1)}, f32[2,3,2,4,16,128]{5,4,3,2,1,0:T(8,128)S(1)}, u32[]{:S(2)}, u32[]{:S(2)}) collective-permute-start(f32[2,3,2,4,16,128]{5,4,3,2,1,0:T(8,128)S(1)} %collective-permute-done.12.refs_5_.refs_4_), channel_id=1, source_target_pairs={{4,0},{8,4},{12,8},{14,12},{10,14},{6,10},{2,6},{0,2},{5,1},{9,5},... | collective-permute-start | bytes 1179656 | tf_op jit(solution)/shard_map/ppermute | solution.py:448
  77.4 1.8 %collective-permute-start.17 = (f32[2,3,2,4,16,128]{5,4,3,2,1,0:T(8,128)S(1)}, f32[2,3,2,4,16,128]{5,4,3,2,1,0:T(8,128)S(1)}, u32[]{:S(2)}, u32[]{:S(2)}) collective-permute-start(f32[2,3,2,4,16,128]{5,4,3,2,1,0:T(8,128)S(1)} %pad_maximum_fusion.3), channel_id=1, source_target_pairs={{0,1},{1,0},{2,3},{3,2},{4,5},{5,4},{6,7},{7,6},{8,9},{9,8},{10,11... | collective-permute-start | bytes 1179656 | tf_op jit(solution)/shard_map/ppermute | solution.py:450
  77.5 11.5 %collective-permute-start.18 = (f32[2,3,2,4,16,128]{5,4,3,2,1,0:T(8,128)S(1)}, f32[2,3,2,4,16,128]{5,4,3,2,1,0:T(8,128)S(1)}, u32[]{:S(2)}, u32[]{:S(2)}) collective-permute-start(f32[2,3,2,4,16,128]{5,4,3,2,1,0:T(8,128)S(1)} %collective-permute-done.14.refs_0_.refs_4_), channel_id=1, source_target_pairs={{0,4},{4,8},{8,12},{12,14},{14,10},{10,6},{6,2},{2,0},{1,5},{5,9},... | collective-permute-start | bytes 1179656 | tf_op jit(solution)/shard_map/ppermute | solution.py:455
  79.2 9.8 %collective-permute-start.19 = (f32[1,3,2,4,16,128]{5,4,3,2,1,0:T(8,128)S(1)}, f32[1,3,2,4,16,128]{5,4,3,2,1,0:T(8,128)S(1)}, u32[]{:S(2)}, u32[]{:S(2)}) collective-permute-start(f32[1,3,2,4,16,128]{5,4,3,2,1,0:T(8,128)S(1)} %slice.37), channel_id=1, source_target_pairs={{4,0},{8,4},{12,8},{14,12},{10,14},{6,10},{2,6},{0,2},{5,1},{9,5},... | collective-permute-start | bytes 589832 | tf_op jit(solution)/shard_map/ppermute | solution.py:455

commit v13 on v12

--- a/solution.py
+++ b/solution.py
@@ -415,7 +415,7 @@
     numbers = jnp.concatenate([jnp.stack([me, lower]).astype(jnp.int32), epoch_owner, valid_rows.reshape(-1)])
     starts = position(me ^ jnp.arange(blocks, dtype=jnp.int32)) * width
     chunks = list(cut(starts, jnp.concatenate([images, variance]), blocks))
-    for step in range(1, blocks):
+    for step in sorted(range(1, blocks), key=lambda step: (step & (step - 1) > 0, step)):
         chunks[step] = lax.ppermute(chunks[step], "vel", [(i, i ^ step) for i in range(blocks)])
     chunks[1], spread_kernel, numbers = lax.optimization_barrier((chunks[1], spread_kernel, numbers))
     bands, floor = make_bands(spread_kernel)

time: 95.7 us -> 95.7 us (level)
  no operation moved by 1% of the time
where the time goes in v13:
time: 95.7 us; the launch traced here: 95.4 us
  Pallas kernels  50.8 us (53%)
  starting transfers between devices  23.6 us (25%)
  waiting for transfers between devices  12.4 us (13%)
  local copies, waits for them, and re-layouts  5.38 us (6%)
  other arithmetic  2.95 us (3%)
    pallas_call x5, Pallas kernels, stack_tiles(): pl.pallas_call(functools.partial(stack_kernel, segments=described, source...  38.1 us
    ppermute x7, starting transfers between devices, local(): lax.ppermute(chunks[step], 'vel', [(i, i ^ step) for i in range(blocks)])  14.7 us
    pallas_call x1, Pallas kernels, correlate(): pl.pallas_call(functools.partial(correlate_kernel, ksize=ksize), in_specs...  6.67 us
    pallas_call x1, Pallas kernels, make_bands(): pl.pallas_call(band_kernel, in_specs=[pl.BlockSpec(memory_space=pltpu.SME...  4.41 us
    ppermute x7, waiting for transfers between devices, local(): lax.ppermute(chunks[step], 'vel', [(i, i ^ step) for i in range(blocks)])  4.39 us
    ppermute x3, starting transfers between devices, local(): lax.ppermute(behind, 'vel', right)  4.35 us
    unnamed x5, local copies, waits for them, and re-layouts  3.26 us
    ppermute x1, waiting for transfers between devices, local(): lax.ppermute(payload, 'vel', left)  3.01 us
  transfers between devices with their start and end apart: 20, of which 11 were waited for; matrix products, arithmetic and copies ran while one was open for 5% of the time, Pallas kernels for 38%

profile of v13, /device:TPU:0, one launch (start us, length us, event | category | flops | bytes accessed | tf_op | source)
XLA Modules:
  0.0 95.4 jit_solution(6517096453476448763)
XLA Ops:
  0.0 1.3 %pad_maximum_fusion.pair = f32[2,32,4096]{2,1,0:T(8,128)S(1)} fusion(f32[1,32,4096]{2,1,0:T(8,128)} %param.7, f32[1,32,4096]{2,1,0:T(8,128)} %param.6), kind=kLoop, calls=%fused_computation | loop fusion | flops 262144 | bytes 2097152 | tf_op jit(solution)/shard_map/concatenate | solution.py:417
  2.1 6.1 %collective-permute-start = (f32[2,136,128]{2,1,0:T(8,128)S(1)}, f32[2,136,128]{2,1,0:T(8,128)S(1)}, u32[]{:S(2)}, u32[]{:S(2)}) collective-permute-start(f32[2,136,128]{2,1,0:T(8,128)S(1)} %get-tuple-element.34), channel_id=1, source_target_pairs={{0,14},{2,12},{4,10},{6,8},{8,6},{10,4},{12,2},{14,0},{1,15},{3,13... | collective-permute-start | bytes 417800 | tf_op jit(solution)/shard_map/ppermute | solution.py:419
  8.7 3.0 %collective-permute-start.3 = (f32[2,136,128]{2,1,0:T(8,128)S(1)}, f32[2,136,128]{2,1,0:T(8,128)S(1)}, u32[]{:S(2)}, u32[]{:S(2)}) collective-permute-start(f32[2,136,128]{2,1,0:T(8,128)S(1)} %get-tuple-element.43), channel_id=1, source_target_pairs={{0,6},{2,4},{4,2},{6,0},{8,14},{10,12},{12,10},{14,8},{1,7},{3,5},... | collective-permute-start | bytes 417800 | tf_op jit(solution)/shard_map/ppermute | solution.py:419
  11.7 1.1 %collective-permute-done.refs_7_ = f32[2,136,128]{2,1,0:T(8,128)S(1)} collective-permute-done((f32[2,136,128]{2,1,0:T(8,128)S(1)}, f32[2,136,128]{2,1,0:T(8,128)S(1)}, u32[]{:S(2)}, u32[]{:S(2)}) %collective-permute-start) | collective-permute-done | bytes 139296 | tf_op jit(solution)/shard_map/ppermute | solution.py:419
  12.7 4.8 %collective-permute-start.5 = (f32[2,136,128]{2,1,0:T(8,128)S(1)}, f32[2,136,128]{2,1,0:T(8,128)S(1)}, u32[]{:S(2)}, u32[]{:S(2)}) collective-permute-start(f32[2,136,128]{2,1,0:T(8,128)S(1)} %get-tuple-element.45), channel_id=1, source_target_pairs={{0,10},{2,8},{4,14},{6,12},{8,2},{10,0},{12,6},{14,4},{1,11},{3,9}... | collective-permute-start | bytes 417800 | tf_op jit(solution)/shard_map/ppermute | solution.py:419
  20.9 4.4 %shard_map.65 = (bf16[2,3456,256]{2,1,0:T(8,128)(2,1)S(1)}, f32[8,128]{1,0:T(8,128)S(1)}) custom-call(f32[441]{0:T(512)S(1)} %reshape.10.taps, f32[21,21]{1,0:T(8,128)S(1)} %copy-done), custom_call_target="tpu_custom_call" | custom-call | bytes 20971520 | tf_op jit(solution)/shard_map/pallas_call | solution.py:54
  25.4 1.8 %copy-done.1 = bf16[2,3456,256]{2,1,0:T(8,128)(2,1)} copy-done((bf16[2,3456,256]{2,1,0:T(8,128)(2,1)}, bf16[2,3456,256]{2,1,0:T(8,128)(2,1)S(1)}, u32[]{:S(2)}) %copy-start.1) | copy-done | bytes 3538968
  27.2 1.0 %collective-permute-done.4.refs_4_ = f32[2,136,128]{2,1,0:T(8,128)S(1)} collective-permute-done((f32[2,136,128]{2,1,0:T(8,128)S(1)}, f32[2,136,128]{2,1,0:T(8,128)S(1)}, u32[]{:S(2)}, u32[]{:S(2)}) %collective-permute-start.4) | collective-permute-done | bytes 139296 | tf_op jit(solution)/shard_map/ppermute | solution.py:419
  28.1 2.4 %collective-permute-done.5.refs_5_ = f32[2,136,128]{2,1,0:T(8,128)S(1)} collective-permute-done((f32[2,136,128]{2,1,0:T(8,128)S(1)}, f32[2,136,128]{2,1,0:T(8,128)S(1)}, u32[]{:S(2)}, u32[]{:S(2)}) %collective-permute-start.5) | collective-permute-done | bytes 139296 | tf_op jit(solution)/shard_map/ppermute | solution.py:419
  31.5 1.4 %collective-permute-done.7.border = f32[3,2,5,16,128]{4,3,2,1,0:T(8,128)S(1)} collective-permute-done((f32[3,2,5,16,128]{4,3,2,1,0:T(8,128)S(1)}, f32[3,2,5,16,128]{4,3,2,1,0:T(8,128)S(1)}, u32[]{:S(2)}, u32[]{:S(2)}) %collective-permute-start.7) | collective-permute-done | bytes 245792 | tf_op jit(solution)/shard_map/ppermute | solution.py:424
  32.9 6.7 %shard_map.67.refs_0_.refs_2_ = f32[2,3,2,4,16,128]{5,4,3,2,1,0:T(8,128)S(1)} custom-call(s32[2]{0:T(128)S(1)} %pad_add_fusion.1.place, f32[3,2,5,32,128]{4,3,2,1,0:T(8,128)S(1)} %get-tuple-element.48.own, f32[3,2,5,16,128]{4,3,2,1,0:T(8,128)S(1)} %collective-permute-done.7.border, bf16[2,3456,256]{2,1,0:T(8,128)(2,1)} %copy-done.1), custom_call_target="tpu_custom_call" | custom-call | flops 3623878656 | bytes 12582912 | tf_op jit(solution)/shard_map/pallas_call | solution.py:233
  39.6 1.5 %collective-permute-start.9 = (f32[2,3,2,4,16,128]{5,4,3,2,1,0:T(8,128)S(1)}, f32[2,3,2,4,16,128]{5,4,3,2,1,0:T(8,128)S(1)}, u32[]{:S(2)}, u32[]{:S(2)}) collective-permute-start(f32[2,3,2,4,16,128]{5,4,3,2,1,0:T(8,128)S(1)} %shard_map.67.refs_0_.refs_2_), channel_id=1, source_target_pairs={{4,0},{8,4},{12,8},{14,12},{10,14},{6,10},{2,6},{0,2},{5,1},{9,5},... | collective-permute-start | bytes 1179656 | tf_op jit(solution)/shard_map/ppermute | solution.py:441
  43.4 4.7 %shard_map.68.refs_5_ = f32[36,32,4096]{2,1,0:T(8,128)} custom-call(s32[4]{0:T(128)S(1)} %pad_add_fusion.2.place, s32[216]{0:T(256)S(1)} %add.193.shifts, f32[1]{0:T(128)} %bitcast.7.floor, f32[2,3,2,4,16,128]{5,4,3,2,1,0:T(8,128)S(1)} %shard_map.67.refs_0_.refs_2_, f32[1,3,2,4,16,128]{5,4,3,2,1,0:T(8,128)S(1)} %collective-permute-done.10.refs_1_.refs_3_), custom_call_target="tpu_custom_call" | custom-call | flops 7077888 | bytes 10616832 | tf_op jit(solution)/shard_map/pallas_call | solution.py:370
  48.1 3.0 %collective-permute-done.9.refs_4_ = f32[2,3,2,4,16,128]{5,4,3,2,1,0:T(8,128)S(1)} collective-permute-done((f32[2,3,2,4,16,128]{5,4,3,2,1,0:T(8,128)S(1)}, f32[2,3,2,4,16,128]{5,4,3,2,1,0:T(8,128)S(1)}, u32[]{:S(2)}, u32[]{:S(2)}) %collective-permute-start.9) | collective-permute-done | bytes 393248 | tf_op jit(solution)/shard_map/ppermute | solution.py:441
  51.1 0.9 collective-permute-done.8.refs_0_.refs_2_
  52.1 1.0 %collective-permute-start.11 = (f32[2,3,2,4,16,128]{5,4,3,2,1,0:T(8,128)S(1)}, f32[2,3,2,4,16,128]{5,4,3,2,1,0:T(8,128)S(1)}, u32[]{:S(2)}, u32[]{:S(2)}) collective-permute-start(f32[2,3,2,4,16,128]{5,4,3,2,1,0:T(8,128)S(1)} %collective-permute-done.8.refs_0_.refs_2_), channel_id=1, source_target_pairs={{0,4},{4,8},{8,12},{12,14},{14,10},{10,6},{6,2},{2,0},{1,5},{5,9},... | collective-permute-start | bytes 1179656 | tf_op jit(solution)/shard_map/ppermute | solution.py:448
  53.1 1.1 %collective-permute-start.12 = (f32[2,3,2,4,16,128]{5,4,3,2,1,0:T(8,128)S(1)}, f32[2,3,2,4,16,128]{5,4,3,2,1,0:T(8,128)S(1)}, u32[]{:S(2)}, u32[]{:S(2)}) collective-permute-start(f32[2,3,2,4,16,128]{5,4,3,2,1,0:T(8,128)S(1)} %collective-permute-done.9.refs_4_), channel_id=1, source_target_pairs={{4,0},{8,4},{12,8},{14,12},{10,14},{6,10},{2,6},{0,2},{5,1},{9,5},... | collective-permute-start | bytes 1179656 | tf_op jit(solution)/shard_map/ppermute | solution.py:448
  54.3 9.1 %shard_map.69.refs_6_ = f32[36,32,4096]{2,1,0:T(8,128)} custom-call(s32[9]{0:T(128)S(1)} %stack.151.place, s32[216]{0:T(256)S(1)} %add.193.shifts, f32[1]{0:T(128)} %bitcast.7.floor, f32[2,3,2,4,16,128]{5,4,3,2,1,0:T(8,128)S(1)} %collective-permute-done.8.refs_0_.refs_2_, ...), custom_call_target="tpu_custom_call", output_to_operand_aliasing={{}: (8, {})} | custom-call | flops 18874368 | bytes 28311552 | tf_op jit(solution)/shard_map/pallas_call | solution.py:370
  64.4 1.7 %collective-permute-start.14 = (f32[2,3,2,4,16,128]{5,4,3,2,1,0:T(8,128)S(1)}, f32[2,3,2,4,16,128]{5,4,3,2,1,0:T(8,128)S(1)}, u32[]{:S(2)}, u32[]{:S(2)}) collective-permute-start(f32[2,3,2,4,16,128]{5,4,3,2,1,0:T(8,128)S(1)} %collective-permute-done.11.refs_0_.refs_2_), channel_id=1, source_target_pairs={{0,4},{4,8},{8,12},{12,14},{14,10},{10,6},{6,2},{2,0},{1,5},{5,9},... | collective-permute-start | bytes 1179656 | tf_op jit(solution)/shard_map/ppermute | solution.py:448
  66.6 9.0 %shard_map.70.refs_6_ = f32[36,32,4096]{2,1,0:T(8,128)} custom-call(s32[9]{0:T(128)S(1)} %stack.160.place, s32[216]{0:T(256)S(1)} %add.193.shifts, f32[1]{0:T(128)} %bitcast.7.floor, f32[2,3,2,4,16,128]{5,4,3,2,1,0:T(8,128)S(1)} %collective-permute-done.11.refs_0_.refs_2_, ...), custom_call_target="tpu_custom_call", output_to_operand_aliasing={{}: (9, {})} | custom-call | flops 18874368 | bytes 28311552 | tf_op jit(solution)/shard_map/pallas_call | solution.py:370
  75.9 1.4 %collective-permute-done.15.refs_5_.refs_0_ = f32[2,3,2,4,16,128]{5,4,3,2,1,0:T(8,128)S(1)} collective-permute-done((f32[2,3,2,4,16,128]{5,4,3,2,1,0:T(8,128)S(1)}, f32[2,3,2,4,16,128]{5,4,3,2,1,0:T(8,128)S(1)}, u32[]{:S(2)}, u32[]{:S(2)}) %collective-permute-start.15) | collective-permute-done | bytes 393248 | tf_op jit(solution)/shard_map/ppermute | solution.py:448
  77.5 1.6 %collective-permute-start.18 = (f32[2,3,2,4,16,128]{5,4,3,2,1,0:T(8,128)S(1)}, f32[2,3,2,4,16,128]{5,4,3,2,1,0:T(8,128)S(1)}, u32[]{:S(2)}, u32[]{:S(2)}) collective-permute-start(f32[2,3,2,4,16,128]{5,4,3,2,1,0:T(8,128)S(1)} %collective-permute-done.14.refs_0_.refs_4_), channel_id=1, source_target_pairs={{0,4},{4,8},{8,12},{12,14},{14,10},{10,6},{6,2},{2,0},{1,5},{5,9},... | collective-permute-start | bytes 1179656 | tf_op jit(solution)/shard_map/ppermute | solution.py:455
  80.0 9.0 %shard_map.71.refs_5_ = f32[36,32,4096]{2,1,0:T(8,128)} custom-call(s32[9]{0:T(128)S(1)} %stack.169.place, s32[216]{0:T(256)S(1)} %add.193.shifts, f32[1]{0:T(128)} %bitcast.7.floor, f32[2,3,2,4,16,128]{5,4,3,2,1,0:T(8,128)S(1)} %collective-permute-done.14.refs_0_.refs_4_, ...), custom_call_target="tpu_custom_call", output_to_operand_aliasing={{}: (9, {})} | custom-call | flops 18874368 | bytes 28311552 | tf_op jit(solution)/shard_map/pallas_call | solution.py:370
  89.0 6.3 %shard_map.72 = f32[36,32,4096]{2,1,0:T(8,128)} custom-call(s32[6]{0:T(128)S(1)} %stack.135.place, s32[216]{0:T(256)S(1)} %add.193.shifts, f32[1]{0:T(128)} %bitcast.7.floor, f32[2,3,2,4,16,128]{5,4,3,2,1,0:T(8,128)S(1)} %collective-permute-done.15.refs_5_.refs_0_, ...), custom_call_target="tpu_custom_call", output_to_operand_aliasing={{}: (8, {})} | custom-call | flops 11796480 | bytes 17694720 | tf_op jit(solution)/shard_map/pallas_call | solution.py:370
  (56 shorter events, 11.1 us)
Async XLA Ops:
  2.1 10.6 %collective-permute-start = (f32[2,136,128]{2,1,0:T(8,128)S(1)}, f32[2,136,128]{2,1,0:T(8,128)S(1)}, u32[]{:S(2)}, u32[]{:S(2)}) collective-permute-start(f32[2,136,128]{2,1,0:T(8,128)S(1)} %get-tuple-element.34), channel_id=1, source_target_pairs={{0,14},{2,12},{4,10},{6,8},{8,6},{10,4},{12,2},{14,0},{1,15},{3,13... | collective-permute-start | bytes 417800 | tf_op jit(solution)/shard_map/ppermute | solution.py:419
  8.2 9.3 %collective-permute-start.1 = (f32[2,136,128]{2,1,0:T(8,128)S(1)}, f32[2,136,128]{2,1,0:T(8,128)S(1)}, u32[]{:S(2)}, u32[]{:S(2)}) collective-permute-start(f32[2,136,128]{2,1,0:T(8,128)S(1)} %get-tuple-element.35), channel_id=1, source_target_pairs={{0,2},{2,0},{4,6},{6,4},{8,10},{10,8},{12,14},{14,12},{1,3},{3,1},... | collective-permute-start | bytes 417800 | tf_op jit(solution)/shard_map/ppermute | solution.py:419
  8.7 18.5 %collective-permute-start.2 = (f32[2,136,128]{2,1,0:T(8,128)S(1)}, f32[2,136,128]{2,1,0:T(8,128)S(1)}, u32[]{:S(2)}, u32[]{:S(2)}) collective-permute-start(f32[2,136,128]{2,1,0:T(8,128)S(1)} %get-tuple-element.42), channel_id=1, source_target_pairs={{0,4},{2,6},{4,0},{6,2},{8,12},{10,14},{12,8},{14,10},{1,5},{3,7},... | collective-permute-start | bytes 417800 | tf_op jit(solution)/shard_map/ppermute | solution.py:419
  8.7 18.5 %collective-permute-start.3 = (f32[2,136,128]{2,1,0:T(8,128)S(1)}, f32[2,136,128]{2,1,0:T(8,128)S(1)}, u32[]{:S(2)}, u32[]{:S(2)}) collective-permute-start(f32[2,136,128]{2,1,0:T(8,128)S(1)} %get-tuple-element.43), channel_id=1, source_target_pairs={{0,6},{2,4},{4,2},{6,0},{8,14},{10,12},{12,10},{14,8},{1,7},{3,5},... | collective-permute-start | bytes 417800 | tf_op jit(solution)/shard_map/ppermute | solution.py:419
  11.7 16.5 %collective-permute-start.4 = (f32[2,136,128]{2,1,0:T(8,128)S(1)}, f32[2,136,128]{2,1,0:T(8,128)S(1)}, u32[]{:S(2)}, u32[]{:S(2)}) collective-permute-start(f32[2,136,128]{2,1,0:T(8,128)S(1)} %get-tuple-element.44), channel_id=1, source_target_pairs={{0,8},{2,10},{4,12},{6,14},{8,0},{10,2},{12,4},{14,6},{1,9},{3,11}... | collective-permute-start | bytes 417800 | tf_op jit(solution)/shard_map/ppermute | solution.py:419
  12.7 17.8 %collective-permute-start.5 = (f32[2,136,128]{2,1,0:T(8,128)S(1)}, f32[2,136,128]{2,1,0:T(8,128)S(1)}, u32[]{:S(2)}, u32[]{:S(2)}) collective-permute-start(f32[2,136,128]{2,1,0:T(8,128)S(1)} %get-tuple-element.45), channel_id=1, source_target_pairs={{0,10},{2,8},{4,14},{6,12},{8,2},{10,0},{12,6},{14,4},{1,11},{3,9}... | collective-permute-start | bytes 417800 | tf_op jit(solution)/shard_map/ppermute | solution.py:419
  17.5 13.0 %collective-permute-start.6 = (f32[2,136,128]{2,1,0:T(8,128)S(1)}, f32[2,136,128]{2,1,0:T(8,128)S(1)}, u32[]{:S(2)}, u32[]{:S(2)}) collective-permute-start(f32[2,136,128]{2,1,0:T(8,128)S(1)} %get-tuple-element.46), channel_id=1, source_target_pairs={{0,12},{2,14},{4,8},{6,10},{8,4},{10,6},{12,0},{14,2},{1,13},{3,15... | collective-permute-start | bytes 417800 | tf_op jit(solution)/shard_map/ppermute | solution.py:419
  20.2 0.7 copy-start
  25.4 1.8 %copy-start.1 = (bf16[2,3456,256]{2,1,0:T(8,128)(2,1)}, bf16[2,3456,256]{2,1,0:T(8,128)(2,1)S(1)}, u32[]{:S(2)}) copy-start(bf16[2,3456,256]{2,1,0:T(8,128)(2,1)S(1)} %get-tuple-element.50.bands_hbm) | copy-start | bytes 10616836
  31.4 1.6 %collective-permute-start.7 = (f32[3,2,5,16,128]{4,3,2,1,0:T(8,128)S(1)}, f32[3,2,5,16,128]{4,3,2,1,0:T(8,128)S(1)}, u32[]{:S(2)}, u32[]{:S(2)}) collective-permute-start(f32[3,2,5,16,128]{4,3,2,1,0:T(8,128)S(1)} %get-tuple-element.49), channel_id=1, source_target_pairs={{0,1},{1,0},{2,3},{3,2},{4,5},{5,4},{6,7},{7,6},{8,9},{9,8},{10,11... | collective-permute-start | bytes 737288 | tf_op jit(solution)/shard_map/ppermute | solution.py:424
  39.6 11.5 %collective-permute-start.9 = (f32[2,3,2,4,16,128]{5,4,3,2,1,0:T(8,128)S(1)}, f32[2,3,2,4,16,128]{5,4,3,2,1,0:T(8,128)S(1)}, u32[]{:S(2)}, u32[]{:S(2)}) collective-permute-start(f32[2,3,2,4,16,128]{5,4,3,2,1,0:T(8,128)S(1)} %shard_map.67.refs_0_.refs_2_), channel_id=1, source_target_pairs={{4,0},{8,4},{12,8},{14,12},{10,14},{6,10},{2,6},{0,2},{5,1},{9,5},... | collective-permute-start | bytes 1179656 | tf_op jit(solution)/shard_map/ppermute | solution.py:441
  41.1 10.9 %collective-permute-start.8 = (f32[2,3,2,4,16,128]{5,4,3,2,1,0:T(8,128)S(1)}, f32[2,3,2,4,16,128]{5,4,3,2,1,0:T(8,128)S(1)}, u32[]{:S(2)}, u32[]{:S(2)}) collective-permute-start(f32[2,3,2,4,16,128]{5,4,3,2,1,0:T(8,128)S(1)} %shard_map.67.refs_0_.refs_2_), channel_id=1, source_target_pairs={{0,4},{4,8},{8,12},{12,14},{14,10},{10,6},{6,2},{2,0},{1,5},{5,9},... | collective-permute-start | bytes 1179656 | tf_op jit(solution)/shard_map/ppermute | solution.py:441
  41.7 1.7 %collective-permute-start.10 = (f32[1,3,2,4,16,128]{5,4,3,2,1,0:T(8,128)S(1)}, f32[1,3,2,4,16,128]{5,4,3,2,1,0:T(8,128)S(1)}, u32[]{:S(2)}, u32[]{:S(2)}) collective-permute-start(f32[1,3,2,4,16,128]{5,4,3,2,1,0:T(8,128)S(1)} %slice.36), channel_id=1, source_target_pairs={{0,1},{1,0},{2,3},{3,2},{4,5},{5,4},{6,7},{7,6},{8,9},{9,8},{10,11... | collective-permute-start | bytes 589832 | tf_op jit(solution)/shard_map/ppermute | solution.py:442
  52.0 2.2 %collective-permute-start.13 = (f32[2,3,2,4,16,128]{5,4,3,2,1,0:T(8,128)S(1)}, f32[2,3,2,4,16,128]{5,4,3,2,1,0:T(8,128)S(1)}, u32[]{:S(2)}, u32[]{:S(2)}) collective-permute-start(f32[2,3,2,4,16,128]{5,4,3,2,1,0:T(8,128)S(1)} %pad_maximum_fusion.1), channel_id=1, source_target_pairs={{0,1},{1,0},{2,3},{3,2},{4,5},{5,4},{6,7},{7,6},{8,9},{9,8},{10,11... | collective-permute-start | bytes 1179656 | tf_op jit(solution)/shard_map/ppermute | solution.py:450
  52.1 11.5 %collective-permute-start.11 = (f32[2,3,2,4,16,128]{5,4,3,2,1,0:T(8,128)S(1)}, f32[2,3,2,4,16,128]{5,4,3,2,1,0:T(8,128)S(1)}, u32[]{:S(2)}, u32[]{:S(2)}) collective-permute-start(f32[2,3,2,4,16,128]{5,4,3,2,1,0:T(8,128)S(1)} %collective-permute-done.8.refs_0_.refs_2_), channel_id=1, source_target_pairs={{0,4},{4,8},{8,12},{12,14},{14,10},{10,6},{6,2},{2,0},{1,5},{5,9},... | collective-permute-start | bytes 1179656 | tf_op jit(solution)/shard_map/ppermute | solution.py:448
  53.1 11.2 %collective-permute-start.12 = (f32[2,3,2,4,16,128]{5,4,3,2,1,0:T(8,128)S(1)}, f32[2,3,2,4,16,128]{5,4,3,2,1,0:T(8,128)S(1)}, u32[]{:S(2)}, u32[]{:S(2)}) collective-permute-start(f32[2,3,2,4,16,128]{5,4,3,2,1,0:T(8,128)S(1)} %collective-permute-done.9.refs_4_), channel_id=1, source_target_pairs={{4,0},{8,4},{12,8},{14,12},{10,14},{6,10},{2,6},{0,2},{5,1},{9,5},... | collective-permute-start | bytes 1179656 | tf_op jit(solution)/shard_map/ppermute | solution.py:448
  64.3 2.2 %collective-permute-start.16 = (f32[2,3,2,4,16,128]{5,4,3,2,1,0:T(8,128)S(1)}, f32[2,3,2,4,16,128]{5,4,3,2,1,0:T(8,128)S(1)}, u32[]{:S(2)}, u32[]{:S(2)}) collective-permute-start(f32[2,3,2,4,16,128]{5,4,3,2,1,0:T(8,128)S(1)} %pad_maximum_fusion.2), channel_id=1, source_target_pairs={{0,1},{1,0},{2,3},{3,2},{4,5},{5,4},{6,7},{7,6},{8,9},{9,8},{10,11... | collective-permute-start | bytes 1179656 | tf_op jit(solution)/shard_map/ppermute | solution.py:450
  64.4 11.5 %collective-permute-start.14 = (f32[2,3,2,4,16,128]{5,4,3,2,1,0:T(8,128)S(1)}, f32[2,3,2,4,16,128]{5,4,3,2,1,0:T(8,128)S(1)}, u32[]{:S(2)}, u32[]{:S(2)}) collective-permute-start(f32[2,3,2,4,16,128]{5,4,3,2,1,0:T(8,128)S(1)} %collective-permute-done.11.refs_0_.refs_2_), channel_id=1, source_target_pairs={{0,4},{4,8},{8,12},{12,14},{14,10},{10,6},{6,2},{2,0},{1,5},{5,9},... | collective-permute-start | bytes 1179656 | tf_op jit(solution)/shard_map/ppermute | solution.py:448
  66.2 11.2 %collective-permute-start.15 = (f32[2,3,2,4,16,128]{5,4,3,2,1,0:T(8,128)S(1)}, f32[2,3,2,4,16,128]{5,4,3,2,1,0:T(8,128)S(1)}, u32[]{:S(2)}, u32[]{:S(2)}) collective-permute-start(f32[2,3,2,4,16,128]{5,4,3,2,1,0:T(8,128)S(1)} %collective-permute-done.12.refs_5_.refs_4_), channel_id=1, source_target_pairs={{4,0},{8,4},{12,8},{14,12},{10,14},{6,10},{2,6},{0,2},{5,1},{9,5},... | collective-permute-start | bytes 1179656 | tf_op jit(solution)/shard_map/ppermute | solution.py:448
  77.4 1.8 %collective-permute-start.17 = (f32[2,3,2,4,16,128]{5,4,3,2,1,0:T(8,128)S(1)}, f32[2,3,2,4,16,128]{5,4,3,2,1,0:T(8,128)S(1)}, u32[]{:S(2)}, u32[]{:S(2)}) collective-permute-start(f32[2,3,2,4,16,128]{5,4,3,2,1,0:T(8,128)S(1)} %pad_maximum_fusion.3), channel_id=1, source_target_pairs={{0,1},{1,0},{2,3},{3,2},{4,5},{5,4},{6,7},{7,6},{8,9},{9,8},{10,11... | collective-permute-start | bytes 1179656 | tf_op jit(solution)/shard_map/ppermute | solution.py:450
  77.5 11.5 %collective-permute-start.18 = (f32[2,3,2,4,16,128]{5,4,3,2,1,0:T(8,128)S(1)}, f32[2,3,2,4,16,128]{5,4,3,2,1,0:T(8,128)S(1)}, u32[]{:S(2)}, u32[]{:S(2)}) collective-permute-start(f32[2,3,2,4,16,128]{5,4,3,2,1,0:T(8,128)S(1)} %collective-permute-done.14.refs_0_.refs_4_), channel_id=1, source_target_pairs={{0,4},{4,8},{8,12},{12,14},{14,10},{10,6},{6,2},{2,0},{1,5},{5,9},... | collective-permute-start | bytes 1179656 | tf_op jit(solution)/shard_map/ppermute | solution.py:455
  79.2 9.8 %collective-permute-start.19 = (f32[1,3,2,4,16,128]{5,4,3,2,1,0:T(8,128)S(1)}, f32[1,3,2,4,16,128]{5,4,3,2,1,0:T(8,128)S(1)}, u32[]{:S(2)}, u32[]{:S(2)}) collective-permute-start(f32[1,3,2,4,16,128]{5,4,3,2,1,0:T(8,128)S(1)} %slice.37), channel_id=1, source_target_pairs={{4,0},{8,4},{12,8},{14,12},{10,14},{6,10},{2,6},{0,2},{5,1},{9,5},... | collective-permute-start | bytes 589832 | tf_op jit(solution)/shard_map/ppermute | solution.py:455
